TPU v7x, 32 devices: a whole 2x2x4 slice. The times are simulated.
32 devices in a mesh: dom: 2 (over y), row: 4 (over z), nbr: 4 (over x, core).
Axes of the slice: x: 2, y: 2, z: 4, core: 2. Of those that a mesh axis runs over, the one named last changes fastest.
Arguments:
- blocks: float32 [24, 12, 128, 128], P(('dom', 'row'), 'nbr'), parts along dimension 0, may hold values from -0.15625 to 0.15625
- partner_ids: int32 [24, 12], P(('dom', 'row'), 'nbr'), parts along dimension 0, may hold values from 0 to 11, as said below
- counts: int32 [24], P(('dom', 'row')), parts along dimension 0, may hold values from 1 to 12, as said below
- start: float32 [3072, 32], P(('dom', 'row')), parts along dimension 0, may hold values from -6 to 6
Outputs:
- basis: float32 [3072, 32], P(('dom', 'row')), parts along dimension 0
- ritz: float32 [64, 32], P('dom'), parts along dimension 0
There are 2 independent parts, one for each index of `dom`. A program takes and returns all parts, laid end to end along the dimension named above; each array names one. Nothing has to cross between parts.
Inputs may be any that keep to these rules, and one draw needn't show every extreme that they name: partner_ids[i,0] == i; slots 1 to counts[i] - 1 hold distinct block columns greater than i; slots from counts[i] on hold i. counts[i] <= min(12, 12 - i); counts[0] == 12.
All inputs are finite; a program needn't handle non-finite values.
Results may differ from a plain program's by a relative error of at most 0.0001.
Values sent between devices are 32-bit elements; how exact they have to be, the bound alone decides.
No kernel may reach another device: no remote copies, remote signals or barrier semaphores. Data moves between devices by JAX's collectives and lax.ppermute only.
A program may use at most 64 MiB of HBM per device.

v0:
```python
import jax
import jax.numpy as jnp
from jax import lax
from jax.sharding import PartitionSpec as P

ITERS = 2


HIGH = lax.Precision.HIGHEST


def orthonormal(image, gram, total):
    lower = jnp.linalg.cholesky(gram / total)
    return lax.linalg.triangular_solve(lower, image, left_side=False, lower=True, transpose_a=True)


def body(blocks, partner_ids, counts, start):
    block_rows, slots_here = partner_ids.shape
    block_size = blocks.shape[2]
    columns = start.shape[1]
    row_count = lax.axis_size("row")
    all_blocks = block_rows * row_count
    total = all_blocks * block_size
    first_row = lax.axis_index("row") * block_rows
    rows_here = first_row + jnp.arange(block_rows, dtype=jnp.int32)
    slot_index = lax.axis_index("nbr") * slots_here + jnp.arange(slots_here, dtype=jnp.int32)
    valid = slot_index[None, :] < counts[:, None]
    weight = jnp.where(valid, jnp.where(partner_ids == rows_here[:, None], 0.5, 1.0), 0.0).astype(
        jnp.float32
    )
    targets = jnp.concatenate([partner_ids.reshape(-1), rows_here])
    whole = lax.all_gather(start, "row", axis=0, tiled=True)
    cross = jnp.zeros((columns, columns), jnp.float32)
    prior = start
    for step in range(ITERS):
        tiles = whole.reshape(all_blocks, block_size, columns)
        far = tiles[partner_ids] * weight[:, :, None, None]
        near = lax.dynamic_slice_in_dim(tiles, first_row, block_rows, 0)
        direct = jnp.einsum("ipab,ipbk->iak", blocks, far, precision=HIGH)
        transposed = (
            jnp.einsum("ipab,iak->ipbk", blocks, near, precision=HIGH) * weight[:, :, None, None]
        )
        items = jnp.concatenate(
            [transposed.reshape(block_rows * slots_here, block_size, columns), direct], axis=0
        )
        placed = jnp.zeros((all_blocks, block_size, columns), jnp.float32).at[targets].add(items)
        summed = lax.psum_scatter(
            placed.reshape(total, columns), "row", scatter_dimension=0, tiled=True
        )
        image = lax.psum(summed, "nbr")
        gram, cross = lax.psum(
            (jnp.dot(image.T, image, precision=HIGH), jnp.dot(prior.T, image, precision=HIGH)),
            "row",
        )
        cross = cross / total
        prior = orthonormal(image, gram, total)
        if step + 1 < ITERS:
            whole = lax.all_gather(prior, "row", axis=0, tiled=True)
    return (prior, cross)


def solution(mesh):
    return jax.shard_map(
        body,
        mesh=mesh,
        in_specs=(
            P(("dom", "row"), "nbr", None, None),
            P(("dom", "row"), "nbr"),
            P(("dom", "row")),
            P(("dom", "row"), None),
        ),
        out_specs=(P(("dom", "row"), None), P("dom", None)),
        check_vma=False,
    )
```

profile of v0, /device:TPU:0, one launch (start us, length us, event | category | flops | bytes accessed | tf_op | source)
XLA Modules:
  0.0 161.9 jit_solution(3839742283190382437)
XLA Ops:
  7.2 0.0 copy-start
  7.2 0.0 copy-start.1
  7.2 0.0 reduce-scatter.3.cloned.1.call-start
  7.2 0.8 concatenate.32
  8.1 0.0 copy-done.1
  8.1 0.1 reshape.123
  8.2 15.7 %all_gather.6 = f32[1536,32]{0,1:T(8,128)S(1)} all-gather(f32[384,32]{0,1:T(8,128)} %param.10), channel_id=1, replica_groups=mesh['dom'=2,'row'=4,'nbr'=4] {'row'}, dimensions={0}, use_global_device_ids=true | all-gather | bytes 245760 | tf_op jit(solution)/shard_map/all_gather | solution.py:32
  23.8 0.6 gather_fusion
  24.4 0.0 copy-start.2
  24.4 0.6 copy-done.2
  25.1 0.1 select_select_fusion.2
  25.1 0.0 copy-done
  25.1 0.5 convolution_multiply_fusion.1
  25.6 0.8 convolution_bitcast_fusion.3
  26.4 0.1 fusion.16
  26.5 1.1 scatter_fusion
  27.6 0.7 copy_bitcast_fusion.1
  28.3 0.0 reduce-scatter.3.cloned.1.call-update
  28.3 0.0 reduce-scatter.5.cloned.1.call-start
  28.4 20.8 %reduce-scatter.3.cloned.1.call-done = f32[384,32]{0,1:T(8,128)} async-done(((f32[1536,32]{0,1:T(8,128)}), f32[384,32]{0,1:T(8,128)}) %reduce-scatter.3.cloned.1.call-update) | async-done | bytes 49168 | tf_op jit(solution)/shard_map/reduce_scatter | solution.py:47
  49.2 11.0 %psum.35 = f32[384,32]{0,1:T(8,128)S(1)} all-reduce(f32[384,32]{0,1:T(8,128)} %reduce-scatter.3.cloned.1.call-done), channel_id=1, replica_groups=mesh['dom'=2,'row'=4,'nbr'=4] {'nbr'}, use_global_device_ids=true, to_apply=%region_2.3 | all-reduce | flops 12288 | bytes 98304 | tf_op jit(solution)/shard_map/psum | solution.py:50
  60.2 0.2 fusion.20
  60.4 15.9 %psum.36 = f32[32,32]{0,1:T(8,128)S(1)} all-reduce(f32[32,32]{0,1:T(8,128)S(1)} %fusion.20), channel_id=1, replica_groups=mesh['dom'=2,'row'=4,'nbr'=4] {'row'}, use_global_device_ids=true, to_apply=%region_3.4 | all-reduce | flops 1024 | bytes 8192 | tf_op jit(solution)/shard_map/psum | solution.py:51
  76.3 0.1 copy.30
  76.3 2.9 %cholesky.44 = f32[32,32]{1,0:T(8,128)S(1)} custom-call(f32[32,32]{1,0:T(8,128)S(1)} %fusion.13), custom_call_target="Cholesky" | custom-call | tf_op jit(solution)/shard_map/jit(cholesky)/cholesky | solution.py:13
  79.3 0.6 compare_reduce_fusion.1
  79.9 0.7 fusion.8
  80.6 2.4 %custom-call.6 = f32[1,32,32]{1,2,0:T(8,128)S(1)} custom-call(f32[1,32,32]{2,1,0:T(8,128)S(1)} %fusion.8), custom_call_target="InvertDiagBlocksLowerTriangular" | custom-call | tf_op jit(solution)/shard_map/triangular_solve/custom-call.0 | solution.py:14
  83.0 0.3 convolution_bitcast_fusion.2
  83.3 13.6 %all_gather.7 = f32[1536,32]{0,1:T(8,128)S(1)} all-gather(f32[384,32]{0,1:T(8,128)S(1)} %convolution_bitcast_fusion.2), channel_id=1, replica_groups=mesh['dom'=2,'row'=4,'nbr'=4] {'row'}, dimensions={0}, use_global_device_ids=true | all-gather | bytes 245760 | tf_op jit(solution)/shard_map/all_gather | solution.py:58
  96.9 0.6 gather_fusion.1
  97.5 0.5 convolution_multiply_fusion
  97.9 0.8 convolution_bitcast_fusion.1
  98.8 1.1 scatter_fusion.1
  99.8 0.7 copy_bitcast_fusion
  100.5 0.0 reduce-scatter.5.cloned.1.call-update
  100.6 18.6 %reduce-scatter.5.cloned.1.call-done = f32[384,32]{0,1:T(8,128)} async-done(((f32[1536,32]{0,1:T(8,128)}), f32[384,32]{0,1:T(8,128)}) %reduce-scatter.5.cloned.1.call-update) | async-done | bytes 49168 | tf_op jit(solution)/shard_map/reduce_scatter | solution.py:47
  119.1 11.0 %psum.37 = f32[384,32]{0,1:T(8,128)S(1)} all-reduce(f32[384,32]{0,1:T(8,128)} %reduce-scatter.5.cloned.1.call-done), channel_id=1, replica_groups=mesh['dom'=2,'row'=4,'nbr'=4] {'nbr'}, use_global_device_ids=true, to_apply=%region_8.11 | all-reduce | flops 12288 | bytes 98304 | tf_op jit(solution)/shard_map/psum | solution.py:50
  130.1 0.2 fusion.22
  130.3 0.2 fusion.21
  130.5 16.2 %all-reduce = (f32[32,32]{0,1:T(8,128)S(1)}, f32[32,32]{0,1:T(8,128)S(1)}) all-reduce(f32[32,32]{0,1:T(8,128)S(1)} %fusion.21, f32[32,32]{0,1:T(8,128)S(1)} %fusion.22), channel_id=1, replica_groups=mesh['dom'=2,'row'=4,'nbr'=4] {'row'}, use_global_device_ids=true, to_apply=%region_9.12 | all-reduce | flops 2048 | bytes 16384 | tf_op jit(solution)/shard_map/psum | solution.py:51
  146.7 0.7 copy.37
  147.4 0.1 copy.35
  147.5 2.9 %cholesky.55 = f32[32,32]{1,0:T(8,128)S(1)} custom-call(f32[32,32]{1,0:T(8,128)S(1)} %fusion.11), custom_call_target="Cholesky" | custom-call | tf_op jit(solution)/shard_map/jit(cholesky)/cholesky | solution.py:13
  150.5 0.6 compare_reduce_fusion
  151.1 0.7 fusion.9
  151.8 2.4 %custom-call.7 = f32[1,32,32]{1,2,0:T(8,128)S(1)} custom-call(f32[1,32,32]{2,1,0:T(8,128)S(1)} %fusion.9), custom_call_target="InvertDiagBlocksLowerTriangular" | custom-call | tf_op jit(solution)/shard_map/triangular_solve/custom-call.0 | solution.py:14
  154.2 0.9 convolution_bitcast_fusion
  (17 shorter events, 0.2 us)
Async XLA Ops:
  7.2 18.0 %copy-start = (f32[3,3,128,128]{3,2,1,0:T(8,128)S(1)}, f32[3,3,128,128]{3,2,1,0:T(8,128)}, u32[]{:S(2)}) copy-start(f32[3,3,128,128]{3,2,1,0:T(8,128)} %param.7) | copy-start | bytes 1769476
  7.2 0.9 copy-start.1
  7.2 42.0 %reduce-scatter.3.cloned.1.call-start = ((), (), s32[]{:S(2)}) async-start(), calls=%async_computation.2 | async-start | bytes 245760 | tf_op jit(solution)/shard_map/reduce_scatter | solution.py:47
  24.4 0.7 copy-start.2
  28.3 90.8 %reduce-scatter.5.cloned.1.call-start = ((), (), s32[]{:S(2)}) async-start(), calls=%async_computation.3 | async-start | bytes 245760 | tf_op jit(solution)/shard_map/reduce_scatter | solution.py:47
Sparse Core Ops, SparseCore 0:
  28.4 20.6 reduce-scatter.2
  100.7 18.3 reduce-scatter.4
where the time goes:
time: 163 us; the launch traced here: 162 us
  blocking collectives  83.3 us (51%)
  waiting for transfers between devices  39.4 us (24%)
  other arithmetic  15.8 us (10%)
  between operations  14.3 us (9%)
  local copies, waits for them, and re-layouts  4.93 us (3%)
  matrix products  4.18 us (3%)
    reduce_scatter x2, waiting for transfers between devices, body(): lax.psum_scatter(placed.reshape(total, columns), 'row', scatter_dimension...  39.3 us
    psum x2, blocking collectives, body(): lax.psum((jnp.dot(image.T, image, precision=HIGH), jnp.dot(prior.T, image...  32.1 us
    psum x2, blocking collectives, body(): image = lax.psum(summed, 'nbr')  22 us
    all_gather x1, blocking collectives, body(): whole = lax.all_gather(start, 'row', axis=0, tiled=True)  15.7 us
    all_gather x1, blocking collectives, body(): whole = lax.all_gather(prior, 'row', axis=0, tiled=True)  13.6 us
    another operation x6, other arithmetic, orthonormal(): lower = jnp.linalg.cholesky(gram / total)  7.19 us
    another operation x4, other arithmetic, orthonormal(): lax.linalg.triangular_solve(lower, image, left_side=False, lower=True, tr...  6.17 us
  transfers between devices with their start and end apart: 2, of which 2 were waited for; matrix products, arithmetic and copies ran while one was open for 0% of the time, Pallas kernels for 0%

commit v1 on v0

v1 whole, which is shorter than its diff:
```python
import functools

import jax
import jax.numpy as jnp
from jax import lax
from jax.experimental import pallas as pl
from jax.experimental.pallas import tpu as pltpu
from jax.sharding import PartitionSpec as P

HIGH = lax.Precision.HIGHEST
F32 = jnp.float32
VMEM = pl.BlockSpec(memory_space=pltpu.VMEM)
SMEM = pl.BlockSpec(memory_space=pltpu.SMEM)
PANEL = 8


def tree(parts):
    while len(parts) > 1:
        parts = [parts[i] + parts[i + 1] for i in range(0, len(parts), 2)]
    return parts[0]


def swap(x, axis, distance):
    return lax.ppermute(x, axis, [(i, i ^ distance) for i in range(lax.axis_size(axis))])


def mm(a, b):
    return lax.dot_general(a, b, (((1,), (0,)), ((), ())), precision=HIGH, preferred_element_type=F32)


def mm_t(a, b):
    return lax.dot_general(a, b, (((1,), (1,)), ((), ())), precision=HIGH, preferred_element_type=F32)


def weight_of(ids, counts, i, p, first_row, first_slot):
    used = first_slot + p < counts[i]
    return jnp.where(used, jnp.where(ids[i, p] == first_row + i, 0.5, 1.0), 0.0).astype(F32)


def transposed_products(blocks, ids, counts, image, out, first_row, first_slot):
    out[...] = jnp.zeros_like(out)
    for i in range(blocks.shape[0]):
        tile = image[i]
        for p in range(blocks.shape[1]):
            w = weight_of(ids, counts, i, p, first_row, first_slot)
            out[ids[i, p]] += mm(tile, blocks[i, p]) * w


def direct_products(blocks, ids, counts, whole, i, first_row, first_slot):
    total = None
    for p in range(blocks.shape[1]):
        w = weight_of(ids, counts, i, p, first_row, first_slot)
        term = mm_t(whole[ids[i, p]] * w, blocks[i, p])
        total = term if total is None else total + term
    return total


def place(block_rows, slots):
    row = lax.axis_index("row")
    return row, row * block_rows, lax.axis_index("nbr") * slots


def fill(messages, products, tiles, row, block_rows):
    for s, out in enumerate(messages, 1):
        peer = row ^ s
        for i in range(block_rows):
            out[i] = jnp.where(row < peer, products[peer * block_rows + i], tiles[i])


def first_kernel(rows, blocks, ids, counts, start, *refs):
    messages, (own, tiles), (products,) = refs[: rows - 1], refs[rows - 1 : rows + 1], refs[rows + 1 :]
    block_rows, slots, size, _ = blocks.shape
    row, first_row, first_slot = place(block_rows, slots)
    for i in range(block_rows):
        tiles[i] = start[i * size : (i + 1) * size, :].T
    transposed_products(blocks, ids, counts, tiles, products, first_row, first_slot)
    fill(messages, products, tiles, row, block_rows)
    own[...] = products[pl.ds(first_row, block_rows)]


def direct_kernel(rows, with_gram, blocks, ids, counts, own, tiles, *refs):
    received, refs = refs[: rows - 1], refs[rows - 1 :]
    if with_gram:
        gram, out, total, whole = refs
    else:
        out, whole = refs
    block_rows, slots, size, _ = blocks.shape
    row, first_row, first_slot = place(block_rows, slots)
    whole[pl.ds(first_row, block_rows)] = tiles[...]
    for s, message in enumerate(received, 1):
        whole[pl.ds((row ^ s) * block_rows, block_rows)] = message[:block_rows]
    for i in range(block_rows):
        value = own[i]
        for s, message in enumerate(received, 1):
            value += jnp.where(row > (row ^ s), message[i], 0.0)
        out[i] = value + direct_products(blocks, ids, counts, whole, i, first_row, first_slot)
    if with_gram:
        total[...] = tree([gram[...]] + [m[block_rows] for m in received])


def second_kernel(rows, parts, blocks, ids, counts, *refs):
    images, refs = refs[:parts], refs[parts:]
    messages, (own, tiles, gram, products) = refs[: rows - 1], refs[rows - 1 :]
    block_rows, slots, size, _ = blocks.shape
    row, first_row, first_slot = place(block_rows, slots)
    partial = None
    for i in range(block_rows):
        tile = tree([image[i] for image in images])
        tiles[i] = tile
        term = mm_t(tile, tile)
        partial = term if partial is None else partial + term
    columns = partial.shape[0]
    gram[...] = jnp.zeros_like(gram)
    gram[:, :columns] = partial
    transposed_products(blocks, ids, counts, tiles, products, first_row, first_slot)
    fill(messages, products, tiles, row, block_rows)
    for message in messages:
        message[block_rows] = gram[...]
    own[...] = products[pl.ds(first_row, block_rows)]


def inverse_factor(gram):
    n = gram.shape[0]
    rows = lax.broadcasted_iota(jnp.int32, (n, 2 * n), 0)
    lanes = lax.broadcasted_iota(jnp.int32, (n, 2 * n), 1)
    both = jnp.concatenate([jnp.where(rows == lanes, 1.0, 0.0)[:, :n], gram], axis=1)
    groups = [both[g : g + 8] for g in range(0, n, 8)]
    height = lax.broadcasted_iota(jnp.int32, (8, 2 * n), 0)
    for first in range(0, n, PANEL):
        g0 = first // 8
        columns = [
            [
                jnp.broadcast_to(group[:, n + first + t : n + first + t + 1], (8, 2 * n))
                for group in groups
            ]
            for t in range(PANEL)
        ]
        for t in range(PANEL):
            k = first + t
            gk, sk = k // 8, k % 8
            pivot = columns[t][gk][sk : sk + 1]
            inverse = 1.0 / pivot
            root = lax.rsqrt(pivot)
            source = groups[gk][sk : sk + 1]
            steps = {}
            for g in range(gk, len(groups)):
                m = columns[t][g] * inverse
                steps[g] = jnp.where(height > sk, m, 0.0) if g == gk else m
            for u in range(t + 1, PANEL):
                head = columns[u][gk][sk : sk + 1]
                for g in range(gk, len(groups)):
                    columns[u][g] = columns[u][g] - steps[g] * head
            for g in range(gk, len(groups)):
                groups[g] = groups[g] - steps[g] * source
            groups[gk] = jnp.where(height == sk, groups[gk] * root, groups[gk])
    return jnp.concatenate(groups, axis=0)[:, :n]


def factor_kernel(total, gram, out):
    columns = gram.shape[0]
    out[...] = inverse_factor(gram[:, :columns] / total)


def gram_kernel(parts, inverse, tiles, *refs):
    images, (image, out) = refs[:parts], refs[parts:]
    lower = inverse[...]
    gram, cross = None, None
    for i in range(tiles.shape[0]):
        tile = mm(lower, tree([part[i] for part in images]))
        prior = mm(lower, tiles[i])
        image[i] = tile
        g, c = mm_t(tile, tile), mm_t(prior, tile)
        gram, cross = (g, c) if gram is None else (gram + g, cross + c)
    out[...] = jnp.concatenate([gram, cross], axis=1)


def last_kernel(rows, total, image, *refs):
    parts, (basis, ritz) = refs[:rows], refs[rows:]
    both = tree([part[...] for part in parts]) / total
    columns = both.shape[0]
    ritz[...] = both[:, columns:]
    lower = inverse_factor(both[:, :columns])
    size = image.shape[2]
    for i in range(image.shape[0]):
        basis[i * size : (i + 1) * size, :] = mm(lower, image[i]).T


def body(blocks, partner_ids, counts, start):
    block_rows, slots, size, _ = blocks.shape
    columns = start.shape[1]
    rows, parts = lax.axis_size("row"), lax.axis_size("nbr")
    all_blocks = block_rows * rows
    total = float(all_blocks * size)
    shape = jax.ShapeDtypeStruct
    tile = shape((block_rows, columns, size), F32)
    longer = shape((block_rows + 1, columns, size), F32)
    wide = shape((columns, size), F32)
    work = [pltpu.VMEM((all_blocks, columns, size), F32)]
    index = [VMEM, SMEM, SMEM]
    stored = (blocks, partner_ids, counts)

    def call(kernel, name, specs, outs, scratch=()):
        return pl.pallas_call(
            kernel, name=name, in_specs=specs, out_specs=[VMEM] * len(outs), out_shape=outs, scratch_shapes=scratch
        )

    *messages, own, tiles = call(
        functools.partial(first_kernel, rows), "start_products", index + [VMEM], [tile] * (rows + 1), work
    )(*stored, start)
    received = [swap(m, "row", s) for s, m in enumerate(messages, 1)]
    (image,) = call(
        functools.partial(direct_kernel, rows, False), "direct_first", index + [VMEM] * (rows + 1), [tile], work
    )(*stored, own, tiles, *received)
    images = [image] + [swap(image, "nbr", s) for s in range(1, parts)]
    *messages, own, tiles, gram = call(
        functools.partial(second_kernel, rows, parts),
        "second_products",
        index + [VMEM] * parts,
        [longer] * (rows - 1) + [tile, tile, wide],
        work,
    )(*stored, *images)
    received = [swap(m, "row", s) for s, m in enumerate(messages, 1)]
    image, gram = call(
        functools.partial(direct_kernel, rows, True), "direct_second", index + [VMEM] * (rows + 2), [tile, wide], work
    )(*stored, own, tiles, *received, gram)
    images = [image] + [swap(image, "nbr", s) for s in range(1, parts)]
    (inverse,) = call(
        functools.partial(factor_kernel, total), "factor", [VMEM], [shape((columns, columns), F32)]
    )(gram)
    image, both = call(
        functools.partial(gram_kernel, parts),
        "gram",
        [VMEM] * (parts + 2),
        [tile, shape((columns, 2 * columns), F32)],
    )(inverse, tiles, *images)
    boths = [both] + [swap(both, "row", s) for s in range(1, rows)]
    basis, ritz = call(
        functools.partial(last_kernel, rows, total),
        "last",
        [VMEM] * (rows + 1),
        [shape(start.shape, F32), shape((columns, columns), F32)],
    )(image, *boths)
    return basis, ritz


def solution(mesh):
    return jax.shard_map(
        body,
        mesh=mesh,
        in_specs=(
            P(("dom", "row"), "nbr", None, None),
            P(("dom", "row"), "nbr"),
            P(("dom", "row")),
            P(("dom", "row"), None),
        ),
        out_specs=(P(("dom", "row"), None), P("dom", None)),
        check_vma=False,
    )
```

time: 163 us -> 61.5 us (0.38)
  blocking collectives: 83.3 us -> 0 us
  waiting for transfers between devices: 39.4 us -> 17 us
  starting transfers between devices: 0.08 us -> 18.1 us
  Pallas kernels: 0 us -> 17.6 us
  other arithmetic: 15.8 us -> 0 us
  between operations: 14.3 us -> 0.69 us
  matrix products: 4.18 us -> 0 us
  local copies, waits for them, and re-layouts: 4.93 us -> 7.58 us
    psum x4 -> x0, blocking collectives: 54.1 us -> none  [the longest x2 32.1 us: body(): lax.psum((jnp.dot(image.T, image, precision=HIGH), jnp.dot(prior.T, image...]
    reduce_scatter x2 -> x0, waiting for transfers between devices: 39.3 us -> none  [body(): lax.psum_scatter(placed.reshape(total, columns), 'row', scatter_dimension...]
    all_gather x2 -> x0, blocking collectives: 29.2 us -> none  [the longest x1 15.7 us: body(): whole = lax.all_gather(start, 'row', axis=0, tiled=True)]
    ppermute x0 -> x15, starting transfers between devices: none -> 18.1 us  [swap(): lax.ppermute(x, axis, [(i, i ^ distance) for i in range(lax.axis_size(axi...]
    pallas_call x0 -> x7, Pallas kernels: none -> 17.6 us  [the longest x1 2.84 us: body(): call(functools.partial(direct_kernel, rows, True), 'direct_second', index...]
    ppermute x0 -> x15, waiting for transfers between devices: none -> 17 us  [swap(): lax.ppermute(x, axis, [(i, i ^ distance) for i in range(lax.axis_size(axi...]
    another operation x10 -> x0, other arithmetic: 13.4 us -> none  [the longest x6 7.19 us: orthonormal(): lower = jnp.linalg.cholesky(gram / total)]
    unnamed x7 -> x31, local copies, waits for them, and re-layouts: 1.34 us -> 5.93 us
  transfers between devices with their start and end apart: 2 -> 15, of which waited for: 2 -> 10; matrix products, arithmetic and copies ran while one was open for 0% -> 0% of each run, Pallas kernels for 0% -> 4%
where the time goes in v1:
time: 61.5 us; the launch traced here: 61 us
  starting transfers between devices  18.1 us (29%)
  Pallas kernels  17.6 us (29%)
  waiting for transfers between devices  17 us (28%)
  local copies, waits for them, and re-layouts  7.58 us (12%)
  between operations  0.69 us (1%)
    ppermute x15, starting transfers between devices, swap(): lax.ppermute(x, axis, [(i, i ^ distance) for i in range(lax.axis_size(axi...  18.1 us
    ppermute x15, waiting for transfers between devices, swap(): lax.ppermute(x, axis, [(i, i ^ distance) for i in range(lax.axis_size(axi...  17 us
    unnamed x31, local copies, waits for them, and re-layouts  5.93 us
    pallas_call x1, Pallas kernels, body(): call(functools.partial(direct_kernel, rows, True), 'direct_second', index...  2.84 us
    pallas_call x1, Pallas kernels, body(): call(functools.partial(direct_kernel, rows, False), 'direct_first', index...  2.79 us
    pallas_call x1, Pallas kernels, body(): call(functools.partial(last_kernel, rows, total), 'last', [VMEM] * (rows...  2.66 us
    pallas_call x1, Pallas kernels, body(): call(functools.partial(second_kernel, rows, parts), 'second_products', in...  2.51 us
    pallas_call x1, Pallas kernels, body(): call(functools.partial(first_kernel, rows), 'start_products', index + [VM...  2.44 us
  transfers between devices with their start and end apart: 15, of which 10 were waited for; matrix products, arithmetic and copies ran while one was open for 0% of the time, Pallas kernels for 4%

profile of v1, /device:TPU:0, one launch (start us, length us, event | category | flops | bytes accessed | tf_op | source)
XLA Modules:
  0.0 61.0 jit_solution(17842816026301469708)
XLA Ops:
  0.6 1.6 %copy.6.start = f32[384,32]{1,0:T(8,128)} copy(f32[384,32]{0,1:T(8,128)} %param.7) | data formatting | bytes 98304 | tf_op args[3]
  2.2 2.4 %start_products.1 = (f32[3,32,128]{2,1,0:T(8,128)}, f32[3,32,128]{2,1,0:T(8,128)}, f32[3,32,128]{2,1,0:T(8,128)}, f32[3,32,128]{2,1,0:T(8,128)}, f32[3,32,128]{2,1,0:T(8,128)}) custom-call(f32[3,3,128,128]{3,2,1,0:T(8,128)} %blocks.7, s32[3,3]{1,0:T(4,128)} %ids.7, s32[3]{0:T(128)} %counts.7, f32[384,32]{1,0:T(8,128)} %copy.6.start), custom_call_target="tpu_custom_call" | custom-call | tf_op jit(solution)/shard_map/start_products/pallas_call | solution.py:207
  4.7 3.0 %collective-permute-start = (f32[3,32,128]{2,1,0:T(8,128)}, f32[3,32,128]{2,1,0:T(8,128)S(1)}, u32[]{:S(2)}, u32[]{:S(2)}) collective-permute-start(f32[3,32,128]{2,1,0:T(8,128)} %get-tuple-element.19), channel_id=1, source_target_pairs={{0,4},{4,0},{8,12},{12,8},{1,5},{5,1},{9,13},{13,9},{2,6},{6,2},{1... | collective-permute-start | bytes 147464 | tf_op jit(solution)/shard_map/ppermute | solution.py:24
  7.7 2.6 %collective-permute-start.1 = (f32[3,32,128]{2,1,0:T(8,128)}, f32[3,32,128]{2,1,0:T(8,128)S(1)}, u32[]{:S(2)}, u32[]{:S(2)}) collective-permute-start(f32[3,32,128]{2,1,0:T(8,128)} %get-tuple-element.20), channel_id=1, source_target_pairs={{0,8},{4,12},{8,0},{12,4},{1,9},{5,13},{9,1},{13,5},{2,10},{6,14},... | collective-permute-start | bytes 147464 | tf_op jit(solution)/shard_map/ppermute | solution.py:24
  10.3 0.0 collective-permute-start.2
  10.3 0.0 collective-permute-done.refs_0_
  10.3 0.0 copy-start.4
  10.3 3.5 %collective-permute-done.1.refs_1_ = f32[3,32,128]{2,1,0:T(8,128)S(1)} collective-permute-done((f32[3,32,128]{2,1,0:T(8,128)}, f32[3,32,128]{2,1,0:T(8,128)S(1)}, u32[]{:S(2)}, u32[]{:S(2)}) %collective-permute-start.1) | collective-permute-done | bytes 49184 | tf_op jit(solution)/shard_map/ppermute | solution.py:24
  13.8 0.0 copy-start.6
  13.8 2.6 %collective-permute-done.2.refs_2_ = f32[3,32,128]{2,1,0:T(8,128)S(1)} collective-permute-done((f32[3,32,128]{2,1,0:T(8,128)}, f32[3,32,128]{2,1,0:T(8,128)S(1)}, u32[]{:S(2)}, u32[]{:S(2)}) %collective-permute-start.2) | collective-permute-done | bytes 49184 | tf_op jit(solution)/shard_map/ppermute | solution.py:24
  16.4 0.0 copy-start.8
  16.4 0.0 copy-done.4
  16.4 0.0 copy-done.6
  16.4 0.6 copy-done.8
  17.0 2.8 %direct_first.1.refs_0_ = f32[3,32,128]{2,1,0:T(8,128)} custom-call(f32[3,3,128,128]{3,2,1,0:T(8,128)} %blocks.7, s32[3,3]{1,0:T(4,128)} %ids.7, s32[3]{0:T(128)} %counts.7, f32[3,32,128]{2,1,0:T(8,128)} %get-tuple-element.17.own, f32[3,32,128]{2,1,0:T(8,128)} %get-tuple-element.18.tiles, f32[3,32,128]{2,1,0:T(8,128)} %copy-done.4, f32[3,32,128]{2,1,0:T(8,128)} %copy-done.6, ...), custom_call_target="tpu_custom_call" | custom-call | tf_op jit(solution)/shard_map/direct_first/pallas_call | solution.py:211
  19.8 0.0 collective-permute-start.5
  19.8 1.5 %collective-permute-start.4 = (f32[3,32,128]{2,1,0:T(8,128)}, f32[3,32,128]{2,1,0:T(8,128)S(1)}, u32[]{:S(2)}, u32[]{:S(2)}) collective-permute-start(f32[3,32,128]{2,1,0:T(8,128)} %direct_first.1.refs_0_), channel_id=1, source_target_pairs={{0,2},{1,3},{2,0},{3,1},{4,6},{5,7},{6,4},{7,5},{8,10},{9,11},{10,... | collective-permute-start | bytes 147464 | tf_op jit(solution)/shard_map/ppermute | solution.py:24
  21.3 0.3 collective-permute-start.3
  21.7 2.3 %collective-permute-done.5.refs_3_ = f32[3,32,128]{2,1,0:T(8,128)S(1)} collective-permute-done((f32[3,32,128]{2,1,0:T(8,128)}, f32[3,32,128]{2,1,0:T(8,128)S(1)}, u32[]{:S(2)}, u32[]{:S(2)}) %collective-permute-start.5) | collective-permute-done | bytes 49184 | tf_op jit(solution)/shard_map/ppermute | solution.py:24
  24.0 0.0 copy-start.9
  24.0 0.9 %collective-permute-done.4.refs_2_ = f32[3,32,128]{2,1,0:T(8,128)S(1)} collective-permute-done((f32[3,32,128]{2,1,0:T(8,128)}, f32[3,32,128]{2,1,0:T(8,128)S(1)}, u32[]{:S(2)}, u32[]{:S(2)}) %collective-permute-start.4) | collective-permute-done | bytes 49184 | tf_op jit(solution)/shard_map/ppermute | solution.py:24
  24.9 0.0 copy-start.10
  24.9 0.0 collective-permute-done.3.refs_1_
  24.9 0.0 copy-done.9
  24.9 0.6 copy-done.10
  25.5 0.0 copy-start.11
  25.5 0.6 %copy-done.11 = f32[3,32,128]{2,1,0:T(8,128)} copy-done((f32[3,32,128]{2,1,0:T(8,128)}, f32[3,32,128]{2,1,0:T(8,128)S(1)}, u32[]{:S(2)}) %copy-start.11) | copy-done | bytes 49176
  26.2 2.5 %second_products.1 = (f32[4,32,128]{2,1,0:T(8,128)}, f32[4,32,128]{2,1,0:T(8,128)}, f32[4,32,128]{2,1,0:T(8,128)}, f32[3,32,128]{2,1,0:T(8,128)}, f32[3,32,128]{2,1,0:T(8,128)}, /*index=5*/f32[32,128]{1,0:T(8,128)}) custom-call(f32[3,3,128,128]{3,2,1,0:T(8,128)} %blocks.7, s32[3,3]{1,0:T(4,128)} %ids.7, s32[3]{0:T(128)} %counts.7, ...), custom_call_target="tpu_custom_call" | custom-call | tf_op jit(solution)/shard_map/second_products/pallas_call | solution.py:215
  28.7 0.0 collective-permute-start.6
  28.7 1.3 %collective-permute-start.7 = (f32[4,32,128]{2,1,0:T(8,128)}, f32[4,32,128]{2,1,0:T(8,128)S(1)}, u32[]{:S(2)}, u32[]{:S(2)}) collective-permute-start(f32[4,32,128]{2,1,0:T(8,128)} %get-tuple-element.25), channel_id=1, source_target_pairs={{0,8},{4,12},{8,0},{12,4},{1,9},{5,13},{9,1},{13,5},{2,10},{6,14},... | collective-permute-start | bytes 196616 | tf_op jit(solution)/shard_map/ppermute | solution.py:24
  30.0 3.1 %collective-permute-start.8 = (f32[4,32,128]{2,1,0:T(8,128)}, f32[4,32,128]{2,1,0:T(8,128)S(1)}, u32[]{:S(2)}, u32[]{:S(2)}) collective-permute-start(f32[4,32,128]{2,1,0:T(8,128)} %get-tuple-element.26), channel_id=1, source_target_pairs={{0,12},{4,8},{8,4},{12,0},{1,13},{5,9},{9,5},{13,1},{2,14},{6,10},... | collective-permute-start | bytes 196616 | tf_op jit(solution)/shard_map/ppermute | solution.py:24
  33.1 1.0 %collective-permute-done.6.refs_0_ = f32[4,32,128]{2,1,0:T(8,128)S(1)} collective-permute-done((f32[4,32,128]{2,1,0:T(8,128)}, f32[4,32,128]{2,1,0:T(8,128)S(1)}, u32[]{:S(2)}, u32[]{:S(2)}) %collective-permute-start.6) | collective-permute-done | bytes 65568 | tf_op jit(solution)/shard_map/ppermute | solution.py:24
  34.0 0.0 copy-start
  34.0 3.4 %collective-permute-done.7.refs_1_ = f32[4,32,128]{2,1,0:T(8,128)S(1)} collective-permute-done((f32[4,32,128]{2,1,0:T(8,128)}, f32[4,32,128]{2,1,0:T(8,128)S(1)}, u32[]{:S(2)}, u32[]{:S(2)}) %collective-permute-start.7) | collective-permute-done | bytes 65568 | tf_op jit(solution)/shard_map/ppermute | solution.py:24
  37.5 0.0 copy-start.1
  37.5 0.0 collective-permute-done.8.refs_2_
  37.5 0.0 copy-start.2
  37.5 0.0 copy-done
  37.5 0.6 %copy-done.1 = f32[4,32,128]{2,1,0:T(8,128)} copy-done((f32[4,32,128]{2,1,0:T(8,128)}, f32[4,32,128]{2,1,0:T(8,128)S(1)}, u32[]{:S(2)}) %copy-start.1) | copy-done | bytes 65560
  38.1 0.0 copy-done.2
  38.1 2.8 %direct_second.1 = (f32[3,32,128]{2,1,0:T(8,128)}, f32[32,128]{1,0:T(8,128)}) custom-call(f32[3,3,128,128]{3,2,1,0:T(8,128)} %blocks.7, s32[3,3]{1,0:T(4,128)} %ids.7, s32[3]{0:T(128)} %counts.7, f32[3,32,128]{2,1,0:T(8,128)} %get-tuple-element.22.own, f32[3,32,128]{2,1,0:T(8,128)} %get-tuple-element.23.tiles, f32[4,32,128]{2,1,0:T(8,128)} %copy-done, ...), custom_call_target="tpu_custom_call" | custom-call | tf_op jit(solution)/shard_map/direct_second/pallas_call | solution.py:223
  41.0 0.0 collective-permute-start.11
  41.0 1.2 %collective-permute-start.10 = (f32[3,32,128]{2,1,0:T(8,128)}, f32[3,32,128]{2,1,0:T(8,128)S(1)}, u32[]{:S(2)}, u32[]{:S(2)}) collective-permute-start(f32[3,32,128]{2,1,0:T(8,128)} %get-tuple-element.29.refs_0_), channel_id=1, source_target_pairs={{0,2},{1,3},{2,0},{3,1},{4,6},{5,7},{6,4},{7,5},{8,10},{9,11},{10,... | collective-permute-start | bytes 147464 | tf_op jit(solution)/shard_map/ppermute | solution.py:24
  42.2 0.7 %collective-permute-start.9 = (f32[3,32,128]{2,1,0:T(8,128)}, f32[3,32,128]{2,1,0:T(8,128)S(1)}, u32[]{:S(2)}, u32[]{:S(2)}) collective-permute-start(f32[3,32,128]{2,1,0:T(8,128)} %get-tuple-element.29.refs_0_), channel_id=1, source_target_pairs={{0,1},{1,0},{2,3},{3,2},{4,5},{5,4},{6,7},{7,6},{8,9},{9,8},{10,11... | collective-permute-start | bytes 147464 | tf_op jit(solution)/shard_map/ppermute | solution.py:24
  42.8 2.2 %factor.1.inverse = f32[32,32]{1,0:T(8,128)} custom-call(f32[32,128]{1,0:T(8,128)} %get-tuple-element.28.gram), custom_call_target="tpu_custom_call" | custom-call | tf_op jit(solution)/shard_map/factor/pallas_call | solution.py:227
  45.0 0.1 collective-permute-done.11.refs_3_
  45.1 0.0 copy-start.3
  45.1 0.7 %collective-permute-done.10.refs_2_ = f32[3,32,128]{2,1,0:T(8,128)S(1)} collective-permute-done((f32[3,32,128]{2,1,0:T(8,128)}, f32[3,32,128]{2,1,0:T(8,128)S(1)}, u32[]{:S(2)}, u32[]{:S(2)}) %collective-permute-start.10) | collective-permute-done | bytes 49184 | tf_op jit(solution)/shard_map/ppermute | solution.py:24
  45.8 0.0 collective-permute-done.9.refs_1_
  45.8 0.0 copy-done.3
  45.8 0.6 copy-done.5
  46.4 0.6 %copy-done.7 = f32[3,32,128]{2,1,0:T(8,128)} copy-done((f32[3,32,128]{2,1,0:T(8,128)}, f32[3,32,128]{2,1,0:T(8,128)S(1)}, u32[]{:S(2)}) %copy-start.7) | copy-done | bytes 49176
  47.0 2.2 %gram.1 = (f32[3,32,128]{2,1,0:T(8,128)}, f32[32,64]{1,0:T(8,128)}) custom-call(f32[32,32]{1,0:T(8,128)} %factor.1.inverse, f32[3,32,128]{2,1,0:T(8,128)} %get-tuple-element.23.tiles, f32[3,32,128]{2,1,0:T(8,128)} %get-tuple-element.29.refs_0_, f32[3,32,128]{2,1,0:T(8,128)} %copy-done.7, f32[3,32,128]{2,1,0:T(8,128)} %copy-done.5, f32[3,32,128]{2,1,0:T(8,128)} %copy-done.3), custom_call_target="tpu_custom_call" | custom-call | tf_op jit(solution)/shard_map/gram/pallas_call | solution.py:230
  49.3 1.9 %collective-permute-start.14 = (f32[32,64]{1,0:T(8,128)}, f32[32,64]{1,0:T(8,128)S(1)}, u32[]{:S(2)}, u32[]{:S(2)}) collective-permute-start(f32[32,64]{1,0:T(8,128)} %get-tuple-element.31.refs_0_), channel_id=1, source_target_pairs={{0,12},{4,8},{8,4},{12,0},{1,13},{5,9},{9,5},{13,1},{2,14},{6,10},... | collective-permute-start | bytes 24584 | tf_op jit(solution)/shard_map/ppermute | solution.py:24
  51.2 0.8 %collective-permute-start.13 = (f32[32,64]{1,0:T(8,128)}, f32[32,64]{1,0:T(8,128)S(1)}, u32[]{:S(2)}, u32[]{:S(2)}) collective-permute-start(f32[32,64]{1,0:T(8,128)} %get-tuple-element.31.refs_0_), channel_id=1, source_target_pairs={{0,8},{4,12},{8,0},{12,4},{1,9},{5,13},{9,1},{13,5},{2,10},{6,14},... | collective-permute-start | bytes 24584 | tf_op jit(solution)/shard_map/ppermute | solution.py:24
  52.0 1.7 %collective-permute-start.12 = (f32[32,64]{1,0:T(8,128)}, f32[32,64]{1,0:T(8,128)S(1)}, u32[]{:S(2)}, u32[]{:S(2)}) collective-permute-start(f32[32,64]{1,0:T(8,128)} %get-tuple-element.31.refs_0_), channel_id=1, source_target_pairs={{0,4},{4,0},{8,12},{12,8},{1,5},{5,1},{9,13},{13,9},{2,6},{6,2},{1... | collective-permute-start | bytes 24584 | tf_op jit(solution)/shard_map/ppermute | solution.py:24
  53.6 1.4 %collective-permute-done.14.refs_3_ = f32[32,64]{1,0:T(8,128)S(1)} collective-permute-done((f32[32,64]{1,0:T(8,128)}, f32[32,64]{1,0:T(8,128)S(1)}, u32[]{:S(2)}, u32[]{:S(2)}) %collective-permute-start.14) | collective-permute-done | bytes 8224 | tf_op jit(solution)/shard_map/ppermute | solution.py:24
  55.1 1.0 %collective-permute-done.13.refs_2_ = f32[32,64]{1,0:T(8,128)S(1)} collective-permute-done((f32[32,64]{1,0:T(8,128)}, f32[32,64]{1,0:T(8,128)S(1)}, u32[]{:S(2)}, u32[]{:S(2)}) %collective-permute-start.13) | collective-permute-done | bytes 8224 | tf_op jit(solution)/shard_map/ppermute | solution.py:24
  56.1 0.0 collective-permute-done.12.refs_1_
  56.1 0.0 copy-done.12
  56.1 0.6 copy-done.13
  56.7 0.0 copy-done.14
  56.7 2.7 %last.1 = (f32[384,32]{1,0:T(8,128)}, f32[32,32]{1,0:T(8,128)}) custom-call(f32[3,32,128]{2,1,0:T(8,128)} %get-tuple-element.30.image, f32[32,64]{1,0:T(8,128)} %get-tuple-element.31.refs_0_, f32[32,64]{1,0:T(8,128)} %copy-done.14, f32[32,64]{1,0:T(8,128)} %copy-done.13, f32[32,64]{1,0:T(8,128)} %copy-done.12), custom_call_target="tpu_custom_call" | custom-call | tf_op jit(solution)/shard_map/last/pallas_call | solution.py:237
  59.4 1.7 %copy.7 = f32[384,32]{0,1:T(8,128)} copy(f32[384,32]{1,0:T(8,128)} %get-tuple-element.32) | data formatting | bytes 98304 | tf_op jit(solution)/shard_map/last/pallas_call | solution.py:237
  (5 shorter events, 0.0 us)
Async XLA Ops:
  4.7 5.6 %collective-permute-start = (f32[3,32,128]{2,1,0:T(8,128)}, f32[3,32,128]{2,1,0:T(8,128)S(1)}, u32[]{:S(2)}, u32[]{:S(2)}) collective-permute-start(f32[3,32,128]{2,1,0:T(8,128)} %get-tuple-element.19), channel_id=1, source_target_pairs={{0,4},{4,0},{8,12},{12,8},{1,5},{5,1},{9,13},{13,9},{2,6},{6,2},{1... | collective-permute-start | bytes 147464 | tf_op jit(solution)/shard_map/ppermute | solution.py:24
  7.7 6.1 %collective-permute-start.1 = (f32[3,32,128]{2,1,0:T(8,128)}, f32[3,32,128]{2,1,0:T(8,128)S(1)}, u32[]{:S(2)}, u32[]{:S(2)}) collective-permute-start(f32[3,32,128]{2,1,0:T(8,128)} %get-tuple-element.20), channel_id=1, source_target_pairs={{0,8},{4,12},{8,0},{12,4},{1,9},{5,13},{9,1},{13,5},{2,10},{6,14},... | collective-permute-start | bytes 147464 | tf_op jit(solution)/shard_map/ppermute | solution.py:24
  10.3 6.1 %collective-permute-start.2 = (f32[3,32,128]{2,1,0:T(8,128)}, f32[3,32,128]{2,1,0:T(8,128)S(1)}, u32[]{:S(2)}, u32[]{:S(2)}) collective-permute-start(f32[3,32,128]{2,1,0:T(8,128)} %get-tuple-element.21), channel_id=1, source_target_pairs={{0,12},{4,8},{8,4},{12,0},{1,13},{5,9},{9,5},{13,1},{2,14},{6,10},... | collective-permute-start | bytes 147464 | tf_op jit(solution)/shard_map/ppermute | solution.py:24
  10.3 6.1 %copy-start.4 = (f32[3,32,128]{2,1,0:T(8,128)}, f32[3,32,128]{2,1,0:T(8,128)S(1)}, u32[]{:S(2)}) copy-start(f32[3,32,128]{2,1,0:T(8,128)S(1)} %collective-permute-done.refs_0_) | copy-start | bytes 147460
  13.8 2.6 %copy-start.6 = (f32[3,32,128]{2,1,0:T(8,128)}, f32[3,32,128]{2,1,0:T(8,128)S(1)}, u32[]{:S(2)}) copy-start(f32[3,32,128]{2,1,0:T(8,128)S(1)} %collective-permute-done.1.refs_1_) | copy-start | bytes 147460
  16.4 0.6 %copy-start.8 = (f32[3,32,128]{2,1,0:T(8,128)}, f32[3,32,128]{2,1,0:T(8,128)S(1)}, u32[]{:S(2)}) copy-start(f32[3,32,128]{2,1,0:T(8,128)S(1)} %collective-permute-done.2.refs_2_) | copy-start | bytes 147460
  19.8 4.2 %collective-permute-start.5 = (f32[3,32,128]{2,1,0:T(8,128)}, f32[3,32,128]{2,1,0:T(8,128)S(1)}, u32[]{:S(2)}, u32[]{:S(2)}) collective-permute-start(f32[3,32,128]{2,1,0:T(8,128)} %direct_first.1.refs_0_), channel_id=1, source_target_pairs={{0,3},{1,2},{2,1},{3,0},{4,7},{5,6},{6,5},{7,4},{8,11},{9,10},{10,... | collective-permute-start | bytes 147464 | tf_op jit(solution)/shard_map/ppermute | solution.py:24
  19.8 5.1 %collective-permute-start.4 = (f32[3,32,128]{2,1,0:T(8,128)}, f32[3,32,128]{2,1,0:T(8,128)S(1)}, u32[]{:S(2)}, u32[]{:S(2)}) collective-permute-start(f32[3,32,128]{2,1,0:T(8,128)} %direct_first.1.refs_0_), channel_id=1, source_target_pairs={{0,2},{1,3},{2,0},{3,1},{4,6},{5,7},{6,4},{7,5},{8,10},{9,11},{10,... | collective-permute-start | bytes 147464 | tf_op jit(solution)/shard_map/ppermute | solution.py:24
  21.3 3.6 %collective-permute-start.3 = (f32[3,32,128]{2,1,0:T(8,128)}, f32[3,32,128]{2,1,0:T(8,128)S(1)}, u32[]{:S(2)}, u32[]{:S(2)}) collective-permute-start(f32[3,32,128]{2,1,0:T(8,128)} %direct_first.1.refs_0_), channel_id=1, source_target_pairs={{0,1},{1,0},{2,3},{3,2},{4,5},{5,4},{6,7},{7,6},{8,9},{9,8},{10,11... | collective-permute-start | bytes 147464 | tf_op jit(solution)/shard_map/ppermute | solution.py:24
  24.0 0.9 %copy-start.9 = (f32[3,32,128]{2,1,0:T(8,128)}, f32[3,32,128]{2,1,0:T(8,128)S(1)}, u32[]{:S(2)}) copy-start(f32[3,32,128]{2,1,0:T(8,128)S(1)} %collective-permute-done.5.refs_3_) | copy-start | bytes 147460
  24.9 0.6 %copy-start.10 = (f32[3,32,128]{2,1,0:T(8,128)}, f32[3,32,128]{2,1,0:T(8,128)S(1)}, u32[]{:S(2)}) copy-start(f32[3,32,128]{2,1,0:T(8,128)S(1)} %collective-permute-done.4.refs_2_) | copy-start | bytes 147460
  25.5 0.6 %copy-start.11 = (f32[3,32,128]{2,1,0:T(8,128)}, f32[3,32,128]{2,1,0:T(8,128)S(1)}, u32[]{:S(2)}) copy-start(f32[3,32,128]{2,1,0:T(8,128)S(1)} %collective-permute-done.3.refs_1_) | copy-start | bytes 147460
  28.7 5.4 %collective-permute-start.6 = (f32[4,32,128]{2,1,0:T(8,128)}, f32[4,32,128]{2,1,0:T(8,128)S(1)}, u32[]{:S(2)}, u32[]{:S(2)}) collective-permute-start(f32[4,32,128]{2,1,0:T(8,128)} %get-tuple-element.24), channel_id=1, source_target_pairs={{0,4},{4,0},{8,12},{12,8},{1,5},{5,1},{9,13},{13,9},{2,6},{6,2},{1... | collective-permute-start | bytes 196616 | tf_op jit(solution)/shard_map/ppermute | solution.py:24
  28.7 8.8 %collective-permute-start.7 = (f32[4,32,128]{2,1,0:T(8,128)}, f32[4,32,128]{2,1,0:T(8,128)S(1)}, u32[]{:S(2)}, u32[]{:S(2)}) collective-permute-start(f32[4,32,128]{2,1,0:T(8,128)} %get-tuple-element.25), channel_id=1, source_target_pairs={{0,8},{4,12},{8,0},{12,4},{1,9},{5,13},{9,1},{13,5},{2,10},{6,14},... | collective-permute-start | bytes 196616 | tf_op jit(solution)/shard_map/ppermute | solution.py:24
  30.0 7.5 %collective-permute-start.8 = (f32[4,32,128]{2,1,0:T(8,128)}, f32[4,32,128]{2,1,0:T(8,128)S(1)}, u32[]{:S(2)}, u32[]{:S(2)}) collective-permute-start(f32[4,32,128]{2,1,0:T(8,128)} %get-tuple-element.26), channel_id=1, source_target_pairs={{0,12},{4,8},{8,4},{12,0},{1,13},{5,9},{9,5},{13,1},{2,14},{6,10},... | collective-permute-start | bytes 196616 | tf_op jit(solution)/shard_map/ppermute | solution.py:24
  34.0 3.4 %copy-start = (f32[4,32,128]{2,1,0:T(8,128)}, f32[4,32,128]{2,1,0:T(8,128)S(1)}, u32[]{:S(2)}) copy-start(f32[4,32,128]{2,1,0:T(8,128)S(1)} %collective-permute-done.6.refs_0_) | copy-start | bytes 196612
  37.5 0.6 %copy-start.1 = (f32[4,32,128]{2,1,0:T(8,128)}, f32[4,32,128]{2,1,0:T(8,128)S(1)}, u32[]{:S(2)}) copy-start(f32[4,32,128]{2,1,0:T(8,128)S(1)} %collective-permute-done.7.refs_1_) | copy-start | bytes 196612
  37.5 0.6 %copy-start.2 = (f32[4,32,128]{2,1,0:T(8,128)}, f32[4,32,128]{2,1,0:T(8,128)S(1)}, u32[]{:S(2)}) copy-start(f32[4,32,128]{2,1,0:T(8,128)S(1)} %collective-permute-done.8.refs_2_) | copy-start | bytes 196612
  41.0 4.1 %collective-permute-start.11 = (f32[3,32,128]{2,1,0:T(8,128)}, f32[3,32,128]{2,1,0:T(8,128)S(1)}, u32[]{:S(2)}, u32[]{:S(2)}) collective-permute-start(f32[3,32,128]{2,1,0:T(8,128)} %get-tuple-element.29.refs_0_), channel_id=1, source_target_pairs={{0,3},{1,2},{2,1},{3,0},{4,7},{5,6},{6,5},{7,4},{8,11},{9,10},{10,... | collective-permute-start | bytes 147464 | tf_op jit(solution)/shard_map/ppermute | solution.py:24
  41.0 4.8 %collective-permute-start.10 = (f32[3,32,128]{2,1,0:T(8,128)}, f32[3,32,128]{2,1,0:T(8,128)S(1)}, u32[]{:S(2)}, u32[]{:S(2)}) collective-permute-start(f32[3,32,128]{2,1,0:T(8,128)} %get-tuple-element.29.refs_0_), channel_id=1, source_target_pairs={{0,2},{1,3},{2,0},{3,1},{4,6},{5,7},{6,4},{7,5},{8,10},{9,11},{10,... | collective-permute-start | bytes 147464 | tf_op jit(solution)/shard_map/ppermute | solution.py:24
  42.2 3.6 %collective-permute-start.9 = (f32[3,32,128]{2,1,0:T(8,128)}, f32[3,32,128]{2,1,0:T(8,128)S(1)}, u32[]{:S(2)}, u32[]{:S(2)}) collective-permute-start(f32[3,32,128]{2,1,0:T(8,128)} %get-tuple-element.29.refs_0_), channel_id=1, source_target_pairs={{0,1},{1,0},{2,3},{3,2},{4,5},{5,4},{6,7},{7,6},{8,9},{9,8},{10,11... | collective-permute-start | bytes 147464 | tf_op jit(solution)/shard_map/ppermute | solution.py:24
  45.1 0.8 %copy-start.3 = (f32[3,32,128]{2,1,0:T(8,128)}, f32[3,32,128]{2,1,0:T(8,128)S(1)}, u32[]{:S(2)}) copy-start(f32[3,32,128]{2,1,0:T(8,128)S(1)} %collective-permute-done.11.refs_3_) | copy-start | bytes 147460
  45.8 0.6 %copy-start.5 = (f32[3,32,128]{2,1,0:T(8,128)}, f32[3,32,128]{2,1,0:T(8,128)S(1)}, u32[]{:S(2)}) copy-start(f32[3,32,128]{2,1,0:T(8,128)S(1)} %collective-permute-done.10.refs_2_) | copy-start | bytes 147460
  46.4 0.6 %copy-start.7 = (f32[3,32,128]{2,1,0:T(8,128)}, f32[3,32,128]{2,1,0:T(8,128)S(1)}, u32[]{:S(2)}) copy-start(f32[3,32,128]{2,1,0:T(8,128)S(1)} %collective-permute-done.9.refs_1_) | copy-start | bytes 147460
  49.3 5.8 %collective-permute-start.14 = (f32[32,64]{1,0:T(8,128)}, f32[32,64]{1,0:T(8,128)S(1)}, u32[]{:S(2)}, u32[]{:S(2)}) collective-permute-start(f32[32,64]{1,0:T(8,128)} %get-tuple-element.31.refs_0_), channel_id=1, source_target_pairs={{0,12},{4,8},{8,4},{12,0},{1,13},{5,9},{9,5},{13,1},{2,14},{6,10},... | collective-permute-start | bytes 24584 | tf_op jit(solution)/shard_map/ppermute | solution.py:24
  51.2 4.9 %collective-permute-start.13 = (f32[32,64]{1,0:T(8,128)}, f32[32,64]{1,0:T(8,128)S(1)}, u32[]{:S(2)}, u32[]{:S(2)}) collective-permute-start(f32[32,64]{1,0:T(8,128)} %get-tuple-element.31.refs_0_), channel_id=1, source_target_pairs={{0,8},{4,12},{8,0},{12,4},{1,9},{5,13},{9,1},{13,5},{2,10},{6,14},... | collective-permute-start | bytes 24584 | tf_op jit(solution)/shard_map/ppermute | solution.py:24
  52.0 4.1 %collective-permute-start.12 = (f32[32,64]{1,0:T(8,128)}, f32[32,64]{1,0:T(8,128)S(1)}, u32[]{:S(2)}, u32[]{:S(2)}) collective-permute-start(f32[32,64]{1,0:T(8,128)} %get-tuple-element.31.refs_0_), channel_id=1, source_target_pairs={{0,4},{4,0},{8,12},{12,8},{1,5},{5,1},{9,13},{13,9},{2,6},{6,2},{1... | collective-permute-start | bytes 24584 | tf_op jit(solution)/shard_map/ppermute | solution.py:24
  55.1 1.0 %copy-start.12 = (f32[32,64]{1,0:T(8,128)}, f32[32,64]{1,0:T(8,128)S(1)}, u32[]{:S(2)}) copy-start(f32[32,64]{1,0:T(8,128)S(1)} %collective-permute-done.14.refs_3_) | copy-start | bytes 24580
  56.1 0.6 copy-start.13
  56.1 0.6 copy-start.14

commit v2 on v1

--- a/solution.py
+++ b/solution.py
@@ -12,6 +12,7 @@
 VMEM = pl.BlockSpec(memory_space=pltpu.VMEM)
 SMEM = pl.BlockSpec(memory_space=pltpu.SMEM)
 PANEL = 8
+PARAMS = pltpu.CompilerParams(vmem_limit_bytes=8 * 2**20)
 
 
 def tree(parts):
@@ -72,7 +73,7 @@
     block_rows, slots, size, _ = blocks.shape
     row, first_row, first_slot = place(block_rows, slots)
     for i in range(block_rows):
-        tiles[i] = start[i * size : (i + 1) * size, :].T
+        tiles[i] = start[:, i * size : (i + 1) * size]
     transposed_products(blocks, ids, counts, tiles, products, first_row, first_slot)
     fill(messages, products, tiles, row, block_rows)
     own[...] = products[pl.ds(first_row, block_rows)]
@@ -182,7 +183,7 @@
     lower = inverse_factor(both[:, :columns])
     size = image.shape[2]
     for i in range(image.shape[0]):
-        basis[i * size : (i + 1) * size, :] = mm(lower, image[i]).T
+        basis[:, i * size : (i + 1) * size] = mm(lower, image[i])
 
 
 def body(blocks, partner_ids, counts, start):
@@ -201,12 +202,18 @@
 
     def call(kernel, name, specs, outs, scratch=()):
         return pl.pallas_call(
-            kernel, name=name, in_specs=specs, out_specs=[VMEM] * len(outs), out_shape=outs, scratch_shapes=scratch
+            kernel,
+            name=name,
+            in_specs=specs,
+            out_specs=[VMEM] * len(outs),
+            out_shape=outs,
+            scratch_shapes=scratch,
+            compiler_params=PARAMS,
         )
 
     *messages, own, tiles = call(
         functools.partial(first_kernel, rows), "start_products", index + [VMEM], [tile] * (rows + 1), work
-    )(*stored, start)
+    )(*stored, start.T)
     received = [swap(m, "row", s) for s, m in enumerate(messages, 1)]
     (image,) = call(
         functools.partial(direct_kernel, rows, False), "direct_first", index + [VMEM] * (rows + 1), [tile], work
@@ -238,9 +245,9 @@
         functools.partial(last_kernel, rows, total),
         "last",
         [VMEM] * (rows + 1),
-        [shape(start.shape, F32), shape((columns, columns), F32)],
+        [shape(start.shape[::-1], F32), shape((columns, columns), F32)],
     )(image, *boths)
-    return basis, ritz
+    return basis.T, ritz
 
 
 def solution(mesh):

time: 61.5 us -> 48.5 us (0.79)
  Pallas kernels: 17.6 us -> 8.7 us
  local copies, waits for them, and re-layouts: 7.58 us -> 3.19 us
    unnamed x31 -> x8, local copies, waits for them, and re-layouts: 5.93 us -> 3.19 us
    pallas_call x1 -> x0, local copies, waits for them, and re-layouts: 1.65 us -> none  [body(): call(functools.partial(last_kernel, rows, total), 'last', [VMEM] * (rows...]
    pallas_call x1, Pallas kernels: 2.22 us -> 0.64 us  [body(): call(functools.partial(gram_kernel, parts), 'gram', [VMEM] * (parts + 2),...]
    pallas_call x1, Pallas kernels: 2.15 us -> 0.82 us  [body(): call(functools.partial(factor_kernel, total), 'factor', [VMEM], [shape((c...]
    pallas_call x1, Pallas kernels: 2.44 us -> 1.16 us  [body(): call(functools.partial(first_kernel, rows), 'start_products', index + [VM...]
    pallas_call x1, Pallas kernels: 2.51 us -> 1.26 us  [body(): call(functools.partial(second_kernel, rows, parts), 'second_products', in...]
    pallas_call x1, Pallas kernels: 2.84 us -> 1.59 us  [body(): call(functools.partial(direct_kernel, rows, True), 'direct_second', index...]
    pallas_call x1, Pallas kernels: 2.79 us -> 1.59 us  [body(): call(functools.partial(direct_kernel, rows, False), 'direct_first', index...]
  transfers between devices with their start and end apart: 15 -> 15, of which waited for: 10 -> 10; matrix products, arithmetic and copies ran while one was open for 0% -> 0% of each run, Pallas kernels for 4% -> 2%
where the time goes in v2:
time: 48.5 us; the launch traced here: 48.3 us
  starting transfers between devices  18.3 us (38%)
  waiting for transfers between devices  17.3 us (36%)
  Pallas kernels  8.7 us (18%)
  local copies, waits for them, and re-layouts  3.19 us (7%)
  between operations  0.72 us (1%)
    ppermute x15, starting transfers between devices, swap(): lax.ppermute(x, axis, [(i, i ^ distance) for i in range(lax.axis_size(axi...  18.3 us
    ppermute x15, waiting for transfers between devices, swap(): lax.ppermute(x, axis, [(i, i ^ distance) for i in range(lax.axis_size(axi...  17.3 us
    unnamed x8, local copies, waits for them, and re-layouts  3.19 us
    pallas_call x1, Pallas kernels, body(): call(functools.partial(last_kernel, rows, total), 'last', [VMEM] * (rows...  1.64 us
    pallas_call x1, Pallas kernels, body(): call(functools.partial(direct_kernel, rows, True), 'direct_second', index...  1.59 us
    pallas_call x1, Pallas kernels, body(): call(functools.partial(direct_kernel, rows, False), 'direct_first', index...  1.59 us
    pallas_call x1, Pallas kernels, body(): call(functools.partial(second_kernel, rows, parts), 'second_products', in...  1.26 us
    pallas_call x1, Pallas kernels, body(): call(functools.partial(first_kernel, rows), 'start_products', index + [VM...  1.16 us
  transfers between devices with their start and end apart: 15, of which 10 were waited for; matrix products, arithmetic and copies ran while one was open for 0% of the time, Pallas kernels for 2%

profile of v2, /device:TPU:0, one launch (start us, length us, event | category | flops | bytes accessed | tf_op | source)
XLA Modules:
  0.0 48.3 jit_solution(17873253300723970300)
XLA Ops:
  0.6 0.0 copy-start.3
  0.6 0.6 %copy-done.3 = s32[3]{0:T(128)S(1)} copy-done((s32[3]{0:T(128)S(1)}, s32[3]{0:T(128)}, u32[]{:S(2)}) %copy-start.3) | copy-done | bytes 36
  1.3 0.0 copy-start
  1.3 1.1 %copy-done = f32[3,3,128,128]{3,2,1,0:T(8,128)S(1)} copy-done((f32[3,3,128,128]{3,2,1,0:T(8,128)S(1)}, f32[3,3,128,128]{3,2,1,0:T(8,128)}, u32[]{:S(2)}) %copy-start) | copy-done | bytes 589848
  2.4 0.0 copy-start.1
  2.4 0.8 %copy-done.1 = f32[384,32]{0,1:T(8,128)S(1)} copy-done((f32[384,32]{0,1:T(8,128)S(1)}, f32[384,32]{0,1:T(8,128)}, u32[]{:S(2)}) %copy-start.1) | copy-done | bytes 49176
  3.2 0.0 copy-start.2
  3.2 0.7 %copy-done.2 = s32[3,3]{1,0:T(4,128)S(1)} copy-done((s32[3,3]{1,0:T(4,128)S(1)}, s32[3,3]{1,0:T(4,128)}, u32[]{:S(2)}) %copy-start.2) | copy-done | bytes 60
  3.8 1.2 %start_products.1 = (f32[3,32,128]{2,1,0:T(8,128)S(1)}, f32[3,32,128]{2,1,0:T(8,128)S(1)}, f32[3,32,128]{2,1,0:T(8,128)S(1)}, f32[3,32,128]{2,1,0:T(8,128)S(1)}, f32[3,32,128]{2,1,0:T(8,128)S(1)}) custom-call(f32[3,3,128,128]{3,2,1,0:T(8,128)S(1)} %copy-done, s32[3,3]{1,0:T(4,128)S(1)} %copy-done.2, s32[3]{0:T(128)S(1)} %copy-done.3, f32[32,384]{1,0:T(8,128)S(1)} %bitcast.2), custom_call_target="tpu_custom_call" | custom-call | tf_op jit(solution)/shard_map/start_products/pallas_call | solution.py:214
  5.0 3.1 %collective-permute-start = (f32[3,32,128]{2,1,0:T(8,128)S(1)}, f32[3,32,128]{2,1,0:T(8,128)S(1)}, u32[]{:S(2)}, u32[]{:S(2)}) collective-permute-start(f32[3,32,128]{2,1,0:T(8,128)S(1)} %get-tuple-element.21), channel_id=1, source_target_pairs={{0,4},{4,0},{8,12},{12,8},{1,5},{5,1},{9,13},{13,9},{2,6},{6,2},{1... | collective-permute-start | bytes 147464 | tf_op jit(solution)/shard_map/ppermute | solution.py:25
  8.1 2.6 %collective-permute-start.1 = (f32[3,32,128]{2,1,0:T(8,128)S(1)}, f32[3,32,128]{2,1,0:T(8,128)S(1)}, u32[]{:S(2)}, u32[]{:S(2)}) collective-permute-start(f32[3,32,128]{2,1,0:T(8,128)S(1)} %get-tuple-element.22), channel_id=1, source_target_pairs={{0,8},{4,12},{8,0},{12,4},{1,9},{5,13},{9,1},{13,5},{2,10},{6,14},... | collective-permute-start | bytes 147464 | tf_op jit(solution)/shard_map/ppermute | solution.py:25
  10.7 0.0 collective-permute-start.2
  10.7 0.0 collective-permute-done.refs_0_
  10.7 3.3 %collective-permute-done.1.refs_1_ = f32[3,32,128]{2,1,0:T(8,128)S(1)} collective-permute-done((f32[3,32,128]{2,1,0:T(8,128)S(1)}, f32[3,32,128]{2,1,0:T(8,128)S(1)}, u32[]{:S(2)}, u32[]{:S(2)}) %collective-permute-start.1) | collective-permute-done | bytes 49184 | tf_op jit(solution)/shard_map/ppermute | solution.py:25
  14.0 2.6 %collective-permute-done.2.refs_2_ = f32[3,32,128]{2,1,0:T(8,128)S(1)} collective-permute-done((f32[3,32,128]{2,1,0:T(8,128)S(1)}, f32[3,32,128]{2,1,0:T(8,128)S(1)}, u32[]{:S(2)}, u32[]{:S(2)}) %collective-permute-start.2) | collective-permute-done | bytes 49184 | tf_op jit(solution)/shard_map/ppermute | solution.py:25
  16.6 1.6 %direct_first.1.refs_0_ = f32[3,32,128]{2,1,0:T(8,128)S(1)} custom-call(f32[3,3,128,128]{3,2,1,0:T(8,128)S(1)} %copy-done, s32[3,3]{1,0:T(4,128)S(1)} %copy-done.2, s32[3]{0:T(128)S(1)} %copy-done.3, f32[3,32,128]{2,1,0:T(8,128)S(1)} %get-tuple-element.19.own, f32[3,32,128]{2,1,0:T(8,128)S(1)} %get-tuple-element.20.tiles, ...), custom_call_target="tpu_custom_call" | custom-call | tf_op jit(solution)/shard_map/direct_first/pallas_call | solution.py:218
  18.2 0.0 collective-permute-start.5
  18.2 1.6 %collective-permute-start.4 = (f32[3,32,128]{2,1,0:T(8,128)S(1)}, f32[3,32,128]{2,1,0:T(8,128)S(1)}, u32[]{:S(2)}, u32[]{:S(2)}) collective-permute-start(f32[3,32,128]{2,1,0:T(8,128)S(1)} %direct_first.1.refs_0_), channel_id=1, source_target_pairs={{0,2},{1,3},{2,0},{3,1},{4,6},{5,7},{6,4},{7,5},{8,10},{9,11},{10,... | collective-permute-start | bytes 147464 | tf_op jit(solution)/shard_map/ppermute | solution.py:25
  19.7 0.3 collective-permute-start.3
  20.0 2.1 %collective-permute-done.5.refs_3_ = f32[3,32,128]{2,1,0:T(8,128)S(1)} collective-permute-done((f32[3,32,128]{2,1,0:T(8,128)S(1)}, f32[3,32,128]{2,1,0:T(8,128)S(1)}, u32[]{:S(2)}, u32[]{:S(2)}) %collective-permute-start.5) | collective-permute-done | bytes 49184 | tf_op jit(solution)/shard_map/ppermute | solution.py:25
  22.2 0.9 %collective-permute-done.4.refs_2_ = f32[3,32,128]{2,1,0:T(8,128)S(1)} collective-permute-done((f32[3,32,128]{2,1,0:T(8,128)S(1)}, f32[3,32,128]{2,1,0:T(8,128)S(1)}, u32[]{:S(2)}, u32[]{:S(2)}) %collective-permute-start.4) | collective-permute-done | bytes 49184 | tf_op jit(solution)/shard_map/ppermute | solution.py:25
  23.1 0.0 collective-permute-done.3.refs_1_
  23.1 1.3 %second_products.1 = (f32[4,32,128]{2,1,0:T(8,128)S(1)}, f32[4,32,128]{2,1,0:T(8,128)S(1)}, f32[4,32,128]{2,1,0:T(8,128)S(1)}, f32[3,32,128]{2,1,0:T(8,128)S(1)}...) custom-call(f32[3,3,128,128]{3,2,1,0:T(8,128)S(1)} %copy-done, s32[3,3]{1,0:T(4,128)S(1)} %copy-done.2, ...), custom_call_target="tpu_custom_call" | custom-call | tf_op jit(solution)/shard_map/second_products/pallas_call | solution.py:222
  24.4 0.1 collective-permute-start.6
  24.4 1.3 %collective-permute-start.7 = (f32[4,32,128]{2,1,0:T(8,128)S(1)}, f32[4,32,128]{2,1,0:T(8,128)S(1)}, u32[]{:S(2)}, u32[]{:S(2)}) collective-permute-start(f32[4,32,128]{2,1,0:T(8,128)S(1)} %get-tuple-element.27), channel_id=1, source_target_pairs={{0,8},{4,12},{8,0},{12,4},{1,9},{5,13},{9,1},{13,5},{2,10},{6,14},... | collective-permute-start | bytes 196616 | tf_op jit(solution)/shard_map/ppermute | solution.py:25
  25.7 3.1 %collective-permute-start.8 = (f32[4,32,128]{2,1,0:T(8,128)S(1)}, f32[4,32,128]{2,1,0:T(8,128)S(1)}, u32[]{:S(2)}, u32[]{:S(2)}) collective-permute-start(f32[4,32,128]{2,1,0:T(8,128)S(1)} %get-tuple-element.28), channel_id=1, source_target_pairs={{0,12},{4,8},{8,4},{12,0},{1,13},{5,9},{9,5},{13,1},{2,14},{6,10},... | collective-permute-start | bytes 196616 | tf_op jit(solution)/shard_map/ppermute | solution.py:25
  28.8 0.8 %collective-permute-done.6.refs_0_ = f32[4,32,128]{2,1,0:T(8,128)S(1)} collective-permute-done((f32[4,32,128]{2,1,0:T(8,128)S(1)}, f32[4,32,128]{2,1,0:T(8,128)S(1)}, u32[]{:S(2)}, u32[]{:S(2)}) %collective-permute-start.6) | collective-permute-done | bytes 65568 | tf_op jit(solution)/shard_map/ppermute | solution.py:25
  29.6 3.4 %collective-permute-done.7.refs_1_ = f32[4,32,128]{2,1,0:T(8,128)S(1)} collective-permute-done((f32[4,32,128]{2,1,0:T(8,128)S(1)}, f32[4,32,128]{2,1,0:T(8,128)S(1)}, u32[]{:S(2)}, u32[]{:S(2)}) %collective-permute-start.7) | collective-permute-done | bytes 65568 | tf_op jit(solution)/shard_map/ppermute | solution.py:25
  33.0 0.0 collective-permute-done.8.refs_2_
  33.0 1.6 %direct_second.1 = (f32[3,32,128]{2,1,0:T(8,128)S(1)}, f32[32,128]{1,0:T(8,128)S(1)}) custom-call(f32[3,3,128,128]{3,2,1,0:T(8,128)S(1)} %copy-done, s32[3,3]{1,0:T(4,128)S(1)} %copy-done.2, s32[3]{0:T(128)S(1)} %copy-done.3, f32[3,32,128]{2,1,0:T(8,128)S(1)} %get-tuple-element.24.own, f32[3,32,128]{2,1,0:T(8,128)S(1)} %get-tuple-element.25.tiles, ...), custom_call_target="tpu_custom_call" | custom-call | tf_op jit(solution)/shard_map/direct_second/pallas_call | solution.py:230
  34.6 0.0 collective-permute-start.11
  34.6 1.2 %collective-permute-start.10 = (f32[3,32,128]{2,1,0:T(8,128)S(1)}, f32[3,32,128]{2,1,0:T(8,128)S(1)}, u32[]{:S(2)}, u32[]{:S(2)}) collective-permute-start(f32[3,32,128]{2,1,0:T(8,128)S(1)} %get-tuple-element.31.refs_0_), channel_id=1, source_target_pairs={{0,2},{1,3},{2,0},{3,1},{4,6},{5,7},{6,4},{7,5},{8,10},{9,11},{10,... | collective-permute-start | bytes 147464 | tf_op jit(solution)/shard_map/ppermute | solution.py:25
  35.8 0.7 %collective-permute-start.9 = (f32[3,32,128]{2,1,0:T(8,128)S(1)}, f32[3,32,128]{2,1,0:T(8,128)S(1)}, u32[]{:S(2)}, u32[]{:S(2)}) collective-permute-start(f32[3,32,128]{2,1,0:T(8,128)S(1)} %get-tuple-element.31.refs_0_), channel_id=1, source_target_pairs={{0,1},{1,0},{2,3},{3,2},{4,5},{5,4},{6,7},{7,6},{8,9},{9,8},{10,11... | collective-permute-start | bytes 147464 | tf_op jit(solution)/shard_map/ppermute | solution.py:25
  36.5 0.8 %factor.1.inverse = f32[32,32]{1,0:T(8,128)S(1)} custom-call(f32[32,128]{1,0:T(8,128)S(1)} %get-tuple-element.30.gram), custom_call_target="tpu_custom_call" | custom-call | tf_op jit(solution)/shard_map/factor/pallas_call | solution.py:234
  37.3 1.1 %collective-permute-done.11.refs_3_ = f32[3,32,128]{2,1,0:T(8,128)S(1)} collective-permute-done((f32[3,32,128]{2,1,0:T(8,128)S(1)}, f32[3,32,128]{2,1,0:T(8,128)S(1)}, u32[]{:S(2)}, u32[]{:S(2)}) %collective-permute-start.11) | collective-permute-done | bytes 49184 | tf_op jit(solution)/shard_map/ppermute | solution.py:25
  38.4 0.8 %collective-permute-done.10.refs_2_ = f32[3,32,128]{2,1,0:T(8,128)S(1)} collective-permute-done((f32[3,32,128]{2,1,0:T(8,128)S(1)}, f32[3,32,128]{2,1,0:T(8,128)S(1)}, u32[]{:S(2)}, u32[]{:S(2)}) %collective-permute-start.10) | collective-permute-done | bytes 49184 | tf_op jit(solution)/shard_map/ppermute | solution.py:25
  39.2 0.0 collective-permute-done.9.refs_1_
  39.2 0.6 %gram.1 = (f32[3,32,128]{2,1,0:T(8,128)S(1)}, f32[32,64]{1,0:T(8,128)S(1)}) custom-call(f32[32,32]{1,0:T(8,128)S(1)} %factor.1.inverse, f32[3,32,128]{2,1,0:T(8,128)S(1)} %get-tuple-element.25.tiles, f32[3,32,128]{2,1,0:T(8,128)S(1)} %get-tuple-element.31.refs_0_, f32[3,32,128]{2,1,0:T(8,128)S(1)} %collective-permute-done.9.refs_1_, ...), custom_call_target="tpu_custom_call" | custom-call | tf_op jit(solution)/shard_map/gram/pallas_call | solution.py:237
  39.9 2.0 %collective-permute-start.14 = (f32[32,64]{1,0:T(8,128)S(1)}, f32[32,64]{1,0:T(8,128)S(1)}, u32[]{:S(2)}, u32[]{:S(2)}) collective-permute-start(f32[32,64]{1,0:T(8,128)S(1)} %get-tuple-element.33.refs_0_), channel_id=1, source_target_pairs={{0,12},{4,8},{8,4},{12,0},{1,13},{5,9},{9,5},{13,1},{2,14},{6,10},... | collective-permute-start | bytes 24584 | tf_op jit(solution)/shard_map/ppermute | solution.py:25
  41.9 0.8 %collective-permute-start.13 = (f32[32,64]{1,0:T(8,128)S(1)}, f32[32,64]{1,0:T(8,128)S(1)}, u32[]{:S(2)}, u32[]{:S(2)}) collective-permute-start(f32[32,64]{1,0:T(8,128)S(1)} %get-tuple-element.33.refs_0_), channel_id=1, source_target_pairs={{0,8},{4,12},{8,0},{12,4},{1,9},{5,13},{9,1},{13,5},{2,10},{6,14},... | collective-permute-start | bytes 24584 | tf_op jit(solution)/shard_map/ppermute | solution.py:25
  42.7 1.7 %collective-permute-start.12 = (f32[32,64]{1,0:T(8,128)S(1)}, f32[32,64]{1,0:T(8,128)S(1)}, u32[]{:S(2)}, u32[]{:S(2)}) collective-permute-start(f32[32,64]{1,0:T(8,128)S(1)} %get-tuple-element.33.refs_0_), channel_id=1, source_target_pairs={{0,4},{4,0},{8,12},{12,8},{1,5},{5,1},{9,13},{13,9},{2,6},{6,2},{1... | collective-permute-start | bytes 24584 | tf_op jit(solution)/shard_map/ppermute | solution.py:25
  44.4 1.2 %collective-permute-done.14.refs_3_ = f32[32,64]{1,0:T(8,128)S(1)} collective-permute-done((f32[32,64]{1,0:T(8,128)S(1)}, f32[32,64]{1,0:T(8,128)S(1)}, u32[]{:S(2)}, u32[]{:S(2)}) %collective-permute-start.14) | collective-permute-done | bytes 8224 | tf_op jit(solution)/shard_map/ppermute | solution.py:25
  45.6 1.0 %collective-permute-done.13.refs_2_ = f32[32,64]{1,0:T(8,128)S(1)} collective-permute-done((f32[32,64]{1,0:T(8,128)S(1)}, f32[32,64]{1,0:T(8,128)S(1)}, u32[]{:S(2)}, u32[]{:S(2)}) %collective-permute-start.13) | collective-permute-done | bytes 8224 | tf_op jit(solution)/shard_map/ppermute | solution.py:25
  46.6 0.0 collective-permute-done.12.refs_1_
  46.6 1.6 %last.1 = (f32[32,384]{1,0:T(8,128)}, f32[32,32]{1,0:T(8,128)}) custom-call(f32[3,32,128]{2,1,0:T(8,128)S(1)} %get-tuple-element.32.image, f32[32,64]{1,0:T(8,128)S(1)} %get-tuple-element.33.refs_0_, f32[32,64]{1,0:T(8,128)S(1)} %collective-permute-done.12.refs_1_, f32[32,64]{1,0:T(8,128)S(1)} %collective-permute-done.13.refs_2_, ...), custom_call_target="tpu_custom_call" | custom-call | tf_op jit(solution)/shard_map/last/pallas_call | solution.py:244
Async XLA Ops:
  0.6 0.7 %copy-start.3 = (s32[3]{0:T(128)S(1)}, s32[3]{0:T(128)}, u32[]{:S(2)}) copy-start(s32[3]{0:T(128)} %counts.7) | copy-start | bytes 40
  1.3 1.1 %copy-start = (f32[3,3,128,128]{3,2,1,0:T(8,128)S(1)}, f32[3,3,128,128]{3,2,1,0:T(8,128)}, u32[]{:S(2)}) copy-start(f32[3,3,128,128]{3,2,1,0:T(8,128)} %blocks.7) | copy-start | bytes 1769476
  2.4 0.8 %copy-start.1 = (f32[384,32]{0,1:T(8,128)S(1)}, f32[384,32]{0,1:T(8,128)}, u32[]{:S(2)}) copy-start(f32[384,32]{0,1:T(8,128)} %param.7) | copy-start | bytes 147460
  3.2 0.7 %copy-start.2 = (s32[3,3]{1,0:T(4,128)S(1)}, s32[3,3]{1,0:T(4,128)}, u32[]{:S(2)}) copy-start(s32[3,3]{1,0:T(4,128)} %ids.7) | copy-start | bytes 112
  5.0 5.7 %collective-permute-start = (f32[3,32,128]{2,1,0:T(8,128)S(1)}, f32[3,32,128]{2,1,0:T(8,128)S(1)}, u32[]{:S(2)}, u32[]{:S(2)}) collective-permute-start(f32[3,32,128]{2,1,0:T(8,128)S(1)} %get-tuple-element.21), channel_id=1, source_target_pairs={{0,4},{4,0},{8,12},{12,8},{1,5},{5,1},{9,13},{13,9},{2,6},{6,2},{1... | collective-permute-start | bytes 147464 | tf_op jit(solution)/shard_map/ppermute | solution.py:25
  8.1 5.9 %collective-permute-start.1 = (f32[3,32,128]{2,1,0:T(8,128)S(1)}, f32[3,32,128]{2,1,0:T(8,128)S(1)}, u32[]{:S(2)}, u32[]{:S(2)}) collective-permute-start(f32[3,32,128]{2,1,0:T(8,128)S(1)} %get-tuple-element.22), channel_id=1, source_target_pairs={{0,8},{4,12},{8,0},{12,4},{1,9},{5,13},{9,1},{13,5},{2,10},{6,14},... | collective-permute-start | bytes 147464 | tf_op jit(solution)/shard_map/ppermute | solution.py:25
  10.7 5.9 %collective-permute-start.2 = (f32[3,32,128]{2,1,0:T(8,128)S(1)}, f32[3,32,128]{2,1,0:T(8,128)S(1)}, u32[]{:S(2)}, u32[]{:S(2)}) collective-permute-start(f32[3,32,128]{2,1,0:T(8,128)S(1)} %get-tuple-element.23), channel_id=1, source_target_pairs={{0,12},{4,8},{8,4},{12,0},{1,13},{5,9},{9,5},{13,1},{2,14},{6,10},... | collective-permute-start | bytes 147464 | tf_op jit(solution)/shard_map/ppermute | solution.py:25
  18.2 4.0 %collective-permute-start.5 = (f32[3,32,128]{2,1,0:T(8,128)S(1)}, f32[3,32,128]{2,1,0:T(8,128)S(1)}, u32[]{:S(2)}, u32[]{:S(2)}) collective-permute-start(f32[3,32,128]{2,1,0:T(8,128)S(1)} %direct_first.1.refs_0_), channel_id=1, source_target_pairs={{0,3},{1,2},{2,1},{3,0},{4,7},{5,6},{6,5},{7,4},{8,11},{9,10},{10,... | collective-permute-start | bytes 147464 | tf_op jit(solution)/shard_map/ppermute | solution.py:25
  18.2 4.9 %collective-permute-start.4 = (f32[3,32,128]{2,1,0:T(8,128)S(1)}, f32[3,32,128]{2,1,0:T(8,128)S(1)}, u32[]{:S(2)}, u32[]{:S(2)}) collective-permute-start(f32[3,32,128]{2,1,0:T(8,128)S(1)} %direct_first.1.refs_0_), channel_id=1, source_target_pairs={{0,2},{1,3},{2,0},{3,1},{4,6},{5,7},{6,4},{7,5},{8,10},{9,11},{10,... | collective-permute-start | bytes 147464 | tf_op jit(solution)/shard_map/ppermute | solution.py:25
  19.7 3.3 %collective-permute-start.3 = (f32[3,32,128]{2,1,0:T(8,128)S(1)}, f32[3,32,128]{2,1,0:T(8,128)S(1)}, u32[]{:S(2)}, u32[]{:S(2)}) collective-permute-start(f32[3,32,128]{2,1,0:T(8,128)S(1)} %direct_first.1.refs_0_), channel_id=1, source_target_pairs={{0,1},{1,0},{2,3},{3,2},{4,5},{5,4},{6,7},{7,6},{8,9},{9,8},{10,11... | collective-permute-start | bytes 147464 | tf_op jit(solution)/shard_map/ppermute | solution.py:25
  24.4 5.2 %collective-permute-start.6 = (f32[4,32,128]{2,1,0:T(8,128)S(1)}, f32[4,32,128]{2,1,0:T(8,128)S(1)}, u32[]{:S(2)}, u32[]{:S(2)}) collective-permute-start(f32[4,32,128]{2,1,0:T(8,128)S(1)} %get-tuple-element.26), channel_id=1, source_target_pairs={{0,4},{4,0},{8,12},{12,8},{1,5},{5,1},{9,13},{13,9},{2,6},{6,2},{1... | collective-permute-start | bytes 196616 | tf_op jit(solution)/shard_map/ppermute | solution.py:25
  24.4 8.6 %collective-permute-start.7 = (f32[4,32,128]{2,1,0:T(8,128)S(1)}, f32[4,32,128]{2,1,0:T(8,128)S(1)}, u32[]{:S(2)}, u32[]{:S(2)}) collective-permute-start(f32[4,32,128]{2,1,0:T(8,128)S(1)} %get-tuple-element.27), channel_id=1, source_target_pairs={{0,8},{4,12},{8,0},{12,4},{1,9},{5,13},{9,1},{13,5},{2,10},{6,14},... | collective-permute-start | bytes 196616 | tf_op jit(solution)/shard_map/ppermute | solution.py:25
  25.7 7.3 %collective-permute-start.8 = (f32[4,32,128]{2,1,0:T(8,128)S(1)}, f32[4,32,128]{2,1,0:T(8,128)S(1)}, u32[]{:S(2)}, u32[]{:S(2)}) collective-permute-start(f32[4,32,128]{2,1,0:T(8,128)S(1)} %get-tuple-element.28), channel_id=1, source_target_pairs={{0,12},{4,8},{8,4},{12,0},{1,13},{5,9},{9,5},{13,1},{2,14},{6,10},... | collective-permute-start | bytes 196616 | tf_op jit(solution)/shard_map/ppermute | solution.py:25
  34.6 3.8 %collective-permute-start.11 = (f32[3,32,128]{2,1,0:T(8,128)S(1)}, f32[3,32,128]{2,1,0:T(8,128)S(1)}, u32[]{:S(2)}, u32[]{:S(2)}) collective-permute-start(f32[3,32,128]{2,1,0:T(8,128)S(1)} %get-tuple-element.31.refs_0_), channel_id=1, source_target_pairs={{0,3},{1,2},{2,1},{3,0},{4,7},{5,6},{6,5},{7,4},{8,11},{9,10},{10,... | collective-permute-start | bytes 147464 | tf_op jit(solution)/shard_map/ppermute | solution.py:25
  34.6 4.6 %collective-permute-start.10 = (f32[3,32,128]{2,1,0:T(8,128)S(1)}, f32[3,32,128]{2,1,0:T(8,128)S(1)}, u32[]{:S(2)}, u32[]{:S(2)}) collective-permute-start(f32[3,32,128]{2,1,0:T(8,128)S(1)} %get-tuple-element.31.refs_0_), channel_id=1, source_target_pairs={{0,2},{1,3},{2,0},{3,1},{4,6},{5,7},{6,4},{7,5},{8,10},{9,11},{10,... | collective-permute-start | bytes 147464 | tf_op jit(solution)/shard_map/ppermute | solution.py:25
  35.8 3.5 %collective-permute-start.9 = (f32[3,32,128]{2,1,0:T(8,128)S(1)}, f32[3,32,128]{2,1,0:T(8,128)S(1)}, u32[]{:S(2)}, u32[]{:S(2)}) collective-permute-start(f32[3,32,128]{2,1,0:T(8,128)S(1)} %get-tuple-element.31.refs_0_), channel_id=1, source_target_pairs={{0,1},{1,0},{2,3},{3,2},{4,5},{5,4},{6,7},{7,6},{8,9},{9,8},{10,11... | collective-permute-start | bytes 147464 | tf_op jit(solution)/shard_map/ppermute | solution.py:25
  39.9 5.7 %collective-permute-start.14 = (f32[32,64]{1,0:T(8,128)S(1)}, f32[32,64]{1,0:T(8,128)S(1)}, u32[]{:S(2)}, u32[]{:S(2)}) collective-permute-start(f32[32,64]{1,0:T(8,128)S(1)} %get-tuple-element.33.refs_0_), channel_id=1, source_target_pairs={{0,12},{4,8},{8,4},{12,0},{1,13},{5,9},{9,5},{13,1},{2,14},{6,10},... | collective-permute-start | bytes 24584 | tf_op jit(solution)/shard_map/ppermute | solution.py:25
  41.9 4.7 %collective-permute-start.13 = (f32[32,64]{1,0:T(8,128)S(1)}, f32[32,64]{1,0:T(8,128)S(1)}, u32[]{:S(2)}, u32[]{:S(2)}) collective-permute-start(f32[32,64]{1,0:T(8,128)S(1)} %get-tuple-element.33.refs_0_), channel_id=1, source_target_pairs={{0,8},{4,12},{8,0},{12,4},{1,9},{5,13},{9,1},{13,5},{2,10},{6,14},... | collective-permute-start | bytes 24584 | tf_op jit(solution)/shard_map/ppermute | solution.py:25
  42.7 3.9 %collective-permute-start.12 = (f32[32,64]{1,0:T(8,128)S(1)}, f32[32,64]{1,0:T(8,128)S(1)}, u32[]{:S(2)}, u32[]{:S(2)}) collective-permute-start(f32[32,64]{1,0:T(8,128)S(1)} %get-tuple-element.33.refs_0_), channel_id=1, source_target_pairs={{0,4},{4,0},{8,12},{12,8},{1,5},{5,1},{9,13},{13,9},{2,6},{6,2},{1... | collective-permute-start | bytes 24584 | tf_op jit(solution)/shard_map/ppermute | solution.py:25

commit v3 on v2

v3 whole, which is shorter than its diff:
```python
import functools

import jax
import jax.numpy as jnp
from jax import lax
from jax.experimental import pallas as pl
from jax.experimental.pallas import tpu as pltpu
from jax.sharding import PartitionSpec as P

F32 = jnp.float32
BF16 = jnp.bfloat16
VMEM = pl.BlockSpec(memory_space=pltpu.VMEM)
SMEM = pl.BlockSpec(memory_space=pltpu.SMEM)
HBM = pl.BlockSpec(memory_space=pltpu.HBM)
DMA = pltpu.SemaphoreType.DMA
PANEL = 8
PARAMS = pltpu.CompilerParams(vmem_limit_bytes=8 * 2**20)


def tree(parts):
    while len(parts) > 1:
        parts = [parts[i] + parts[i + 1] for i in range(0, len(parts), 2)]
    return parts[0]


def split(x):
    high = x.astype(BF16)
    rest = x - high.astype(F32)
    middle = rest.astype(BF16)
    return high, middle, (rest - middle.astype(F32)).astype(BF16)


def product(a_parts, b_parts, contract=0):
    n = a_parts[0].shape[0]

    def dot(a, b):
        return lax.dot_general(a, b, (((1,), (contract,)), ((), ())), preferred_element_type=F32)

    stacked = jnp.concatenate(a_parts, axis=0)
    high = dot(stacked, b_parts[0])
    middle = dot(stacked[: 2 * n], b_parts[1])
    low = dot(a_parts[0], b_parts[2])
    return high[:n] + ((high[n : 2 * n] + middle[:n]) + ((high[2 * n :] + middle[n:]) + low))


def joined(parts, axis):
    return [jnp.concatenate(level, axis=axis) for level in zip(*parts)]


def swap(x, axis, distance):
    return lax.ppermute(x, axis, [(i, i ^ distance) for i in range(lax.axis_size(axis))])


def swap_rows(x, even, odd):
    rows, parts = lax.axis_size("row"), lax.axis_size("nbr")
    pairs = [
        (r * parts + n, (r ^ (odd if n % 2 else even)) * parts + n) for r in range(rows) for n in range(parts)
    ]
    return lax.ppermute(x, ("row", "nbr"), pairs)


class Place:
    def __init__(self, rows, block_rows, slots):
        self.row = lax.axis_index("row")
        self.part = lax.axis_index("nbr")
        self.odd = self.part & 1
        self.block_rows, self.slots = block_rows, slots
        self.first_row = self.row * block_rows
        self.half = rows // 2
        self.peers = [self.row ^ (k + self.odd * self.half) for k in range(1, self.half)]
        self.middle = self.row ^ self.half

    def weight(self, ids, counts, member, i, p):
        slot = (self.part ^ member) * self.slots + p
        used = slot < counts[i]
        return jnp.where(used, jnp.where(ids[i, p] == self.first_row + i, 0.5, 1.0), 0.0).astype(F32)


def transposed_products(place, blocks, ids, counts, tiles, out):
    out[...] = jnp.zeros_like(out)
    size = out.shape[2]
    for i in range(place.block_rows):
        stored = [split(b[i, p]) for b in blocks for p in range(place.slots)]
        value = product(split(tiles[i]), joined(stored, 1))
        for m in range(len(blocks)):
            for p in range(place.slots):
                at = (m * place.slots + p) * size
                out[ids[m][i, p]] += value[:, at : at + size] * place.weight(ids[m], counts, m, i, p)


def direct_products(place, blocks, ids, counts, whole, i):
    stored, far = [], []
    for m, b in enumerate(blocks):
        for p in range(place.slots):
            stored.append(split(b[i, p].T))
            far.append(split(whole[ids[m][i, p]] * place.weight(ids[m], counts, m, i, p)))
    return product(joined(far, 1), joined(stored, 0))


def fill(place, messages, shared, products, tiles):
    n = place.block_rows
    for peer, out in zip(place.peers, messages):
        for i in range(n):
            out[i] = jnp.where(place.row < peer, products[peer * n + i], tiles[i])
    height = shared.shape[1]
    columns = pl.ds(place.odd * height, height)
    for i in range(n):
        shared[i] = jnp.where(
            place.row < place.middle, products[place.middle * n + i, columns], tiles[i, columns]
        )


def own_products(place, products, own):
    mine = products[pl.ds(place.first_row, place.block_rows)]
    own[...] = jnp.where(place.odd == 0, mine, 0.0)


def first_kernel(rows, blocks, other, ids, other_ids, counts, start, *refs):
    half = rows // 2
    messages, refs = refs[: half - 1], refs[half - 1 :]
    shared, own, tiles, held, products, ids_s, other_s, counts_s, sems = refs
    block_rows, slots, size, _ = blocks.shape
    place = Place(rows, block_rows, slots)
    copies = [
        pltpu.make_async_copy(blocks, held, sems.at[0]),
        pltpu.make_async_copy(ids, ids_s, sems.at[1]),
        pltpu.make_async_copy(other_ids, other_s, sems.at[2]),
        pltpu.make_async_copy(counts, counts_s, sems.at[3]),
    ]
    for i in range(block_rows):
        copies.append(pltpu.make_async_copy(start.at[:, i * size : (i + 1) * size], tiles.at[i], sems.at[4 + i]))
    for copy in copies:
        copy.start()
    for copy in copies:
        copy.wait()
    transposed_products(place, (held, other), (ids_s, other_s), counts_s, tiles, products)
    fill(place, messages, shared, products, tiles)
    own_products(place, products, own)


def direct_kernel(rows, with_gram, held, other, ids, other_ids, counts, own, tiles, *refs):
    half = rows // 2
    received, shared, refs = refs[: half - 1], refs[half - 1], refs[half:]
    if with_gram:
        gram, out, longer, whole = refs
    else:
        out, whole = refs
    block_rows, slots, size, _ = held.shape
    place = Place(rows, block_rows, slots)
    whole[...] = jnp.zeros_like(whole)
    whole[pl.ds(place.first_row, block_rows)] = jnp.where(place.odd == 0, tiles[...], 0.0)
    for peer, message in zip(place.peers, received):
        whole[pl.ds(peer * block_rows, block_rows)] = message[:block_rows]
    height = shared.shape[1]
    columns = pl.ds(place.odd * height, height)
    for i in range(block_rows):
        whole[place.middle * block_rows + i, columns] = shared[i]
    for i in range(block_rows):
        value = own[i]
        for peer, message in zip(place.peers, received):
            value += jnp.where(place.row > peer, message[i], 0.0)
        out[i] = value + direct_products(place, (held, other), (ids, other_ids), counts, whole, i)
        out[i, columns] += jnp.where(place.row > place.middle, shared[i], 0.0)
    if with_gram:
        for i in range(block_rows):
            longer[i] = out[i]
        n = 2 * height
        packed = shared[block_rows]
        middle = jnp.concatenate([packed[:, :n], packed[:, n : 2 * n]], axis=0)
        first = jnp.where(place.odd == 0, gram[:, :n], middle)
        longer[block_rows] = jnp.zeros_like(longer[block_rows])
        longer[block_rows, :, :n] = tree([first] + [message[block_rows][:, :n] for message in received])


def second_kernel(rows, parts, held, other, ids, other_ids, counts, *refs):
    images, refs = refs[:parts], refs[parts:]
    half = rows // 2
    messages, refs = refs[: half - 1], refs[half - 1 :]
    shared, own, tiles, gram, products = refs
    block_rows, slots, size, _ = held.shape
    place = Place(rows, block_rows, slots)
    for i in range(block_rows):
        tiles[i] = tree([image[i] for image in images])
    transposed_products(place, (held, other), (ids, other_ids), counts, tiles, products)
    fill(place, messages, shared, products, tiles)
    own_products(place, products, own)
    whole = joined([split(tiles[i]) for i in range(block_rows)], 1)
    partial = product(whole, whole, 1)
    gram[...] = jnp.zeros_like(gram)
    gram[:, : partial.shape[0]] = partial
    for message in messages:
        message[block_rows] = gram[...]
    height = shared.shape[1]
    shared[block_rows] = jnp.zeros_like(shared[block_rows])
    shared[block_rows, :, : 4 * height] = jnp.concatenate([partial[:height], partial[height:]], axis=1)


def inverse_factor(gram):
    n = gram.shape[0]
    rows = lax.broadcasted_iota(jnp.int32, (n, 2 * n), 0)
    lanes = lax.broadcasted_iota(jnp.int32, (n, 2 * n), 1)
    both = jnp.concatenate([jnp.where(rows == lanes, 1.0, 0.0)[:, :n], gram], axis=1)
    groups = [both[g : g + 8] for g in range(0, n, 8)]
    height = lax.broadcasted_iota(jnp.int32, (8, 2 * n), 0)
    for first in range(0, n, PANEL):
        columns = [
            [
                jnp.broadcast_to(group[:, n + first + t : n + first + t + 1], (8, 2 * n))
                for group in groups
            ]
            for t in range(PANEL)
        ]
        for t in range(PANEL):
            k = first + t
            gk, sk = k // 8, k % 8
            pivot = columns[t][gk][sk : sk + 1]
            inverse = 1.0 / pivot
            root = lax.rsqrt(pivot)
            source = groups[gk][sk : sk + 1]
            steps = {}
            for g in range(gk, len(groups)):
                m = columns[t][g] * inverse
                steps[g] = jnp.where(height > sk, m, 0.0) if g == gk else m
            for u in range(t + 1, PANEL):
                head = columns[u][gk][sk : sk + 1]
                for g in range(gk, len(groups)):
                    columns[u][g] = columns[u][g] - steps[g] * head
            for g in range(gk, len(groups)):
                groups[g] = groups[g] - steps[g] * source
            groups[gk] = jnp.where(height == sk, groups[gk] * root, groups[gk])
    return jnp.concatenate(groups, axis=0)[:, :n]


def factor_kernel(total, mine, others, out):
    block_rows = mine.shape[0] - 1
    columns = mine.shape[1]
    gram = mine[block_rows] + others[block_rows]
    out[...] = inverse_factor(gram[:, :columns] / total)


def gram_kernel(parts, inverse, tiles, *refs):
    images, (image, out) = refs[:parts], refs[parts:]
    block_rows, columns, size = tiles.shape
    lower = split(inverse[...])
    new = [tree([part[i] for part in images]) for i in range(block_rows)]
    value = product(lower, joined([split(new[i]) for i in range(block_rows)], 1))
    prior = product(lower, joined([split(tiles[i]) for i in range(block_rows)], 1))
    for i in range(block_rows):
        image[i] = value[:, i * size : (i + 1) * size]
    value = split(value)
    out[:, :columns] = product(value, value, 1)
    out[:, columns:] = product(split(prior), value, 1)


def last_kernel(rows, total, image, *refs):
    parts, (basis, ritz) = refs[:rows], refs[rows:]
    both = tree([part[...] for part in parts]) / total
    columns = both.shape[0]
    ritz[...] = both[:, columns:]
    lower = split(inverse_factor(both[:, :columns]))
    basis[...] = product(lower, joined([split(image[i]) for i in range(image.shape[0])], 1))


def body(blocks, partner_ids, counts, start):
    block_rows, slots, size, _ = blocks.shape
    columns = start.shape[1]
    rows, parts = lax.axis_size("row"), lax.axis_size("nbr")
    half = rows // 2
    all_blocks = block_rows * rows
    total = float(all_blocks * size)
    shape = jax.ShapeDtypeStruct
    tile = shape((block_rows, columns, size), F32)
    longer = shape((block_rows + 1, columns, size), F32)
    shorter = shape((block_rows, columns // 2, size), F32)
    shorter_longer = shape((block_rows + 1, columns // 2, size), F32)
    wide = shape((columns, size), F32)
    work = pltpu.VMEM((all_blocks, columns, size), F32)

    def call(kernel, name, specs, outs, scratch=()):
        return pl.pallas_call(
            kernel,
            name=name,
            in_specs=specs,
            out_specs=[VMEM] * len(outs),
            out_shape=outs,
            scratch_shapes=scratch,
            compiler_params=PARAMS,
        )

    def round_over_rows(messages, shared):
        return [swap_rows(m, k, k + half) for k, m in enumerate(messages, 1)], swap(shared, "row", half)

    def sum_over_parts(image):
        return [image] + [swap(image, "nbr", s) for s in range(1, parts)]

    other = swap(blocks, "nbr", 1)
    other_ids = swap(partner_ids, "nbr", 1)
    *messages, shared, own, tiles, held = call(
        functools.partial(first_kernel, rows),
        "first_transposed",
        [HBM, VMEM, HBM, HBM, HBM, HBM],
        [tile] * (half - 1) + [shorter, tile, tile, shape(blocks.shape, F32)],
        [
            work,
            pltpu.SMEM(partner_ids.shape, jnp.int32),
            pltpu.SMEM(partner_ids.shape, jnp.int32),
            pltpu.SMEM(counts.shape, jnp.int32),
            DMA((4 + block_rows,)),
        ],
    )(blocks, other, partner_ids, other_ids, counts, start.T)
    stored = (held, other, partner_ids, other_ids, counts)
    index = [VMEM, VMEM, SMEM, SMEM, SMEM]
    received, shared = round_over_rows(messages, shared)
    (image,) = call(
        functools.partial(direct_kernel, rows, False), "first_direct", index + [VMEM] * (half + 2), [tile], [work]
    )(*stored, own, tiles, *received, shared)
    images = sum_over_parts(image)
    *messages, shared, own, tiles, gram = call(
        functools.partial(second_kernel, rows, parts),
        "second_transposed",
        index + [VMEM] * parts,
        [longer] * (half - 1) + [shorter_longer, tile, tile, wide],
        [work],
    )(*stored, *images)
    received, shared = round_over_rows(messages, shared)
    image, mine = call(
        functools.partial(direct_kernel, rows, True),
        "second_direct",
        index + [VMEM] * (half + 3),
        [tile, longer],
        [work],
    )(*stored, own, tiles, *received, shared, gram)
    pair = swap(mine, "nbr", 1)
    images = [image, pair] + [swap(image, "nbr", s) for s in range(2, parts)]
    (inverse,) = call(
        functools.partial(factor_kernel, total), "factor", [VMEM] * 2, [shape((columns, columns), F32)]
    )(mine, pair)
    image, both = call(
        functools.partial(gram_kernel, parts),
        "gram",
        [VMEM] * (parts + 2),
        [tile, shape((columns, 2 * columns), F32)],
    )(inverse, tiles, *images)
    boths = [both] + [swap(both, "row", s) for s in range(1, rows)]
    basis, ritz = call(
        functools.partial(last_kernel, rows, total),
        "last",
        [VMEM] * (rows + 1),
        [shape(start.shape[::-1], F32), shape((columns, columns), F32)],
    )(image, *boths)
    return basis.T, ritz


def solution(mesh):
    return jax.shard_map(
        body,
        mesh=mesh,
        in_specs=(
            P(("dom", "row"), "nbr", None, None),
            P(("dom", "row"), "nbr"),
            P(("dom", "row")),
            P(("dom", "row"), None),
        ),
        out_specs=(P(("dom", "row"), None), P("dom", None)),
        check_vma=False,
    )
```

time: 48.5 us -> 45.2 us (0.932)
  waiting for transfers between devices: 17.3 us -> 16.3 us
  Pallas kernels: 8.7 us -> 7.89 us
  starting transfers between devices: 18.3 us -> 17.5 us
  local copies, waits for them, and re-layouts: 3.19 us -> 2.55 us
    ppermute x15 -> x13, starting transfers between devices: 18.3 us -> 14.3 us  [swap(): lax.ppermute(x, axis, [(i, i ^ distance) for i in range(lax.axis_size(axi...]
    ppermute x0 -> x2, starting transfers between devices: none -> 3.24 us  [swap_rows(): return lax.ppermute(x, ('row', 'nbr'), pairs)]
    ppermute x15 -> x13, waiting for transfers between devices: 17.3 us -> 16.2 us  [swap(): lax.ppermute(x, axis, [(i, i ^ distance) for i in range(lax.axis_size(axi...]
    unnamed x8 -> x10, local copies, waits for them, and re-layouts: 3.19 us -> 2.55 us
    pallas_call x5, Pallas kernels: 6.43 us -> 5.79 us  [the longest x1 1.3 us: body(): call(functools.partial(first_kernel, rows), 'first_transposed', [HBM, VME...]
  transfers between devices with their start and end apart: 15 -> 15, of which waited for: 10 -> 9; matrix products, arithmetic and copies ran while one was open for 0% -> 0% of each run, Pallas kernels for 2% -> 2%
where the time goes in v3:
time: 45.2 us; the launch traced here: 44.9 us
  starting transfers between devices  17.5 us (39%)
  waiting for transfers between devices  16.3 us (36%)
  Pallas kernels  7.89 us (17%)
  local copies, waits for them, and re-layouts  2.55 us (6%)
  between operations  0.68 us (2%)
    ppermute x13, waiting for transfers between devices, swap(): lax.ppermute(x, axis, [(i, i ^ distance) for i in range(lax.axis_size(axi...  16.2 us
    ppermute x13, starting transfers between devices, swap(): lax.ppermute(x, axis, [(i, i ^ distance) for i in range(lax.axis_size(axi...  14.3 us
    ppermute x2, starting transfers between devices, swap_rows(): return lax.ppermute(x, ('row', 'nbr'), pairs)  3.24 us
    unnamed x10, local copies, waits for them, and re-layouts  2.55 us
    pallas_call x1, Pallas kernels, body(): call(functools.partial(last_kernel, rows, total), 'last', [VMEM] * (rows...  1.64 us
    pallas_call x1, Pallas kernels, body(): call(functools.partial(first_kernel, rows), 'first_transposed', [HBM, VME...  1.3 us
    pallas_call x1, Pallas kernels, body(): call(functools.partial(direct_kernel, rows, True), 'second_direct', index...  1.23 us
    pallas_call x1, Pallas kernels, body(): call(functools.partial(second_kernel, rows, parts), 'second_transposed',...  1.22 us
  transfers between devices with their start and end apart: 15, of which 9 were waited for; matrix products, arithmetic and copies ran while one was open for 0% of the time, Pallas kernels for 2%

profile of v3, /device:TPU:0, one launch (start us, length us, event | category | flops | bytes accessed | tf_op | source)
XLA Modules:
  0.0 44.9 jit_solution(10217028727266934405)
XLA Ops:
  0.6 0.0 copy-start.4
  0.6 0.5 %collective-permute-start = (f32[3,3,128,128]{3,2,1,0:T(8,128)}, f32[3,3,128,128]{3,2,1,0:T(8,128)S(1)}, u32[]{:S(2)}, u32[]{:S(2)}) collective-permute-start(f32[3,3,128,128]{3,2,1,0:T(8,128)} %blocks.1), channel_id=1, source_target_pairs={{0,1},{1,0},{2,3},{3,2},{4,5},{5,4},{6,7},{7,6},{8,9},{9,8},{10,11... | collective-permute-start | bytes 1769480 | tf_op jit(solution)/shard_map/ppermute | solution.py:51
  1.2 0.1 collective-permute-start.1
  1.2 1.8 %collective-permute-done.1.other_ids = s32[3,3]{1,0:T(4,128)S(1)} collective-permute-done((s32[3,3]{1,0:T(4,128)}, s32[3,3]{1,0:T(4,128)S(1)}, u32[]{:S(2)}, u32[]{:S(2)}) %collective-permute-start.1) | collective-permute-done | bytes 68 | tf_op jit(solution)/shard_map/ppermute | solution.py:51
  3.0 0.0 collective-permute-done.other
  3.0 0.0 copy-done.4
  3.0 0.0 copy-start
  3.0 1.1 %copy-done = f32[3,3,128,128]{3,2,1,0:T(8,128)S(1)} copy-done((f32[3,3,128,128]{3,2,1,0:T(8,128)S(1)}, f32[3,3,128,128]{3,2,1,0:T(8,128)}, u32[]{:S(2)}) %copy-start) | copy-done | bytes 589848
  4.1 0.0 copy-start.1
  4.1 0.8 %copy-done.1 = f32[384,32]{0,1:T(8,128)S(1)} copy-done((f32[384,32]{0,1:T(8,128)S(1)}, f32[384,32]{0,1:T(8,128)}, u32[]{:S(2)}) %copy-start.1) | copy-done | bytes 49176
  4.9 0.0 copy-start.2
  4.9 0.7 %copy-done.2 = s32[3,3]{1,0:T(4,128)S(1)} copy-done((s32[3,3]{1,0:T(4,128)S(1)}, s32[3,3]{1,0:T(4,128)}, u32[]{:S(2)}) %copy-start.2) | copy-done | bytes 60
  5.6 1.3 %first_transposed.1 = (f32[3,32,128]{2,1,0:T(8,128)S(1)}, f32[3,16,128]{2,1,0:T(8,128)S(1)}, f32[3,32,128]{2,1,0:T(8,128)S(1)}, f32[3,32,128]{2,1,0:T(8,128)S(1)}, f32[3,3,128,128]{3,2,1,0:T(8,128)S(1)}) custom-call(f32[3,3,128,128]{3,2,1,0:T(8,128)S(1)} %copy-done, f32[3,3,128,128]{3,2,1,0:T(8,128)S(1)} %collective-permute-done.other, ...), custom_call_target="tpu_custom_call" | custom-call | tf_op jit(solution)/shard_map/first_transposed/pallas_call | solution.py:298
  6.9 3.0 %collective-permute-start.2 = (f32[3,32,128]{2,1,0:T(8,128)S(1)}, f32[3,32,128]{2,1,0:T(8,128)S(1)}, u32[]{:S(2)}, u32[]{:S(2)}) collective-permute-start(f32[3,32,128]{2,1,0:T(8,128)S(1)} %get-tuple-element.21), channel_id=1, source_target_pairs={{0,4},{1,13},{2,6},{3,15},{4,0},{5,9},{6,2},{7,11},{8,12},{9,5},{1... | collective-permute-start | bytes 147464 | tf_op jit(solution)/shard_map/ppermute | solution.py:59
  9.9 2.6 %collective-permute-start.3 = (f32[3,16,128]{2,1,0:T(8,128)S(1)}, f32[3,16,128]{2,1,0:T(8,128)S(1)}, u32[]{:S(2)}, u32[]{:S(2)}) collective-permute-start(f32[3,16,128]{2,1,0:T(8,128)S(1)} %get-tuple-element.22), channel_id=1, source_target_pairs={{0,8},{4,12},{8,0},{12,4},{1,9},{5,13},{9,1},{13,5},{2,10},{6,14},... | collective-permute-start | bytes 73736 | tf_op jit(solution)/shard_map/ppermute | solution.py:51
  12.5 2.3 %collective-permute-done.3.refs_1_ = f32[3,16,128]{2,1,0:T(8,128)S(1)} collective-permute-done((f32[3,16,128]{2,1,0:T(8,128)S(1)}, f32[3,16,128]{2,1,0:T(8,128)S(1)}, u32[]{:S(2)}, u32[]{:S(2)}) %collective-permute-start.3) | collective-permute-done | bytes 24608 | tf_op jit(solution)/shard_map/ppermute | solution.py:51
  14.8 0.0 collective-permute-done.2.refs_0_
  14.8 0.0 copy-start.3
  14.8 1.2 %first_direct.1.refs_0_ = f32[3,32,128]{2,1,0:T(8,128)S(1)} custom-call(f32[3,3,128,128]{3,2,1,0:T(8,128)S(1)} %get-tuple-element.18.held, f32[3,3,128,128]{3,2,1,0:T(8,128)S(1)} %collective-permute-done.other, s32[3,3]{1,0:T(4,128)S(1)} %copy-done.2, s32[3,3]{1,0:T(4,128)S(1)} %collective-permute-done.1.other_ids, s32[3]{0:T(128)S(1)} %copy-done.4, ...), custom_call_target="tpu_custom_call" | custom-call | tf_op jit(solution)/shard_map/first_direct/pallas_call | solution.py:314
  16.0 1.7 %collective-permute-start.6 = (f32[3,32,128]{2,1,0:T(8,128)S(1)}, f32[3,32,128]{2,1,0:T(8,128)S(1)}, u32[]{:S(2)}, u32[]{:S(2)}) collective-permute-start(f32[3,32,128]{2,1,0:T(8,128)S(1)} %first_direct.1.refs_0_), channel_id=1, source_target_pairs={{0,3},{1,2},{2,1},{3,0},{4,7},{5,6},{6,5},{7,4},{8,11},{9,10},{10,... | collective-permute-start | bytes 147464 | tf_op jit(solution)/shard_map/ppermute | solution.py:51
  17.7 0.5 %collective-permute-start.5 = (f32[3,32,128]{2,1,0:T(8,128)S(1)}, f32[3,32,128]{2,1,0:T(8,128)S(1)}, u32[]{:S(2)}, u32[]{:S(2)}) collective-permute-start(f32[3,32,128]{2,1,0:T(8,128)S(1)} %first_direct.1.refs_0_), channel_id=1, source_target_pairs={{0,2},{1,3},{2,0},{3,1},{4,6},{5,7},{6,4},{7,5},{8,10},{9,11},{10,... | collective-permute-start | bytes 147464 | tf_op jit(solution)/shard_map/ppermute | solution.py:51
  18.3 0.0 collective-permute-start.4
  18.3 1.5 %collective-permute-done.6.refs_3_ = f32[3,32,128]{2,1,0:T(8,128)S(1)} collective-permute-done((f32[3,32,128]{2,1,0:T(8,128)S(1)}, f32[3,32,128]{2,1,0:T(8,128)S(1)}, u32[]{:S(2)}, u32[]{:S(2)}) %collective-permute-start.6) | collective-permute-done | bytes 49184 | tf_op jit(solution)/shard_map/ppermute | solution.py:51
  19.8 2.0 %collective-permute-done.5.refs_2_ = f32[3,32,128]{2,1,0:T(8,128)S(1)} collective-permute-done((f32[3,32,128]{2,1,0:T(8,128)S(1)}, f32[3,32,128]{2,1,0:T(8,128)S(1)}, u32[]{:S(2)}, u32[]{:S(2)}) %collective-permute-start.5) | collective-permute-done | bytes 49184 | tf_op jit(solution)/shard_map/ppermute | solution.py:51
  21.8 0.0 collective-permute-done.4.refs_1_
  21.8 0.0 copy-done.3
  21.8 1.2 %second_transposed.1 = (f32[4,32,128]{2,1,0:T(8,128)S(1)}, f32[4,16,128]{2,1,0:T(8,128)S(1)}, f32[3,32,128]{2,1,0:T(8,128)S(1)}, f32[3,32,128]{2,1,0:T(8,128)S(1)}, f32[32,128]{1,0:T(8,128)S(1)}) custom-call(f32[3,3,128,128]{3,2,1,0:T(8,128)S(1)} %get-tuple-element.18.held, f32[3,3,128,128]{3,2,1,0:T(8,128)S(1)} %collective-permute-done.other, ...), custom_call_target="tpu_custom_call" | custom-call | tf_op jit(solution)/shard_map/second_transposed/pallas_call | solution.py:318
  23.1 0.2 collective-permute-start.7
  23.3 2.2 %collective-permute-start.8 = (f32[4,16,128]{2,1,0:T(8,128)S(1)}, f32[4,16,128]{2,1,0:T(8,128)S(1)}, u32[]{:S(2)}, u32[]{:S(2)}) collective-permute-start(f32[4,16,128]{2,1,0:T(8,128)S(1)} %get-tuple-element.26), channel_id=1, source_target_pairs={{0,8},{4,12},{8,0},{12,4},{1,9},{5,13},{9,1},{13,5},{2,10},{6,14},... | collective-permute-start | bytes 98312 | tf_op jit(solution)/shard_map/ppermute | solution.py:51
  25.5 2.8 %collective-permute-done.8.refs_1_ = f32[4,16,128]{2,1,0:T(8,128)S(1)} collective-permute-done((f32[4,16,128]{2,1,0:T(8,128)S(1)}, f32[4,16,128]{2,1,0:T(8,128)S(1)}, u32[]{:S(2)}, u32[]{:S(2)}) %collective-permute-start.8) | collective-permute-done | bytes 32800 | tf_op jit(solution)/shard_map/ppermute | solution.py:51
  28.3 0.0 collective-permute-done.7.refs_0_
  28.3 1.2 %second_direct.1 = (f32[3,32,128]{2,1,0:T(8,128)S(1)}, f32[4,32,128]{2,1,0:T(8,128)S(1)}) custom-call(f32[3,3,128,128]{3,2,1,0:T(8,128)S(1)} %get-tuple-element.18.held, f32[3,3,128,128]{3,2,1,0:T(8,128)S(1)} %collective-permute-done.other, s32[3,3]{1,0:T(4,128)S(1)} %copy-done.3, s32[3,3]{1,0:T(4,128)S(1)} %collective-permute-done.1.other_ids, ...), custom_call_target="tpu_custom_call" | custom-call | tf_op jit(solution)/shard_map/second_direct/pallas_call | solution.py:326
  29.5 0.4 collective-permute-start.9
  29.9 1.2 %collective-permute-start.11 = (f32[3,32,128]{2,1,0:T(8,128)S(1)}, f32[3,32,128]{2,1,0:T(8,128)S(1)}, u32[]{:S(2)}, u32[]{:S(2)}) collective-permute-start(f32[3,32,128]{2,1,0:T(8,128)S(1)} %get-tuple-element.29.refs_0_), channel_id=1, source_target_pairs={{0,3},{1,2},{2,1},{3,0},{4,7},{5,6},{6,5},{7,4},{8,11},{9,10},{10,... | collective-permute-start | bytes 147464 | tf_op jit(solution)/shard_map/ppermute | solution.py:51
  31.1 0.6 %collective-permute-start.10 = (f32[3,32,128]{2,1,0:T(8,128)S(1)}, f32[3,32,128]{2,1,0:T(8,128)S(1)}, u32[]{:S(2)}, u32[]{:S(2)}) collective-permute-start(f32[3,32,128]{2,1,0:T(8,128)S(1)} %get-tuple-element.29.refs_0_), channel_id=1, source_target_pairs={{0,2},{1,3},{2,0},{3,1},{4,6},{5,7},{6,4},{7,5},{8,10},{9,11},{10,... | collective-permute-start | bytes 147464 | tf_op jit(solution)/shard_map/ppermute | solution.py:51
  31.8 0.0 collective-permute-done.9.others.refs_1_
  31.8 0.8 %factor.1.inverse = f32[32,32]{1,0:T(8,128)S(1)} custom-call(f32[4,32,128]{2,1,0:T(8,128)S(1)} %get-tuple-element.28.mine, f32[4,32,128]{2,1,0:T(8,128)S(1)} %collective-permute-done.9.others.refs_1_), custom_call_target="tpu_custom_call" | custom-call | tf_op jit(solution)/shard_map/factor/pallas_call | solution.py:335
  32.6 1.1 %collective-permute-done.11.refs_3_ = f32[3,32,128]{2,1,0:T(8,128)S(1)} collective-permute-done((f32[3,32,128]{2,1,0:T(8,128)S(1)}, f32[3,32,128]{2,1,0:T(8,128)S(1)}, u32[]{:S(2)}, u32[]{:S(2)}) %collective-permute-start.11) | collective-permute-done | bytes 49184 | tf_op jit(solution)/shard_map/ppermute | solution.py:51
  33.7 1.5 %collective-permute-done.10.refs_2_ = f32[3,32,128]{2,1,0:T(8,128)S(1)} collective-permute-done((f32[3,32,128]{2,1,0:T(8,128)S(1)}, f32[3,32,128]{2,1,0:T(8,128)S(1)}, u32[]{:S(2)}, u32[]{:S(2)}) %collective-permute-start.10) | collective-permute-done | bytes 49184 | tf_op jit(solution)/shard_map/ppermute | solution.py:51
  35.2 0.5 %gram.1 = (f32[3,32,128]{2,1,0:T(8,128)S(1)}, f32[32,64]{1,0:T(8,128)S(1)}) custom-call(f32[32,32]{1,0:T(8,128)S(1)} %factor.1.inverse, f32[3,32,128]{2,1,0:T(8,128)S(1)} %get-tuple-element.24.tiles, f32[3,32,128]{2,1,0:T(8,128)S(1)} %get-tuple-element.29.refs_0_, f32[4,32,128]{2,1,0:T(8,128)S(1)} %collective-permute-done.9.others.refs_1_, ...), custom_call_target="tpu_custom_call" | custom-call | tf_op jit(solution)/shard_map/gram/pallas_call | solution.py:338
  35.7 3.0 %collective-permute-start.14 = (f32[32,64]{1,0:T(8,128)S(1)}, f32[32,64]{1,0:T(8,128)S(1)}, u32[]{:S(2)}, u32[]{:S(2)}) collective-permute-start(f32[32,64]{1,0:T(8,128)S(1)} %get-tuple-element.31.refs_0_), channel_id=1, source_target_pairs={{0,12},{4,8},{8,4},{12,0},{1,13},{5,9},{9,5},{13,1},{2,14},{6,10},... | collective-permute-start | bytes 24584 | tf_op jit(solution)/shard_map/ppermute | solution.py:51
  38.6 0.0 collective-permute-start.13
  38.6 1.4 %collective-permute-start.12 = (f32[32,64]{1,0:T(8,128)S(1)}, f32[32,64]{1,0:T(8,128)S(1)}, u32[]{:S(2)}, u32[]{:S(2)}) collective-permute-start(f32[32,64]{1,0:T(8,128)S(1)} %get-tuple-element.31.refs_0_), channel_id=1, source_target_pairs={{0,4},{4,0},{8,12},{12,8},{1,5},{5,1},{9,13},{13,9},{2,6},{6,2},{1... | collective-permute-start | bytes 24584 | tf_op jit(solution)/shard_map/ppermute | solution.py:51
  40.1 1.1 %collective-permute-done.14.refs_3_ = f32[32,64]{1,0:T(8,128)S(1)} collective-permute-done((f32[32,64]{1,0:T(8,128)S(1)}, f32[32,64]{1,0:T(8,128)S(1)}, u32[]{:S(2)}, u32[]{:S(2)}) %collective-permute-start.14) | collective-permute-done | bytes 8224 | tf_op jit(solution)/shard_map/ppermute | solution.py:51
  41.2 2.1 %collective-permute-done.13.refs_2_ = f32[32,64]{1,0:T(8,128)S(1)} collective-permute-done((f32[32,64]{1,0:T(8,128)S(1)}, f32[32,64]{1,0:T(8,128)S(1)}, u32[]{:S(2)}, u32[]{:S(2)}) %collective-permute-start.13) | collective-permute-done | bytes 8224 | tf_op jit(solution)/shard_map/ppermute | solution.py:51
  43.3 0.0 collective-permute-done.12.refs_1_
  43.3 1.6 %last.1 = (f32[32,384]{1,0:T(8,128)}, f32[32,32]{1,0:T(8,128)}) custom-call(f32[3,32,128]{2,1,0:T(8,128)S(1)} %get-tuple-element.30.image, f32[32,64]{1,0:T(8,128)S(1)} %get-tuple-element.31.refs_0_, f32[32,64]{1,0:T(8,128)S(1)} %collective-permute-done.12.refs_1_, f32[32,64]{1,0:T(8,128)S(1)} %collective-permute-done.13.refs_2_, ...), custom_call_target="tpu_custom_call" | custom-call | tf_op jit(solution)/shard_map/last/pallas_call | solution.py:345
Async XLA Ops:
  0.6 2.4 %copy-start.4 = (s32[3]{0:T(128)S(1)}, s32[3]{0:T(128)}, u32[]{:S(2)}) copy-start(s32[3]{0:T(128)} %counts.7) | copy-start | bytes 40
  0.6 2.4 %collective-permute-start = (f32[3,3,128,128]{3,2,1,0:T(8,128)}, f32[3,3,128,128]{3,2,1,0:T(8,128)S(1)}, u32[]{:S(2)}, u32[]{:S(2)}) collective-permute-start(f32[3,3,128,128]{3,2,1,0:T(8,128)} %blocks.1), channel_id=1, source_target_pairs={{0,1},{1,0},{2,3},{3,2},{4,5},{5,4},{6,7},{7,6},{8,9},{9,8},{10,11... | collective-permute-start | bytes 1769480 | tf_op jit(solution)/shard_map/ppermute | solution.py:51
  1.2 1.8 %collective-permute-start.1 = (s32[3,3]{1,0:T(4,128)}, s32[3,3]{1,0:T(4,128)S(1)}, u32[]{:S(2)}, u32[]{:S(2)}) collective-permute-start(s32[3,3]{1,0:T(4,128)} %ids.7), channel_id=1, source_target_pairs={{0,1},{1,0},{2,3},{3,2},{4,5},{5,4},{6,7},{7,6},{8,9},{9,8},{10,11... | collective-permute-start | bytes 116 | tf_op jit(solution)/shard_map/ppermute | solution.py:51
  3.0 1.1 %copy-start = (f32[3,3,128,128]{3,2,1,0:T(8,128)S(1)}, f32[3,3,128,128]{3,2,1,0:T(8,128)}, u32[]{:S(2)}) copy-start(f32[3,3,128,128]{3,2,1,0:T(8,128)} %blocks.1) | copy-start | bytes 1769476
  4.1 0.8 %copy-start.1 = (f32[384,32]{0,1:T(8,128)S(1)}, f32[384,32]{0,1:T(8,128)}, u32[]{:S(2)}) copy-start(f32[384,32]{0,1:T(8,128)} %param.7) | copy-start | bytes 147460
  4.9 0.7 %copy-start.2 = (s32[3,3]{1,0:T(4,128)S(1)}, s32[3,3]{1,0:T(4,128)}, u32[]{:S(2)}) copy-start(s32[3,3]{1,0:T(4,128)} %ids.7) | copy-start | bytes 112
  6.9 7.9 %collective-permute-start.2 = (f32[3,32,128]{2,1,0:T(8,128)S(1)}, f32[3,32,128]{2,1,0:T(8,128)S(1)}, u32[]{:S(2)}, u32[]{:S(2)}) collective-permute-start(f32[3,32,128]{2,1,0:T(8,128)S(1)} %get-tuple-element.21), channel_id=1, source_target_pairs={{0,4},{1,13},{2,6},{3,15},{4,0},{5,9},{6,2},{7,11},{8,12},{9,5},{1... | collective-permute-start | bytes 147464 | tf_op jit(solution)/shard_map/ppermute | solution.py:59
  9.9 4.9 %collective-permute-start.3 = (f32[3,16,128]{2,1,0:T(8,128)S(1)}, f32[3,16,128]{2,1,0:T(8,128)S(1)}, u32[]{:S(2)}, u32[]{:S(2)}) collective-permute-start(f32[3,16,128]{2,1,0:T(8,128)S(1)} %get-tuple-element.22), channel_id=1, source_target_pairs={{0,8},{4,12},{8,0},{12,4},{1,9},{5,13},{9,1},{13,5},{2,10},{6,14},... | collective-permute-start | bytes 73736 | tf_op jit(solution)/shard_map/ppermute | solution.py:51
  14.8 7.1 %copy-start.3 = (s32[3,3]{1,0:T(4,128)S(1)}, s32[3,3]{1,0:T(4,128)}, u32[]{:S(2)}) copy-start(s32[3,3]{1,0:T(4,128)} %ids.7) | copy-start | bytes 112
  16.0 3.8 %collective-permute-start.6 = (f32[3,32,128]{2,1,0:T(8,128)S(1)}, f32[3,32,128]{2,1,0:T(8,128)S(1)}, u32[]{:S(2)}, u32[]{:S(2)}) collective-permute-start(f32[3,32,128]{2,1,0:T(8,128)S(1)} %first_direct.1.refs_0_), channel_id=1, source_target_pairs={{0,3},{1,2},{2,1},{3,0},{4,7},{5,6},{6,5},{7,4},{8,11},{9,10},{10,... | collective-permute-start | bytes 147464 | tf_op jit(solution)/shard_map/ppermute | solution.py:51
  17.7 4.1 %collective-permute-start.5 = (f32[3,32,128]{2,1,0:T(8,128)S(1)}, f32[3,32,128]{2,1,0:T(8,128)S(1)}, u32[]{:S(2)}, u32[]{:S(2)}) collective-permute-start(f32[3,32,128]{2,1,0:T(8,128)S(1)} %first_direct.1.refs_0_), channel_id=1, source_target_pairs={{0,2},{1,3},{2,0},{3,1},{4,6},{5,7},{6,4},{7,5},{8,10},{9,11},{10,... | collective-permute-start | bytes 147464 | tf_op jit(solution)/shard_map/ppermute | solution.py:51
  18.3 3.6 %collective-permute-start.4 = (f32[3,32,128]{2,1,0:T(8,128)S(1)}, f32[3,32,128]{2,1,0:T(8,128)S(1)}, u32[]{:S(2)}, u32[]{:S(2)}) collective-permute-start(f32[3,32,128]{2,1,0:T(8,128)S(1)} %first_direct.1.refs_0_), channel_id=1, source_target_pairs={{0,1},{1,0},{2,3},{3,2},{4,5},{5,4},{6,7},{7,6},{8,9},{9,8},{10,11... | collective-permute-start | bytes 147464 | tf_op jit(solution)/shard_map/ppermute | solution.py:51
  23.1 5.2 %collective-permute-start.7 = (f32[4,32,128]{2,1,0:T(8,128)S(1)}, f32[4,32,128]{2,1,0:T(8,128)S(1)}, u32[]{:S(2)}, u32[]{:S(2)}) collective-permute-start(f32[4,32,128]{2,1,0:T(8,128)S(1)} %get-tuple-element.25), channel_id=1, source_target_pairs={{0,4},{1,13},{2,6},{3,15},{4,0},{5,9},{6,2},{7,11},{8,12},{9,5},{1... | collective-permute-start | bytes 196616 | tf_op jit(solution)/shard_map/ppermute | solution.py:59
  23.3 5.0 %collective-permute-start.8 = (f32[4,16,128]{2,1,0:T(8,128)S(1)}, f32[4,16,128]{2,1,0:T(8,128)S(1)}, u32[]{:S(2)}, u32[]{:S(2)}) collective-permute-start(f32[4,16,128]{2,1,0:T(8,128)S(1)} %get-tuple-element.26), channel_id=1, source_target_pairs={{0,8},{4,12},{8,0},{12,4},{1,9},{5,13},{9,1},{13,5},{2,10},{6,14},... | collective-permute-start | bytes 98312 | tf_op jit(solution)/shard_map/ppermute | solution.py:51
  29.5 2.2 %collective-permute-start.9 = (f32[4,32,128]{2,1,0:T(8,128)S(1)}, f32[4,32,128]{2,1,0:T(8,128)S(1)}, u32[]{:S(2)}, u32[]{:S(2)}) collective-permute-start(f32[4,32,128]{2,1,0:T(8,128)S(1)} %get-tuple-element.28.mine), channel_id=1, source_target_pairs={{0,1},{1,0},{2,3},{3,2},{4,5},{5,4},{6,7},{7,6},{8,9},{9,8},{10,11... | collective-permute-start | bytes 196616 | tf_op jit(solution)/shard_map/ppermute | solution.py:51
  29.9 3.8 %collective-permute-start.11 = (f32[3,32,128]{2,1,0:T(8,128)S(1)}, f32[3,32,128]{2,1,0:T(8,128)S(1)}, u32[]{:S(2)}, u32[]{:S(2)}) collective-permute-start(f32[3,32,128]{2,1,0:T(8,128)S(1)} %get-tuple-element.29.refs_0_), channel_id=1, source_target_pairs={{0,3},{1,2},{2,1},{3,0},{4,7},{5,6},{6,5},{7,4},{8,11},{9,10},{10,... | collective-permute-start | bytes 147464 | tf_op jit(solution)/shard_map/ppermute | solution.py:51
  31.1 4.1 %collective-permute-start.10 = (f32[3,32,128]{2,1,0:T(8,128)S(1)}, f32[3,32,128]{2,1,0:T(8,128)S(1)}, u32[]{:S(2)}, u32[]{:S(2)}) collective-permute-start(f32[3,32,128]{2,1,0:T(8,128)S(1)} %get-tuple-element.29.refs_0_), channel_id=1, source_target_pairs={{0,2},{1,3},{2,0},{3,1},{4,6},{5,7},{6,4},{7,5},{8,10},{9,11},{10,... | collective-permute-start | bytes 147464 | tf_op jit(solution)/shard_map/ppermute | solution.py:51
  35.7 5.5 %collective-permute-start.14 = (f32[32,64]{1,0:T(8,128)S(1)}, f32[32,64]{1,0:T(8,128)S(1)}, u32[]{:S(2)}, u32[]{:S(2)}) collective-permute-start(f32[32,64]{1,0:T(8,128)S(1)} %get-tuple-element.31.refs_0_), channel_id=1, source_target_pairs={{0,12},{4,8},{8,4},{12,0},{1,13},{5,9},{9,5},{13,1},{2,14},{6,10},... | collective-permute-start | bytes 24584 | tf_op jit(solution)/shard_map/ppermute | solution.py:51
  38.6 4.6 %collective-permute-start.13 = (f32[32,64]{1,0:T(8,128)S(1)}, f32[32,64]{1,0:T(8,128)S(1)}, u32[]{:S(2)}, u32[]{:S(2)}) collective-permute-start(f32[32,64]{1,0:T(8,128)S(1)} %get-tuple-element.31.refs_0_), channel_id=1, source_target_pairs={{0,8},{4,12},{8,0},{12,4},{1,9},{5,13},{9,1},{13,5},{2,10},{6,14},... | collective-permute-start | bytes 24584 | tf_op jit(solution)/shard_map/ppermute | solution.py:51
  38.6 4.6 %collective-permute-start.12 = (f32[32,64]{1,0:T(8,128)S(1)}, f32[32,64]{1,0:T(8,128)S(1)}, u32[]{:S(2)}, u32[]{:S(2)}) collective-permute-start(f32[32,64]{1,0:T(8,128)S(1)} %get-tuple-element.31.refs_0_), channel_id=1, source_target_pairs={{0,4},{4,0},{8,12},{12,8},{1,5},{5,1},{9,13},{13,9},{2,6},{6,2},{1... | collective-permute-start | bytes 24584 | tf_op jit(solution)/shard_map/ppermute | solution.py:51

commit v4 on v3

--- a/solution.py
+++ b/solution.py
@@ -76,12 +76,16 @@
         return jnp.where(used, jnp.where(ids[i, p] == self.first_row + i, 0.5, 1.0), 0.0).astype(F32)
 
 
-def transposed_products(place, blocks, ids, counts, tiles, out):
+def transposed_products(place, blocks, ids, counts, tiles, out, copy=None):
     out[...] = jnp.zeros_like(out)
     size = out.shape[2]
+    values = []
     for i in range(place.block_rows):
         stored = [split(b[i, p]) for b in blocks for p in range(place.slots)]
-        value = product(split(tiles[i]), joined(stored, 1))
+        values.append(product(split(tiles[i]), joined(stored, 1)))
+    if copy is not None:
+        copy.wait()
+    for i, value in enumerate(values):
         for m in range(len(blocks)):
             for p in range(place.slots):
                 at = (m * place.slots + p) * size
@@ -115,25 +119,30 @@
     own[...] = jnp.where(place.odd == 0, mine, 0.0)
 
 
-def first_kernel(rows, blocks, other, ids, other_ids, counts, start, *refs):
-    half = rows // 2
-    messages, refs = refs[: half - 1], refs[half - 1 :]
-    shared, own, tiles, held, products, ids_s, other_s, counts_s, sems = refs
-    block_rows, slots, size, _ = blocks.shape
-    place = Place(rows, block_rows, slots)
+def load_kernel(blocks, ids, counts, start, held, ids_s, counts_s, tiles, sems):
+    size = blocks.shape[2]
     copies = [
         pltpu.make_async_copy(blocks, held, sems.at[0]),
         pltpu.make_async_copy(ids, ids_s, sems.at[1]),
-        pltpu.make_async_copy(other_ids, other_s, sems.at[2]),
-        pltpu.make_async_copy(counts, counts_s, sems.at[3]),
+        pltpu.make_async_copy(counts, counts_s, sems.at[2]),
     ]
-    for i in range(block_rows):
-        copies.append(pltpu.make_async_copy(start.at[:, i * size : (i + 1) * size], tiles.at[i], sems.at[4 + i]))
+    for i in range(blocks.shape[0]):
+        copies.append(pltpu.make_async_copy(start.at[:, i * size : (i + 1) * size], tiles.at[i], sems.at[3 + i]))
     for copy in copies:
         copy.start()
     for copy in copies:
         copy.wait()
-    transposed_products(place, (held, other), (ids_s, other_s), counts_s, tiles, products)
+
+
+def first_kernel(rows, held, other, ids, other_ids, counts, tiles, *refs):
+    half = rows // 2
+    messages, refs = refs[: half - 1], refs[half - 1 :]
+    shared, own, other_s, products, sem = refs
+    block_rows, slots, size, _ = held.shape
+    place = Place(rows, block_rows, slots)
+    copy = pltpu.make_async_copy(other_ids, other_s, sem.at[0])
+    copy.start()
+    transposed_products(place, (held, other), (ids, other_s), counts, tiles, products, copy)
     fill(place, messages, shared, products, tiles)
     own_products(place, products, own)
 
@@ -276,12 +285,15 @@
     wide = shape((columns, size), F32)
     work = pltpu.VMEM((all_blocks, columns, size), F32)
 
+    def spec_of(out):
+        return SMEM if out.dtype == jnp.int32 else VMEM
+
     def call(kernel, name, specs, outs, scratch=()):
         return pl.pallas_call(
             kernel,
             name=name,
             in_specs=specs,
-            out_specs=[VMEM] * len(outs),
+            out_specs=[spec_of(out) for out in outs],
             out_shape=outs,
             scratch_shapes=scratch,
             compiler_params=PARAMS,
@@ -295,20 +307,22 @@
 
     other = swap(blocks, "nbr", 1)
     other_ids = swap(partner_ids, "nbr", 1)
-    *messages, shared, own, tiles, held = call(
+    table = pltpu.SMEM(partner_ids.shape, jnp.int32)
+    held, ids, counts, tiles = call(
+        load_kernel,
+        "load",
+        [HBM] * 4,
+        [shape(blocks.shape, F32), table, pltpu.SMEM(counts.shape, jnp.int32), tile],
+        [DMA((3 + block_rows,))],
+    )(*[pltpu.with_memory_space_constraint(x, pltpu.HBM) for x in (blocks, partner_ids, counts, start.T)])
+    *messages, shared, own, other_ids = call(
         functools.partial(first_kernel, rows),
         "first_transposed",
-        [HBM, VMEM, HBM, HBM, HBM, HBM],
-        [tile] * (half - 1) + [shorter, tile, tile, shape(blocks.shape, F32)],
-        [
-            work,
-            pltpu.SMEM(partner_ids.shape, jnp.int32),
-            pltpu.SMEM(partner_ids.shape, jnp.int32),
-            pltpu.SMEM(counts.shape, jnp.int32),
-            DMA((4 + block_rows,)),
-        ],
-    )(blocks, other, partner_ids, other_ids, counts, start.T)
-    stored = (held, other, partner_ids, other_ids, counts)
+        [VMEM, VMEM, SMEM, VMEM, SMEM, VMEM],
+        [tile] * (half - 1) + [shorter, tile, table],
+        [work, DMA((1,))],
+    )(held, other, ids, other_ids, counts, tiles)
+    stored = (held, other, ids, other_ids, counts)
     index = [VMEM, VMEM, SMEM, SMEM, SMEM]
     received, shared = round_over_rows(messages, shared)
     (image,) = call(

time: 45.2 us -> 39.9 us (0.88)
  local copies, waits for them, and re-layouts: 2.55 us -> 0 us
  waiting for transfers between devices: 16.3 us -> 14.8 us
  Pallas kernels: 7.89 us -> 6.52 us
    unnamed x10 -> x0, local copies, waits for them, and re-layouts: 2.55 us -> none
    ppermute x13, waiting for transfers between devices: 16.2 us -> 14.8 us  [swap(): lax.ppermute(x, axis, [(i, i ^ distance) for i in range(lax.axis_size(axi...]
    pallas_call x1, Pallas kernels: 1.22 us -> 0.56 us  [body(): call(functools.partial(second_kernel, rows, parts), 'second_transposed',...]
    pallas_call x1, Pallas kernels: 1.23 us -> 0.61 us  [body(): call(functools.partial(direct_kernel, rows, True), 'second_direct', index...]
    pallas_call x1, Pallas kernels: 1.22 us -> 0.61 us  [body(): call(functools.partial(direct_kernel, rows, False), 'first_direct', index...]
    pallas_call x1 -> x2, Pallas kernels: 1.3 us -> 1.82 us  [the longest x1 1.14 us: body(): call(load_kernel, 'load', [HBM] * 4, [shape(blocks.shape, F32), table, pl...]
  transfers between devices with their start and end apart: 15 -> 15, of which waited for: 9 -> 9; matrix products, arithmetic and copies ran while one was open for 0% -> 0% of each run, Pallas kernels for 2% -> 5%
where the time goes in v4:
time: 39.9 us; the launch traced here: 39.6 us
  starting transfers between devices  17.6 us (44%)
  waiting for transfers between devices  14.8 us (37%)
  Pallas kernels  6.52 us (16%)
  between operations  0.68 us (2%)
    ppermute x13, waiting for transfers between devices, swap(): lax.ppermute(x, axis, [(i, i ^ distance) for i in range(lax.axis_size(axi...  14.8 us
    ppermute x13, starting transfers between devices, swap(): lax.ppermute(x, axis, [(i, i ^ distance) for i in range(lax.axis_size(axi...  14.4 us
    ppermute x2, starting transfers between devices, swap_rows(): return lax.ppermute(x, ('row', 'nbr'), pairs)  3.18 us
    pallas_call x1, Pallas kernels, body(): call(functools.partial(last_kernel, rows, total), 'last', [VMEM] * (rows...  1.64 us
    pallas_call x1, Pallas kernels, body(): call(load_kernel, 'load', [HBM] * 4, [shape(blocks.shape, F32), table, pl...  1.14 us
    pallas_call x1, Pallas kernels, body(): call(functools.partial(factor_kernel, total), 'factor', [VMEM] * 2, [shap...  0.82 us
  transfers between devices with their start and end apart: 15, of which 9 were waited for; matrix products, arithmetic and copies ran while one was open for 0% of the time, Pallas kernels for 5%

profile of v4, /device:TPU:0, one launch (start us, length us, event | category | flops | bytes accessed | tf_op | source)
XLA Modules:
  0.0 39.6 jit_solution(1839598656154849487)
XLA Ops:
  0.6 0.5 %collective-permute-start = (f32[3,3,128,128]{3,2,1,0:T(8,128)}, f32[3,3,128,128]{3,2,1,0:T(8,128)S(1)}, u32[]{:S(2)}, u32[]{:S(2)}) collective-permute-start(f32[3,3,128,128]{3,2,1,0:T(8,128)} %blocks.1), channel_id=1, source_target_pairs={{0,1},{1,0},{2,3},{3,2},{4,5},{5,4},{6,7},{7,6},{8,9},{9,8},{10,11... | collective-permute-start | bytes 1769480 | tf_op jit(solution)/shard_map/ppermute | solution.py:51
  1.1 0.1 collective-permute-start.1
  1.2 1.1 %load.1 = (f32[3,3,128,128]{3,2,1,0:T(8,128)S(1)}, s32[3,3]{1,0:T(4,128)S(4)}, s32[3]{0:T(128)S(4)}, f32[3,32,128]{2,1,0:T(8,128)S(1)}) custom-call(f32[3,3,128,128]{3,2,1,0:T(8,128)} %blocks.1, s32[3,3]{1,0:T(4,128)} %ids.1, s32[3]{0:T(128)} %counts.1, f32[32,384]{1,0:T(8,128)} %bitcast.2), custom_call_target="tpu_custom_call" | custom-call | tf_op jit(solution)/shard_map/load/pallas_call | solution.py:311
  2.4 0.6 %collective-permute-done.1.other_ids = s32[3,3]{1,0:T(4,128)S(1)} collective-permute-done((s32[3,3]{1,0:T(4,128)}, s32[3,3]{1,0:T(4,128)S(1)}, u32[]{:S(2)}, u32[]{:S(2)}) %collective-permute-start.1) | collective-permute-done | bytes 68 | tf_op jit(solution)/shard_map/ppermute | solution.py:51
  3.0 0.0 collective-permute-done.other
  3.0 0.7 %first_transposed.1 = (f32[3,32,128]{2,1,0:T(8,128)S(1)}, f32[3,16,128]{2,1,0:T(8,128)S(1)}, f32[3,32,128]{2,1,0:T(8,128)S(1)}, s32[3,3]{1,0:T(4,128)S(4)}) custom-call(f32[3,3,128,128]{3,2,1,0:T(8,128)S(1)} %get-tuple-element.21.held, f32[3,3,128,128]{3,2,1,0:T(8,128)S(1)} %collective-permute-done.other, s32[3,3]{1,0:T(4,128)S(4)} %get-tuple-element.22.ids, ...), custom_call_target="tpu_custom_call" | custom-call | tf_op jit(solution)/shard_map/first_transposed/pallas_call | solution.py:318
  3.7 3.0 %collective-permute-start.2 = (f32[3,32,128]{2,1,0:T(8,128)S(1)}, f32[3,32,128]{2,1,0:T(8,128)S(1)}, u32[]{:S(2)}, u32[]{:S(2)}) collective-permute-start(f32[3,32,128]{2,1,0:T(8,128)S(1)} %get-tuple-element.27), channel_id=1, source_target_pairs={{0,4},{1,13},{2,6},{3,15},{4,0},{5,9},{6,2},{7,11},{8,12},{9,5},{1... | collective-permute-start | bytes 147464 | tf_op jit(solution)/shard_map/ppermute | solution.py:59
  6.7 2.6 %collective-permute-start.3 = (f32[3,16,128]{2,1,0:T(8,128)S(1)}, f32[3,16,128]{2,1,0:T(8,128)S(1)}, u32[]{:S(2)}, u32[]{:S(2)}) collective-permute-start(f32[3,16,128]{2,1,0:T(8,128)S(1)} %get-tuple-element.28), channel_id=1, source_target_pairs={{0,8},{4,12},{8,0},{12,4},{1,9},{5,13},{9,1},{13,5},{2,10},{6,14},... | collective-permute-start | bytes 73736 | tf_op jit(solution)/shard_map/ppermute | solution.py:51
  9.3 2.3 %collective-permute-done.3.refs_1_ = f32[3,16,128]{2,1,0:T(8,128)S(1)} collective-permute-done((f32[3,16,128]{2,1,0:T(8,128)S(1)}, f32[3,16,128]{2,1,0:T(8,128)S(1)}, u32[]{:S(2)}, u32[]{:S(2)}) %collective-permute-start.3) | collective-permute-done | bytes 24608 | tf_op jit(solution)/shard_map/ppermute | solution.py:51
  11.6 0.0 collective-permute-done.2.refs_0_
  11.6 0.6 %first_direct.1.refs_0_ = f32[3,32,128]{2,1,0:T(8,128)S(1)} custom-call(f32[3,3,128,128]{3,2,1,0:T(8,128)S(1)} %get-tuple-element.21.held, f32[3,3,128,128]{3,2,1,0:T(8,128)S(1)} %collective-permute-done.other, s32[3,3]{1,0:T(4,128)S(4)} %get-tuple-element.22.ids, s32[3,3]{1,0:T(4,128)S(4)} %get-tuple-element.25.other_ids, s32[3]{0:T(128)S(4)} %get-tuple-element.23.counts, ...), custom_call_target="tpu_custom_call" | custom-call | tf_op jit(solution)/shard_map/first_direct/pallas_call | solution.py:328
  12.2 1.7 %collective-permute-start.6 = (f32[3,32,128]{2,1,0:T(8,128)S(1)}, f32[3,32,128]{2,1,0:T(8,128)S(1)}, u32[]{:S(2)}, u32[]{:S(2)}) collective-permute-start(f32[3,32,128]{2,1,0:T(8,128)S(1)} %first_direct.1.refs_0_), channel_id=1, source_target_pairs={{0,3},{1,2},{2,1},{3,0},{4,7},{5,6},{6,5},{7,4},{8,11},{9,10},{10,... | collective-permute-start | bytes 147464 | tf_op jit(solution)/shard_map/ppermute | solution.py:51
  14.0 0.5 %collective-permute-start.5 = (f32[3,32,128]{2,1,0:T(8,128)S(1)}, f32[3,32,128]{2,1,0:T(8,128)S(1)}, u32[]{:S(2)}, u32[]{:S(2)}) collective-permute-start(f32[3,32,128]{2,1,0:T(8,128)S(1)} %first_direct.1.refs_0_), channel_id=1, source_target_pairs={{0,2},{1,3},{2,0},{3,1},{4,6},{5,7},{6,4},{7,5},{8,10},{9,11},{10,... | collective-permute-start | bytes 147464 | tf_op jit(solution)/shard_map/ppermute | solution.py:51
  14.5 0.0 collective-permute-start.4
  14.5 1.4 %collective-permute-done.6.refs_3_ = f32[3,32,128]{2,1,0:T(8,128)S(1)} collective-permute-done((f32[3,32,128]{2,1,0:T(8,128)S(1)}, f32[3,32,128]{2,1,0:T(8,128)S(1)}, u32[]{:S(2)}, u32[]{:S(2)}) %collective-permute-start.6) | collective-permute-done | bytes 49184 | tf_op jit(solution)/shard_map/ppermute | solution.py:51
  15.9 2.2 %collective-permute-done.5.refs_2_ = f32[3,32,128]{2,1,0:T(8,128)S(1)} collective-permute-done((f32[3,32,128]{2,1,0:T(8,128)S(1)}, f32[3,32,128]{2,1,0:T(8,128)S(1)}, u32[]{:S(2)}, u32[]{:S(2)}) %collective-permute-start.5) | collective-permute-done | bytes 49184 | tf_op jit(solution)/shard_map/ppermute | solution.py:51
  18.0 0.0 collective-permute-done.4.refs_1_
  18.1 0.6 %second_transposed.1 = (f32[4,32,128]{2,1,0:T(8,128)S(1)}, f32[4,16,128]{2,1,0:T(8,128)S(1)}, f32[3,32,128]{2,1,0:T(8,128)S(1)}, f32[3,32,128]{2,1,0:T(8,128)S(1)}, f32[32,128]{1,0:T(8,128)S(1)}) custom-call(f32[3,3,128,128]{3,2,1,0:T(8,128)S(1)} %get-tuple-element.21.held, f32[3,3,128,128]{3,2,1,0:T(8,128)S(1)} %collective-permute-done.other, ...), custom_call_target="tpu_custom_call" | custom-call | tf_op jit(solution)/shard_map/second_transposed/pallas_call | solution.py:332
  18.6 0.2 collective-permute-start.7
  18.8 2.3 %collective-permute-start.8 = (f32[4,16,128]{2,1,0:T(8,128)S(1)}, f32[4,16,128]{2,1,0:T(8,128)S(1)}, u32[]{:S(2)}, u32[]{:S(2)}) collective-permute-start(f32[4,16,128]{2,1,0:T(8,128)S(1)} %get-tuple-element.32), channel_id=1, source_target_pairs={{0,8},{4,12},{8,0},{12,4},{1,9},{5,13},{9,1},{13,5},{2,10},{6,14},... | collective-permute-start | bytes 98312 | tf_op jit(solution)/shard_map/ppermute | solution.py:51
  21.1 2.6 %collective-permute-done.8.refs_1_ = f32[4,16,128]{2,1,0:T(8,128)S(1)} collective-permute-done((f32[4,16,128]{2,1,0:T(8,128)S(1)}, f32[4,16,128]{2,1,0:T(8,128)S(1)}, u32[]{:S(2)}, u32[]{:S(2)}) %collective-permute-start.8) | collective-permute-done | bytes 32800 | tf_op jit(solution)/shard_map/ppermute | solution.py:51
  23.7 0.0 collective-permute-done.7.refs_0_
  23.7 0.6 %second_direct.1 = (f32[3,32,128]{2,1,0:T(8,128)S(1)}, f32[4,32,128]{2,1,0:T(8,128)S(1)}) custom-call(f32[3,3,128,128]{3,2,1,0:T(8,128)S(1)} %get-tuple-element.21.held, f32[3,3,128,128]{3,2,1,0:T(8,128)S(1)} %collective-permute-done.other, s32[3,3]{1,0:T(4,128)S(4)} %get-tuple-element.22.ids, s32[3,3]{1,0:T(4,128)S(4)} %get-tuple-element.25.other_ids, ...), custom_call_target="tpu_custom_call" | custom-call | tf_op jit(solution)/shard_map/second_direct/pallas_call | solution.py:340
  24.3 0.6 %collective-permute-start.9 = (f32[4,32,128]{2,1,0:T(8,128)S(1)}, f32[4,32,128]{2,1,0:T(8,128)S(1)}, u32[]{:S(2)}, u32[]{:S(2)}) collective-permute-start(f32[4,32,128]{2,1,0:T(8,128)S(1)} %get-tuple-element.34.mine), channel_id=1, source_target_pairs={{0,1},{1,0},{2,3},{3,2},{4,5},{5,4},{6,7},{7,6},{8,9},{9,8},{10,11... | collective-permute-start | bytes 196616 | tf_op jit(solution)/shard_map/ppermute | solution.py:51
  24.9 0.8 %collective-permute-start.11 = (f32[3,32,128]{2,1,0:T(8,128)S(1)}, f32[3,32,128]{2,1,0:T(8,128)S(1)}, u32[]{:S(2)}, u32[]{:S(2)}) collective-permute-start(f32[3,32,128]{2,1,0:T(8,128)S(1)} %get-tuple-element.35.refs_0_), channel_id=1, source_target_pairs={{0,3},{1,2},{2,1},{3,0},{4,7},{5,6},{6,5},{7,4},{8,11},{9,10},{10,... | collective-permute-start | bytes 147464 | tf_op jit(solution)/shard_map/ppermute | solution.py:51
  25.7 0.9 %collective-permute-start.10 = (f32[3,32,128]{2,1,0:T(8,128)S(1)}, f32[3,32,128]{2,1,0:T(8,128)S(1)}, u32[]{:S(2)}, u32[]{:S(2)}) collective-permute-start(f32[3,32,128]{2,1,0:T(8,128)S(1)} %get-tuple-element.35.refs_0_), channel_id=1, source_target_pairs={{0,2},{1,3},{2,0},{3,1},{4,6},{5,7},{6,4},{7,5},{8,10},{9,11},{10,... | collective-permute-start | bytes 147464 | tf_op jit(solution)/shard_map/ppermute | solution.py:51
  26.6 0.0 collective-permute-done.9.others.refs_1_
  26.6 0.8 %factor.1.inverse = f32[32,32]{1,0:T(8,128)S(1)} custom-call(f32[4,32,128]{2,1,0:T(8,128)S(1)} %get-tuple-element.34.mine, f32[4,32,128]{2,1,0:T(8,128)S(1)} %collective-permute-done.9.others.refs_1_), custom_call_target="tpu_custom_call" | custom-call | tf_op jit(solution)/shard_map/factor/pallas_call | solution.py:349
  27.4 1.2 %collective-permute-done.11.refs_3_ = f32[3,32,128]{2,1,0:T(8,128)S(1)} collective-permute-done((f32[3,32,128]{2,1,0:T(8,128)S(1)}, f32[3,32,128]{2,1,0:T(8,128)S(1)}, u32[]{:S(2)}, u32[]{:S(2)}) %collective-permute-start.11) | collective-permute-done | bytes 49184 | tf_op jit(solution)/shard_map/ppermute | solution.py:51
  28.7 1.3 %collective-permute-done.10.refs_2_ = f32[3,32,128]{2,1,0:T(8,128)S(1)} collective-permute-done((f32[3,32,128]{2,1,0:T(8,128)S(1)}, f32[3,32,128]{2,1,0:T(8,128)S(1)}, u32[]{:S(2)}, u32[]{:S(2)}) %collective-permute-start.10) | collective-permute-done | bytes 49184 | tf_op jit(solution)/shard_map/ppermute | solution.py:51
  30.0 0.5 %gram.1 = (f32[3,32,128]{2,1,0:T(8,128)S(1)}, f32[32,64]{1,0:T(8,128)S(1)}) custom-call(f32[32,32]{1,0:T(8,128)S(1)} %factor.1.inverse, f32[3,32,128]{2,1,0:T(8,128)S(1)} %get-tuple-element.30.tiles, f32[3,32,128]{2,1,0:T(8,128)S(1)} %get-tuple-element.35.refs_0_, f32[4,32,128]{2,1,0:T(8,128)S(1)} %collective-permute-done.9.others.refs_1_, ...), custom_call_target="tpu_custom_call" | custom-call | tf_op jit(solution)/shard_map/gram/pallas_call | solution.py:352
  30.4 2.9 %collective-permute-start.14 = (f32[32,64]{1,0:T(8,128)S(1)}, f32[32,64]{1,0:T(8,128)S(1)}, u32[]{:S(2)}, u32[]{:S(2)}) collective-permute-start(f32[32,64]{1,0:T(8,128)S(1)} %get-tuple-element.37.refs_0_), channel_id=1, source_target_pairs={{0,12},{4,8},{8,4},{12,0},{1,13},{5,9},{9,5},{13,1},{2,14},{6,10},... | collective-permute-start | bytes 24584 | tf_op jit(solution)/shard_map/ppermute | solution.py:51
  33.4 0.0 collective-permute-start.13
  33.4 1.5 %collective-permute-start.12 = (f32[32,64]{1,0:T(8,128)S(1)}, f32[32,64]{1,0:T(8,128)S(1)}, u32[]{:S(2)}, u32[]{:S(2)}) collective-permute-start(f32[32,64]{1,0:T(8,128)S(1)} %get-tuple-element.37.refs_0_), channel_id=1, source_target_pairs={{0,4},{4,0},{8,12},{12,8},{1,5},{5,1},{9,13},{13,9},{2,6},{6,2},{1... | collective-permute-start | bytes 24584 | tf_op jit(solution)/shard_map/ppermute | solution.py:51
  34.8 1.1 %collective-permute-done.14.refs_3_ = f32[32,64]{1,0:T(8,128)S(1)} collective-permute-done((f32[32,64]{1,0:T(8,128)S(1)}, f32[32,64]{1,0:T(8,128)S(1)}, u32[]{:S(2)}, u32[]{:S(2)}) %collective-permute-start.14) | collective-permute-done | bytes 8224 | tf_op jit(solution)/shard_map/ppermute | solution.py:51
  36.0 2.0 %collective-permute-done.13.refs_2_ = f32[32,64]{1,0:T(8,128)S(1)} collective-permute-done((f32[32,64]{1,0:T(8,128)S(1)}, f32[32,64]{1,0:T(8,128)S(1)}, u32[]{:S(2)}, u32[]{:S(2)}) %collective-permute-start.13) | collective-permute-done | bytes 8224 | tf_op jit(solution)/shard_map/ppermute | solution.py:51
  38.0 0.0 collective-permute-done.12.refs_1_
  38.0 1.6 %last.1 = (f32[32,384]{1,0:T(8,128)}, f32[32,32]{1,0:T(8,128)}) custom-call(f32[3,32,128]{2,1,0:T(8,128)S(1)} %get-tuple-element.36.image, f32[32,64]{1,0:T(8,128)S(1)} %get-tuple-element.37.refs_0_, f32[32,64]{1,0:T(8,128)S(1)} %collective-permute-done.12.refs_1_, f32[32,64]{1,0:T(8,128)S(1)} %collective-permute-done.13.refs_2_, ...), custom_call_target="tpu_custom_call" | custom-call | tf_op jit(solution)/shard_map/last/pallas_call | solution.py:359
Async XLA Ops:
  0.6 2.4 %collective-permute-start = (f32[3,3,128,128]{3,2,1,0:T(8,128)}, f32[3,3,128,128]{3,2,1,0:T(8,128)S(1)}, u32[]{:S(2)}, u32[]{:S(2)}) collective-permute-start(f32[3,3,128,128]{3,2,1,0:T(8,128)} %blocks.1), channel_id=1, source_target_pairs={{0,1},{1,0},{2,3},{3,2},{4,5},{5,4},{6,7},{7,6},{8,9},{9,8},{10,11... | collective-permute-start | bytes 1769480 | tf_op jit(solution)/shard_map/ppermute | solution.py:51
  1.1 1.8 %collective-permute-start.1 = (s32[3,3]{1,0:T(4,128)}, s32[3,3]{1,0:T(4,128)S(1)}, u32[]{:S(2)}, u32[]{:S(2)}) collective-permute-start(s32[3,3]{1,0:T(4,128)} %ids.1), channel_id=1, source_target_pairs={{0,1},{1,0},{2,3},{3,2},{4,5},{5,4},{6,7},{7,6},{8,9},{9,8},{10,11... | collective-permute-start | bytes 116 | tf_op jit(solution)/shard_map/ppermute | solution.py:51
  3.7 7.9 %collective-permute-start.2 = (f32[3,32,128]{2,1,0:T(8,128)S(1)}, f32[3,32,128]{2,1,0:T(8,128)S(1)}, u32[]{:S(2)}, u32[]{:S(2)}) collective-permute-start(f32[3,32,128]{2,1,0:T(8,128)S(1)} %get-tuple-element.27), channel_id=1, source_target_pairs={{0,4},{1,13},{2,6},{3,15},{4,0},{5,9},{6,2},{7,11},{8,12},{9,5},{1... | collective-permute-start | bytes 147464 | tf_op jit(solution)/shard_map/ppermute | solution.py:59
  6.7 4.9 %collective-permute-start.3 = (f32[3,16,128]{2,1,0:T(8,128)S(1)}, f32[3,16,128]{2,1,0:T(8,128)S(1)}, u32[]{:S(2)}, u32[]{:S(2)}) collective-permute-start(f32[3,16,128]{2,1,0:T(8,128)S(1)} %get-tuple-element.28), channel_id=1, source_target_pairs={{0,8},{4,12},{8,0},{12,4},{1,9},{5,13},{9,1},{13,5},{2,10},{6,14},... | collective-permute-start | bytes 73736 | tf_op jit(solution)/shard_map/ppermute | solution.py:51
  12.2 3.7 %collective-permute-start.6 = (f32[3,32,128]{2,1,0:T(8,128)S(1)}, f32[3,32,128]{2,1,0:T(8,128)S(1)}, u32[]{:S(2)}, u32[]{:S(2)}) collective-permute-start(f32[3,32,128]{2,1,0:T(8,128)S(1)} %first_direct.1.refs_0_), channel_id=1, source_target_pairs={{0,3},{1,2},{2,1},{3,0},{4,7},{5,6},{6,5},{7,4},{8,11},{9,10},{10,... | collective-permute-start | bytes 147464 | tf_op jit(solution)/shard_map/ppermute | solution.py:51
  14.0 4.1 %collective-permute-start.5 = (f32[3,32,128]{2,1,0:T(8,128)S(1)}, f32[3,32,128]{2,1,0:T(8,128)S(1)}, u32[]{:S(2)}, u32[]{:S(2)}) collective-permute-start(f32[3,32,128]{2,1,0:T(8,128)S(1)} %first_direct.1.refs_0_), channel_id=1, source_target_pairs={{0,2},{1,3},{2,0},{3,1},{4,6},{5,7},{6,4},{7,5},{8,10},{9,11},{10,... | collective-permute-start | bytes 147464 | tf_op jit(solution)/shard_map/ppermute | solution.py:51
  14.5 3.6 %collective-permute-start.4 = (f32[3,32,128]{2,1,0:T(8,128)S(1)}, f32[3,32,128]{2,1,0:T(8,128)S(1)}, u32[]{:S(2)}, u32[]{:S(2)}) collective-permute-start(f32[3,32,128]{2,1,0:T(8,128)S(1)} %first_direct.1.refs_0_), channel_id=1, source_target_pairs={{0,1},{1,0},{2,3},{3,2},{4,5},{5,4},{6,7},{7,6},{8,9},{9,8},{10,11... | collective-permute-start | bytes 147464 | tf_op jit(solution)/shard_map/ppermute | solution.py:51
  18.6 5.1 %collective-permute-start.7 = (f32[4,32,128]{2,1,0:T(8,128)S(1)}, f32[4,32,128]{2,1,0:T(8,128)S(1)}, u32[]{:S(2)}, u32[]{:S(2)}) collective-permute-start(f32[4,32,128]{2,1,0:T(8,128)S(1)} %get-tuple-element.31), channel_id=1, source_target_pairs={{0,4},{1,13},{2,6},{3,15},{4,0},{5,9},{6,2},{7,11},{8,12},{9,5},{1... | collective-permute-start | bytes 196616 | tf_op jit(solution)/shard_map/ppermute | solution.py:59
  18.8 4.9 %collective-permute-start.8 = (f32[4,16,128]{2,1,0:T(8,128)S(1)}, f32[4,16,128]{2,1,0:T(8,128)S(1)}, u32[]{:S(2)}, u32[]{:S(2)}) collective-permute-start(f32[4,16,128]{2,1,0:T(8,128)S(1)} %get-tuple-element.32), channel_id=1, source_target_pairs={{0,8},{4,12},{8,0},{12,4},{1,9},{5,13},{9,1},{13,5},{2,10},{6,14},... | collective-permute-start | bytes 98312 | tf_op jit(solution)/shard_map/ppermute | solution.py:51
  24.3 2.3 %collective-permute-start.9 = (f32[4,32,128]{2,1,0:T(8,128)S(1)}, f32[4,32,128]{2,1,0:T(8,128)S(1)}, u32[]{:S(2)}, u32[]{:S(2)}) collective-permute-start(f32[4,32,128]{2,1,0:T(8,128)S(1)} %get-tuple-element.34.mine), channel_id=1, source_target_pairs={{0,1},{1,0},{2,3},{3,2},{4,5},{5,4},{6,7},{7,6},{8,9},{9,8},{10,11... | collective-permute-start | bytes 196616 | tf_op jit(solution)/shard_map/ppermute | solution.py:51
  24.9 3.8 %collective-permute-start.11 = (f32[3,32,128]{2,1,0:T(8,128)S(1)}, f32[3,32,128]{2,1,0:T(8,128)S(1)}, u32[]{:S(2)}, u32[]{:S(2)}) collective-permute-start(f32[3,32,128]{2,1,0:T(8,128)S(1)} %get-tuple-element.35.refs_0_), channel_id=1, source_target_pairs={{0,3},{1,2},{2,1},{3,0},{4,7},{5,6},{6,5},{7,4},{8,11},{9,10},{10,... | collective-permute-start | bytes 147464 | tf_op jit(solution)/shard_map/ppermute | solution.py:51
  25.7 4.3 %collective-permute-start.10 = (f32[3,32,128]{2,1,0:T(8,128)S(1)}, f32[3,32,128]{2,1,0:T(8,128)S(1)}, u32[]{:S(2)}, u32[]{:S(2)}) collective-permute-start(f32[3,32,128]{2,1,0:T(8,128)S(1)} %get-tuple-element.35.refs_0_), channel_id=1, source_target_pairs={{0,2},{1,3},{2,0},{3,1},{4,6},{5,7},{6,4},{7,5},{8,10},{9,11},{10,... | collective-permute-start | bytes 147464 | tf_op jit(solution)/shard_map/ppermute | solution.py:51
  30.4 5.5 %collective-permute-start.14 = (f32[32,64]{1,0:T(8,128)S(1)}, f32[32,64]{1,0:T(8,128)S(1)}, u32[]{:S(2)}, u32[]{:S(2)}) collective-permute-start(f32[32,64]{1,0:T(8,128)S(1)} %get-tuple-element.37.refs_0_), channel_id=1, source_target_pairs={{0,12},{4,8},{8,4},{12,0},{1,13},{5,9},{9,5},{13,1},{2,14},{6,10},... | collective-permute-start | bytes 24584 | tf_op jit(solution)/shard_map/ppermute | solution.py:51
  33.4 4.6 %collective-permute-start.13 = (f32[32,64]{1,0:T(8,128)S(1)}, f32[32,64]{1,0:T(8,128)S(1)}, u32[]{:S(2)}, u32[]{:S(2)}) collective-permute-start(f32[32,64]{1,0:T(8,128)S(1)} %get-tuple-element.37.refs_0_), channel_id=1, source_target_pairs={{0,8},{4,12},{8,0},{12,4},{1,9},{5,13},{9,1},{13,5},{2,10},{6,14},... | collective-permute-start | bytes 24584 | tf_op jit(solution)/shard_map/ppermute | solution.py:51
  33.4 4.6 %collective-permute-start.12 = (f32[32,64]{1,0:T(8,128)S(1)}, f32[32,64]{1,0:T(8,128)S(1)}, u32[]{:S(2)}, u32[]{:S(2)}) collective-permute-start(f32[32,64]{1,0:T(8,128)S(1)} %get-tuple-element.37.refs_0_), channel_id=1, source_target_pairs={{0,4},{4,0},{8,12},{12,8},{1,5},{5,1},{9,13},{13,9},{2,6},{6,2},{1... | collective-permute-start | bytes 24584 | tf_op jit(solution)/shard_map/ppermute | solution.py:51

commit v5 on v4

--- a/solution.py
+++ b/solution.py
@@ -66,9 +66,8 @@
         self.odd = self.part & 1
         self.block_rows, self.slots = block_rows, slots
         self.first_row = self.row * block_rows
-        self.half = rows // 2
-        self.peers = [self.row ^ (k + self.odd * self.half) for k in range(1, self.half)]
-        self.middle = self.row ^ self.half
+        self.peers = [self.row ^ (k + self.odd) for k in range(2, rows, 2)]
+        self.middle = self.row ^ 1
 
     def weight(self, ids, counts, member, i, p):
         slot = (self.part ^ member) * self.slots + p
@@ -261,9 +260,14 @@
     out[:, columns:] = product(split(prior), value, 1)
 
 
-def last_kernel(rows, total, image, *refs):
-    parts, (basis, ritz) = refs[:rows], refs[rows:]
-    both = tree([part[...] for part in parts]) / total
+def half_sum_kernel(mine, shared, *refs):
+    received, out = refs[:-1], refs[-1]
+    first = jnp.where((lax.axis_index("nbr") & 1) == 0, mine[...], shared[...])
+    out[...] = tree([first] + [part[...] for part in received])
+
+
+def last_kernel(total, image, mine, others, basis, ritz):
+    both = (mine[...] + others[...]) / total
     columns = both.shape[0]
     ritz[...] = both[:, columns:]
     lower = split(inverse_factor(both[:, :columns]))
@@ -300,7 +304,7 @@
         )
 
     def round_over_rows(messages, shared):
-        return [swap_rows(m, k, k + half) for k, m in enumerate(messages, 1)], swap(shared, "row", half)
+        return [swap_rows(m, 2 * k, 2 * k + 1) for k, m in enumerate(messages, 1)], swap(shared, "row", 1)
 
     def sum_over_parts(image):
         return [image] + [swap(image, "nbr", s) for s in range(1, parts)]
@@ -355,13 +359,16 @@
         [VMEM] * (parts + 2),
         [tile, shape((columns, 2 * columns), F32)],
     )(inverse, tiles, *images)
-    boths = [both] + [swap(both, "row", s) for s in range(1, rows)]
+    received, shared = round_over_rows([both] * (half - 1), both)
+    (both,) = call(
+        half_sum_kernel, "half_sum", [VMEM] * (half + 1), [shape((columns, 2 * columns), F32)]
+    )(both, shared, *received)
     basis, ritz = call(
-        functools.partial(last_kernel, rows, total),
+        functools.partial(last_kernel, total),
         "last",
-        [VMEM] * (rows + 1),
+        [VMEM] * 3,
         [shape(start.shape[::-1], F32), shape((columns, columns), F32)],
-    )(image, *boths)
+    )(image, both, swap(both, "nbr", 1))
     return basis.T, ritz
 
 

time: 39.9 us -> 39.2 us (0.982)
  starting transfers between devices: 17.6 us -> 16.4 us
  waiting for transfers between devices: 14.8 us -> 15.5 us
    ppermute x13 -> x12, starting transfers between devices: 14.4 us -> 10.7 us  [swap(): lax.ppermute(x, axis, [(i, i ^ distance) for i in range(lax.axis_size(axi...]
    ppermute x2 -> x3, waiting for transfers between devices: 0.01 us -> 2.52 us  [swap_rows(): return lax.ppermute(x, ('row', 'nbr'), pairs)]
    ppermute x2 -> x3, starting transfers between devices: 3.18 us -> 5.66 us  [swap_rows(): return lax.ppermute(x, ('row', 'nbr'), pairs)]
    ppermute x13 -> x12, waiting for transfers between devices: 14.8 us -> 12.9 us  [swap(): lax.ppermute(x, axis, [(i, i ^ distance) for i in range(lax.axis_size(axi...]
    pallas_call x1 -> x2, Pallas kernels: 1.64 us -> 1.64 us  [the longest x1 1.63 us: body(): call(functools.partial(last_kernel, total), 'last', [VMEM] * 3, [shape(st...]
  transfers between devices with their start and end apart: 15 -> 15, of which waited for: 9 -> 10; matrix products, arithmetic and copies ran while one was open for 0% -> 0% of each run, Pallas kernels for 5% -> 5%
where the time goes in v5:
time: 39.2 us; the launch traced here: 39.1 us
  starting transfers between devices  16.4 us (42%)
  waiting for transfers between devices  15.5 us (40%)
  Pallas kernels  6.53 us (17%)
  between operations  0.69 us (2%)
    ppermute x12, waiting for transfers between devices, swap(): lax.ppermute(x, axis, [(i, i ^ distance) for i in range(lax.axis_size(axi...  12.9 us
    ppermute x12, starting transfers between devices, swap(): lax.ppermute(x, axis, [(i, i ^ distance) for i in range(lax.axis_size(axi...  10.7 us
    ppermute x3, starting transfers between devices, swap_rows(): return lax.ppermute(x, ('row', 'nbr'), pairs)  5.66 us
    ppermute x3, waiting for transfers between devices, swap_rows(): return lax.ppermute(x, ('row', 'nbr'), pairs)  2.52 us
    pallas_call x1, Pallas kernels, body(): call(functools.partial(last_kernel, total), 'last', [VMEM] * 3, [shape(st...  1.63 us
    pallas_call x1, Pallas kernels, body(): call(load_kernel, 'load', [HBM] * 4, [shape(blocks.shape, F32), table, pl...  1.14 us
    pallas_call x1, Pallas kernels, body(): call(functools.partial(factor_kernel, total), 'factor', [VMEM] * 2, [shap...  0.82 us
  transfers between devices with their start and end apart: 15, of which 10 were waited for; matrix products, arithmetic and copies ran while one was open for 0% of the time, Pallas kernels for 5%

profile of v5, /device:TPU:0, one launch (start us, length us, event | category | flops | bytes accessed | tf_op | source)
XLA Modules:
  0.0 39.1 jit_solution(80146750844797122)
XLA Ops:
  0.6 0.5 %collective-permute-start = (f32[3,3,128,128]{3,2,1,0:T(8,128)}, f32[3,3,128,128]{3,2,1,0:T(8,128)S(1)}, u32[]{:S(2)}, u32[]{:S(2)}) collective-permute-start(f32[3,3,128,128]{3,2,1,0:T(8,128)} %blocks.1), channel_id=1, source_target_pairs={{0,1},{1,0},{2,3},{3,2},{4,5},{5,4},{6,7},{7,6},{8,9},{9,8},{10,11... | collective-permute-start | bytes 1769480 | tf_op jit(solution)/shard_map/ppermute | solution.py:51
  1.1 0.1 collective-permute-start.1
  1.2 1.1 %load.1 = (f32[3,3,128,128]{3,2,1,0:T(8,128)S(1)}, s32[3,3]{1,0:T(4,128)S(4)}, s32[3]{0:T(128)S(4)}, f32[3,32,128]{2,1,0:T(8,128)S(1)}) custom-call(f32[3,3,128,128]{3,2,1,0:T(8,128)} %blocks.1, s32[3,3]{1,0:T(4,128)} %ids.1, s32[3]{0:T(128)} %counts.1, f32[32,384]{1,0:T(8,128)} %bitcast.2), custom_call_target="tpu_custom_call" | custom-call | tf_op jit(solution)/shard_map/load/pallas_call | solution.py:315
  2.4 0.6 %collective-permute-done.1.other_ids = s32[3,3]{1,0:T(4,128)S(1)} collective-permute-done((s32[3,3]{1,0:T(4,128)}, s32[3,3]{1,0:T(4,128)S(1)}, u32[]{:S(2)}, u32[]{:S(2)}) %collective-permute-start.1) | collective-permute-done | bytes 68 | tf_op jit(solution)/shard_map/ppermute | solution.py:51
  3.0 0.0 collective-permute-done.other
  3.0 0.7 %first_transposed.1 = (f32[3,32,128]{2,1,0:T(8,128)S(1)}, f32[3,16,128]{2,1,0:T(8,128)S(1)}, f32[3,32,128]{2,1,0:T(8,128)S(1)}, s32[3,3]{1,0:T(4,128)S(4)}) custom-call(f32[3,3,128,128]{3,2,1,0:T(8,128)S(1)} %get-tuple-element.21.held, f32[3,3,128,128]{3,2,1,0:T(8,128)S(1)} %collective-permute-done.other, s32[3,3]{1,0:T(4,128)S(4)} %get-tuple-element.22.ids, ...), custom_call_target="tpu_custom_call" | custom-call | tf_op jit(solution)/shard_map/first_transposed/pallas_call | solution.py:322
  3.7 4.0 %collective-permute-start.2 = (f32[3,32,128]{2,1,0:T(8,128)S(1)}, f32[3,32,128]{2,1,0:T(8,128)S(1)}, u32[]{:S(2)}, u32[]{:S(2)}) collective-permute-start(f32[3,32,128]{2,1,0:T(8,128)S(1)} %get-tuple-element.27), channel_id=1, source_target_pairs={{0,8},{1,13},{2,10},{3,15},{4,12},{5,9},{6,14},{7,11},{8,0},{9,5},... | collective-permute-start | bytes 147464 | tf_op jit(solution)/shard_map/ppermute | solution.py:59
  7.7 1.6 %collective-permute-start.3 = (f32[3,16,128]{2,1,0:T(8,128)S(1)}, f32[3,16,128]{2,1,0:T(8,128)S(1)}, u32[]{:S(2)}, u32[]{:S(2)}) collective-permute-start(f32[3,16,128]{2,1,0:T(8,128)S(1)} %get-tuple-element.28), channel_id=1, source_target_pairs={{0,4},{4,0},{8,12},{12,8},{1,5},{5,1},{9,13},{13,9},{2,6},{6,2},{1... | collective-permute-start | bytes 73736 | tf_op jit(solution)/shard_map/ppermute | solution.py:51
  9.3 2.4 %collective-permute-done.3.refs_1_ = f32[3,16,128]{2,1,0:T(8,128)S(1)} collective-permute-done((f32[3,16,128]{2,1,0:T(8,128)S(1)}, f32[3,16,128]{2,1,0:T(8,128)S(1)}, u32[]{:S(2)}, u32[]{:S(2)}) %collective-permute-start.3) | collective-permute-done | bytes 24608 | tf_op jit(solution)/shard_map/ppermute | solution.py:51
  11.7 0.0 collective-permute-done.2.refs_0_
  11.7 0.6 %first_direct.1.refs_0_ = f32[3,32,128]{2,1,0:T(8,128)S(1)} custom-call(f32[3,3,128,128]{3,2,1,0:T(8,128)S(1)} %get-tuple-element.21.held, f32[3,3,128,128]{3,2,1,0:T(8,128)S(1)} %collective-permute-done.other, s32[3,3]{1,0:T(4,128)S(4)} %get-tuple-element.22.ids, s32[3,3]{1,0:T(4,128)S(4)} %get-tuple-element.25.other_ids, s32[3]{0:T(128)S(4)} %get-tuple-element.23.counts, ...), custom_call_target="tpu_custom_call" | custom-call | tf_op jit(solution)/shard_map/first_direct/pallas_call | solution.py:332
  12.3 1.2 %collective-permute-start.6 = (f32[3,32,128]{2,1,0:T(8,128)S(1)}, f32[3,32,128]{2,1,0:T(8,128)S(1)}, u32[]{:S(2)}, u32[]{:S(2)}) collective-permute-start(f32[3,32,128]{2,1,0:T(8,128)S(1)} %first_direct.1.refs_0_), channel_id=1, source_target_pairs={{0,3},{1,2},{2,1},{3,0},{4,7},{5,6},{6,5},{7,4},{8,11},{9,10},{10,... | collective-permute-start | bytes 147464 | tf_op jit(solution)/shard_map/ppermute | solution.py:51
  13.5 0.5 %collective-permute-start.5 = (f32[3,32,128]{2,1,0:T(8,128)S(1)}, f32[3,32,128]{2,1,0:T(8,128)S(1)}, u32[]{:S(2)}, u32[]{:S(2)}) collective-permute-start(f32[3,32,128]{2,1,0:T(8,128)S(1)} %first_direct.1.refs_0_), channel_id=1, source_target_pairs={{0,2},{1,3},{2,0},{3,1},{4,6},{5,7},{6,4},{7,5},{8,10},{9,11},{10,... | collective-permute-start | bytes 147464 | tf_op jit(solution)/shard_map/ppermute | solution.py:51
  14.0 0.2 collective-permute-start.4
  14.3 2.0 %collective-permute-done.6.refs_3_ = f32[3,32,128]{2,1,0:T(8,128)S(1)} collective-permute-done((f32[3,32,128]{2,1,0:T(8,128)S(1)}, f32[3,32,128]{2,1,0:T(8,128)S(1)}, u32[]{:S(2)}, u32[]{:S(2)}) %collective-permute-start.6) | collective-permute-done | bytes 49184 | tf_op jit(solution)/shard_map/ppermute | solution.py:51
  16.2 1.4 %collective-permute-done.5.refs_2_ = f32[3,32,128]{2,1,0:T(8,128)S(1)} collective-permute-done((f32[3,32,128]{2,1,0:T(8,128)S(1)}, f32[3,32,128]{2,1,0:T(8,128)S(1)}, u32[]{:S(2)}, u32[]{:S(2)}) %collective-permute-start.5) | collective-permute-done | bytes 49184 | tf_op jit(solution)/shard_map/ppermute | solution.py:51
  17.7 0.0 collective-permute-done.4.refs_1_
  17.7 0.6 %second_transposed.1 = (f32[4,32,128]{2,1,0:T(8,128)S(1)}, f32[4,16,128]{2,1,0:T(8,128)S(1)}, f32[3,32,128]{2,1,0:T(8,128)S(1)}, f32[3,32,128]{2,1,0:T(8,128)S(1)}, f32[32,128]{1,0:T(8,128)S(1)}) custom-call(f32[3,3,128,128]{3,2,1,0:T(8,128)S(1)} %get-tuple-element.21.held, f32[3,3,128,128]{3,2,1,0:T(8,128)S(1)} %collective-permute-done.other, ...), custom_call_target="tpu_custom_call" | custom-call | tf_op jit(solution)/shard_map/second_transposed/pallas_call | solution.py:336
  18.2 1.0 %collective-permute-start.7 = (f32[4,32,128]{2,1,0:T(8,128)S(1)}, f32[4,32,128]{2,1,0:T(8,128)S(1)}, u32[]{:S(2)}, u32[]{:S(2)}) collective-permute-start(f32[4,32,128]{2,1,0:T(8,128)S(1)} %get-tuple-element.31), channel_id=1, source_target_pairs={{0,8},{1,13},{2,10},{3,15},{4,12},{5,9},{6,14},{7,11},{8,0},{9,5},... | collective-permute-start | bytes 196616 | tf_op jit(solution)/shard_map/ppermute | solution.py:59
  19.3 2.2 %collective-permute-start.8 = (f32[4,16,128]{2,1,0:T(8,128)S(1)}, f32[4,16,128]{2,1,0:T(8,128)S(1)}, u32[]{:S(2)}, u32[]{:S(2)}) collective-permute-start(f32[4,16,128]{2,1,0:T(8,128)S(1)} %get-tuple-element.32), channel_id=1, source_target_pairs={{0,4},{4,0},{8,12},{12,8},{1,5},{5,1},{9,13},{13,9},{2,6},{6,2},{1... | collective-permute-start | bytes 98312 | tf_op jit(solution)/shard_map/ppermute | solution.py:51
  21.5 2.5 %collective-permute-done.8.refs_1_ = f32[4,16,128]{2,1,0:T(8,128)S(1)} collective-permute-done((f32[4,16,128]{2,1,0:T(8,128)S(1)}, f32[4,16,128]{2,1,0:T(8,128)S(1)}, u32[]{:S(2)}, u32[]{:S(2)}) %collective-permute-start.8) | collective-permute-done | bytes 32800 | tf_op jit(solution)/shard_map/ppermute | solution.py:51
  24.0 0.4 %collective-permute-done.7.refs_0_ = f32[4,32,128]{2,1,0:T(8,128)S(1)} collective-permute-done((f32[4,32,128]{2,1,0:T(8,128)S(1)}, f32[4,32,128]{2,1,0:T(8,128)S(1)}, u32[]{:S(2)}, u32[]{:S(2)}) %collective-permute-start.7) | collective-permute-done | bytes 65568 | tf_op jit(solution)/shard_map/ppermute | solution.py:59
  24.4 0.6 %second_direct.1 = (f32[3,32,128]{2,1,0:T(8,128)S(1)}, f32[4,32,128]{2,1,0:T(8,128)S(1)}) custom-call(f32[3,3,128,128]{3,2,1,0:T(8,128)S(1)} %get-tuple-element.21.held, f32[3,3,128,128]{3,2,1,0:T(8,128)S(1)} %collective-permute-done.other, s32[3,3]{1,0:T(4,128)S(4)} %get-tuple-element.22.ids, s32[3,3]{1,0:T(4,128)S(4)} %get-tuple-element.25.other_ids, ...), custom_call_target="tpu_custom_call" | custom-call | tf_op jit(solution)/shard_map/second_direct/pallas_call | solution.py:344
  25.1 0.1 collective-permute-start.9
  25.1 1.7 %collective-permute-start.11 = (f32[3,32,128]{2,1,0:T(8,128)S(1)}, f32[3,32,128]{2,1,0:T(8,128)S(1)}, u32[]{:S(2)}, u32[]{:S(2)}) collective-permute-start(f32[3,32,128]{2,1,0:T(8,128)S(1)} %get-tuple-element.35.refs_0_), channel_id=1, source_target_pairs={{0,3},{1,2},{2,1},{3,0},{4,7},{5,6},{6,5},{7,4},{8,11},{9,10},{10,... | collective-permute-start | bytes 147464 | tf_op jit(solution)/shard_map/ppermute | solution.py:51
  26.8 0.5 %collective-permute-start.10 = (f32[3,32,128]{2,1,0:T(8,128)S(1)}, f32[3,32,128]{2,1,0:T(8,128)S(1)}, u32[]{:S(2)}, u32[]{:S(2)}) collective-permute-start(f32[3,32,128]{2,1,0:T(8,128)S(1)} %get-tuple-element.35.refs_0_), channel_id=1, source_target_pairs={{0,2},{1,3},{2,0},{3,1},{4,6},{5,7},{6,4},{7,5},{8,10},{9,11},{10,... | collective-permute-start | bytes 147464 | tf_op jit(solution)/shard_map/ppermute | solution.py:51
  27.3 0.0 collective-permute-done.9.others.refs_1_
  27.3 0.8 %factor.1.inverse = f32[32,32]{1,0:T(8,128)S(1)} custom-call(f32[4,32,128]{2,1,0:T(8,128)S(1)} %get-tuple-element.34.mine, f32[4,32,128]{2,1,0:T(8,128)S(1)} %collective-permute-done.9.others.refs_1_), custom_call_target="tpu_custom_call" | custom-call | tf_op jit(solution)/shard_map/factor/pallas_call | solution.py:353
  28.1 0.7 %collective-permute-done.11.refs_3_ = f32[3,32,128]{2,1,0:T(8,128)S(1)} collective-permute-done((f32[3,32,128]{2,1,0:T(8,128)S(1)}, f32[3,32,128]{2,1,0:T(8,128)S(1)}, u32[]{:S(2)}, u32[]{:S(2)}) %collective-permute-start.11) | collective-permute-done | bytes 49184 | tf_op jit(solution)/shard_map/ppermute | solution.py:51
  28.9 2.0 %collective-permute-done.10.refs_2_ = f32[3,32,128]{2,1,0:T(8,128)S(1)} collective-permute-done((f32[3,32,128]{2,1,0:T(8,128)S(1)}, f32[3,32,128]{2,1,0:T(8,128)S(1)}, u32[]{:S(2)}, u32[]{:S(2)}) %collective-permute-start.10) | collective-permute-done | bytes 49184 | tf_op jit(solution)/shard_map/ppermute | solution.py:51
  30.9 0.5 %gram.1 = (f32[3,32,128]{2,1,0:T(8,128)S(1)}, f32[32,64]{1,0:T(8,128)S(1)}) custom-call(f32[32,32]{1,0:T(8,128)S(1)} %factor.1.inverse, f32[3,32,128]{2,1,0:T(8,128)S(1)} %get-tuple-element.30.tiles, f32[3,32,128]{2,1,0:T(8,128)S(1)} %get-tuple-element.35.refs_0_, f32[4,32,128]{2,1,0:T(8,128)S(1)} %collective-permute-done.9.others.refs_1_, ...), custom_call_target="tpu_custom_call" | custom-call | tf_op jit(solution)/shard_map/gram/pallas_call | solution.py:356
  31.3 0.6 %collective-permute-start.13 = (f32[32,64]{1,0:T(8,128)S(1)}, f32[32,64]{1,0:T(8,128)S(1)}, u32[]{:S(2)}, u32[]{:S(2)}) collective-permute-start(f32[32,64]{1,0:T(8,128)S(1)} %get-tuple-element.37.mine), channel_id=1, source_target_pairs={{0,8},{1,13},{2,10},{3,15},{4,12},{5,9},{6,14},{7,11},{8,0},{9,5},... | collective-permute-start | bytes 24584 | tf_op jit(solution)/shard_map/ppermute | solution.py:59
  31.9 2.2 %collective-permute-start.12 = (f32[32,64]{1,0:T(8,128)S(1)}, f32[32,64]{1,0:T(8,128)S(1)}, u32[]{:S(2)}, u32[]{:S(2)}) collective-permute-start(f32[32,64]{1,0:T(8,128)S(1)} %get-tuple-element.37.mine), channel_id=1, source_target_pairs={{0,4},{4,0},{8,12},{12,8},{1,5},{5,1},{9,13},{13,9},{2,6},{6,2},{1... | collective-permute-start | bytes 24584 | tf_op jit(solution)/shard_map/ppermute | solution.py:51
  34.1 2.1 %collective-permute-done.13.refs_0_ = f32[32,64]{1,0:T(8,128)S(1)} collective-permute-done((f32[32,64]{1,0:T(8,128)S(1)}, f32[32,64]{1,0:T(8,128)S(1)}, u32[]{:S(2)}, u32[]{:S(2)}) %collective-permute-start.13) | collective-permute-done | bytes 8224 | tf_op jit(solution)/shard_map/ppermute | solution.py:59
  36.2 0.0 collective-permute-done.12.shared
  36.2 0.1 collective-permute-start.14
  36.3 1.2 %collective-permute-done.14.others = f32[32,64]{1,0:T(8,128)S(1)} collective-permute-done((f32[32,64]{1,0:T(8,128)S(1)}, f32[32,64]{1,0:T(8,128)S(1)}, u32[]{:S(2)}, u32[]{:S(2)}) %collective-permute-start.14) | collective-permute-done | bytes 8224 | tf_op jit(solution)/shard_map/ppermute | solution.py:51
  37.4 1.6 %last.1 = (f32[32,384]{1,0:T(8,128)}, f32[32,32]{1,0:T(8,128)}) custom-call(f32[3,32,128]{2,1,0:T(8,128)S(1)} %get-tuple-element.36.image, f32[32,64]{1,0:T(8,128)S(1)} %half_sum.1.mine, f32[32,64]{1,0:T(8,128)S(1)} %collective-permute-done.14.others), custom_call_target="tpu_custom_call" | custom-call | tf_op jit(solution)/shard_map/last/pallas_call | solution.py:366
  (1 shorter events, 0.0 us)
Async XLA Ops:
  0.6 2.4 %collective-permute-start = (f32[3,3,128,128]{3,2,1,0:T(8,128)}, f32[3,3,128,128]{3,2,1,0:T(8,128)S(1)}, u32[]{:S(2)}, u32[]{:S(2)}) collective-permute-start(f32[3,3,128,128]{3,2,1,0:T(8,128)} %blocks.1), channel_id=1, source_target_pairs={{0,1},{1,0},{2,3},{3,2},{4,5},{5,4},{6,7},{7,6},{8,9},{9,8},{10,11... | collective-permute-start | bytes 1769480 | tf_op jit(solution)/shard_map/ppermute | solution.py:51
  1.1 1.8 %collective-permute-start.1 = (s32[3,3]{1,0:T(4,128)}, s32[3,3]{1,0:T(4,128)S(1)}, u32[]{:S(2)}, u32[]{:S(2)}) collective-permute-start(s32[3,3]{1,0:T(4,128)} %ids.1), channel_id=1, source_target_pairs={{0,1},{1,0},{2,3},{3,2},{4,5},{5,4},{6,7},{7,6},{8,9},{9,8},{10,11... | collective-permute-start | bytes 116 | tf_op jit(solution)/shard_map/ppermute | solution.py:51
  3.7 8.0 %collective-permute-start.2 = (f32[3,32,128]{2,1,0:T(8,128)S(1)}, f32[3,32,128]{2,1,0:T(8,128)S(1)}, u32[]{:S(2)}, u32[]{:S(2)}) collective-permute-start(f32[3,32,128]{2,1,0:T(8,128)S(1)} %get-tuple-element.27), channel_id=1, source_target_pairs={{0,8},{1,13},{2,10},{3,15},{4,12},{5,9},{6,14},{7,11},{8,0},{9,5},... | collective-permute-start | bytes 147464 | tf_op jit(solution)/shard_map/ppermute | solution.py:59
  7.7 4.0 %collective-permute-start.3 = (f32[3,16,128]{2,1,0:T(8,128)S(1)}, f32[3,16,128]{2,1,0:T(8,128)S(1)}, u32[]{:S(2)}, u32[]{:S(2)}) collective-permute-start(f32[3,16,128]{2,1,0:T(8,128)S(1)} %get-tuple-element.28), channel_id=1, source_target_pairs={{0,4},{4,0},{8,12},{12,8},{1,5},{5,1},{9,13},{13,9},{2,6},{6,2},{1... | collective-permute-start | bytes 73736 | tf_op jit(solution)/shard_map/ppermute | solution.py:51
  12.3 3.9 %collective-permute-start.6 = (f32[3,32,128]{2,1,0:T(8,128)S(1)}, f32[3,32,128]{2,1,0:T(8,128)S(1)}, u32[]{:S(2)}, u32[]{:S(2)}) collective-permute-start(f32[3,32,128]{2,1,0:T(8,128)S(1)} %first_direct.1.refs_0_), channel_id=1, source_target_pairs={{0,3},{1,2},{2,1},{3,0},{4,7},{5,6},{6,5},{7,4},{8,11},{9,10},{10,... | collective-permute-start | bytes 147464 | tf_op jit(solution)/shard_map/ppermute | solution.py:51
  13.5 4.1 %collective-permute-start.5 = (f32[3,32,128]{2,1,0:T(8,128)S(1)}, f32[3,32,128]{2,1,0:T(8,128)S(1)}, u32[]{:S(2)}, u32[]{:S(2)}) collective-permute-start(f32[3,32,128]{2,1,0:T(8,128)S(1)} %first_direct.1.refs_0_), channel_id=1, source_target_pairs={{0,2},{1,3},{2,0},{3,1},{4,6},{5,7},{6,4},{7,5},{8,10},{9,11},{10,... | collective-permute-start | bytes 147464 | tf_op jit(solution)/shard_map/ppermute | solution.py:51
  14.0 3.6 %collective-permute-start.4 = (f32[3,32,128]{2,1,0:T(8,128)S(1)}, f32[3,32,128]{2,1,0:T(8,128)S(1)}, u32[]{:S(2)}, u32[]{:S(2)}) collective-permute-start(f32[3,32,128]{2,1,0:T(8,128)S(1)} %first_direct.1.refs_0_), channel_id=1, source_target_pairs={{0,1},{1,0},{2,3},{3,2},{4,5},{5,4},{6,7},{7,6},{8,9},{9,8},{10,11... | collective-permute-start | bytes 147464 | tf_op jit(solution)/shard_map/ppermute | solution.py:51
  18.2 6.2 %collective-permute-start.7 = (f32[4,32,128]{2,1,0:T(8,128)S(1)}, f32[4,32,128]{2,1,0:T(8,128)S(1)}, u32[]{:S(2)}, u32[]{:S(2)}) collective-permute-start(f32[4,32,128]{2,1,0:T(8,128)S(1)} %get-tuple-element.31), channel_id=1, source_target_pairs={{0,8},{1,13},{2,10},{3,15},{4,12},{5,9},{6,14},{7,11},{8,0},{9,5},... | collective-permute-start | bytes 196616 | tf_op jit(solution)/shard_map/ppermute | solution.py:59
  19.3 4.7 %collective-permute-start.8 = (f32[4,16,128]{2,1,0:T(8,128)S(1)}, f32[4,16,128]{2,1,0:T(8,128)S(1)}, u32[]{:S(2)}, u32[]{:S(2)}) collective-permute-start(f32[4,16,128]{2,1,0:T(8,128)S(1)} %get-tuple-element.32), channel_id=1, source_target_pairs={{0,4},{4,0},{8,12},{12,8},{1,5},{5,1},{9,13},{13,9},{2,6},{6,2},{1... | collective-permute-start | bytes 98312 | tf_op jit(solution)/shard_map/ppermute | solution.py:51
  25.1 2.2 %collective-permute-start.9 = (f32[4,32,128]{2,1,0:T(8,128)S(1)}, f32[4,32,128]{2,1,0:T(8,128)S(1)}, u32[]{:S(2)}, u32[]{:S(2)}) collective-permute-start(f32[4,32,128]{2,1,0:T(8,128)S(1)} %get-tuple-element.34.mine), channel_id=1, source_target_pairs={{0,1},{1,0},{2,3},{3,2},{4,5},{5,4},{6,7},{7,6},{8,9},{9,8},{10,11... | collective-permute-start | bytes 196616 | tf_op jit(solution)/shard_map/ppermute | solution.py:51
  25.1 3.7 %collective-permute-start.11 = (f32[3,32,128]{2,1,0:T(8,128)S(1)}, f32[3,32,128]{2,1,0:T(8,128)S(1)}, u32[]{:S(2)}, u32[]{:S(2)}) collective-permute-start(f32[3,32,128]{2,1,0:T(8,128)S(1)} %get-tuple-element.35.refs_0_), channel_id=1, source_target_pairs={{0,3},{1,2},{2,1},{3,0},{4,7},{5,6},{6,5},{7,4},{8,11},{9,10},{10,... | collective-permute-start | bytes 147464 | tf_op jit(solution)/shard_map/ppermute | solution.py:51
  26.8 4.1 %collective-permute-start.10 = (f32[3,32,128]{2,1,0:T(8,128)S(1)}, f32[3,32,128]{2,1,0:T(8,128)S(1)}, u32[]{:S(2)}, u32[]{:S(2)}) collective-permute-start(f32[3,32,128]{2,1,0:T(8,128)S(1)} %get-tuple-element.35.refs_0_), channel_id=1, source_target_pairs={{0,2},{1,3},{2,0},{3,1},{4,6},{5,7},{6,4},{7,5},{8,10},{9,11},{10,... | collective-permute-start | bytes 147464 | tf_op jit(solution)/shard_map/ppermute | solution.py:51
  31.3 4.8 %collective-permute-start.13 = (f32[32,64]{1,0:T(8,128)S(1)}, f32[32,64]{1,0:T(8,128)S(1)}, u32[]{:S(2)}, u32[]{:S(2)}) collective-permute-start(f32[32,64]{1,0:T(8,128)S(1)} %get-tuple-element.37.mine), channel_id=1, source_target_pairs={{0,8},{1,13},{2,10},{3,15},{4,12},{5,9},{6,14},{7,11},{8,0},{9,5},... | collective-permute-start | bytes 24584 | tf_op jit(solution)/shard_map/ppermute | solution.py:59
  31.9 4.2 %collective-permute-start.12 = (f32[32,64]{1,0:T(8,128)S(1)}, f32[32,64]{1,0:T(8,128)S(1)}, u32[]{:S(2)}, u32[]{:S(2)}) collective-permute-start(f32[32,64]{1,0:T(8,128)S(1)} %get-tuple-element.37.mine), channel_id=1, source_target_pairs={{0,4},{4,0},{8,12},{12,8},{1,5},{5,1},{9,13},{13,9},{2,6},{6,2},{1... | collective-permute-start | bytes 24584 | tf_op jit(solution)/shard_map/ppermute | solution.py:51
  36.2 1.2 %collective-permute-start.14 = (f32[32,64]{1,0:T(8,128)S(1)}, f32[32,64]{1,0:T(8,128)S(1)}, u32[]{:S(2)}, u32[]{:S(2)}) collective-permute-start(f32[32,64]{1,0:T(8,128)S(1)} %half_sum.1.mine), channel_id=1, source_target_pairs={{0,1},{1,0},{2,3},{3,2},{4,5},{5,4},{6,7},{7,6},{8,9},{9,8},{10,11... | collective-permute-start | bytes 24584 | tf_op jit(solution)/shard_map/ppermute | solution.py:51

commit v6 on v5

v6 whole, which is shorter than its diff:
```python
import functools

import jax
import jax.numpy as jnp
from jax import lax
from jax.experimental import pallas as pl
from jax.experimental.pallas import tpu as pltpu
from jax.sharding import PartitionSpec as P

F32 = jnp.float32
BF16 = jnp.bfloat16
VMEM = pl.BlockSpec(memory_space=pltpu.VMEM)
SMEM = pl.BlockSpec(memory_space=pltpu.SMEM)
HBM = pl.BlockSpec(memory_space=pltpu.HBM)
DMA = pltpu.SemaphoreType.DMA
PARAMS = pltpu.CompilerParams(vmem_limit_bytes=8 * 2**20)
PANEL = 16


def tree(parts):
    while len(parts) > 1:
        parts = [parts[i] + parts[i + 1] for i in range(0, len(parts), 2)]
    return parts[0]


def split(x):
    high = x.astype(BF16)
    rest = x - high.astype(F32)
    middle = rest.astype(BF16)
    return high, middle, (rest - middle.astype(F32)).astype(BF16)


def product(a_parts, b_parts, contract=0):
    n = a_parts[0].shape[0]

    def dot(a, b):
        return lax.dot_general(a, b, (((1,), (contract,)), ((), ())), preferred_element_type=F32)

    stacked = jnp.concatenate(a_parts, axis=0)
    high = dot(stacked, b_parts[0])
    middle = dot(stacked[: 2 * n], b_parts[1])
    low = dot(a_parts[0], b_parts[2])
    return high[:n] + ((high[n : 2 * n] + middle[:n]) + ((high[2 * n :] + middle[n:]) + low))


def joined(parts, axis):
    return [jnp.concatenate(level, axis=axis) for level in zip(*parts)]


def folded(x, lanes):
    fold = lanes // x.shape[1]
    height = x.shape[0] // fold
    return jnp.concatenate([x[g * height : (g + 1) * height] for g in range(fold)], axis=1)


def unfolded(x, columns):
    return jnp.concatenate([x[:, g : g + columns] for g in range(0, x.shape[1], columns)], axis=0)


def swap(x, axis, distance):
    return lax.ppermute(x, axis, [(i, i ^ distance) for i in range(lax.axis_size(axis))])


def swap_rows(x, even, odd):
    rows, parts = lax.axis_size("row"), lax.axis_size("nbr")
    pairs = [
        (r * parts + n, (r ^ (odd if n % 2 else even)) * parts + n) for r in range(rows) for n in range(parts)
    ]
    return lax.ppermute(x, ("row", "nbr"), pairs)


class Place:
    def __init__(self, rows, blocks, columns):
        self.row = lax.axis_index("row")
        self.part = lax.axis_index("nbr")
        self.odd = self.part & 1
        self.block_rows, self.slots = blocks.shape[:2]
        self.first_row = self.row * self.block_rows
        self.peers = [self.row ^ (k + self.odd) for k in range(2, rows, 2)]
        self.middle = self.row ^ 1
        self.columns = columns
        self.height = columns // 2
        self.half = pl.ds(pl.multiple_of(self.odd * self.height, self.height), self.height)

    def weight(self, ids, counts, member, i, p):
        used = (self.part ^ member) * self.slots + p < counts[i]
        return jnp.where(used, jnp.where(ids[i, p] == self.first_row + i, 0.5, 1.0), 0.0).astype(F32)

    def tile(self, i):
        return slice(i * self.columns, (i + 1) * self.columns)

    def half_tile(self, i):
        return slice(i * self.height, (i + 1) * self.height)


def transposed_products(place, blocks, ids, counts, tiles, out, copies=()):
    out[...] = jnp.zeros_like(out)
    size = out.shape[2]
    values = []
    for i in range(place.block_rows):
        stored = [split(b[i, p]) for b in blocks for p in range(place.slots)]
        values.append(product(split(tiles[place.tile(i)]), joined(stored, 1)))
    for copy in copies:
        copy.wait()
    for i, value in enumerate(values):
        for m in range(len(blocks)):
            for p in range(place.slots):
                at = (m * place.slots + p) * size
                out[ids[m][i, p]] += value[:, at : at + size] * place.weight(ids[m], counts, m, i, p)


def direct_products(place, blocks, ids, counts, whole, i):
    stored, far = [], []
    for m, b in enumerate(blocks):
        for p in range(place.slots):
            stored.append(split(b[i, p].T))
            far.append(split(whole[ids[m][i, p]] * place.weight(ids[m], counts, m, i, p)))
    return product(joined(far, 1), joined(stored, 0))


def fill(place, messages, shared, products, tiles, own):
    n = place.block_rows
    for i in range(n):
        tile = tiles[place.tile(i)]
        for peer, out in zip(place.peers, messages):
            out[place.tile(i)] = jnp.where(place.row < peer, products[peer * n + i], tile)
        shared[place.half_tile(i)] = jnp.where(
            place.row < place.middle,
            products[place.middle * n + i, place.half],
            tiles[pl.ds(pl.multiple_of(i * place.columns + place.odd * place.height, 8), place.height)],
        )
        own[place.tile(i)] = jnp.where(place.odd == 0, products[place.first_row + i], 0.0)


def load_kernel(blocks, ids, counts, start, held, ids_s, counts_s, tiles, sems):
    size, columns = blocks.shape[2], start.shape[0]
    copies = [
        pltpu.make_async_copy(blocks, held, sems.at[0]),
        pltpu.make_async_copy(ids, ids_s, sems.at[1]),
        pltpu.make_async_copy(counts, counts_s, sems.at[2]),
    ]
    for i in range(blocks.shape[0]):
        source = start.at[:, i * size : (i + 1) * size]
        copies.append(pltpu.make_async_copy(source, tiles.at[i * columns : (i + 1) * columns], sems.at[3 + i]))
    for copy in copies:
        copy.start()
    for copy in copies:
        copy.wait()


def first_kernel(rows, held, other, ids, other_ids, counts, tiles, *refs):
    messages, refs = refs[: rows // 2 - 1], refs[rows // 2 - 1 :]
    shared, own, other_s, products, sem = refs
    place = Place(rows, held, products.shape[1])
    copy = pltpu.make_async_copy(other_ids, other_s, sem.at[0])
    copy.start()
    transposed_products(place, (held, other), (ids, other_s), counts, tiles, products, [copy])
    fill(place, messages, shared, products, tiles, own)


def direct_kernel(rows, held, other, ids, other_ids, counts, own, tiles, *refs):
    received, refs = refs[: rows // 2 - 1], refs[rows // 2 - 1 :]
    shared, *gram, out, whole = refs
    n, columns, size = held.shape[0], whole.shape[1], whole.shape[2]
    place = Place(rows, held, columns)
    whole[...] = jnp.zeros_like(whole)
    for i in range(n):
        whole[place.first_row + i] = jnp.where(place.odd == 0, tiles[place.tile(i)], 0.0)
        for peer, message in zip(place.peers, received):
            whole[peer * n + i] = message[place.tile(i)]
        whole[place.middle * n + i, place.half] = shared[place.half_tile(i)]
    for i in range(n):
        value = own[place.tile(i)]
        for peer, message in zip(place.peers, received):
            value += jnp.where(place.row > peer, message[place.tile(i)], 0.0)
        out[place.tile(i)] = value + direct_products(place, (held, other), (ids, other_ids), counts, whole, i)
        mine = pl.ds(pl.multiple_of(i * columns + place.odd * place.height, 8), place.height)
        out[mine] += jnp.where(place.row > place.middle, shared[place.half_tile(i)], 0.0)
    if gram:
        first = jnp.where(place.odd == 0, gram[0][...], shared[n * place.height :])
        out[n * columns :] = tree([first] + [message[n * columns :] for message in received])


def second_kernel(rows, parts, held, other, ids, other_ids, counts, *refs):
    images, refs = refs[:parts], refs[parts:]
    messages, refs = refs[: rows // 2 - 1], refs[rows // 2 - 1 :]
    shared, own, tiles, gram, products = refs
    n, columns, size = held.shape[0], products.shape[1], products.shape[2]
    place = Place(rows, held, columns)
    tiles[...] = tree([image[...] for image in images])
    transposed_products(place, (held, other), (ids, other_ids), counts, tiles, products)
    fill(place, messages, shared, products, tiles, own)
    whole = joined([split(tiles[place.tile(i)]) for i in range(n)], 1)
    packed = folded(product(whole, whole, 1), size)
    gram[...] = packed
    for message in messages:
        message[n * columns :] = packed
    shared[n * place.height :] = packed


def eliminated(gram, rest):
    n, width = gram.shape[0], rest.shape[1]
    groups = [[gram[g : g + 8], rest[g : g + 8]] for g in range(0, n, 8)]
    height = lax.broadcasted_iota(jnp.int32, (8, 1), 0)
    for first in range(0, n, PANEL):
        columns = [
            [jnp.broadcast_to(group[0][:, first + t : first + t + 1], (8, 128)) for group in groups]
            for t in range(PANEL)
        ]
        for t in range(PANEL):
            k = first + t
            gk, sk = k // 8, k % 8
            pivot = columns[t][gk][sk : sk + 1]
            inverse = 1.0 / pivot
            root = lax.rsqrt(pivot)
            source = [x[sk : sk + 1] for x in groups[gk]]
            steps = {}
            for g in range(gk, len(groups)):
                m = columns[t][g] * inverse
                steps[g] = jnp.where(height > sk, m, 0.0) if g == gk else m
            for u in range(t + 1, PANEL):
                head = columns[u][gk][sk : sk + 1]
                for g in range(gk, len(groups)):
                    columns[u][g] = columns[u][g] - steps[g] * head
            for g in range(gk, len(groups)):
                groups[g] = [x - wide(steps[g], x.shape[1]) * s for x, s in zip(groups[g], source)]
            groups[gk][1] = jnp.where(height == sk, groups[gk][1] * wide(root, width), groups[gk][1])
    return jnp.concatenate([group[1] for group in groups], axis=0)


def wide(x, lanes):
    if lanes <= x.shape[1]:
        return x[:, :lanes]
    return jnp.concatenate([x] * (lanes // x.shape[1]), axis=1)


def identity(n):
    rows = lax.broadcasted_iota(jnp.int32, (n, n), 0)
    return jnp.where(rows == lax.broadcasted_iota(jnp.int32, (n, n), 1), 1.0, 0.0)


def pair_kernel(mine, others, image, gram):
    tall = image.shape[0]
    image[...] = mine[:tall] + others[:tall]
    gram[...] = unfolded(mine[tall:] + others[tall:], gram.shape[0])


def factor_kernel(total, gram, tiles, inverse, prior):
    columns = gram.shape[0]
    lower = eliminated(gram[...] / total, identity(columns))
    inverse[...] = lower
    parts = [split(tiles[i : i + columns]) for i in range(0, tiles.shape[0], columns)]
    prior[...] = product(split(lower), joined(parts, 1))


def gram_kernel(inverse, prior, *refs):
    images, (image, out) = refs[:-2], refs[-2:]
    columns = inverse.shape[0]
    new = split(tree([part[...] for part in images]))
    rows = range(0, new[0].shape[0], columns)
    value = product(split(inverse[...]), [jnp.concatenate([x[i : i + columns] for i in rows], axis=1) for x in new])
    image[...] = value
    value = split(value)
    both = product(joined([value, split(prior[...])], 0), value, 1)
    out[...] = folded(both, out.shape[1])


def half_sum_kernel(mine, shared, *refs):
    received, out = refs[:-1], refs[-1]
    first = jnp.where((lax.axis_index("nbr") & 1) == 0, mine[...], shared[...])
    out[...] = tree([first] + [part[...] for part in received])


def last_kernel(total, image, mine, others, basis, ritz):
    columns = ritz.shape[0]
    both = unfolded((mine[...] + others[...]) / total, columns)
    ritz[...] = both[columns:]
    basis[...] = eliminated(both[:columns], image[...])


def body(blocks, partner_ids, counts, start):
    block_rows, slots, size, _ = blocks.shape
    columns = start.shape[1]
    rows, parts = lax.axis_size("row"), lax.axis_size("nbr")
    half = rows // 2
    all_blocks = block_rows * rows
    total = float(all_blocks * size)
    extra = columns * columns // size

    def flat(height):
        return jax.ShapeDtypeStruct((height, size), F32)

    tall = block_rows * columns
    tile, square = flat(tall), jax.ShapeDtypeStruct((columns, columns), F32)
    across = jax.ShapeDtypeStruct(start.shape[::-1], F32)
    table = pltpu.SMEM(partner_ids.shape, jnp.int32)
    work = pltpu.VMEM((all_blocks, columns, size), F32)

    def call(kernel, name, specs, outs, scratch=()):
        return pl.pallas_call(
            kernel,
            name=name,
            in_specs=specs,
            out_specs=[VMEM if isinstance(out, jax.ShapeDtypeStruct) else SMEM for out in outs],
            out_shape=outs,
            scratch_shapes=scratch,
            compiler_params=PARAMS,
        )

    def round_over_rows(messages, shared):
        return [swap_rows(m, 2 * k, 2 * k + 1) for k, m in enumerate(messages, 1)], swap(shared, "row", 1)

    def sum_over_pairs(image):
        return [image] + [swap(image, "nbr", s) for s in range(2, parts, 2)]

    other = swap(blocks, "nbr", 1)
    other_ids = swap(partner_ids, "nbr", 1)
    held, ids, counts, tiles = call(
        load_kernel,
        "load",
        [HBM] * 4,
        [jax.ShapeDtypeStruct(blocks.shape, F32), table, pltpu.SMEM(counts.shape, jnp.int32), tile],
        [DMA((3 + block_rows,))],
    )(*[pltpu.with_memory_space_constraint(x, pltpu.HBM) for x in (blocks, partner_ids, counts, start.T)])
    *messages, shared, own, other_ids = call(
        functools.partial(first_kernel, rows),
        "first_transposed",
        [VMEM, VMEM, SMEM, VMEM, SMEM, VMEM],
        [tile] * (half - 1) + [flat(tall // 2), tile, table],
        [work, DMA((1,))],
    )(held, other, ids, other_ids, counts, tiles)
    stored = (held, other, ids, other_ids, counts)
    index = [VMEM, VMEM, SMEM, SMEM, SMEM]
    received, shared = round_over_rows(messages, shared)
    (image,) = call(
        functools.partial(direct_kernel, rows), "first_direct", index + [VMEM] * (half + 2), [tile], [work]
    )(*stored, own, tiles, *received, shared)
    images = sum_over_pairs(image + swap(image, "nbr", 1))
    *messages, shared, own, tiles, gram = call(
        functools.partial(second_kernel, rows, parts // 2),
        "second_transposed",
        index + [VMEM] * (parts // 2),
        [flat(tall + extra)] * (half - 1) + [flat(tall // 2 + extra), tile, tile, flat(extra)],
        [work],
    )(*stored, *images)
    received, shared = round_over_rows(messages, shared)
    (mine,) = call(
        functools.partial(direct_kernel, rows),
        "second_direct",
        index + [VMEM] * (half + 3),
        [flat(tall + extra)],
        [work],
    )(*stored, own, tiles, *received, shared, gram)
    image, gram = call(pair_kernel, "pair", [VMEM] * 2, [tile, square])(mine, swap(mine, "nbr", 1))
    images = sum_over_pairs(image)
    inverse, prior = call(functools.partial(factor_kernel, total), "factor", [VMEM] * 2, [square, across])(gram, tiles)
    image, both = call(gram_kernel, "gram", [VMEM] * (parts // 2 + 2), [across, flat(2 * extra)])(
        inverse, prior, *images
    )
    received, shared = round_over_rows([both] * (half - 1), both)
    (both,) = call(half_sum_kernel, "half_sum", [VMEM] * (half + 1), [flat(2 * extra)])(both, shared, *received)
    basis, ritz = call(functools.partial(last_kernel, total), "last", [VMEM] * 3, [across, square])(
        image, both, swap(both, "nbr", 1)
    )
    return basis.T, ritz


def solution(mesh):
    return jax.shard_map(
        body,
        mesh=mesh,
        in_specs=(
            P(("dom", "row"), "nbr", None, None),
            P(("dom", "row"), "nbr"),
            P(("dom", "row")),
            P(("dom", "row"), None),
        ),
        out_specs=(P(("dom", "row"), None), P("dom", None)),
        check_vma=False,
    )
```

time: 39.2 us -> 38.1 us (0.972)
  waiting for transfers between devices: 15.5 us -> 14.7 us
    ppermute x3, waiting for transfers between devices: 2.52 us -> 1.17 us  [swap_rows(): return lax.ppermute(x, ('row', 'nbr'), pairs)]
    ppermute x12 -> x10, starting transfers between devices: 10.7 us -> 9.41 us  [swap(): lax.ppermute(x, axis, [(i, i ^ distance) for i in range(lax.axis_size(axi...]
    ppermute x3, starting transfers between devices: 5.66 us -> 6.97 us  [swap_rows(): return lax.ppermute(x, ('row', 'nbr'), pairs)]
    ppermute x12 -> x10, waiting for transfers between devices: 12.9 us -> 13.5 us  [swap(): lax.ppermute(x, axis, [(i, i ^ distance) for i in range(lax.axis_size(axi...]
    pallas_call x8 -> x9, Pallas kernels: 5.85 us -> 5.52 us  [the longest x1 1.24 us: body(): call(functools.partial(last_kernel, total), 'last', [VMEM] * 3, [across,...]
  transfers between devices with their start and end apart: 15 -> 13, of which waited for: 10 -> 10; matrix products, arithmetic and copies ran while one was open for 0% -> 0% of each run, Pallas kernels for 5% -> 5%
where the time goes in v6:
time: 38.1 us; the launch traced here: 38 us
  starting transfers between devices  16.4 us (43%)
  waiting for transfers between devices  14.7 us (39%)
  Pallas kernels  6.19 us (16%)
  between operations  0.69 us (2%)
    ppermute x10, waiting for transfers between devices, swap(): lax.ppermute(x, axis, [(i, i ^ distance) for i in range(lax.axis_size(axi...  13.5 us
    ppermute x10, starting transfers between devices, swap(): lax.ppermute(x, axis, [(i, i ^ distance) for i in range(lax.axis_size(axi...  9.41 us
    ppermute x3, starting transfers between devices, swap_rows(): return lax.ppermute(x, ('row', 'nbr'), pairs)  6.97 us
    pallas_call x1, Pallas kernels, body(): call(functools.partial(last_kernel, total), 'last', [VMEM] * 3, [across,...  1.24 us
    ppermute x3, waiting for transfers between devices, swap_rows(): return lax.ppermute(x, ('row', 'nbr'), pairs)  1.17 us
    pallas_call x1, Pallas kernels, body(): call(load_kernel, 'load', [HBM] * 4, [jax.ShapeDtypeStruct(blocks.shape,...  1.14 us
  transfers between devices with their start and end apart: 13, of which 10 were waited for; matrix products, arithmetic and copies ran while one was open for 0% of the time, Pallas kernels for 5%

profile of v6, /device:TPU:0, one launch (start us, length us, event | category | flops | bytes accessed | tf_op | source)
XLA Modules:
  0.0 38.0 jit_solution(126648815837520679)
XLA Ops:
  0.6 0.5 %collective-permute-start = (f32[3,3,128,128]{3,2,1,0:T(8,128)}, f32[3,3,128,128]{3,2,1,0:T(8,128)S(1)}, u32[]{:S(2)}, u32[]{:S(2)}) collective-permute-start(f32[3,3,128,128]{3,2,1,0:T(8,128)} %blocks.1), channel_id=1, source_target_pairs={{0,1},{1,0},{2,3},{3,2},{4,5},{5,4},{6,7},{7,6},{8,9},{9,8},{10,11... | collective-permute-start | bytes 1769480 | tf_op jit(solution)/shard_map/ppermute | solution.py:61
  1.1 0.1 collective-permute-start.1
  1.2 1.1 %load.1 = (f32[3,3,128,128]{3,2,1,0:T(8,128)S(1)}, s32[3,3]{1,0:T(4,128)S(4)}, s32[3]{0:T(128)S(4)}, f32[96,128]{1,0:T(8,128)S(1)}) custom-call(f32[3,3,128,128]{3,2,1,0:T(8,128)} %blocks.1, s32[3,3]{1,0:T(4,128)} %ids.1, s32[3]{0:T(128)} %counts.1, f32[32,384]{1,0:T(8,128)} %bitcast.2), custom_call_target="tpu_custom_call" | custom-call | tf_op jit(solution)/shard_map/load/pallas_call | solution.py:318
  2.4 0.6 %collective-permute-done.1.other_ids = s32[3,3]{1,0:T(4,128)S(1)} collective-permute-done((s32[3,3]{1,0:T(4,128)}, s32[3,3]{1,0:T(4,128)S(1)}, u32[]{:S(2)}, u32[]{:S(2)}) %collective-permute-start.1) | collective-permute-done | bytes 68 | tf_op jit(solution)/shard_map/ppermute | solution.py:61
  3.0 0.0 collective-permute-done.other
  3.0 0.7 %first_transposed.1 = (f32[96,128]{1,0:T(8,128)S(1)}, f32[48,128]{1,0:T(8,128)S(1)}, f32[96,128]{1,0:T(8,128)S(1)}, s32[3,3]{1,0:T(4,128)S(4)}) custom-call(f32[3,3,128,128]{3,2,1,0:T(8,128)S(1)} %get-tuple-element.23.held, f32[3,3,128,128]{3,2,1,0:T(8,128)S(1)} %collective-permute-done.other, s32[3,3]{1,0:T(4,128)S(4)} %get-tuple-element.24.ids, ...), custom_call_target="tpu_custom_call" | custom-call | tf_op jit(solution)/shard_map/first_transposed/pallas_call | solution.py:325
  3.7 4.0 %collective-permute-start.2 = (f32[96,128]{1,0:T(8,128)S(1)}, f32[96,128]{1,0:T(8,128)S(1)}, u32[]{:S(2)}, u32[]{:S(2)}) collective-permute-start(f32[96,128]{1,0:T(8,128)S(1)} %get-tuple-element.29), channel_id=1, source_target_pairs={{0,8},{1,13},{2,10},{3,15},{4,12},{5,9},{6,14},{7,11},{8,0},{9,5},... | collective-permute-start | bytes 147464 | tf_op jit(solution)/shard_map/ppermute | solution.py:69
  7.7 1.6 %collective-permute-start.3 = (f32[48,128]{1,0:T(8,128)S(1)}, f32[48,128]{1,0:T(8,128)S(1)}, u32[]{:S(2)}, u32[]{:S(2)}) collective-permute-start(f32[48,128]{1,0:T(8,128)S(1)} %get-tuple-element.30), channel_id=1, source_target_pairs={{0,4},{4,0},{8,12},{12,8},{1,5},{5,1},{9,13},{13,9},{2,6},{6,2},{1... | collective-permute-start | bytes 73736 | tf_op jit(solution)/shard_map/ppermute | solution.py:61
  9.3 2.4 %collective-permute-done.3.refs_1_ = f32[48,128]{1,0:T(8,128)S(1)} collective-permute-done((f32[48,128]{1,0:T(8,128)S(1)}, f32[48,128]{1,0:T(8,128)S(1)}, u32[]{:S(2)}, u32[]{:S(2)}) %collective-permute-start.3) | collective-permute-done | bytes 24608 | tf_op jit(solution)/shard_map/ppermute | solution.py:61
  11.7 0.0 collective-permute-done.2.refs_0_
  11.7 0.6 %first_direct.1 = f32[96,128]{1,0:T(8,128)S(1)} custom-call(f32[3,3,128,128]{3,2,1,0:T(8,128)S(1)} %get-tuple-element.23.held, f32[3,3,128,128]{3,2,1,0:T(8,128)S(1)} %collective-permute-done.other, s32[3,3]{1,0:T(4,128)S(4)} %get-tuple-element.24.ids, s32[3,3]{1,0:T(4,128)S(4)} %get-tuple-element.27.other_ids, s32[3]{0:T(128)S(4)} %get-tuple-element.25.counts, ...), custom_call_target="tpu_custom_call" | custom-call | tf_op jit(solution)/shard_map/first_direct/pallas_call | solution.py:335
  12.3 0.1 collective-permute-start.4
  12.4 1.2 %collective-permute-done.4 = f32[96,128]{1,0:T(8,128)S(1)} collective-permute-done((f32[96,128]{1,0:T(8,128)S(1)}, f32[96,128]{1,0:T(8,128)S(1)}, u32[]{:S(2)}, u32[]{:S(2)}) %collective-permute-start.4) | collective-permute-done | bytes 49184 | tf_op jit(solution)/shard_map/ppermute | solution.py:61
  13.6 1.6 %collective-permute-start.5 = (f32[96,128]{1,0:T(8,128)S(1)}, f32[96,128]{1,0:T(8,128)S(1)}, u32[]{:S(2)}, u32[]{:S(2)}) collective-permute-start(f32[96,128]{1,0:T(8,128)S(1)} %add.3.refs_0_), channel_id=1, source_target_pairs={{0,2},{1,3},{2,0},{3,1},{4,6},{5,7},{6,4},{7,5},{8,10},{9,11},{10,... | collective-permute-start | bytes 147464 | tf_op jit(solution)/shard_map/ppermute | solution.py:61
  15.2 2.6 %collective-permute-done.5.refs_1_ = f32[96,128]{1,0:T(8,128)S(1)} collective-permute-done((f32[96,128]{1,0:T(8,128)S(1)}, f32[96,128]{1,0:T(8,128)S(1)}, u32[]{:S(2)}, u32[]{:S(2)}) %collective-permute-start.5) | collective-permute-done | bytes 49184 | tf_op jit(solution)/shard_map/ppermute | solution.py:61
  17.8 0.6 %second_transposed.1 = (f32[104,128]{1,0:T(8,128)S(1)}, f32[56,128]{1,0:T(8,128)S(1)}, f32[96,128]{1,0:T(8,128)S(1)}, f32[96,128]{1,0:T(8,128)S(1)}, f32[8,128]{1,0:T(8,128)S(1)}) custom-call(f32[3,3,128,128]{3,2,1,0:T(8,128)S(1)} %get-tuple-element.23.held, f32[3,3,128,128]{3,2,1,0:T(8,128)S(1)} %collective-permute-done.other, ...), custom_call_target="tpu_custom_call" | custom-call | tf_op jit(solution)/shard_map/second_transposed/pallas_call | solution.py:339
  18.4 1.4 %collective-permute-start.6 = (f32[104,128]{1,0:T(8,128)S(1)}, f32[104,128]{1,0:T(8,128)S(1)}, u32[]{:S(2)}, u32[]{:S(2)}) collective-permute-start(f32[104,128]{1,0:T(8,128)S(1)} %get-tuple-element.33), channel_id=1, source_target_pairs={{0,8},{1,13},{2,10},{3,15},{4,12},{5,9},{6,14},{7,11},{8,0},{9,5},... | collective-permute-start | bytes 159752 | tf_op jit(solution)/shard_map/ppermute | solution.py:69
  19.8 2.1 %collective-permute-start.7 = (f32[56,128]{1,0:T(8,128)S(1)}, f32[56,128]{1,0:T(8,128)S(1)}, u32[]{:S(2)}, u32[]{:S(2)}) collective-permute-start(f32[56,128]{1,0:T(8,128)S(1)} %get-tuple-element.34), channel_id=1, source_target_pairs={{0,4},{4,0},{8,12},{12,8},{1,5},{5,1},{9,13},{13,9},{2,6},{6,2},{1... | collective-permute-start | bytes 86024 | tf_op jit(solution)/shard_map/ppermute | solution.py:61
  21.9 1.9 %collective-permute-done.7.refs_1_ = f32[56,128]{1,0:T(8,128)S(1)} collective-permute-done((f32[56,128]{1,0:T(8,128)S(1)}, f32[56,128]{1,0:T(8,128)S(1)}, u32[]{:S(2)}, u32[]{:S(2)}) %collective-permute-start.7) | collective-permute-done | bytes 28704 | tf_op jit(solution)/shard_map/ppermute | solution.py:61
  23.8 0.0 collective-permute-done.6.refs_0_
  23.8 0.6 %second_direct.1.mine = f32[104,128]{1,0:T(8,128)S(1)} custom-call(f32[3,3,128,128]{3,2,1,0:T(8,128)S(1)} %get-tuple-element.23.held, f32[3,3,128,128]{3,2,1,0:T(8,128)S(1)} %collective-permute-done.other, s32[3,3]{1,0:T(4,128)S(4)} %get-tuple-element.24.ids, s32[3,3]{1,0:T(4,128)S(4)} %get-tuple-element.27.other_ids, s32[3]{0:T(128)S(4)} %get-tuple-element.25.counts, ...), custom_call_target="tpu_custom_call" | custom-call | tf_op jit(solution)/shard_map/second_direct/pallas_call | solution.py:347
  24.4 0.1 collective-permute-start.8
  24.5 1.2 %collective-permute-done.8.others = f32[104,128]{1,0:T(8,128)S(1)} collective-permute-done((f32[104,128]{1,0:T(8,128)S(1)}, f32[104,128]{1,0:T(8,128)S(1)}, u32[]{:S(2)}, u32[]{:S(2)}) %collective-permute-start.8) | collective-permute-done | bytes 53280 | tf_op jit(solution)/shard_map/ppermute | solution.py:61
  25.7 0.1 pair.1
  25.8 1.5 %collective-permute-start.9 = (f32[96,128]{1,0:T(8,128)S(1)}, f32[96,128]{1,0:T(8,128)S(1)}, u32[]{:S(2)}, u32[]{:S(2)}) collective-permute-start(f32[96,128]{1,0:T(8,128)S(1)} %get-tuple-element.39.refs_0_), channel_id=1, source_target_pairs={{0,2},{1,3},{2,0},{3,1},{4,6},{5,7},{6,4},{7,5},{8,10},{9,11},{10,... | collective-permute-start | bytes 147464 | tf_op jit(solution)/shard_map/ppermute | solution.py:61
  27.3 0.8 %factor.1 = (f32[32,32]{1,0:T(8,128)S(1)}, f32[32,384]{1,0:T(8,128)S(1)}) custom-call(f32[32,32]{1,0:T(8,128)S(1)} %get-tuple-element.36.gram, f32[96,128]{1,0:T(8,128)S(1)} %get-tuple-element.32.tiles), custom_call_target="tpu_custom_call" | custom-call | tf_op jit(solution)/shard_map/factor/pallas_call | solution.py:356
  28.1 1.8 %collective-permute-done.9.refs_1_ = f32[96,128]{1,0:T(8,128)S(1)} collective-permute-done((f32[96,128]{1,0:T(8,128)S(1)}, f32[96,128]{1,0:T(8,128)S(1)}, u32[]{:S(2)}, u32[]{:S(2)}) %collective-permute-start.9) | collective-permute-done | bytes 49184 | tf_op jit(solution)/shard_map/ppermute | solution.py:61
  29.9 0.5 %gram.1 = (f32[32,384]{1,0:T(8,128)S(1)}, f32[16,128]{1,0:T(8,128)S(1)}) custom-call(f32[32,32]{1,0:T(8,128)S(1)} %get-tuple-element.37.inverse, f32[32,384]{1,0:T(8,128)S(1)} %get-tuple-element.38.prior, f32[96,128]{1,0:T(8,128)S(1)} %get-tuple-element.39.refs_0_, f32[96,128]{1,0:T(8,128)S(1)} %collective-permute-done.9.refs_1_), custom_call_target="tpu_custom_call" | custom-call | tf_op jit(solution)/shard_map/gram/pallas_call | solution.py:357
  30.4 1.5 %collective-permute-start.11 = (f32[16,128]{1,0:T(8,128)S(1)}, f32[16,128]{1,0:T(8,128)S(1)}, u32[]{:S(2)}, u32[]{:S(2)}) collective-permute-start(f32[16,128]{1,0:T(8,128)S(1)} %get-tuple-element.41.mine), channel_id=1, source_target_pairs={{0,8},{1,13},{2,10},{3,15},{4,12},{5,9},{6,14},{7,11},{8,0},{9,5},... | collective-permute-start | bytes 24584 | tf_op jit(solution)/shard_map/ppermute | solution.py:69
  31.9 1.8 %collective-permute-start.10 = (f32[16,128]{1,0:T(8,128)S(1)}, f32[16,128]{1,0:T(8,128)S(1)}, u32[]{:S(2)}, u32[]{:S(2)}) collective-permute-start(f32[16,128]{1,0:T(8,128)S(1)} %get-tuple-element.41.mine), channel_id=1, source_target_pairs={{0,4},{4,0},{8,12},{12,8},{1,5},{5,1},{9,13},{13,9},{2,6},{6,2},{1... | collective-permute-start | bytes 24584 | tf_op jit(solution)/shard_map/ppermute | solution.py:61
  33.8 1.2 %collective-permute-done.11.refs_0_ = f32[16,128]{1,0:T(8,128)S(1)} collective-permute-done((f32[16,128]{1,0:T(8,128)S(1)}, f32[16,128]{1,0:T(8,128)S(1)}, u32[]{:S(2)}, u32[]{:S(2)}) %collective-permute-start.11) | collective-permute-done | bytes 8224 | tf_op jit(solution)/shard_map/ppermute | solution.py:69
  34.9 0.6 %collective-permute-done.10.shared = f32[16,128]{1,0:T(8,128)S(1)} collective-permute-done((f32[16,128]{1,0:T(8,128)S(1)}, f32[16,128]{1,0:T(8,128)S(1)}, u32[]{:S(2)}, u32[]{:S(2)}) %collective-permute-start.10) | collective-permute-done | bytes 8224 | tf_op jit(solution)/shard_map/ppermute | solution.py:61
  35.6 0.0 collective-permute-start.12
  35.6 1.2 %collective-permute-done.12.others = f32[16,128]{1,0:T(8,128)S(1)} collective-permute-done((f32[16,128]{1,0:T(8,128)S(1)}, f32[16,128]{1,0:T(8,128)S(1)}, u32[]{:S(2)}, u32[]{:S(2)}) %collective-permute-start.12) | collective-permute-done | bytes 8224 | tf_op jit(solution)/shard_map/ppermute | solution.py:61
  36.7 1.2 %last.1 = (f32[32,384]{1,0:T(8,128)}, f32[32,32]{1,0:T(8,128)}) custom-call(f32[32,384]{1,0:T(8,128)S(1)} %get-tuple-element.40.image, f32[16,128]{1,0:T(8,128)S(1)} %half_sum.1.mine, f32[16,128]{1,0:T(8,128)S(1)} %collective-permute-done.12.others), custom_call_target="tpu_custom_call" | custom-call | tf_op jit(solution)/shard_map/last/pallas_call | solution.py:362
  (2 shorter events, 0.0 us)
Async XLA Ops:
  0.6 2.4 %collective-permute-start = (f32[3,3,128,128]{3,2,1,0:T(8,128)}, f32[3,3,128,128]{3,2,1,0:T(8,128)S(1)}, u32[]{:S(2)}, u32[]{:S(2)}) collective-permute-start(f32[3,3,128,128]{3,2,1,0:T(8,128)} %blocks.1), channel_id=1, source_target_pairs={{0,1},{1,0},{2,3},{3,2},{4,5},{5,4},{6,7},{7,6},{8,9},{9,8},{10,11... | collective-permute-start | bytes 1769480 | tf_op jit(solution)/shard_map/ppermute | solution.py:61
  1.1 1.8 %collective-permute-start.1 = (s32[3,3]{1,0:T(4,128)}, s32[3,3]{1,0:T(4,128)S(1)}, u32[]{:S(2)}, u32[]{:S(2)}) collective-permute-start(s32[3,3]{1,0:T(4,128)} %ids.1), channel_id=1, source_target_pairs={{0,1},{1,0},{2,3},{3,2},{4,5},{5,4},{6,7},{7,6},{8,9},{9,8},{10,11... | collective-permute-start | bytes 116 | tf_op jit(solution)/shard_map/ppermute | solution.py:61
  3.7 8.0 %collective-permute-start.2 = (f32[96,128]{1,0:T(8,128)S(1)}, f32[96,128]{1,0:T(8,128)S(1)}, u32[]{:S(2)}, u32[]{:S(2)}) collective-permute-start(f32[96,128]{1,0:T(8,128)S(1)} %get-tuple-element.29), channel_id=1, source_target_pairs={{0,8},{1,13},{2,10},{3,15},{4,12},{5,9},{6,14},{7,11},{8,0},{9,5},... | collective-permute-start | bytes 147464 | tf_op jit(solution)/shard_map/ppermute | solution.py:69
  7.7 4.0 %collective-permute-start.3 = (f32[48,128]{1,0:T(8,128)S(1)}, f32[48,128]{1,0:T(8,128)S(1)}, u32[]{:S(2)}, u32[]{:S(2)}) collective-permute-start(f32[48,128]{1,0:T(8,128)S(1)} %get-tuple-element.30), channel_id=1, source_target_pairs={{0,4},{4,0},{8,12},{12,8},{1,5},{5,1},{9,13},{13,9},{2,6},{6,2},{1... | collective-permute-start | bytes 73736 | tf_op jit(solution)/shard_map/ppermute | solution.py:61
  12.3 1.3 %collective-permute-start.4 = (f32[96,128]{1,0:T(8,128)S(1)}, f32[96,128]{1,0:T(8,128)S(1)}, u32[]{:S(2)}, u32[]{:S(2)}) collective-permute-start(f32[96,128]{1,0:T(8,128)S(1)} %first_direct.1), channel_id=1, source_target_pairs={{0,1},{1,0},{2,3},{3,2},{4,5},{5,4},{6,7},{7,6},{8,9},{9,8},{10,11... | collective-permute-start | bytes 147464 | tf_op jit(solution)/shard_map/ppermute | solution.py:61
  13.6 4.2 %collective-permute-start.5 = (f32[96,128]{1,0:T(8,128)S(1)}, f32[96,128]{1,0:T(8,128)S(1)}, u32[]{:S(2)}, u32[]{:S(2)}) collective-permute-start(f32[96,128]{1,0:T(8,128)S(1)} %add.3.refs_0_), channel_id=1, source_target_pairs={{0,2},{1,3},{2,0},{3,1},{4,6},{5,7},{6,4},{7,5},{8,10},{9,11},{10,... | collective-permute-start | bytes 147464 | tf_op jit(solution)/shard_map/ppermute | solution.py:61
  18.4 5.4 %collective-permute-start.6 = (f32[104,128]{1,0:T(8,128)S(1)}, f32[104,128]{1,0:T(8,128)S(1)}, u32[]{:S(2)}, u32[]{:S(2)}) collective-permute-start(f32[104,128]{1,0:T(8,128)S(1)} %get-tuple-element.33), channel_id=1, source_target_pairs={{0,8},{1,13},{2,10},{3,15},{4,12},{5,9},{6,14},{7,11},{8,0},{9,5},... | collective-permute-start | bytes 159752 | tf_op jit(solution)/shard_map/ppermute | solution.py:69
  19.8 4.0 %collective-permute-start.7 = (f32[56,128]{1,0:T(8,128)S(1)}, f32[56,128]{1,0:T(8,128)S(1)}, u32[]{:S(2)}, u32[]{:S(2)}) collective-permute-start(f32[56,128]{1,0:T(8,128)S(1)} %get-tuple-element.34), channel_id=1, source_target_pairs={{0,4},{4,0},{8,12},{12,8},{1,5},{5,1},{9,13},{13,9},{2,6},{6,2},{1... | collective-permute-start | bytes 86024 | tf_op jit(solution)/shard_map/ppermute | solution.py:61
  24.4 1.3 %collective-permute-start.8 = (f32[104,128]{1,0:T(8,128)S(1)}, f32[104,128]{1,0:T(8,128)S(1)}, u32[]{:S(2)}, u32[]{:S(2)}) collective-permute-start(f32[104,128]{1,0:T(8,128)S(1)} %second_direct.1.mine), channel_id=1, source_target_pairs={{0,1},{1,0},{2,3},{3,2},{4,5},{5,4},{6,7},{7,6},{8,9},{9,8},{10,11... | collective-permute-start | bytes 159752 | tf_op jit(solution)/shard_map/ppermute | solution.py:61
  25.8 4.1 %collective-permute-start.9 = (f32[96,128]{1,0:T(8,128)S(1)}, f32[96,128]{1,0:T(8,128)S(1)}, u32[]{:S(2)}, u32[]{:S(2)}) collective-permute-start(f32[96,128]{1,0:T(8,128)S(1)} %get-tuple-element.39.refs_0_), channel_id=1, source_target_pairs={{0,2},{1,3},{2,0},{3,1},{4,6},{5,7},{6,4},{7,5},{8,10},{9,11},{10,... | collective-permute-start | bytes 147464 | tf_op jit(solution)/shard_map/ppermute | solution.py:61
  30.4 4.6 %collective-permute-start.11 = (f32[16,128]{1,0:T(8,128)S(1)}, f32[16,128]{1,0:T(8,128)S(1)}, u32[]{:S(2)}, u32[]{:S(2)}) collective-permute-start(f32[16,128]{1,0:T(8,128)S(1)} %get-tuple-element.41.mine), channel_id=1, source_target_pairs={{0,8},{1,13},{2,10},{3,15},{4,12},{5,9},{6,14},{7,11},{8,0},{9,5},... | collective-permute-start | bytes 24584 | tf_op jit(solution)/shard_map/ppermute | solution.py:69
  31.9 3.7 %collective-permute-start.10 = (f32[16,128]{1,0:T(8,128)S(1)}, f32[16,128]{1,0:T(8,128)S(1)}, u32[]{:S(2)}, u32[]{:S(2)}) collective-permute-start(f32[16,128]{1,0:T(8,128)S(1)} %get-tuple-element.41.mine), channel_id=1, source_target_pairs={{0,4},{4,0},{8,12},{12,8},{1,5},{5,1},{9,13},{13,9},{2,6},{6,2},{1... | collective-permute-start | bytes 24584 | tf_op jit(solution)/shard_map/ppermute | solution.py:61
  35.6 1.2 %collective-permute-start.12 = (f32[16,128]{1,0:T(8,128)S(1)}, f32[16,128]{1,0:T(8,128)S(1)}, u32[]{:S(2)}, u32[]{:S(2)}) collective-permute-start(f32[16,128]{1,0:T(8,128)S(1)} %half_sum.1.mine), channel_id=1, source_target_pairs={{0,1},{1,0},{2,3},{3,2},{4,5},{5,4},{6,7},{7,6},{8,9},{9,8},{10,11... | collective-permute-start | bytes 24584 | tf_op jit(solution)/shard_map/ppermute | solution.py:61

commit v7 on v6

--- a/solution.py
+++ b/solution.py
@@ -30,17 +30,33 @@
     return high, middle, (rest - middle.astype(F32)).astype(BF16)
 
 
+def dot(a, b, contract=0):
+    return lax.dot_general(a, b, (((1,), (contract,)), ((), ())), preferred_element_type=F32)
+
+
 def product(a_parts, b_parts, contract=0):
     n = a_parts[0].shape[0]
-
-    def dot(a, b):
-        return lax.dot_general(a, b, (((1,), (contract,)), ((), ())), preferred_element_type=F32)
-
     stacked = jnp.concatenate(a_parts, axis=0)
-    high = dot(stacked, b_parts[0])
-    middle = dot(stacked[: 2 * n], b_parts[1])
+    high = dot(stacked, b_parts[0], contract)
+    middle = dot(stacked[: 2 * n], b_parts[1], contract)
+    low = dot(a_parts[0], b_parts[2], contract)
+    return high[:n] + ((high[n : 2 * n] + middle[:n]) + ((high[2 * n :] + middle[n:]) + low))
+
+
+def shallow_product(a_parts, b_parts):
+    n = a_parts[0].shape[0]
+    stacked = jnp.concatenate(a_parts, axis=0)
+    most = dot(jnp.concatenate([stacked, stacked], axis=1), jnp.concatenate(b_parts[:2], axis=0))
     low = dot(a_parts[0], b_parts[2])
-    return high[:n] + ((high[n : 2 * n] + middle[:n]) + ((high[2 * n :] + middle[n:]) + low))
+    return most[:n] + (most[n : 2 * n] + (most[2 * n :] + low))
+
+
+def narrow_product(a_parts, b_pair, b_low):
+    n, width = a_parts[0].shape[0], b_low.shape[1]
+    most = dot(jnp.concatenate(a_parts, axis=0), b_pair)
+    high, middle = most[:, :width], most[:, width:]
+    low = dot(a_parts[0], b_low)
+    return high[:n] + ((high[n : 2 * n] + middle[:n]) + ((high[2 * n :] + middle[n : 2 * n]) + low))
 
 
 def joined(parts, axis):
@@ -70,11 +86,11 @@
 
 
 class Place:
-    def __init__(self, rows, blocks, columns):
+    def __init__(self, rows, block_rows, slots, columns):
         self.row = lax.axis_index("row")
         self.part = lax.axis_index("nbr")
         self.odd = self.part & 1
-        self.block_rows, self.slots = blocks.shape[:2]
+        self.block_rows, self.slots = block_rows, slots
         self.first_row = self.row * self.block_rows
         self.peers = [self.row ^ (k + self.odd) for k in range(2, rows, 2)]
         self.middle = self.row ^ 1
@@ -99,7 +115,7 @@
     values = []
     for i in range(place.block_rows):
         stored = [split(b[i, p]) for b in blocks for p in range(place.slots)]
-        values.append(product(split(tiles[place.tile(i)]), joined(stored, 1)))
+        values.append(shallow_product(split(tiles[place.tile(i)]), joined(stored, 1)))
     for copy in copies:
         copy.wait()
     for i, value in enumerate(values):
@@ -109,13 +125,13 @@
                 out[ids[m][i, p]] += value[:, at : at + size] * place.weight(ids[m], counts, m, i, p)
 
 
-def direct_products(place, blocks, ids, counts, whole, i):
-    stored, far = [], []
-    for m, b in enumerate(blocks):
+def direct_products(place, pair, low, ids, counts, whole, i):
+    far = []
+    for m in range(len(ids)):
         for p in range(place.slots):
-            stored.append(split(b[i, p].T))
             far.append(split(whole[ids[m][i, p]] * place.weight(ids[m], counts, m, i, p)))
-    return product(joined(far, 1), joined(stored, 0))
+    at = slice(i * len(far) * pair.shape[1] // 2, (i + 1) * len(far) * pair.shape[1] // 2)
+    return narrow_product(joined(far, 1), pair[at], low[at])
 
 
 def fill(place, messages, shared, products, tiles, own):
@@ -151,18 +167,31 @@
 def first_kernel(rows, held, other, ids, other_ids, counts, tiles, *refs):
     messages, refs = refs[: rows // 2 - 1], refs[rows // 2 - 1 :]
     shared, own, other_s, products, sem = refs
-    place = Place(rows, held, products.shape[1])
+    place = Place(rows, *held.shape[:2], products.shape[1])
     copy = pltpu.make_async_copy(other_ids, other_s, sem.at[0])
     copy.start()
     transposed_products(place, (held, other), (ids, other_s), counts, tiles, products, [copy])
     fill(place, messages, shared, products, tiles, own)
 
 
-def direct_kernel(rows, held, other, ids, other_ids, counts, own, tiles, *refs):
+def split_kernel(held, other, after, pair, low):
+    block_rows, slots, size, _ = held.shape
+    at = 0
+    for i in range(block_rows):
+        for b in (held, other):
+            for p in range(slots):
+                high, middle, rest = split(b[i, p].T)
+                pair[at : at + size, :size] = high
+                pair[at : at + size, size:] = middle
+                low[at : at + size] = rest
+                at += size
+
+
+def direct_kernel(rows, block_rows, slots, pair, low, ids, other_ids, counts, own, tiles, *refs):
     received, refs = refs[: rows // 2 - 1], refs[rows // 2 - 1 :]
     shared, *gram, out, whole = refs
-    n, columns, size = held.shape[0], whole.shape[1], whole.shape[2]
-    place = Place(rows, held, columns)
+    n, columns = block_rows, whole.shape[1]
+    place = Place(rows, block_rows, slots, columns)
     whole[...] = jnp.zeros_like(whole)
     for i in range(n):
         whole[place.first_row + i] = jnp.where(place.odd == 0, tiles[place.tile(i)], 0.0)
@@ -173,7 +202,9 @@
         value = own[place.tile(i)]
         for peer, message in zip(place.peers, received):
             value += jnp.where(place.row > peer, message[place.tile(i)], 0.0)
-        out[place.tile(i)] = value + direct_products(place, (held, other), (ids, other_ids), counts, whole, i)
+        out[place.tile(i)] = value + direct_products(
+            place, pair, low, (ids, other_ids), counts, whole, i
+        )
         mine = pl.ds(pl.multiple_of(i * columns + place.odd * place.height, 8), place.height)
         out[mine] += jnp.where(place.row > place.middle, shared[place.half_tile(i)], 0.0)
     if gram:
@@ -186,7 +217,7 @@
     messages, refs = refs[: rows // 2 - 1], refs[rows // 2 - 1 :]
     shared, own, tiles, gram, products = refs
     n, columns, size = held.shape[0], products.shape[1], products.shape[2]
-    place = Place(rows, held, columns)
+    place = Place(rows, *held.shape[:2], columns)
     tiles[...] = tree([image[...] for image in images])
     transposed_products(place, (held, other), (ids, other_ids), counts, tiles, products)
     fill(place, messages, shared, products, tiles, own)
@@ -242,12 +273,12 @@
 def pair_kernel(mine, others, image, gram):
     tall = image.shape[0]
     image[...] = mine[:tall] + others[:tall]
-    gram[...] = unfolded(mine[tall:] + others[tall:], gram.shape[0])
+    gram[...] = mine[tall:] + others[tall:]
 
 
 def factor_kernel(total, gram, tiles, inverse, prior):
-    columns = gram.shape[0]
-    lower = eliminated(gram[...] / total, identity(columns))
+    columns = inverse.shape[0]
+    lower = eliminated(unfolded(gram[...], columns) / total, identity(columns))
     inverse[...] = lower
     parts = [split(tiles[i : i + columns]) for i in range(0, tiles.shape[0], columns)]
     prior[...] = product(split(lower), joined(parts, 1))
@@ -332,9 +363,18 @@
     stored = (held, other, ids, other_ids, counts)
     index = [VMEM, VMEM, SMEM, SMEM, SMEM]
     received, shared = round_over_rows(messages, shared)
-    (image,) = call(
-        functools.partial(direct_kernel, rows), "first_direct", index + [VMEM] * (half + 2), [tile], [work]
-    )(*stored, own, tiles, *received, shared)
+    deep = 2 * block_rows * slots * size
+    pair, low = call(
+        split_kernel,
+        "split",
+        [VMEM] * 3,
+        [jax.ShapeDtypeStruct((deep, 2 * size), BF16), jax.ShapeDtypeStruct((deep, size), BF16)],
+    )(held, other, own)
+    parted = (pair, low, ids, other_ids, counts)
+    direct = functools.partial(direct_kernel, rows, block_rows, slots)
+    (image,) = call(direct, "first_direct", index + [VMEM] * (half + 2), [tile], [work])(
+        *parted, own, tiles, *received, shared
+    )
     images = sum_over_pairs(image + swap(image, "nbr", 1))
     *messages, shared, own, tiles, gram = call(
         functools.partial(second_kernel, rows, parts // 2),
@@ -344,14 +384,10 @@
         [work],
     )(*stored, *images)
     received, shared = round_over_rows(messages, shared)
-    (mine,) = call(
-        functools.partial(direct_kernel, rows),
-        "second_direct",
-        index + [VMEM] * (half + 3),
-        [flat(tall + extra)],
-        [work],
-    )(*stored, own, tiles, *received, shared, gram)
-    image, gram = call(pair_kernel, "pair", [VMEM] * 2, [tile, square])(mine, swap(mine, "nbr", 1))
+    (mine,) = call(direct, "second_direct", index + [VMEM] * (half + 3), [flat(tall + extra)], [work])(
+        *parted, own, tiles, *received, shared, gram
+    )
+    image, gram = call(pair_kernel, "pair", [VMEM] * 2, [tile, flat(extra)])(mine, swap(mine, "nbr", 1))
     images = sum_over_pairs(image)
     inverse, prior = call(functools.partial(factor_kernel, total), "factor", [VMEM] * 2, [square, across])(gram, tiles)
     image, both = call(gram_kernel, "gram", [VMEM] * (parts // 2 + 2), [across, flat(2 * extra)])(

time: 38.1 us -> 37.7 us (0.990)
  waiting for transfers between devices: 14.7 us -> 14.3 us
    ppermute x10, waiting for transfers between devices: 13.5 us -> 13.1 us  [swap(): lax.ppermute(x, axis, [(i, i ^ distance) for i in range(lax.axis_size(axi...]
    pallas_call x3 -> x4, Pallas kernels: 1.31 us -> 1.19 us  [the longest x1 0.4 us: body(): call(direct, 'first_direct', index + [VMEM] * (half + 2), [tile], [work])]
  transfers between devices with their start and end apart: 13 -> 13, of which waited for: 10 -> 10; matrix products, arithmetic and copies ran while one was open for 0% -> 0% of each run, Pallas kernels for 5% -> 6%
where the time goes in v7:
time: 37.7 us; the launch traced here: 37.5 us
  starting transfers between devices  16.4 us (44%)
  waiting for transfers between devices  14.3 us (38%)
  Pallas kernels  6.08 us (16%)
  between operations  0.7 us (2%)
    ppermute x10, waiting for transfers between devices, swap(): lax.ppermute(x, axis, [(i, i ^ distance) for i in range(lax.axis_size(axi...  13.1 us
    ppermute x10, starting transfers between devices, swap(): lax.ppermute(x, axis, [(i, i ^ distance) for i in range(lax.axis_size(axi...  9.49 us
    ppermute x3, starting transfers between devices, swap_rows(): return lax.ppermute(x, ('row', 'nbr'), pairs)  6.96 us
    pallas_call x1, Pallas kernels, body(): call(functools.partial(last_kernel, total), 'last', [VMEM] * 3, [across,...  1.24 us
    ppermute x3, waiting for transfers between devices, swap_rows(): return lax.ppermute(x, ('row', 'nbr'), pairs)  1.16 us
    pallas_call x1, Pallas kernels, body(): call(load_kernel, 'load', [HBM] * 4, [jax.ShapeDtypeStruct(blocks.shape,...  1.14 us
    pallas_call x1, Pallas kernels, body(): call(functools.partial(factor_kernel, total), 'factor', [VMEM] * 2, [squa...  0.8 us
  transfers between devices with their start and end apart: 13, of which 10 were waited for; matrix products, arithmetic and copies ran while one was open for 0% of the time, Pallas kernels for 6%

profile of v7, /device:TPU:0, one launch (start us, length us, event | category | flops | bytes accessed | tf_op | source)
XLA Modules:
  0.0 37.5 jit_solution(14646681420339848492)
XLA Ops:
  0.6 0.5 %collective-permute-start = (f32[3,3,128,128]{3,2,1,0:T(8,128)}, f32[3,3,128,128]{3,2,1,0:T(8,128)S(1)}, u32[]{:S(2)}, u32[]{:S(2)}) collective-permute-start(f32[3,3,128,128]{3,2,1,0:T(8,128)} %blocks.1), channel_id=1, source_target_pairs={{0,1},{1,0},{2,3},{3,2},{4,5},{5,4},{6,7},{7,6},{8,9},{9,8},{10,11... | collective-permute-start | bytes 1769480 | tf_op jit(solution)/shard_map/ppermute | solution.py:77
  1.1 0.1 collective-permute-start.1
  1.2 1.1 %load.1 = (f32[3,3,128,128]{3,2,1,0:T(8,128)S(1)}, s32[3,3]{1,0:T(4,128)S(4)}, s32[3]{0:T(128)S(4)}, f32[96,128]{1,0:T(8,128)S(1)}) custom-call(f32[3,3,128,128]{3,2,1,0:T(8,128)} %blocks.1, s32[3,3]{1,0:T(4,128)} %ids.1, s32[3]{0:T(128)} %counts.1, f32[32,384]{1,0:T(8,128)} %bitcast.2), custom_call_target="tpu_custom_call" | custom-call | tf_op jit(solution)/shard_map/load/pallas_call | solution.py:349
  2.4 0.6 %collective-permute-done.1.other_ids = s32[3,3]{1,0:T(4,128)S(1)} collective-permute-done((s32[3,3]{1,0:T(4,128)}, s32[3,3]{1,0:T(4,128)S(1)}, u32[]{:S(2)}, u32[]{:S(2)}) %collective-permute-start.1) | collective-permute-done | bytes 68 | tf_op jit(solution)/shard_map/ppermute | solution.py:77
  3.0 0.0 collective-permute-done.other
  3.0 0.7 %first_transposed.1 = (f32[96,128]{1,0:T(8,128)S(1)}, f32[48,128]{1,0:T(8,128)S(1)}, f32[96,128]{1,0:T(8,128)S(1)}, s32[3,3]{1,0:T(4,128)S(4)}) custom-call(f32[3,3,128,128]{3,2,1,0:T(8,128)S(1)} %get-tuple-element.25.held, f32[3,3,128,128]{3,2,1,0:T(8,128)S(1)} %collective-permute-done.other, s32[3,3]{1,0:T(4,128)S(4)} %get-tuple-element.26.ids, ...), custom_call_target="tpu_custom_call" | custom-call | tf_op jit(solution)/shard_map/first_transposed/pallas_call | solution.py:356
  3.7 4.0 %collective-permute-start.2 = (f32[96,128]{1,0:T(8,128)S(1)}, f32[96,128]{1,0:T(8,128)S(1)}, u32[]{:S(2)}, u32[]{:S(2)}) collective-permute-start(f32[96,128]{1,0:T(8,128)S(1)} %get-tuple-element.33), channel_id=1, source_target_pairs={{0,8},{1,13},{2,10},{3,15},{4,12},{5,9},{6,14},{7,11},{8,0},{9,5},... | collective-permute-start | bytes 147464 | tf_op jit(solution)/shard_map/ppermute | solution.py:85
  7.7 1.6 %collective-permute-start.3 = (f32[48,128]{1,0:T(8,128)S(1)}, f32[48,128]{1,0:T(8,128)S(1)}, u32[]{:S(2)}, u32[]{:S(2)}) collective-permute-start(f32[48,128]{1,0:T(8,128)S(1)} %get-tuple-element.34), channel_id=1, source_target_pairs={{0,4},{4,0},{8,12},{12,8},{1,5},{5,1},{9,13},{13,9},{2,6},{6,2},{1... | collective-permute-start | bytes 73736 | tf_op jit(solution)/shard_map/ppermute | solution.py:77
  9.3 0.4 split.1
  9.7 2.0 %collective-permute-done.3.refs_1_ = f32[48,128]{1,0:T(8,128)S(1)} collective-permute-done((f32[48,128]{1,0:T(8,128)S(1)}, f32[48,128]{1,0:T(8,128)S(1)}, u32[]{:S(2)}, u32[]{:S(2)}) %collective-permute-start.3) | collective-permute-done | bytes 24608 | tf_op jit(solution)/shard_map/ppermute | solution.py:77
  11.7 0.0 collective-permute-done.2.refs_0_
  11.7 0.4 %first_direct.1 = f32[96,128]{1,0:T(8,128)S(1)} custom-call(bf16[2304,256]{1,0:T(8,128)(2,1)S(1)} %get-tuple-element.30.pair, bf16[2304,128]{1,0:T(8,128)(2,1)S(1)} %get-tuple-element.31.low, s32[3,3]{1,0:T(4,128)S(4)} %get-tuple-element.26.ids, s32[3,3]{1,0:T(4,128)S(4)} %get-tuple-element.32.other_ids, s32[3]{0:T(128)S(4)} %get-tuple-element.27.counts, ...), custom_call_target="tpu_custom_call" | custom-call | tf_op jit(solution)/shard_map/first_direct/pallas_call | solution.py:375
  12.1 0.1 collective-permute-start.4
  12.2 1.2 %collective-permute-done.4 = f32[96,128]{1,0:T(8,128)S(1)} collective-permute-done((f32[96,128]{1,0:T(8,128)S(1)}, f32[96,128]{1,0:T(8,128)S(1)}, u32[]{:S(2)}, u32[]{:S(2)}) %collective-permute-start.4) | collective-permute-done | bytes 49184 | tf_op jit(solution)/shard_map/ppermute | solution.py:77
  13.4 1.6 %collective-permute-start.5 = (f32[96,128]{1,0:T(8,128)S(1)}, f32[96,128]{1,0:T(8,128)S(1)}, u32[]{:S(2)}, u32[]{:S(2)}) collective-permute-start(f32[96,128]{1,0:T(8,128)S(1)} %add.3.refs_0_), channel_id=1, source_target_pairs={{0,2},{1,3},{2,0},{3,1},{4,6},{5,7},{6,4},{7,5},{8,10},{9,11},{10,... | collective-permute-start | bytes 147464 | tf_op jit(solution)/shard_map/ppermute | solution.py:77
  15.0 2.6 %collective-permute-done.5.refs_1_ = f32[96,128]{1,0:T(8,128)S(1)} collective-permute-done((f32[96,128]{1,0:T(8,128)S(1)}, f32[96,128]{1,0:T(8,128)S(1)}, u32[]{:S(2)}, u32[]{:S(2)}) %collective-permute-start.5) | collective-permute-done | bytes 49184 | tf_op jit(solution)/shard_map/ppermute | solution.py:77
  17.6 0.6 %second_transposed.1 = (f32[104,128]{1,0:T(8,128)S(1)}, f32[56,128]{1,0:T(8,128)S(1)}, f32[96,128]{1,0:T(8,128)S(1)}, f32[96,128]{1,0:T(8,128)S(1)}, f32[8,128]{1,0:T(8,128)S(1)}) custom-call(f32[3,3,128,128]{3,2,1,0:T(8,128)S(1)} %get-tuple-element.25.held, f32[3,3,128,128]{3,2,1,0:T(8,128)S(1)} %collective-permute-done.other, ...), custom_call_target="tpu_custom_call" | custom-call | tf_op jit(solution)/shard_map/second_transposed/pallas_call | solution.py:379
  18.1 1.4 %collective-permute-start.6 = (f32[104,128]{1,0:T(8,128)S(1)}, f32[104,128]{1,0:T(8,128)S(1)}, u32[]{:S(2)}, u32[]{:S(2)}) collective-permute-start(f32[104,128]{1,0:T(8,128)S(1)} %get-tuple-element.37), channel_id=1, source_target_pairs={{0,8},{1,13},{2,10},{3,15},{4,12},{5,9},{6,14},{7,11},{8,0},{9,5},... | collective-permute-start | bytes 159752 | tf_op jit(solution)/shard_map/ppermute | solution.py:85
  19.5 2.1 %collective-permute-start.7 = (f32[56,128]{1,0:T(8,128)S(1)}, f32[56,128]{1,0:T(8,128)S(1)}, u32[]{:S(2)}, u32[]{:S(2)}) collective-permute-start(f32[56,128]{1,0:T(8,128)S(1)} %get-tuple-element.38), channel_id=1, source_target_pairs={{0,4},{4,0},{8,12},{12,8},{1,5},{5,1},{9,13},{13,9},{2,6},{6,2},{1... | collective-permute-start | bytes 86024 | tf_op jit(solution)/shard_map/ppermute | solution.py:77
  21.7 1.9 %collective-permute-done.7.refs_1_ = f32[56,128]{1,0:T(8,128)S(1)} collective-permute-done((f32[56,128]{1,0:T(8,128)S(1)}, f32[56,128]{1,0:T(8,128)S(1)}, u32[]{:S(2)}, u32[]{:S(2)}) %collective-permute-start.7) | collective-permute-done | bytes 28704 | tf_op jit(solution)/shard_map/ppermute | solution.py:77
  23.5 0.0 collective-permute-done.6.refs_0_
  23.6 0.4 %second_direct.1.mine = f32[104,128]{1,0:T(8,128)S(1)} custom-call(bf16[2304,256]{1,0:T(8,128)(2,1)S(1)} %get-tuple-element.30.pair, bf16[2304,128]{1,0:T(8,128)(2,1)S(1)} %get-tuple-element.31.low, s32[3,3]{1,0:T(4,128)S(4)} %get-tuple-element.26.ids, s32[3,3]{1,0:T(4,128)S(4)} %get-tuple-element.32.other_ids, s32[3]{0:T(128)S(4)} %get-tuple-element.27.counts, ...), custom_call_target="tpu_custom_call" | custom-call | tf_op jit(solution)/shard_map/second_direct/pallas_call | solution.py:387
  24.0 0.1 collective-permute-start.8
  24.0 1.2 %collective-permute-done.8.others = f32[104,128]{1,0:T(8,128)S(1)} collective-permute-done((f32[104,128]{1,0:T(8,128)S(1)}, f32[104,128]{1,0:T(8,128)S(1)}, u32[]{:S(2)}, u32[]{:S(2)}) %collective-permute-start.8) | collective-permute-done | bytes 53280 | tf_op jit(solution)/shard_map/ppermute | solution.py:77
  25.3 1.6 %collective-permute-start.9 = (f32[96,128]{1,0:T(8,128)S(1)}, f32[96,128]{1,0:T(8,128)S(1)}, u32[]{:S(2)}, u32[]{:S(2)}) collective-permute-start(f32[96,128]{1,0:T(8,128)S(1)} %get-tuple-element.43.refs_0_), channel_id=1, source_target_pairs={{0,2},{1,3},{2,0},{3,1},{4,6},{5,7},{6,4},{7,5},{8,10},{9,11},{10,... | collective-permute-start | bytes 147464 | tf_op jit(solution)/shard_map/ppermute | solution.py:77
  26.9 0.8 %factor.1 = (f32[32,32]{1,0:T(8,128)S(1)}, f32[32,384]{1,0:T(8,128)S(1)}) custom-call(f32[8,128]{1,0:T(8,128)S(1)} %get-tuple-element.40.gram, f32[96,128]{1,0:T(8,128)S(1)} %get-tuple-element.36.tiles), custom_call_target="tpu_custom_call" | custom-call | tf_op jit(solution)/shard_map/factor/pallas_call | solution.py:392
  27.7 1.8 %collective-permute-done.9.refs_1_ = f32[96,128]{1,0:T(8,128)S(1)} collective-permute-done((f32[96,128]{1,0:T(8,128)S(1)}, f32[96,128]{1,0:T(8,128)S(1)}, u32[]{:S(2)}, u32[]{:S(2)}) %collective-permute-start.9) | collective-permute-done | bytes 49184 | tf_op jit(solution)/shard_map/ppermute | solution.py:77
  29.4 0.5 %gram.1 = (f32[32,384]{1,0:T(8,128)S(1)}, f32[16,128]{1,0:T(8,128)S(1)}) custom-call(f32[32,32]{1,0:T(8,128)S(1)} %get-tuple-element.41.inverse, f32[32,384]{1,0:T(8,128)S(1)} %get-tuple-element.42.prior, f32[96,128]{1,0:T(8,128)S(1)} %get-tuple-element.43.refs_0_, f32[96,128]{1,0:T(8,128)S(1)} %collective-permute-done.9.refs_1_), custom_call_target="tpu_custom_call" | custom-call | tf_op jit(solution)/shard_map/gram/pallas_call | solution.py:393
  29.9 1.5 %collective-permute-start.11 = (f32[16,128]{1,0:T(8,128)S(1)}, f32[16,128]{1,0:T(8,128)S(1)}, u32[]{:S(2)}, u32[]{:S(2)}) collective-permute-start(f32[16,128]{1,0:T(8,128)S(1)} %get-tuple-element.45.mine), channel_id=1, source_target_pairs={{0,8},{1,13},{2,10},{3,15},{4,12},{5,9},{6,14},{7,11},{8,0},{9,5},... | collective-permute-start | bytes 24584 | tf_op jit(solution)/shard_map/ppermute | solution.py:85
  31.4 1.9 %collective-permute-start.10 = (f32[16,128]{1,0:T(8,128)S(1)}, f32[16,128]{1,0:T(8,128)S(1)}, u32[]{:S(2)}, u32[]{:S(2)}) collective-permute-start(f32[16,128]{1,0:T(8,128)S(1)} %get-tuple-element.45.mine), channel_id=1, source_target_pairs={{0,4},{4,0},{8,12},{12,8},{1,5},{5,1},{9,13},{13,9},{2,6},{6,2},{1... | collective-permute-start | bytes 24584 | tf_op jit(solution)/shard_map/ppermute | solution.py:77
  33.3 1.2 %collective-permute-done.11.refs_0_ = f32[16,128]{1,0:T(8,128)S(1)} collective-permute-done((f32[16,128]{1,0:T(8,128)S(1)}, f32[16,128]{1,0:T(8,128)S(1)}, u32[]{:S(2)}, u32[]{:S(2)}) %collective-permute-start.11) | collective-permute-done | bytes 8224 | tf_op jit(solution)/shard_map/ppermute | solution.py:85
  34.5 0.6 %collective-permute-done.10.shared = f32[16,128]{1,0:T(8,128)S(1)} collective-permute-done((f32[16,128]{1,0:T(8,128)S(1)}, f32[16,128]{1,0:T(8,128)S(1)}, u32[]{:S(2)}, u32[]{:S(2)}) %collective-permute-start.10) | collective-permute-done | bytes 8224 | tf_op jit(solution)/shard_map/ppermute | solution.py:77
  35.1 0.0 collective-permute-start.12
  35.1 1.2 %collective-permute-done.12.others = f32[16,128]{1,0:T(8,128)S(1)} collective-permute-done((f32[16,128]{1,0:T(8,128)S(1)}, f32[16,128]{1,0:T(8,128)S(1)}, u32[]{:S(2)}, u32[]{:S(2)}) %collective-permute-start.12) | collective-permute-done | bytes 8224 | tf_op jit(solution)/shard_map/ppermute | solution.py:77
  36.3 1.2 %last.1 = (f32[32,384]{1,0:T(8,128)}, f32[32,32]{1,0:T(8,128)}) custom-call(f32[32,384]{1,0:T(8,128)S(1)} %get-tuple-element.44.image, f32[16,128]{1,0:T(8,128)S(1)} %half_sum.1.mine, f32[16,128]{1,0:T(8,128)S(1)} %collective-permute-done.12.others), custom_call_target="tpu_custom_call" | custom-call | tf_op jit(solution)/shard_map/last/pallas_call | solution.py:398
  (3 shorter events, 0.0 us)
Async XLA Ops:
  0.6 2.4 %collective-permute-start = (f32[3,3,128,128]{3,2,1,0:T(8,128)}, f32[3,3,128,128]{3,2,1,0:T(8,128)S(1)}, u32[]{:S(2)}, u32[]{:S(2)}) collective-permute-start(f32[3,3,128,128]{3,2,1,0:T(8,128)} %blocks.1), channel_id=1, source_target_pairs={{0,1},{1,0},{2,3},{3,2},{4,5},{5,4},{6,7},{7,6},{8,9},{9,8},{10,11... | collective-permute-start | bytes 1769480 | tf_op jit(solution)/shard_map/ppermute | solution.py:77
  1.1 1.8 %collective-permute-start.1 = (s32[3,3]{1,0:T(4,128)}, s32[3,3]{1,0:T(4,128)S(1)}, u32[]{:S(2)}, u32[]{:S(2)}) collective-permute-start(s32[3,3]{1,0:T(4,128)} %ids.1), channel_id=1, source_target_pairs={{0,1},{1,0},{2,3},{3,2},{4,5},{5,4},{6,7},{7,6},{8,9},{9,8},{10,11... | collective-permute-start | bytes 116 | tf_op jit(solution)/shard_map/ppermute | solution.py:77
  3.7 8.0 %collective-permute-start.2 = (f32[96,128]{1,0:T(8,128)S(1)}, f32[96,128]{1,0:T(8,128)S(1)}, u32[]{:S(2)}, u32[]{:S(2)}) collective-permute-start(f32[96,128]{1,0:T(8,128)S(1)} %get-tuple-element.33), channel_id=1, source_target_pairs={{0,8},{1,13},{2,10},{3,15},{4,12},{5,9},{6,14},{7,11},{8,0},{9,5},... | collective-permute-start | bytes 147464 | tf_op jit(solution)/shard_map/ppermute | solution.py:85
  7.7 4.0 %collective-permute-start.3 = (f32[48,128]{1,0:T(8,128)S(1)}, f32[48,128]{1,0:T(8,128)S(1)}, u32[]{:S(2)}, u32[]{:S(2)}) collective-permute-start(f32[48,128]{1,0:T(8,128)S(1)} %get-tuple-element.34), channel_id=1, source_target_pairs={{0,4},{4,0},{8,12},{12,8},{1,5},{5,1},{9,13},{13,9},{2,6},{6,2},{1... | collective-permute-start | bytes 73736 | tf_op jit(solution)/shard_map/ppermute | solution.py:77
  12.1 1.3 %collective-permute-start.4 = (f32[96,128]{1,0:T(8,128)S(1)}, f32[96,128]{1,0:T(8,128)S(1)}, u32[]{:S(2)}, u32[]{:S(2)}) collective-permute-start(f32[96,128]{1,0:T(8,128)S(1)} %first_direct.1), channel_id=1, source_target_pairs={{0,1},{1,0},{2,3},{3,2},{4,5},{5,4},{6,7},{7,6},{8,9},{9,8},{10,11... | collective-permute-start | bytes 147464 | tf_op jit(solution)/shard_map/ppermute | solution.py:77
  13.4 4.2 %collective-permute-start.5 = (f32[96,128]{1,0:T(8,128)S(1)}, f32[96,128]{1,0:T(8,128)S(1)}, u32[]{:S(2)}, u32[]{:S(2)}) collective-permute-start(f32[96,128]{1,0:T(8,128)S(1)} %add.3.refs_0_), channel_id=1, source_target_pairs={{0,2},{1,3},{2,0},{3,1},{4,6},{5,7},{6,4},{7,5},{8,10},{9,11},{10,... | collective-permute-start | bytes 147464 | tf_op jit(solution)/shard_map/ppermute | solution.py:77
  18.1 5.4 %collective-permute-start.6 = (f32[104,128]{1,0:T(8,128)S(1)}, f32[104,128]{1,0:T(8,128)S(1)}, u32[]{:S(2)}, u32[]{:S(2)}) collective-permute-start(f32[104,128]{1,0:T(8,128)S(1)} %get-tuple-element.37), channel_id=1, source_target_pairs={{0,8},{1,13},{2,10},{3,15},{4,12},{5,9},{6,14},{7,11},{8,0},{9,5},... | collective-permute-start | bytes 159752 | tf_op jit(solution)/shard_map/ppermute | solution.py:85
  19.5 4.0 %collective-permute-start.7 = (f32[56,128]{1,0:T(8,128)S(1)}, f32[56,128]{1,0:T(8,128)S(1)}, u32[]{:S(2)}, u32[]{:S(2)}) collective-permute-start(f32[56,128]{1,0:T(8,128)S(1)} %get-tuple-element.38), channel_id=1, source_target_pairs={{0,4},{4,0},{8,12},{12,8},{1,5},{5,1},{9,13},{13,9},{2,6},{6,2},{1... | collective-permute-start | bytes 86024 | tf_op jit(solution)/shard_map/ppermute | solution.py:77
  24.0 1.3 %collective-permute-start.8 = (f32[104,128]{1,0:T(8,128)S(1)}, f32[104,128]{1,0:T(8,128)S(1)}, u32[]{:S(2)}, u32[]{:S(2)}) collective-permute-start(f32[104,128]{1,0:T(8,128)S(1)} %second_direct.1.mine), channel_id=1, source_target_pairs={{0,1},{1,0},{2,3},{3,2},{4,5},{5,4},{6,7},{7,6},{8,9},{9,8},{10,11... | collective-permute-start | bytes 159752 | tf_op jit(solution)/shard_map/ppermute | solution.py:77
  25.3 4.2 %collective-permute-start.9 = (f32[96,128]{1,0:T(8,128)S(1)}, f32[96,128]{1,0:T(8,128)S(1)}, u32[]{:S(2)}, u32[]{:S(2)}) collective-permute-start(f32[96,128]{1,0:T(8,128)S(1)} %get-tuple-element.43.refs_0_), channel_id=1, source_target_pairs={{0,2},{1,3},{2,0},{3,1},{4,6},{5,7},{6,4},{7,5},{8,10},{9,11},{10,... | collective-permute-start | bytes 147464 | tf_op jit(solution)/shard_map/ppermute | solution.py:77
  29.9 4.6 %collective-permute-start.11 = (f32[16,128]{1,0:T(8,128)S(1)}, f32[16,128]{1,0:T(8,128)S(1)}, u32[]{:S(2)}, u32[]{:S(2)}) collective-permute-start(f32[16,128]{1,0:T(8,128)S(1)} %get-tuple-element.45.mine), channel_id=1, source_target_pairs={{0,8},{1,13},{2,10},{3,15},{4,12},{5,9},{6,14},{7,11},{8,0},{9,5},... | collective-permute-start | bytes 24584 | tf_op jit(solution)/shard_map/ppermute | solution.py:85
  31.4 3.7 %collective-permute-start.10 = (f32[16,128]{1,0:T(8,128)S(1)}, f32[16,128]{1,0:T(8,128)S(1)}, u32[]{:S(2)}, u32[]{:S(2)}) collective-permute-start(f32[16,128]{1,0:T(8,128)S(1)} %get-tuple-element.45.mine), channel_id=1, source_target_pairs={{0,4},{4,0},{8,12},{12,8},{1,5},{5,1},{9,13},{13,9},{2,6},{6,2},{1... | collective-permute-start | bytes 24584 | tf_op jit(solution)/shard_map/ppermute | solution.py:77
  35.1 1.2 %collective-permute-start.12 = (f32[16,128]{1,0:T(8,128)S(1)}, f32[16,128]{1,0:T(8,128)S(1)}, u32[]{:S(2)}, u32[]{:S(2)}) collective-permute-start(f32[16,128]{1,0:T(8,128)S(1)} %half_sum.1.mine), channel_id=1, source_target_pairs={{0,1},{1,0},{2,3},{3,2},{4,5},{5,4},{6,7},{7,6},{8,9},{9,8},{10,11... | collective-permute-start | bytes 24584 | tf_op jit(solution)/shard_map/ppermute | solution.py:77

commit v8 on v7

--- a/solution.py
+++ b/solution.py
@@ -43,11 +43,11 @@
     return high[:n] + ((high[n : 2 * n] + middle[:n]) + ((high[2 * n :] + middle[n:]) + low))
 
 
-def shallow_product(a_parts, b_parts):
+def shallow_product(a_parts, b_pair, b_low):
     n = a_parts[0].shape[0]
     stacked = jnp.concatenate(a_parts, axis=0)
-    most = dot(jnp.concatenate([stacked, stacked], axis=1), jnp.concatenate(b_parts[:2], axis=0))
-    low = dot(a_parts[0], b_parts[2])
+    most = dot(jnp.concatenate([stacked, stacked], axis=1), b_pair)
+    low = dot(a_parts[0], b_low)
     return most[:n] + (most[n : 2 * n] + (most[2 * n :] + low))
 
 
@@ -109,20 +109,18 @@
         return slice(i * self.height, (i + 1) * self.height)
 
 
-def transposed_products(place, blocks, ids, counts, tiles, out, copies=()):
-    out[...] = jnp.zeros_like(out)
+def stacked_blocks(blocks, i):
+    slots = range(blocks[0].shape[1])
+    high, middle, low = joined([split(b[i, p]) for b in blocks for p in slots], 1)
+    return jnp.concatenate([high, middle], axis=0), low
+
+
+def scatter(place, value, ids, counts, i, out):
     size = out.shape[2]
-    values = []
-    for i in range(place.block_rows):
-        stored = [split(b[i, p]) for b in blocks for p in range(place.slots)]
-        values.append(shallow_product(split(tiles[place.tile(i)]), joined(stored, 1)))
-    for copy in copies:
-        copy.wait()
-    for i, value in enumerate(values):
-        for m in range(len(blocks)):
-            for p in range(place.slots):
-                at = (m * place.slots + p) * size
-                out[ids[m][i, p]] += value[:, at : at + size] * place.weight(ids[m], counts, m, i, p)
+    for m, table in enumerate(ids):
+        for p in range(place.slots):
+            at = (m * place.slots + p) * size
+            out[table[i, p]] += value[:, at : at + size] * place.weight(table, counts, m, i, p)
 
 
 def direct_products(place, pair, low, ids, counts, whole, i):
@@ -164,27 +162,51 @@
         copy.wait()
 
 
-def first_kernel(rows, held, other, ids, other_ids, counts, tiles, *refs):
+def own_kernel(rows, held, ids, counts, tiles, products):
+    place = Place(rows, *held.shape[:2], products.shape[1])
+    products[...] = jnp.zeros_like(products)
+    for i in range(place.block_rows):
+        value = shallow_product(split(tiles[place.tile(i)]), *stacked_blocks((held,), i))
+        scatter(place, value, (ids,), counts, i, products)
+
+
+def first_kernel(rows, other, other_ids, counts, tiles, started, *refs):
     messages, refs = refs[: rows // 2 - 1], refs[rows // 2 - 1 :]
-    shared, own, other_s, products, sem = refs
-    place = Place(rows, *held.shape[:2], products.shape[1])
+    shared, own, products = refs
+    size = products.shape[2]
+    place = Place(rows, *other.shape[:2], products.shape[1])
+    terms = []
+    for i in range(place.block_rows):
+        value = shallow_product(split(tiles[place.tile(i)]), *stacked_blocks((other,), i))
+        for p in range(place.slots):
+            used = (place.part ^ 1) * place.slots + p < counts[i]
+            j = jnp.broadcast_to(other_ids[i : i + 1, p : p + 1], (8, size))
+            c = jnp.where(j == place.first_row + i, 0.5, 1.0)
+            terms.append((jnp.where(used, j, -1), c, value[:, p * size : (p + 1) * size]))
+    copies = place.columns // 8
+    for block in range(products.shape[0]):
+        total = started[block]
+        for j, c, value in terms:
+            total += jnp.concatenate([jnp.where(j == block, c, 0.0)] * copies, axis=0) * value
+        products[block] = total
+    fill(place, messages, shared, products, tiles, own)
+
+
+def split_kernel(held, other, other_ids, after, direct_pair, direct_low, pair, low, other_s, sem):
+    block_rows, slots, size, _ = held.shape
     copy = pltpu.make_async_copy(other_ids, other_s, sem.at[0])
     copy.start()
-    transposed_products(place, (held, other), (ids, other_s), counts, tiles, products, [copy])
-    fill(place, messages, shared, products, tiles, own)
-
-
-def split_kernel(held, other, after, pair, low):
-    block_rows, slots, size, _ = held.shape
     at = 0
     for i in range(block_rows):
         for b in (held, other):
             for p in range(slots):
                 high, middle, rest = split(b[i, p].T)
-                pair[at : at + size, :size] = high
-                pair[at : at + size, size:] = middle
-                low[at : at + size] = rest
+                direct_pair[at : at + size, :size] = high
+                direct_pair[at : at + size, size:] = middle
+                direct_low[at : at + size] = rest
                 at += size
+        pair[2 * i * size : 2 * (i + 1) * size], low[i * size : (i + 1) * size] = stacked_blocks((held, other), i)
+    copy.wait()
 
 
 def direct_kernel(rows, block_rows, slots, pair, low, ids, other_ids, counts, own, tiles, *refs):
@@ -212,14 +234,21 @@
         out[n * columns :] = tree([first] + [message[n * columns :] for message in received])
 
 
-def second_kernel(rows, parts, held, other, ids, other_ids, counts, *refs):
+def second_kernel(rows, parts, block_rows, slots, pair, low, ids, other_ids, counts, *refs):
     images, refs = refs[:parts], refs[parts:]
     messages, refs = refs[: rows // 2 - 1], refs[rows // 2 - 1 :]
     shared, own, tiles, gram, products = refs
-    n, columns, size = held.shape[0], products.shape[1], products.shape[2]
-    place = Place(rows, *held.shape[:2], columns)
+    n, columns, size = block_rows, products.shape[1], products.shape[2]
+    place = Place(rows, block_rows, slots, columns)
     tiles[...] = tree([image[...] for image in images])
-    transposed_products(place, (held, other), (ids, other_ids), counts, tiles, products)
+    products[...] = jnp.zeros_like(products)
+    for i in range(n):
+        value = shallow_product(
+            split(tiles[place.tile(i)]),
+            pair[2 * i * size : 2 * (i + 1) * size],
+            low[i * size : (i + 1) * size],
+        )
+        scatter(place, value, (ids, other_ids), counts, i, products)
     fill(place, messages, shared, products, tiles, own)
     whole = joined([split(tiles[place.tile(i)]) for i in range(n)], 1)
     packed = folded(product(whole, whole, 1), size)
@@ -353,36 +382,49 @@
         [jax.ShapeDtypeStruct(blocks.shape, F32), table, pltpu.SMEM(counts.shape, jnp.int32), tile],
         [DMA((3 + block_rows,))],
     )(*[pltpu.with_memory_space_constraint(x, pltpu.HBM) for x in (blocks, partner_ids, counts, start.T)])
-    *messages, shared, own, other_ids = call(
+    (started,) = call(
+        functools.partial(own_kernel, rows),
+        "own_transposed",
+        [VMEM, SMEM, SMEM, VMEM],
+        [jax.ShapeDtypeStruct(work.shape, F32)],
+    )(held, ids, counts, tiles)
+    *messages, shared, own = call(
         functools.partial(first_kernel, rows),
         "first_transposed",
-        [VMEM, VMEM, SMEM, VMEM, SMEM, VMEM],
-        [tile] * (half - 1) + [flat(tall // 2), tile, table],
-        [work, DMA((1,))],
-    )(held, other, ids, other_ids, counts, tiles)
-    stored = (held, other, ids, other_ids, counts)
+        [VMEM, VMEM, SMEM, VMEM, VMEM],
+        [tile] * (half - 1) + [flat(tall // 2), tile],
+        [work],
+    )(other, other_ids, counts, tiles, started)
     index = [VMEM, VMEM, SMEM, SMEM, SMEM]
     received, shared = round_over_rows(messages, shared)
     deep = 2 * block_rows * slots * size
-    pair, low = call(
+    wide_row = 2 * slots * size
+    direct_pair, direct_low, pair, low, other_ids = call(
         split_kernel,
         "split",
-        [VMEM] * 3,
-        [jax.ShapeDtypeStruct((deep, 2 * size), BF16), jax.ShapeDtypeStruct((deep, size), BF16)],
-    )(held, other, own)
-    parted = (pair, low, ids, other_ids, counts)
+        [VMEM] * 4,
+        [
+            jax.ShapeDtypeStruct((deep, 2 * size), BF16),
+            jax.ShapeDtypeStruct((deep, size), BF16),
+            jax.ShapeDtypeStruct((2 * block_rows * size, wide_row), BF16),
+            jax.ShapeDtypeStruct((block_rows * size, wide_row), BF16),
+            table,
+        ],
+        [DMA((1,))],
+    )(held, other, other_ids, own)
+    parted = (direct_pair, direct_low, ids, other_ids, counts)
     direct = functools.partial(direct_kernel, rows, block_rows, slots)
     (image,) = call(direct, "first_direct", index + [VMEM] * (half + 2), [tile], [work])(
         *parted, own, tiles, *received, shared
     )
     images = sum_over_pairs(image + swap(image, "nbr", 1))
     *messages, shared, own, tiles, gram = call(
-        functools.partial(second_kernel, rows, parts // 2),
+        functools.partial(second_kernel, rows, parts // 2, block_rows, slots),
         "second_transposed",
         index + [VMEM] * (parts // 2),
         [flat(tall + extra)] * (half - 1) + [flat(tall // 2 + extra), tile, tile, flat(extra)],
         [work],
-    )(*stored, *images)
+    )(pair, low, ids, other_ids, counts, *images)
     received, shared = round_over_rows(messages, shared)
     (mine,) = call(direct, "second_direct", index + [VMEM] * (half + 3), [flat(tall + extra)], [work])(
         *parted, own, tiles, *received, shared, gram

time: 37.7 us -> 37.4 us (level)
  waiting for transfers between devices: 14.3 us -> 13.6 us
  Pallas kernels: 6.08 us -> 6.48 us
    pallas_call x2 -> x3, Pallas kernels: 0.93 us -> 1.61 us  [the longest x1 0.79 us: body(): call(split_kernel, 'split', [VMEM] * 4, [jax.ShapeDtypeStruct((deep, 2 *...]
    ppermute x10, waiting for transfers between devices: 13.1 us -> 12.5 us  [swap(): lax.ppermute(x, axis, [(i, i ^ distance) for i in range(lax.axis_size(axi...]
  transfers between devices with their start and end apart: 13 -> 13, of which waited for: 10 -> 10; matrix products, arithmetic and copies ran while one was open for 0% -> 0% of each run, Pallas kernels for 6% -> 8%
where the time goes in v8:
time: 37.4 us; the launch traced here: 37.2 us
  starting transfers between devices  16.4 us (44%)
  waiting for transfers between devices  13.6 us (36%)
  Pallas kernels  6.48 us (17%)
  between operations  0.71 us (2%)
    ppermute x10, waiting for transfers between devices, swap(): lax.ppermute(x, axis, [(i, i ^ distance) for i in range(lax.axis_size(axi...  12.5 us
    ppermute x10, starting transfers between devices, swap(): lax.ppermute(x, axis, [(i, i ^ distance) for i in range(lax.axis_size(axi...  9.35 us
    ppermute x3, starting transfers between devices, swap_rows(): return lax.ppermute(x, ('row', 'nbr'), pairs)  7.01 us
    pallas_call x1, Pallas kernels, body(): call(functools.partial(last_kernel, total), 'last', [VMEM] * 3, [across,...  1.24 us
    ppermute x3, waiting for transfers between devices, swap_rows(): return lax.ppermute(x, ('row', 'nbr'), pairs)  1.19 us
    pallas_call x1, Pallas kernels, body(): call(load_kernel, 'load', [HBM] * 4, [jax.ShapeDtypeStruct(blocks.shape,...  1.14 us
    pallas_call x1, Pallas kernels, body(): call(functools.partial(factor_kernel, total), 'factor', [VMEM] * 2, [squa...  0.8 us
    pallas_call x1, Pallas kernels, body(): call(split_kernel, 'split', [VMEM] * 4, [jax.ShapeDtypeStruct((deep, 2 *...  0.79 us
  transfers between devices with their start and end apart: 13, of which 10 were waited for; matrix products, arithmetic and copies ran while one was open for 0% of the time, Pallas kernels for 8%

profile of v8, /device:TPU:0, one launch (start us, length us, event | category | flops | bytes accessed | tf_op | source)
XLA Modules:
  0.0 37.2 jit_solution(17616016658112688562)
XLA Ops:
  0.6 0.5 %collective-permute-start = (f32[3,3,128,128]{3,2,1,0:T(8,128)}, f32[3,3,128,128]{3,2,1,0:T(8,128)S(1)}, u32[]{:S(2)}, u32[]{:S(2)}) collective-permute-start(f32[3,3,128,128]{3,2,1,0:T(8,128)} %blocks.1), channel_id=1, source_target_pairs={{0,1},{1,0},{2,3},{3,2},{4,5},{5,4},{6,7},{7,6},{8,9},{9,8},{10,11... | collective-permute-start | bytes 1769480 | tf_op jit(solution)/shard_map/ppermute | solution.py:77
  1.1 0.1 collective-permute-start.1
  1.2 1.1 %load.1 = (f32[3,3,128,128]{3,2,1,0:T(8,128)S(1)}, s32[3,3]{1,0:T(4,128)S(4)}, s32[3]{0:T(128)S(4)}, f32[96,128]{1,0:T(8,128)S(1)}) custom-call(f32[3,3,128,128]{3,2,1,0:T(8,128)} %blocks.1, s32[3,3]{1,0:T(4,128)} %ids.1, s32[3]{0:T(128)} %counts.1, f32[32,384]{1,0:T(8,128)} %bitcast.2), custom_call_target="tpu_custom_call" | custom-call | tf_op jit(solution)/shard_map/load/pallas_call | solution.py:378
  2.4 0.3 own_transposed.1.started
  2.7 0.3 collective-permute-done.1.other_ids
  3.0 0.0 collective-permute-done.other
  3.0 0.4 %first_transposed.1 = (f32[96,128]{1,0:T(8,128)S(1)}, f32[48,128]{1,0:T(8,128)S(1)}, f32[96,128]{1,0:T(8,128)S(1)}) custom-call(f32[3,3,128,128]{3,2,1,0:T(8,128)S(1)} %collective-permute-done.other, s32[3,3]{1,0:T(4,128)S(1)} %collective-permute-done.1.other_ids, s32[3]{0:T(128)S(4)} %get-tuple-element.28.counts, f32[96,128]{1,0:T(8,128)S(1)} %get-tuple-element.29.tiles, ...), custom_call_target="tpu_custom_call" | custom-call | tf_op jit(solution)/shard_map/first_transposed/pallas_call | solution.py:391
  3.4 4.0 %collective-permute-start.2 = (f32[96,128]{1,0:T(8,128)S(1)}, f32[96,128]{1,0:T(8,128)S(1)}, u32[]{:S(2)}, u32[]{:S(2)}) collective-permute-start(f32[96,128]{1,0:T(8,128)S(1)} %get-tuple-element.37), channel_id=1, source_target_pairs={{0,8},{1,13},{2,10},{3,15},{4,12},{5,9},{6,14},{7,11},{8,0},{9,5},... | collective-permute-start | bytes 147464 | tf_op jit(solution)/shard_map/ppermute | solution.py:85
  7.4 1.6 %collective-permute-start.3 = (f32[48,128]{1,0:T(8,128)S(1)}, f32[48,128]{1,0:T(8,128)S(1)}, u32[]{:S(2)}, u32[]{:S(2)}) collective-permute-start(f32[48,128]{1,0:T(8,128)S(1)} %get-tuple-element.38), channel_id=1, source_target_pairs={{0,4},{4,0},{8,12},{12,8},{1,5},{5,1},{9,13},{13,9},{2,6},{6,2},{1... | collective-permute-start | bytes 73736 | tf_op jit(solution)/shard_map/ppermute | solution.py:77
  9.0 0.8 %split.1 = (bf16[2304,256]{1,0:T(8,128)(2,1)S(1)}, bf16[2304,128]{1,0:T(8,128)(2,1)S(1)}, bf16[768,768]{1,0:T(8,128)(2,1)S(1)}, bf16[384,768]{1,0:T(8,128)(2,1)S(1)}, s32[3,3]{1,0:T(4,128)S(4)}) custom-call(f32[3,3,128,128]{3,2,1,0:T(8,128)S(1)} %get-tuple-element.27.held, f32[3,3,128,128]{3,2,1,0:T(8,128)S(1)} %collective-permute-done.other, ...), custom_call_target="tpu_custom_call" | custom-call | tf_op jit(solution)/shard_map/split/pallas_call | solution.py:402
  9.8 1.6 %collective-permute-done.3.refs_1_ = f32[48,128]{1,0:T(8,128)S(1)} collective-permute-done((f32[48,128]{1,0:T(8,128)S(1)}, f32[48,128]{1,0:T(8,128)S(1)}, u32[]{:S(2)}, u32[]{:S(2)}) %collective-permute-start.3) | collective-permute-done | bytes 24608 | tf_op jit(solution)/shard_map/ppermute | solution.py:77
  11.4 0.0 collective-permute-done.2.refs_0_
  11.4 0.4 %first_direct.1 = f32[96,128]{1,0:T(8,128)S(1)} custom-call(bf16[2304,256]{1,0:T(8,128)(2,1)S(1)} %get-tuple-element.32.pair, bf16[2304,128]{1,0:T(8,128)(2,1)S(1)} %get-tuple-element.33.low, s32[3,3]{1,0:T(4,128)S(4)} %get-tuple-element.30.ids, s32[3,3]{1,0:T(4,128)S(4)} %get-tuple-element.34.other_ids, s32[3]{0:T(128)S(4)} %get-tuple-element.28.counts, ...), custom_call_target="tpu_custom_call" | custom-call | tf_op jit(solution)/shard_map/first_direct/pallas_call | solution.py:417
  11.8 0.1 collective-permute-start.4
  11.9 1.2 %collective-permute-done.4 = f32[96,128]{1,0:T(8,128)S(1)} collective-permute-done((f32[96,128]{1,0:T(8,128)S(1)}, f32[96,128]{1,0:T(8,128)S(1)}, u32[]{:S(2)}, u32[]{:S(2)}) %collective-permute-start.4) | collective-permute-done | bytes 49184 | tf_op jit(solution)/shard_map/ppermute | solution.py:77
  13.1 1.6 %collective-permute-start.5 = (f32[96,128]{1,0:T(8,128)S(1)}, f32[96,128]{1,0:T(8,128)S(1)}, u32[]{:S(2)}, u32[]{:S(2)}) collective-permute-start(f32[96,128]{1,0:T(8,128)S(1)} %add.3.refs_0_), channel_id=1, source_target_pairs={{0,2},{1,3},{2,0},{3,1},{4,6},{5,7},{6,4},{7,5},{8,10},{9,11},{10,... | collective-permute-start | bytes 147464 | tf_op jit(solution)/shard_map/ppermute | solution.py:77
  14.7 2.6 %collective-permute-done.5.refs_1_ = f32[96,128]{1,0:T(8,128)S(1)} collective-permute-done((f32[96,128]{1,0:T(8,128)S(1)}, f32[96,128]{1,0:T(8,128)S(1)}, u32[]{:S(2)}, u32[]{:S(2)}) %collective-permute-start.5) | collective-permute-done | bytes 49184 | tf_op jit(solution)/shard_map/ppermute | solution.py:77
  17.3 0.5 %second_transposed.1 = (f32[104,128]{1,0:T(8,128)S(1)}, f32[56,128]{1,0:T(8,128)S(1)}, f32[96,128]{1,0:T(8,128)S(1)}, f32[96,128]{1,0:T(8,128)S(1)}, f32[8,128]{1,0:T(8,128)S(1)}) custom-call(bf16[768,768]{1,0:T(8,128)(2,1)S(1)} %get-tuple-element.35.pair, bf16[384,768]{1,0:T(8,128)(2,1)S(1)} %get-tuple-element.36.low, s32[3,3]{1,0:T(4,128)S(4)} %get-tuple-element.30.ids, ...), custom_call_target="tpu_custom_call" | custom-call | tf_op jit(solution)/shard_map/second_transposed/pallas_call | solution.py:421
  17.8 1.4 %collective-permute-start.6 = (f32[104,128]{1,0:T(8,128)S(1)}, f32[104,128]{1,0:T(8,128)S(1)}, u32[]{:S(2)}, u32[]{:S(2)}) collective-permute-start(f32[104,128]{1,0:T(8,128)S(1)} %get-tuple-element.41), channel_id=1, source_target_pairs={{0,8},{1,13},{2,10},{3,15},{4,12},{5,9},{6,14},{7,11},{8,0},{9,5},... | collective-permute-start | bytes 159752 | tf_op jit(solution)/shard_map/ppermute | solution.py:85
  19.2 2.1 %collective-permute-start.7 = (f32[56,128]{1,0:T(8,128)S(1)}, f32[56,128]{1,0:T(8,128)S(1)}, u32[]{:S(2)}, u32[]{:S(2)}) collective-permute-start(f32[56,128]{1,0:T(8,128)S(1)} %get-tuple-element.42), channel_id=1, source_target_pairs={{0,4},{4,0},{8,12},{12,8},{1,5},{5,1},{9,13},{13,9},{2,6},{6,2},{1... | collective-permute-start | bytes 86024 | tf_op jit(solution)/shard_map/ppermute | solution.py:77
  21.3 1.9 %collective-permute-done.7.refs_1_ = f32[56,128]{1,0:T(8,128)S(1)} collective-permute-done((f32[56,128]{1,0:T(8,128)S(1)}, f32[56,128]{1,0:T(8,128)S(1)}, u32[]{:S(2)}, u32[]{:S(2)}) %collective-permute-start.7) | collective-permute-done | bytes 28704 | tf_op jit(solution)/shard_map/ppermute | solution.py:77
  23.2 0.0 collective-permute-done.6.refs_0_
  23.2 0.4 %second_direct.1.mine = f32[104,128]{1,0:T(8,128)S(1)} custom-call(bf16[2304,256]{1,0:T(8,128)(2,1)S(1)} %get-tuple-element.32.pair, bf16[2304,128]{1,0:T(8,128)(2,1)S(1)} %get-tuple-element.33.low, s32[3,3]{1,0:T(4,128)S(4)} %get-tuple-element.30.ids, s32[3,3]{1,0:T(4,128)S(4)} %get-tuple-element.34.other_ids, s32[3]{0:T(128)S(4)} %get-tuple-element.28.counts, ...), custom_call_target="tpu_custom_call" | custom-call | tf_op jit(solution)/shard_map/second_direct/pallas_call | solution.py:429
  23.6 0.1 collective-permute-start.8
  23.7 1.2 %collective-permute-done.8.others = f32[104,128]{1,0:T(8,128)S(1)} collective-permute-done((f32[104,128]{1,0:T(8,128)S(1)}, f32[104,128]{1,0:T(8,128)S(1)}, u32[]{:S(2)}, u32[]{:S(2)}) %collective-permute-start.8) | collective-permute-done | bytes 53280 | tf_op jit(solution)/shard_map/ppermute | solution.py:77
  25.0 1.6 %collective-permute-start.9 = (f32[96,128]{1,0:T(8,128)S(1)}, f32[96,128]{1,0:T(8,128)S(1)}, u32[]{:S(2)}, u32[]{:S(2)}) collective-permute-start(f32[96,128]{1,0:T(8,128)S(1)} %get-tuple-element.47.refs_0_), channel_id=1, source_target_pairs={{0,2},{1,3},{2,0},{3,1},{4,6},{5,7},{6,4},{7,5},{8,10},{9,11},{10,... | collective-permute-start | bytes 147464 | tf_op jit(solution)/shard_map/ppermute | solution.py:77
  26.5 0.8 %factor.1 = (f32[32,32]{1,0:T(8,128)S(1)}, f32[32,384]{1,0:T(8,128)S(1)}) custom-call(f32[8,128]{1,0:T(8,128)S(1)} %get-tuple-element.44.gram, f32[96,128]{1,0:T(8,128)S(1)} %get-tuple-element.40.tiles), custom_call_target="tpu_custom_call" | custom-call | tf_op jit(solution)/shard_map/factor/pallas_call | solution.py:434
  27.3 1.8 %collective-permute-done.9.refs_1_ = f32[96,128]{1,0:T(8,128)S(1)} collective-permute-done((f32[96,128]{1,0:T(8,128)S(1)}, f32[96,128]{1,0:T(8,128)S(1)}, u32[]{:S(2)}, u32[]{:S(2)}) %collective-permute-start.9) | collective-permute-done | bytes 49184 | tf_op jit(solution)/shard_map/ppermute | solution.py:77
  29.1 0.5 %gram.1 = (f32[32,384]{1,0:T(8,128)S(1)}, f32[16,128]{1,0:T(8,128)S(1)}) custom-call(f32[32,32]{1,0:T(8,128)S(1)} %get-tuple-element.45.inverse, f32[32,384]{1,0:T(8,128)S(1)} %get-tuple-element.46.prior, f32[96,128]{1,0:T(8,128)S(1)} %get-tuple-element.47.refs_0_, f32[96,128]{1,0:T(8,128)S(1)} %collective-permute-done.9.refs_1_), custom_call_target="tpu_custom_call" | custom-call | tf_op jit(solution)/shard_map/gram/pallas_call | solution.py:435
  29.6 1.5 %collective-permute-start.11 = (f32[16,128]{1,0:T(8,128)S(1)}, f32[16,128]{1,0:T(8,128)S(1)}, u32[]{:S(2)}, u32[]{:S(2)}) collective-permute-start(f32[16,128]{1,0:T(8,128)S(1)} %get-tuple-element.49.mine), channel_id=1, source_target_pairs={{0,8},{1,13},{2,10},{3,15},{4,12},{5,9},{6,14},{7,11},{8,0},{9,5},... | collective-permute-start | bytes 24584 | tf_op jit(solution)/shard_map/ppermute | solution.py:85
  31.1 1.8 %collective-permute-start.10 = (f32[16,128]{1,0:T(8,128)S(1)}, f32[16,128]{1,0:T(8,128)S(1)}, u32[]{:S(2)}, u32[]{:S(2)}) collective-permute-start(f32[16,128]{1,0:T(8,128)S(1)} %get-tuple-element.49.mine), channel_id=1, source_target_pairs={{0,4},{4,0},{8,12},{12,8},{1,5},{5,1},{9,13},{13,9},{2,6},{6,2},{1... | collective-permute-start | bytes 24584 | tf_op jit(solution)/shard_map/ppermute | solution.py:77
  33.0 1.2 %collective-permute-done.11.refs_0_ = f32[16,128]{1,0:T(8,128)S(1)} collective-permute-done((f32[16,128]{1,0:T(8,128)S(1)}, f32[16,128]{1,0:T(8,128)S(1)}, u32[]{:S(2)}, u32[]{:S(2)}) %collective-permute-start.11) | collective-permute-done | bytes 8224 | tf_op jit(solution)/shard_map/ppermute | solution.py:85
  34.1 0.6 %collective-permute-done.10.shared = f32[16,128]{1,0:T(8,128)S(1)} collective-permute-done((f32[16,128]{1,0:T(8,128)S(1)}, f32[16,128]{1,0:T(8,128)S(1)}, u32[]{:S(2)}, u32[]{:S(2)}) %collective-permute-start.10) | collective-permute-done | bytes 8224 | tf_op jit(solution)/shard_map/ppermute | solution.py:77
  34.8 0.0 collective-permute-start.12
  34.8 1.2 %collective-permute-done.12.others = f32[16,128]{1,0:T(8,128)S(1)} collective-permute-done((f32[16,128]{1,0:T(8,128)S(1)}, f32[16,128]{1,0:T(8,128)S(1)}, u32[]{:S(2)}, u32[]{:S(2)}) %collective-permute-start.12) | collective-permute-done | bytes 8224 | tf_op jit(solution)/shard_map/ppermute | solution.py:77
  36.0 1.2 %last.1 = (f32[32,384]{1,0:T(8,128)}, f32[32,32]{1,0:T(8,128)}) custom-call(f32[32,384]{1,0:T(8,128)S(1)} %get-tuple-element.48.image, f32[16,128]{1,0:T(8,128)S(1)} %half_sum.1.mine, f32[16,128]{1,0:T(8,128)S(1)} %collective-permute-done.12.others), custom_call_target="tpu_custom_call" | custom-call | tf_op jit(solution)/shard_map/last/pallas_call | solution.py:440
  (3 shorter events, 0.0 us)
Async XLA Ops:
  0.6 2.4 %collective-permute-start = (f32[3,3,128,128]{3,2,1,0:T(8,128)}, f32[3,3,128,128]{3,2,1,0:T(8,128)S(1)}, u32[]{:S(2)}, u32[]{:S(2)}) collective-permute-start(f32[3,3,128,128]{3,2,1,0:T(8,128)} %blocks.1), channel_id=1, source_target_pairs={{0,1},{1,0},{2,3},{3,2},{4,5},{5,4},{6,7},{7,6},{8,9},{9,8},{10,11... | collective-permute-start | bytes 1769480 | tf_op jit(solution)/shard_map/ppermute | solution.py:77
  1.1 1.8 %collective-permute-start.1 = (s32[3,3]{1,0:T(4,128)}, s32[3,3]{1,0:T(4,128)S(1)}, u32[]{:S(2)}, u32[]{:S(2)}) collective-permute-start(s32[3,3]{1,0:T(4,128)} %ids.1), channel_id=1, source_target_pairs={{0,1},{1,0},{2,3},{3,2},{4,5},{5,4},{6,7},{7,6},{8,9},{9,8},{10,11... | collective-permute-start | bytes 116 | tf_op jit(solution)/shard_map/ppermute | solution.py:77
  3.4 8.0 %collective-permute-start.2 = (f32[96,128]{1,0:T(8,128)S(1)}, f32[96,128]{1,0:T(8,128)S(1)}, u32[]{:S(2)}, u32[]{:S(2)}) collective-permute-start(f32[96,128]{1,0:T(8,128)S(1)} %get-tuple-element.37), channel_id=1, source_target_pairs={{0,8},{1,13},{2,10},{3,15},{4,12},{5,9},{6,14},{7,11},{8,0},{9,5},... | collective-permute-start | bytes 147464 | tf_op jit(solution)/shard_map/ppermute | solution.py:85
  7.4 4.0 %collective-permute-start.3 = (f32[48,128]{1,0:T(8,128)S(1)}, f32[48,128]{1,0:T(8,128)S(1)}, u32[]{:S(2)}, u32[]{:S(2)}) collective-permute-start(f32[48,128]{1,0:T(8,128)S(1)} %get-tuple-element.38), channel_id=1, source_target_pairs={{0,4},{4,0},{8,12},{12,8},{1,5},{5,1},{9,13},{13,9},{2,6},{6,2},{1... | collective-permute-start | bytes 73736 | tf_op jit(solution)/shard_map/ppermute | solution.py:77
  11.8 1.3 %collective-permute-start.4 = (f32[96,128]{1,0:T(8,128)S(1)}, f32[96,128]{1,0:T(8,128)S(1)}, u32[]{:S(2)}, u32[]{:S(2)}) collective-permute-start(f32[96,128]{1,0:T(8,128)S(1)} %first_direct.1), channel_id=1, source_target_pairs={{0,1},{1,0},{2,3},{3,2},{4,5},{5,4},{6,7},{7,6},{8,9},{9,8},{10,11... | collective-permute-start | bytes 147464 | tf_op jit(solution)/shard_map/ppermute | solution.py:77
  13.1 4.2 %collective-permute-start.5 = (f32[96,128]{1,0:T(8,128)S(1)}, f32[96,128]{1,0:T(8,128)S(1)}, u32[]{:S(2)}, u32[]{:S(2)}) collective-permute-start(f32[96,128]{1,0:T(8,128)S(1)} %add.3.refs_0_), channel_id=1, source_target_pairs={{0,2},{1,3},{2,0},{3,1},{4,6},{5,7},{6,4},{7,5},{8,10},{9,11},{10,... | collective-permute-start | bytes 147464 | tf_op jit(solution)/shard_map/ppermute | solution.py:77
  17.8 5.4 %collective-permute-start.6 = (f32[104,128]{1,0:T(8,128)S(1)}, f32[104,128]{1,0:T(8,128)S(1)}, u32[]{:S(2)}, u32[]{:S(2)}) collective-permute-start(f32[104,128]{1,0:T(8,128)S(1)} %get-tuple-element.41), channel_id=1, source_target_pairs={{0,8},{1,13},{2,10},{3,15},{4,12},{5,9},{6,14},{7,11},{8,0},{9,5},... | collective-permute-start | bytes 159752 | tf_op jit(solution)/shard_map/ppermute | solution.py:85
  19.2 4.0 %collective-permute-start.7 = (f32[56,128]{1,0:T(8,128)S(1)}, f32[56,128]{1,0:T(8,128)S(1)}, u32[]{:S(2)}, u32[]{:S(2)}) collective-permute-start(f32[56,128]{1,0:T(8,128)S(1)} %get-tuple-element.42), channel_id=1, source_target_pairs={{0,4},{4,0},{8,12},{12,8},{1,5},{5,1},{9,13},{13,9},{2,6},{6,2},{1... | collective-permute-start | bytes 86024 | tf_op jit(solution)/shard_map/ppermute | solution.py:77
  23.6 1.3 %collective-permute-start.8 = (f32[104,128]{1,0:T(8,128)S(1)}, f32[104,128]{1,0:T(8,128)S(1)}, u32[]{:S(2)}, u32[]{:S(2)}) collective-permute-start(f32[104,128]{1,0:T(8,128)S(1)} %second_direct.1.mine), channel_id=1, source_target_pairs={{0,1},{1,0},{2,3},{3,2},{4,5},{5,4},{6,7},{7,6},{8,9},{9,8},{10,11... | collective-permute-start | bytes 159752 | tf_op jit(solution)/shard_map/ppermute | solution.py:77
  25.0 4.2 %collective-permute-start.9 = (f32[96,128]{1,0:T(8,128)S(1)}, f32[96,128]{1,0:T(8,128)S(1)}, u32[]{:S(2)}, u32[]{:S(2)}) collective-permute-start(f32[96,128]{1,0:T(8,128)S(1)} %get-tuple-element.47.refs_0_), channel_id=1, source_target_pairs={{0,2},{1,3},{2,0},{3,1},{4,6},{5,7},{6,4},{7,5},{8,10},{9,11},{10,... | collective-permute-start | bytes 147464 | tf_op jit(solution)/shard_map/ppermute | solution.py:77
  29.6 4.6 %collective-permute-start.11 = (f32[16,128]{1,0:T(8,128)S(1)}, f32[16,128]{1,0:T(8,128)S(1)}, u32[]{:S(2)}, u32[]{:S(2)}) collective-permute-start(f32[16,128]{1,0:T(8,128)S(1)} %get-tuple-element.49.mine), channel_id=1, source_target_pairs={{0,8},{1,13},{2,10},{3,15},{4,12},{5,9},{6,14},{7,11},{8,0},{9,5},... | collective-permute-start | bytes 24584 | tf_op jit(solution)/shard_map/ppermute | solution.py:85
  31.1 3.7 %collective-permute-start.10 = (f32[16,128]{1,0:T(8,128)S(1)}, f32[16,128]{1,0:T(8,128)S(1)}, u32[]{:S(2)}, u32[]{:S(2)}) collective-permute-start(f32[16,128]{1,0:T(8,128)S(1)} %get-tuple-element.49.mine), channel_id=1, source_target_pairs={{0,4},{4,0},{8,12},{12,8},{1,5},{5,1},{9,13},{13,9},{2,6},{6,2},{1... | collective-permute-start | bytes 24584 | tf_op jit(solution)/shard_map/ppermute | solution.py:77
  34.8 1.2 %collective-permute-start.12 = (f32[16,128]{1,0:T(8,128)S(1)}, f32[16,128]{1,0:T(8,128)S(1)}, u32[]{:S(2)}, u32[]{:S(2)}) collective-permute-start(f32[16,128]{1,0:T(8,128)S(1)} %half_sum.1.mine), channel_id=1, source_target_pairs={{0,1},{1,0},{2,3},{3,2},{4,5},{5,4},{6,7},{7,6},{8,9},{9,8},{10,11... | collective-permute-start | bytes 24584 | tf_op jit(solution)/shard_map/ppermute | solution.py:77

commit v9 on v8

--- a/solution.py
+++ b/solution.py
@@ -92,11 +92,9 @@
         self.odd = self.part & 1
         self.block_rows, self.slots = block_rows, slots
         self.first_row = self.row * self.block_rows
-        self.peers = [self.row ^ (k + self.odd) for k in range(2, rows, 2)]
-        self.middle = self.row ^ 1
+        self.peers = [self.row ^ 1] + [self.row ^ (k + self.odd) for k in range(2, rows, 2)]
+        self.others_peers = [self.row ^ (k + 1 - self.odd) for k in range(2, rows, 2)]
         self.columns = columns
-        self.height = columns // 2
-        self.half = pl.ds(pl.multiple_of(self.odd * self.height, self.height), self.height)
 
     def weight(self, ids, counts, member, i, p):
         used = (self.part ^ member) * self.slots + p < counts[i]
@@ -105,8 +103,9 @@
     def tile(self, i):
         return slice(i * self.columns, (i + 1) * self.columns)
 
-    def half_tile(self, i):
-        return slice(i * self.height, (i + 1) * self.height)
+    def by_distance(self, mine, received, handed):
+        both = [(jnp.where(self.odd == 0, a, b), jnp.where(self.odd == 0, b, a)) for a, b in zip(received[1:], handed)]
+        return [mine, received[0]] + [x for pair in both for x in pair]
 
 
 def stacked_blocks(blocks, i):
@@ -132,18 +131,13 @@
     return narrow_product(joined(far, 1), pair[at], low[at])
 
 
-def fill(place, messages, shared, products, tiles, own):
+def fill(place, messages, products, tiles, own):
     n = place.block_rows
     for i in range(n):
         tile = tiles[place.tile(i)]
         for peer, out in zip(place.peers, messages):
             out[place.tile(i)] = jnp.where(place.row < peer, products[peer * n + i], tile)
-        shared[place.half_tile(i)] = jnp.where(
-            place.row < place.middle,
-            products[place.middle * n + i, place.half],
-            tiles[pl.ds(pl.multiple_of(i * place.columns + place.odd * place.height, 8), place.height)],
-        )
-        own[place.tile(i)] = jnp.where(place.odd == 0, products[place.first_row + i], 0.0)
+        own[place.tile(i)] = products[place.first_row + i]
 
 
 def load_kernel(blocks, ids, counts, start, held, ids_s, counts_s, tiles, sems):
@@ -171,8 +165,7 @@
 
 
 def first_kernel(rows, other, other_ids, counts, tiles, started, *refs):
-    messages, refs = refs[: rows // 2 - 1], refs[rows // 2 - 1 :]
-    shared, own, products = refs
+    messages, (own, products) = refs[:-2], refs[-2:]
     size = products.shape[2]
     place = Place(rows, *other.shape[:2], products.shape[1])
     terms = []
@@ -189,7 +182,7 @@
         for j, c, value in terms:
             total += jnp.concatenate([jnp.where(j == block, c, 0.0)] * copies, axis=0) * value
         products[block] = total
-    fill(place, messages, shared, products, tiles, own)
+    fill(place, messages, products, tiles, own)
 
 
 def split_kernel(held, other, other_ids, after, direct_pair, direct_low, pair, low, other_s, sem):
@@ -210,34 +203,33 @@
 
 
 def direct_kernel(rows, block_rows, slots, pair, low, ids, other_ids, counts, own, tiles, *refs):
-    received, refs = refs[: rows // 2 - 1], refs[rows // 2 - 1 :]
-    shared, *gram, out, whole = refs
+    half = rows // 2
+    received, handed, refs = refs[:half], refs[half : rows - 1], refs[rows - 1 :]
+    *gram, whole = refs
     n, columns = block_rows, whole.shape[1]
     place = Place(rows, block_rows, slots, columns)
-    whole[...] = jnp.zeros_like(whole)
     for i in range(n):
-        whole[place.first_row + i] = jnp.where(place.odd == 0, tiles[place.tile(i)], 0.0)
-        for peer, message in zip(place.peers, received):
+        whole[place.first_row + i] = tiles[place.tile(i)]
+        for peer, message in zip(place.peers + place.others_peers, received + handed):
             whole[peer * n + i] = message[place.tile(i)]
-        whole[place.middle * n + i, place.half] = shared[place.half_tile(i)]
+    if len(gram) == 1:
+        (out,) = gram
+    else:
+        mine, out, total = gram
+        tall = n * columns
+        total[...] = tree(place.by_distance(mine[...], [m[tall:] for m in received], [m[tall:] for m in handed]))
     for i in range(n):
-        value = own[place.tile(i)]
-        for peer, message in zip(place.peers, received):
-            value += jnp.where(place.row > peer, message[place.tile(i)], 0.0)
-        out[place.tile(i)] = value + direct_products(
-            place, pair, low, (ids, other_ids), counts, whole, i
-        )
-        mine = pl.ds(pl.multiple_of(i * columns + place.odd * place.height, 8), place.height)
-        out[mine] += jnp.where(place.row > place.middle, shared[place.half_tile(i)], 0.0)
-    if gram:
-        first = jnp.where(place.odd == 0, gram[0][...], shared[n * place.height :])
-        out[n * columns :] = tree([first] + [message[n * columns :] for message in received])
+        at = place.tile(i)
+        arrived = place.by_distance(own[at], [m[at] for m in received], [m[at] for m in handed])
+        value = arrived[0]
+        for s in range(1, rows):
+            value += jnp.where(place.row > (place.row ^ s), arrived[s], 0.0)
+        out[at] = value + direct_products(place, pair, low, (ids, other_ids), counts, whole, i)
 
 
 def second_kernel(rows, parts, block_rows, slots, pair, low, ids, other_ids, counts, *refs):
     images, refs = refs[:parts], refs[parts:]
-    messages, refs = refs[: rows // 2 - 1], refs[rows // 2 - 1 :]
-    shared, own, tiles, gram, products = refs
+    messages, (own, tiles, gram, products) = refs[: rows // 2], refs[rows // 2 :]
     n, columns, size = block_rows, products.shape[1], products.shape[2]
     place = Place(rows, block_rows, slots, columns)
     tiles[...] = tree([image[...] for image in images])
@@ -249,13 +241,12 @@
             low[i * size : (i + 1) * size],
         )
         scatter(place, value, (ids, other_ids), counts, i, products)
-    fill(place, messages, shared, products, tiles, own)
+    fill(place, messages, products, tiles, own)
     whole = joined([split(tiles[place.tile(i)]) for i in range(n)], 1)
     packed = folded(product(whole, whole, 1), size)
     gram[...] = packed
     for message in messages:
         message[n * columns :] = packed
-    shared[n * place.height :] = packed
 
 
 def eliminated(gram, rest):
@@ -299,12 +290,6 @@
     return jnp.where(rows == lax.broadcasted_iota(jnp.int32, (n, n), 1), 1.0, 0.0)
 
 
-def pair_kernel(mine, others, image, gram):
-    tall = image.shape[0]
-    image[...] = mine[:tall] + others[:tall]
-    gram[...] = mine[tall:] + others[tall:]
-
-
 def factor_kernel(total, gram, tiles, inverse, prior):
     columns = inverse.shape[0]
     lower = eliminated(unfolded(gram[...], columns) / total, identity(columns))
@@ -325,15 +310,13 @@
     out[...] = folded(both, out.shape[1])
 
 
-def half_sum_kernel(mine, shared, *refs):
-    received, out = refs[:-1], refs[-1]
-    first = jnp.where((lax.axis_index("nbr") & 1) == 0, mine[...], shared[...])
-    out[...] = tree([first] + [part[...] for part in received])
-
-
-def last_kernel(total, image, mine, others, basis, ritz):
+def last_kernel(rows, total, image, mine, *refs):
+    half = rows // 2
+    received, handed, (basis, ritz) = refs[:half], refs[half : rows - 1], refs[rows - 1 :]
     columns = ritz.shape[0]
-    both = unfolded((mine[...] + others[...]) / total, columns)
+    place = Place(rows, 0, 0, columns)
+    parts = place.by_distance(mine[...], [m[...] for m in received], [m[...] for m in handed])
+    both = unfolded(tree(parts) / total, columns)
     ritz[...] = both[columns:]
     basis[...] = eliminated(both[:columns], image[...])
 
@@ -367,8 +350,10 @@
             compiler_params=PARAMS,
         )
 
-    def round_over_rows(messages, shared):
-        return [swap_rows(m, 2 * k, 2 * k + 1) for k, m in enumerate(messages, 1)], swap(shared, "row", 1)
+    def round_over_rows(messages):
+        received = [swap_rows(m, 2 * k, 2 * k + 1) for k, m in enumerate(messages[1:], 1)]
+        near = swap(messages[0], "row", 1)
+        return [near] + received + [swap(m, "nbr", 1) for m in received]
 
     def sum_over_pairs(image):
         return [image] + [swap(image, "nbr", s) for s in range(2, parts, 2)]
@@ -388,15 +373,15 @@
         [VMEM, SMEM, SMEM, VMEM],
         [jax.ShapeDtypeStruct(work.shape, F32)],
     )(held, ids, counts, tiles)
-    *messages, shared, own = call(
+    *messages, own = call(
         functools.partial(first_kernel, rows),
         "first_transposed",
         [VMEM, VMEM, SMEM, VMEM, VMEM],
-        [tile] * (half - 1) + [flat(tall // 2), tile],
+        [tile] * (half + 1),
         [work],
     )(other, other_ids, counts, tiles, started)
     index = [VMEM, VMEM, SMEM, SMEM, SMEM]
-    received, shared = round_over_rows(messages, shared)
+    arrived = round_over_rows(messages)
     deep = 2 * block_rows * slots * size
     wide_row = 2 * slots * size
     direct_pair, direct_low, pair, low, other_ids = call(
@@ -414,32 +399,30 @@
     )(held, other, other_ids, own)
     parted = (direct_pair, direct_low, ids, other_ids, counts)
     direct = functools.partial(direct_kernel, rows, block_rows, slots)
-    (image,) = call(direct, "first_direct", index + [VMEM] * (half + 2), [tile], [work])(
-        *parted, own, tiles, *received, shared
+    (image,) = call(direct, "first_direct", index + [VMEM] * (rows + 1), [tile], [work])(
+        *parted, own, tiles, *arrived
     )
-    images = sum_over_pairs(image + swap(image, "nbr", 1))
-    *messages, shared, own, tiles, gram = call(
+    images = sum_over_pairs(image)
+    *messages, own, tiles, gram = call(
         functools.partial(second_kernel, rows, parts // 2, block_rows, slots),
         "second_transposed",
         index + [VMEM] * (parts // 2),
-        [flat(tall + extra)] * (half - 1) + [flat(tall // 2 + extra), tile, tile, flat(extra)],
+        [flat(tall + extra)] * half + [tile, tile, flat(extra)],
         [work],
     )(pair, low, ids, other_ids, counts, *images)
-    received, shared = round_over_rows(messages, shared)
-    (mine,) = call(direct, "second_direct", index + [VMEM] * (half + 3), [flat(tall + extra)], [work])(
-        *parted, own, tiles, *received, shared, gram
+    arrived = round_over_rows(messages)
+    image, gram = call(direct, "second_direct", index + [VMEM] * (rows + 2), [tile, flat(extra)], [work])(
+        *parted, own, tiles, *arrived, gram
     )
-    image, gram = call(pair_kernel, "pair", [VMEM] * 2, [tile, flat(extra)])(mine, swap(mine, "nbr", 1))
     images = sum_over_pairs(image)
     inverse, prior = call(functools.partial(factor_kernel, total), "factor", [VMEM] * 2, [square, across])(gram, tiles)
     image, both = call(gram_kernel, "gram", [VMEM] * (parts // 2 + 2), [across, flat(2 * extra)])(
         inverse, prior, *images
     )
-    received, shared = round_over_rows([both] * (half - 1), both)
-    (both,) = call(half_sum_kernel, "half_sum", [VMEM] * (half + 1), [flat(2 * extra)])(both, shared, *received)
-    basis, ritz = call(functools.partial(last_kernel, total), "last", [VMEM] * 3, [across, square])(
-        image, both, swap(both, "nbr", 1)
-    )
+    arrived = round_over_rows([both] * half)
+    basis, ritz = call(
+        functools.partial(last_kernel, rows, total), "last", [VMEM] * (rows + 1), [across, square]
+    )(image, both, *arrived)
     return basis.T, ritz
 
 

time: 37.4 us -> 36 us (0.963)
  waiting for transfers between devices: 13.6 us -> 10.8 us
  starting transfers between devices: 16.4 us -> 17.9 us
    ppermute x10, waiting for transfers between devices: 12.5 us -> 8.63 us  [swap(): lax.ppermute(x, axis, [(i, i ^ distance) for i in range(lax.axis_size(axi...]
    ppermute x3, starting transfers between devices: 7.01 us -> 8.7 us  [swap_rows(): return lax.ppermute(x, ('row', 'nbr'), pairs)]
    ppermute x3, waiting for transfers between devices: 1.19 us -> 2.16 us  [swap_rows(): return lax.ppermute(x, ('row', 'nbr'), pairs)]
    pallas_call x5 -> x3, Pallas kernels: 2.08 us -> 2.05 us  [the longest x1 1.25 us: body(): call(functools.partial(last_kernel, rows, total), 'last', [VMEM] * (rows...]
  transfers between devices with their start and end apart: 13 -> 13, of which waited for: 10 -> 9; matrix products, arithmetic and copies ran while one was open for 0% -> 0% of each run, Pallas kernels for 8% -> 8%
where the time goes in v9:
time: 36 us; the launch traced here: 35.9 us
  starting transfers between devices  17.9 us (50%)
  waiting for transfers between devices  10.8 us (30%)
  Pallas kernels  6.47 us (18%)
  between operations  0.7 us (2%)
    ppermute x10, starting transfers between devices, swap(): lax.ppermute(x, axis, [(i, i ^ distance) for i in range(lax.axis_size(axi...  9.22 us
    ppermute x3, starting transfers between devices, swap_rows(): return lax.ppermute(x, ('row', 'nbr'), pairs)  8.7 us
    ppermute x10, waiting for transfers between devices, swap(): lax.ppermute(x, axis, [(i, i ^ distance) for i in range(lax.axis_size(axi...  8.63 us
    ppermute x3, waiting for transfers between devices, swap_rows(): return lax.ppermute(x, ('row', 'nbr'), pairs)  2.16 us
    pallas_call x1, Pallas kernels, body(): call(functools.partial(last_kernel, rows, total), 'last', [VMEM] * (rows...  1.25 us
    pallas_call x1, Pallas kernels, body(): call(load_kernel, 'load', [HBM] * 4, [jax.ShapeDtypeStruct(blocks.shape,...  1.14 us
    pallas_call x1, Pallas kernels, body(): call(functools.partial(factor_kernel, total), 'factor', [VMEM] * 2, [squa...  0.8 us
    pallas_call x1, Pallas kernels, body(): call(split_kernel, 'split', [VMEM] * 4, [jax.ShapeDtypeStruct((deep, 2 *...  0.79 us
  transfers between devices with their start and end apart: 13, of which 9 were waited for; matrix products, arithmetic and copies ran while one was open for 0% of the time, Pallas kernels for 8%

profile of v9, /device:TPU:0, one launch (start us, length us, event | category | flops | bytes accessed | tf_op | source)
XLA Modules:
  0.0 35.9 jit_solution(10428179523097546194)
XLA Ops:
  0.6 0.5 %collective-permute-start = (f32[3,3,128,128]{3,2,1,0:T(8,128)}, f32[3,3,128,128]{3,2,1,0:T(8,128)S(1)}, u32[]{:S(2)}, u32[]{:S(2)}) collective-permute-start(f32[3,3,128,128]{3,2,1,0:T(8,128)} %blocks.1), channel_id=1, source_target_pairs={{0,1},{1,0},{2,3},{3,2},{4,5},{5,4},{6,7},{7,6},{8,9},{9,8},{10,11... | collective-permute-start | bytes 1769480 | tf_op jit(solution)/shard_map/ppermute | solution.py:77
  1.1 0.1 collective-permute-start.1
  1.2 1.1 %load.1 = (f32[3,3,128,128]{3,2,1,0:T(8,128)S(1)}, s32[3,3]{1,0:T(4,128)S(4)}, s32[3]{0:T(128)S(4)}, f32[96,128]{1,0:T(8,128)S(1)}) custom-call(f32[3,3,128,128]{3,2,1,0:T(8,128)} %blocks.1, s32[3,3]{1,0:T(4,128)} %ids.1, s32[3]{0:T(128)} %counts.1, f32[32,384]{1,0:T(8,128)} %bitcast.2), custom_call_target="tpu_custom_call" | custom-call | tf_op jit(solution)/shard_map/load/pallas_call | solution.py:363
  2.4 0.3 own_transposed.1.started
  2.7 0.3 collective-permute-done.1.other_ids
  3.0 0.0 collective-permute-done.other
  3.0 0.4 %first_transposed.1 = (f32[96,128]{1,0:T(8,128)S(1)}, f32[96,128]{1,0:T(8,128)S(1)}, f32[96,128]{1,0:T(8,128)S(1)}) custom-call(f32[3,3,128,128]{3,2,1,0:T(8,128)S(1)} %collective-permute-done.other, s32[3,3]{1,0:T(4,128)S(1)} %collective-permute-done.1.other_ids, s32[3]{0:T(128)S(4)} %get-tuple-element.28.counts, f32[96,128]{1,0:T(8,128)S(1)} %get-tuple-element.29.tiles, ...), custom_call_target="tpu_custom_call" | custom-call | tf_op jit(solution)/shard_map/first_transposed/pallas_call | solution.py:376
  3.4 4.0 %collective-permute-start.3 = (f32[96,128]{1,0:T(8,128)S(1)}, f32[96,128]{1,0:T(8,128)S(1)}, u32[]{:S(2)}, u32[]{:S(2)}) collective-permute-start(f32[96,128]{1,0:T(8,128)S(1)} %get-tuple-element.38), channel_id=1, source_target_pairs={{0,8},{1,13},{2,10},{3,15},{4,12},{5,9},{6,14},{7,11},{8,0},{9,5},... | collective-permute-start | bytes 147464 | tf_op jit(solution)/shard_map/ppermute | solution.py:85
  7.4 1.6 %collective-permute-start.2 = (f32[96,128]{1,0:T(8,128)S(1)}, f32[96,128]{1,0:T(8,128)S(1)}, u32[]{:S(2)}, u32[]{:S(2)}) collective-permute-start(f32[96,128]{1,0:T(8,128)S(1)} %get-tuple-element.37), channel_id=1, source_target_pairs={{0,4},{4,0},{8,12},{12,8},{1,5},{5,1},{9,13},{13,9},{2,6},{6,2},{1... | collective-permute-start | bytes 147464 | tf_op jit(solution)/shard_map/ppermute | solution.py:77
  9.0 1.2 %collective-permute-done.3.refs_1_ = f32[96,128]{1,0:T(8,128)S(1)} collective-permute-done((f32[96,128]{1,0:T(8,128)S(1)}, f32[96,128]{1,0:T(8,128)S(1)}, u32[]{:S(2)}, u32[]{:S(2)}) %collective-permute-start.3) | collective-permute-done | bytes 49184 | tf_op jit(solution)/shard_map/ppermute | solution.py:85
  10.1 0.0 collective-permute-start.4
  10.1 0.8 %split.1 = (bf16[2304,256]{1,0:T(8,128)(2,1)S(1)}, bf16[2304,128]{1,0:T(8,128)(2,1)S(1)}, bf16[768,768]{1,0:T(8,128)(2,1)S(1)}, bf16[384,768]{1,0:T(8,128)(2,1)S(1)}, s32[3,3]{1,0:T(4,128)S(4)}) custom-call(f32[3,3,128,128]{3,2,1,0:T(8,128)S(1)} %get-tuple-element.27.held, f32[3,3,128,128]{3,2,1,0:T(8,128)S(1)} %collective-permute-done.other, ...), custom_call_target="tpu_custom_call" | custom-call | tf_op jit(solution)/shard_map/split/pallas_call | solution.py:387
  10.9 1.0 %collective-permute-done.2.refs_0_ = f32[96,128]{1,0:T(8,128)S(1)} collective-permute-done((f32[96,128]{1,0:T(8,128)S(1)}, f32[96,128]{1,0:T(8,128)S(1)}, u32[]{:S(2)}, u32[]{:S(2)}) %collective-permute-start.2) | collective-permute-done | bytes 49184 | tf_op jit(solution)/shard_map/ppermute | solution.py:77
  11.9 0.0 collective-permute-done.4.refs_2_
  11.9 0.4 %first_direct.1.refs_0_ = f32[96,128]{1,0:T(8,128)S(1)} custom-call(bf16[2304,256]{1,0:T(8,128)(2,1)S(1)} %get-tuple-element.32.pair, bf16[2304,128]{1,0:T(8,128)(2,1)S(1)} %get-tuple-element.33.low, s32[3,3]{1,0:T(4,128)S(4)} %get-tuple-element.30.ids, s32[3,3]{1,0:T(4,128)S(4)} %get-tuple-element.34.other_ids, s32[3]{0:T(128)S(4)} %get-tuple-element.28.counts, ...), custom_call_target="tpu_custom_call" | custom-call | tf_op jit(solution)/shard_map/first_direct/pallas_call | solution.py:402
  12.3 1.6 %collective-permute-start.5 = (f32[96,128]{1,0:T(8,128)S(1)}, f32[96,128]{1,0:T(8,128)S(1)}, u32[]{:S(2)}, u32[]{:S(2)}) collective-permute-start(f32[96,128]{1,0:T(8,128)S(1)} %first_direct.1.refs_0_), channel_id=1, source_target_pairs={{0,2},{1,3},{2,0},{3,1},{4,6},{5,7},{6,4},{7,5},{8,10},{9,11},{10,... | collective-permute-start | bytes 147464 | tf_op jit(solution)/shard_map/ppermute | solution.py:77
  13.9 2.6 %collective-permute-done.5.refs_1_ = f32[96,128]{1,0:T(8,128)S(1)} collective-permute-done((f32[96,128]{1,0:T(8,128)S(1)}, f32[96,128]{1,0:T(8,128)S(1)}, u32[]{:S(2)}, u32[]{:S(2)}) %collective-permute-start.5) | collective-permute-done | bytes 49184 | tf_op jit(solution)/shard_map/ppermute | solution.py:77
  16.5 0.5 %second_transposed.1 = (f32[104,128]{1,0:T(8,128)S(1)}, f32[104,128]{1,0:T(8,128)S(1)}, f32[96,128]{1,0:T(8,128)S(1)}, f32[96,128]{1,0:T(8,128)S(1)}, f32[8,128]{1,0:T(8,128)S(1)}) custom-call(bf16[768,768]{1,0:T(8,128)(2,1)S(1)} %get-tuple-element.35.pair, bf16[384,768]{1,0:T(8,128)(2,1)S(1)} %get-tuple-element.36.low, s32[3,3]{1,0:T(4,128)S(4)} %get-tuple-element.30.ids, ...), custom_call_target="tpu_custom_call" | custom-call | tf_op jit(solution)/shard_map/second_transposed/pallas_call | solution.py:406
  17.0 2.1 %collective-permute-start.7 = (f32[104,128]{1,0:T(8,128)S(1)}, f32[104,128]{1,0:T(8,128)S(1)}, u32[]{:S(2)}, u32[]{:S(2)}) collective-permute-start(f32[104,128]{1,0:T(8,128)S(1)} %get-tuple-element.42), channel_id=1, source_target_pairs={{0,8},{1,13},{2,10},{3,15},{4,12},{5,9},{6,14},{7,11},{8,0},{9,5},... | collective-permute-start | bytes 159752 | tf_op jit(solution)/shard_map/ppermute | solution.py:85
  19.2 2.1 %collective-permute-start.6 = (f32[104,128]{1,0:T(8,128)S(1)}, f32[104,128]{1,0:T(8,128)S(1)}, u32[]{:S(2)}, u32[]{:S(2)}) collective-permute-start(f32[104,128]{1,0:T(8,128)S(1)} %get-tuple-element.41), channel_id=1, source_target_pairs={{0,4},{4,0},{8,12},{12,8},{1,5},{5,1},{9,13},{13,9},{2,6},{6,2},{1... | collective-permute-start | bytes 159752 | tf_op jit(solution)/shard_map/ppermute | solution.py:77
  21.3 0.8 %collective-permute-done.7.refs_1_ = f32[104,128]{1,0:T(8,128)S(1)} collective-permute-done((f32[104,128]{1,0:T(8,128)S(1)}, f32[104,128]{1,0:T(8,128)S(1)}, u32[]{:S(2)}, u32[]{:S(2)}) %collective-permute-start.7) | collective-permute-done | bytes 53280 | tf_op jit(solution)/shard_map/ppermute | solution.py:85
  22.1 0.0 collective-permute-start.8
  22.1 1.3 %collective-permute-done.6.refs_0_ = f32[104,128]{1,0:T(8,128)S(1)} collective-permute-done((f32[104,128]{1,0:T(8,128)S(1)}, f32[104,128]{1,0:T(8,128)S(1)}, u32[]{:S(2)}, u32[]{:S(2)}) %collective-permute-start.6) | collective-permute-done | bytes 53280 | tf_op jit(solution)/shard_map/ppermute | solution.py:77
  23.4 0.0 collective-permute-done.8.refs_2_
  23.4 0.4 %second_direct.1 = (f32[96,128]{1,0:T(8,128)S(1)}, f32[8,128]{1,0:T(8,128)S(1)}) custom-call(bf16[2304,256]{1,0:T(8,128)(2,1)S(1)} %get-tuple-element.32.pair, bf16[2304,128]{1,0:T(8,128)(2,1)S(1)} %get-tuple-element.33.low, s32[3,3]{1,0:T(4,128)S(4)} %get-tuple-element.30.ids, s32[3,3]{1,0:T(4,128)S(4)} %get-tuple-element.34.other_ids, ...), custom_call_target="tpu_custom_call" | custom-call | tf_op jit(solution)/shard_map/second_direct/pallas_call | solution.py:414
  23.8 1.6 %collective-permute-start.9 = (f32[96,128]{1,0:T(8,128)S(1)}, f32[96,128]{1,0:T(8,128)S(1)}, u32[]{:S(2)}, u32[]{:S(2)}) collective-permute-start(f32[96,128]{1,0:T(8,128)S(1)} %get-tuple-element.47.refs_0_), channel_id=1, source_target_pairs={{0,2},{1,3},{2,0},{3,1},{4,6},{5,7},{6,4},{7,5},{8,10},{9,11},{10,... | collective-permute-start | bytes 147464 | tf_op jit(solution)/shard_map/ppermute | solution.py:77
  25.3 0.8 %factor.1 = (f32[32,32]{1,0:T(8,128)S(1)}, f32[32,384]{1,0:T(8,128)S(1)}) custom-call(f32[8,128]{1,0:T(8,128)S(1)} %get-tuple-element.44.gram, f32[96,128]{1,0:T(8,128)S(1)} %get-tuple-element.40.tiles), custom_call_target="tpu_custom_call" | custom-call | tf_op jit(solution)/shard_map/factor/pallas_call | solution.py:418
  26.2 1.8 %collective-permute-done.9.refs_1_ = f32[96,128]{1,0:T(8,128)S(1)} collective-permute-done((f32[96,128]{1,0:T(8,128)S(1)}, f32[96,128]{1,0:T(8,128)S(1)}, u32[]{:S(2)}, u32[]{:S(2)}) %collective-permute-start.9) | collective-permute-done | bytes 49184 | tf_op jit(solution)/shard_map/ppermute | solution.py:77
  27.9 0.5 %gram.1 = (f32[32,384]{1,0:T(8,128)S(1)}, f32[16,128]{1,0:T(8,128)S(1)}) custom-call(f32[32,32]{1,0:T(8,128)S(1)} %get-tuple-element.45.inverse, f32[32,384]{1,0:T(8,128)S(1)} %get-tuple-element.46.prior, f32[96,128]{1,0:T(8,128)S(1)} %get-tuple-element.47.refs_0_, f32[96,128]{1,0:T(8,128)S(1)} %collective-permute-done.9.refs_1_), custom_call_target="tpu_custom_call" | custom-call | tf_op jit(solution)/shard_map/gram/pallas_call | solution.py:419
  28.4 2.5 %collective-permute-start.11 = (f32[16,128]{1,0:T(8,128)S(1)}, f32[16,128]{1,0:T(8,128)S(1)}, u32[]{:S(2)}, u32[]{:S(2)}) collective-permute-start(f32[16,128]{1,0:T(8,128)S(1)} %get-tuple-element.49.mine), channel_id=1, source_target_pairs={{0,8},{1,13},{2,10},{3,15},{4,12},{5,9},{6,14},{7,11},{8,0},{9,5},... | collective-permute-start | bytes 24584 | tf_op jit(solution)/shard_map/ppermute | solution.py:85
  31.0 1.8 %collective-permute-start.10 = (f32[16,128]{1,0:T(8,128)S(1)}, f32[16,128]{1,0:T(8,128)S(1)}, u32[]{:S(2)}, u32[]{:S(2)}) collective-permute-start(f32[16,128]{1,0:T(8,128)S(1)} %get-tuple-element.49.mine), channel_id=1, source_target_pairs={{0,4},{4,0},{8,12},{12,8},{1,5},{5,1},{9,13},{13,9},{2,6},{6,2},{1... | collective-permute-start | bytes 24584 | tf_op jit(solution)/shard_map/ppermute | solution.py:77
  32.8 0.2 collective-permute-done.11.refs_1_
  33.0 0.0 collective-permute-start.12
  33.0 1.6 %collective-permute-done.10.refs_0_ = f32[16,128]{1,0:T(8,128)S(1)} collective-permute-done((f32[16,128]{1,0:T(8,128)S(1)}, f32[16,128]{1,0:T(8,128)S(1)}, u32[]{:S(2)}, u32[]{:S(2)}) %collective-permute-start.10) | collective-permute-done | bytes 8224 | tf_op jit(solution)/shard_map/ppermute | solution.py:77
  34.6 0.0 collective-permute-done.12.refs_2_
  34.6 1.3 %last.1 = (f32[32,384]{1,0:T(8,128)}, f32[32,32]{1,0:T(8,128)}) custom-call(f32[32,384]{1,0:T(8,128)S(1)} %get-tuple-element.48.image, f32[16,128]{1,0:T(8,128)S(1)} %get-tuple-element.49.mine, f32[16,128]{1,0:T(8,128)S(1)} %collective-permute-done.10.refs_0_, f32[16,128]{1,0:T(8,128)S(1)} %collective-permute-done.11.refs_1_, ...), custom_call_target="tpu_custom_call" | custom-call | tf_op jit(solution)/shard_map/last/pallas_call | solution.py:423
Async XLA Ops:
  0.6 2.4 %collective-permute-start = (f32[3,3,128,128]{3,2,1,0:T(8,128)}, f32[3,3,128,128]{3,2,1,0:T(8,128)S(1)}, u32[]{:S(2)}, u32[]{:S(2)}) collective-permute-start(f32[3,3,128,128]{3,2,1,0:T(8,128)} %blocks.1), channel_id=1, source_target_pairs={{0,1},{1,0},{2,3},{3,2},{4,5},{5,4},{6,7},{7,6},{8,9},{9,8},{10,11... | collective-permute-start | bytes 1769480 | tf_op jit(solution)/shard_map/ppermute | solution.py:77
  1.1 1.8 %collective-permute-start.1 = (s32[3,3]{1,0:T(4,128)}, s32[3,3]{1,0:T(4,128)S(1)}, u32[]{:S(2)}, u32[]{:S(2)}) collective-permute-start(s32[3,3]{1,0:T(4,128)} %ids.1), channel_id=1, source_target_pairs={{0,1},{1,0},{2,3},{3,2},{4,5},{5,4},{6,7},{7,6},{8,9},{9,8},{10,11... | collective-permute-start | bytes 116 | tf_op jit(solution)/shard_map/ppermute | solution.py:77
  3.4 6.8 %collective-permute-start.3 = (f32[96,128]{1,0:T(8,128)S(1)}, f32[96,128]{1,0:T(8,128)S(1)}, u32[]{:S(2)}, u32[]{:S(2)}) collective-permute-start(f32[96,128]{1,0:T(8,128)S(1)} %get-tuple-element.38), channel_id=1, source_target_pairs={{0,8},{1,13},{2,10},{3,15},{4,12},{5,9},{6,14},{7,11},{8,0},{9,5},... | collective-permute-start | bytes 147464 | tf_op jit(solution)/shard_map/ppermute | solution.py:85
  7.4 4.5 %collective-permute-start.2 = (f32[96,128]{1,0:T(8,128)S(1)}, f32[96,128]{1,0:T(8,128)S(1)}, u32[]{:S(2)}, u32[]{:S(2)}) collective-permute-start(f32[96,128]{1,0:T(8,128)S(1)} %get-tuple-element.37), channel_id=1, source_target_pairs={{0,4},{4,0},{8,12},{12,8},{1,5},{5,1},{9,13},{13,9},{2,6},{6,2},{1... | collective-permute-start | bytes 147464 | tf_op jit(solution)/shard_map/ppermute | solution.py:77
  10.1 1.8 %collective-permute-start.4 = (f32[96,128]{1,0:T(8,128)S(1)}, f32[96,128]{1,0:T(8,128)S(1)}, u32[]{:S(2)}, u32[]{:S(2)}) collective-permute-start(f32[96,128]{1,0:T(8,128)S(1)} %collective-permute-done.3.refs_1_), channel_id=1, source_target_pairs={{0,1},{1,0},{2,3},{3,2},{4,5},{5,4},{6,7},{7,6},{8,9},{9,8},{10,11... | collective-permute-start | bytes 147464 | tf_op jit(solution)/shard_map/ppermute | solution.py:77
  12.3 4.2 %collective-permute-start.5 = (f32[96,128]{1,0:T(8,128)S(1)}, f32[96,128]{1,0:T(8,128)S(1)}, u32[]{:S(2)}, u32[]{:S(2)}) collective-permute-start(f32[96,128]{1,0:T(8,128)S(1)} %first_direct.1.refs_0_), channel_id=1, source_target_pairs={{0,2},{1,3},{2,0},{3,1},{4,6},{5,7},{6,4},{7,5},{8,10},{9,11},{10,... | collective-permute-start | bytes 147464 | tf_op jit(solution)/shard_map/ppermute | solution.py:77
  17.0 5.0 %collective-permute-start.7 = (f32[104,128]{1,0:T(8,128)S(1)}, f32[104,128]{1,0:T(8,128)S(1)}, u32[]{:S(2)}, u32[]{:S(2)}) collective-permute-start(f32[104,128]{1,0:T(8,128)S(1)} %get-tuple-element.42), channel_id=1, source_target_pairs={{0,8},{1,13},{2,10},{3,15},{4,12},{5,9},{6,14},{7,11},{8,0},{9,5},... | collective-permute-start | bytes 159752 | tf_op jit(solution)/shard_map/ppermute | solution.py:85
  19.2 4.2 %collective-permute-start.6 = (f32[104,128]{1,0:T(8,128)S(1)}, f32[104,128]{1,0:T(8,128)S(1)}, u32[]{:S(2)}, u32[]{:S(2)}) collective-permute-start(f32[104,128]{1,0:T(8,128)S(1)} %get-tuple-element.41), channel_id=1, source_target_pairs={{0,4},{4,0},{8,12},{12,8},{1,5},{5,1},{9,13},{13,9},{2,6},{6,2},{1... | collective-permute-start | bytes 159752 | tf_op jit(solution)/shard_map/ppermute | solution.py:77
  22.1 1.3 %collective-permute-start.8 = (f32[104,128]{1,0:T(8,128)S(1)}, f32[104,128]{1,0:T(8,128)S(1)}, u32[]{:S(2)}, u32[]{:S(2)}) collective-permute-start(f32[104,128]{1,0:T(8,128)S(1)} %collective-permute-done.7.refs_1_), channel_id=1, source_target_pairs={{0,1},{1,0},{2,3},{3,2},{4,5},{5,4},{6,7},{7,6},{8,9},{9,8},{10,11... | collective-permute-start | bytes 159752 | tf_op jit(solution)/shard_map/ppermute | solution.py:77
  23.8 4.2 %collective-permute-start.9 = (f32[96,128]{1,0:T(8,128)S(1)}, f32[96,128]{1,0:T(8,128)S(1)}, u32[]{:S(2)}, u32[]{:S(2)}) collective-permute-start(f32[96,128]{1,0:T(8,128)S(1)} %get-tuple-element.47.refs_0_), channel_id=1, source_target_pairs={{0,2},{1,3},{2,0},{3,1},{4,6},{5,7},{6,4},{7,5},{8,10},{9,11},{10,... | collective-permute-start | bytes 147464 | tf_op jit(solution)/shard_map/ppermute | solution.py:77
  28.4 4.6 %collective-permute-start.11 = (f32[16,128]{1,0:T(8,128)S(1)}, f32[16,128]{1,0:T(8,128)S(1)}, u32[]{:S(2)}, u32[]{:S(2)}) collective-permute-start(f32[16,128]{1,0:T(8,128)S(1)} %get-tuple-element.49.mine), channel_id=1, source_target_pairs={{0,8},{1,13},{2,10},{3,15},{4,12},{5,9},{6,14},{7,11},{8,0},{9,5},... | collective-permute-start | bytes 24584 | tf_op jit(solution)/shard_map/ppermute | solution.py:85
  31.0 3.7 %collective-permute-start.10 = (f32[16,128]{1,0:T(8,128)S(1)}, f32[16,128]{1,0:T(8,128)S(1)}, u32[]{:S(2)}, u32[]{:S(2)}) collective-permute-start(f32[16,128]{1,0:T(8,128)S(1)} %get-tuple-element.49.mine), channel_id=1, source_target_pairs={{0,4},{4,0},{8,12},{12,8},{1,5},{5,1},{9,13},{13,9},{2,6},{6,2},{1... | collective-permute-start | bytes 24584 | tf_op jit(solution)/shard_map/ppermute | solution.py:77
  33.0 1.6 %collective-permute-start.12 = (f32[16,128]{1,0:T(8,128)S(1)}, f32[16,128]{1,0:T(8,128)S(1)}, u32[]{:S(2)}, u32[]{:S(2)}) collective-permute-start(f32[16,128]{1,0:T(8,128)S(1)} %collective-permute-done.11.refs_1_), channel_id=1, source_target_pairs={{0,1},{1,0},{2,3},{3,2},{4,5},{5,4},{6,7},{7,6},{8,9},{9,8},{10,11... | collective-permute-start | bytes 24584 | tf_op jit(solution)/shard_map/ppermute | solution.py:77

commit v10 on v9

--- a/solution.py
+++ b/solution.py
@@ -96,9 +96,13 @@
         self.others_peers = [self.row ^ (k + 1 - self.odd) for k in range(2, rows, 2)]
         self.columns = columns
 
-    def weight(self, ids, counts, member, i, p):
-        used = (self.part ^ member) * self.slots + p < counts[i]
-        return jnp.where(used, jnp.where(ids[i, p] == self.first_row + i, 0.5, 1.0), 0.0).astype(F32)
+    def column(self, ids, m, i, p):
+        own, other = ids
+        return jnp.where(self.odd == m, own[i, p], other[i, p])
+
+    def weight(self, column, counts, m, i, p):
+        used = (self.part - self.odd + m) * self.slots + p < counts[i]
+        return jnp.where(used, jnp.where(column == self.first_row + i, 0.5, 1.0), 0.0).astype(F32)
 
     def tile(self, i):
         return slice(i * self.columns, (i + 1) * self.columns)
@@ -108,25 +112,26 @@
         return [mine, received[0]] + [x for pair in both for x in pair]
 
 
-def stacked_blocks(blocks, i):
-    slots = range(blocks[0].shape[1])
-    high, middle, low = joined([split(b[i, p]) for b in blocks for p in slots], 1)
+def stacked_blocks(blocks):
+    high, middle, low = joined([split(b) for b in blocks], 1)
     return jnp.concatenate([high, middle], axis=0), low
 
 
 def scatter(place, value, ids, counts, i, out):
     size = out.shape[2]
-    for m, table in enumerate(ids):
+    for m in range(2):
         for p in range(place.slots):
             at = (m * place.slots + p) * size
-            out[table[i, p]] += value[:, at : at + size] * place.weight(table, counts, m, i, p)
+            j = place.column(ids, m, i, p)
+            out[j] += value[:, at : at + size] * place.weight(j, counts, m, i, p)
 
 
 def direct_products(place, pair, low, ids, counts, whole, i):
     far = []
-    for m in range(len(ids)):
+    for m in range(2):
         for p in range(place.slots):
-            far.append(split(whole[ids[m][i, p]] * place.weight(ids[m], counts, m, i, p)))
+            j = place.column(ids, m, i, p)
+            far.append(split(whole[j] * place.weight(j, counts, m, i, p)))
     at = slice(i * len(far) * pair.shape[1] // 2, (i + 1) * len(far) * pair.shape[1] // 2)
     return narrow_product(joined(far, 1), pair[at], low[at])
 
@@ -158,10 +163,14 @@
 
 def own_kernel(rows, held, ids, counts, tiles, products):
     place = Place(rows, *held.shape[:2], products.shape[1])
+    size = products.shape[2]
     products[...] = jnp.zeros_like(products)
     for i in range(place.block_rows):
-        value = shallow_product(split(tiles[place.tile(i)]), *stacked_blocks((held,), i))
-        scatter(place, value, (ids,), counts, i, products)
+        stored = stacked_blocks([held[i, p] for p in range(place.slots)])
+        value = shallow_product(split(tiles[place.tile(i)]), *stored)
+        for p in range(place.slots):
+            j = ids[i, p]
+            products[j] += value[:, p * size : (p + 1) * size] * place.weight(j, counts, place.odd, i, p)
 
 
 def first_kernel(rows, other, other_ids, counts, tiles, started, *refs):
@@ -170,35 +179,37 @@
     place = Place(rows, *other.shape[:2], products.shape[1])
     terms = []
     for i in range(place.block_rows):
-        value = shallow_product(split(tiles[place.tile(i)]), *stacked_blocks((other,), i))
+        stored = stacked_blocks([other[i, p] for p in range(place.slots)])
+        value = shallow_product(split(tiles[place.tile(i)]), *stored)
         for p in range(place.slots):
-            used = (place.part ^ 1) * place.slots + p < counts[i]
+            used = (place.part + 1 - 2 * place.odd) * place.slots + p < counts[i]
             j = jnp.broadcast_to(other_ids[i : i + 1, p : p + 1], (8, size))
             c = jnp.where(j == place.first_row + i, 0.5, 1.0)
             terms.append((jnp.where(used, j, -1), c, value[:, p * size : (p + 1) * size]))
     copies = place.columns // 8
     for block in range(products.shape[0]):
-        total = started[block]
+        total = jnp.zeros_like(started[block])
         for j, c, value in terms:
             total += jnp.concatenate([jnp.where(j == block, c, 0.0)] * copies, axis=0) * value
-        products[block] = total
+        products[block] = started[block] + total
     fill(place, messages, products, tiles, own)
 
 
 def split_kernel(held, other, other_ids, after, direct_pair, direct_low, pair, low, other_s, sem):
     block_rows, slots, size, _ = held.shape
+    odd = lax.axis_index("nbr") & 1
     copy = pltpu.make_async_copy(other_ids, other_s, sem.at[0])
     copy.start()
     at = 0
     for i in range(block_rows):
-        for b in (held, other):
-            for p in range(slots):
-                high, middle, rest = split(b[i, p].T)
-                direct_pair[at : at + size, :size] = high
-                direct_pair[at : at + size, size:] = middle
-                direct_low[at : at + size] = rest
-                at += size
-        pair[2 * i * size : 2 * (i + 1) * size], low[i * size : (i + 1) * size] = stacked_blocks((held, other), i)
+        stored = [jnp.where(odd == m, held[i, p], other[i, p]) for m in range(2) for p in range(slots)]
+        for b in stored:
+            high, middle, rest = split(b.T)
+            direct_pair[at : at + size, :size] = high
+            direct_pair[at : at + size, size:] = middle
+            direct_low[at : at + size] = rest
+            at += size
+        pair[2 * i * size : 2 * (i + 1) * size], low[i * size : (i + 1) * size] = stacked_blocks(stored)
     copy.wait()
 
 

time: 36 us -> 36 us (level)
  no operation moved by 1% of the time
where the time goes in v10:
time: 36 us; the launch traced here: 35.9 us
  starting transfers between devices  17.9 us (50%)
  waiting for transfers between devices  10.9 us (30%)
  Pallas kernels  6.34 us (18%)
  between operations  0.7 us (2%)
    ppermute x10, starting transfers between devices, swap(): lax.ppermute(x, axis, [(i, i ^ distance) for i in range(lax.axis_size(axi...  9.22 us
    ppermute x10, waiting for transfers between devices, swap(): lax.ppermute(x, axis, [(i, i ^ distance) for i in range(lax.axis_size(axi...  8.79 us
    ppermute x3, starting transfers between devices, swap_rows(): return lax.ppermute(x, ('row', 'nbr'), pairs)  8.69 us
    ppermute x3, waiting for transfers between devices, swap_rows(): return lax.ppermute(x, ('row', 'nbr'), pairs)  2.16 us
    pallas_call x1, Pallas kernels, body(): call(functools.partial(last_kernel, rows, total), 'last', [VMEM] * (rows...  1.25 us
    pallas_call x1, Pallas kernels, body(): call(load_kernel, 'load', [HBM] * 4, [jax.ShapeDtypeStruct(blocks.shape,...  1.14 us
    pallas_call x1, Pallas kernels, body(): call(functools.partial(factor_kernel, total), 'factor', [VMEM] * 2, [squa...  0.8 us
  transfers between devices with their start and end apart: 13, of which 9 were waited for; matrix products, arithmetic and copies ran while one was open for 0% of the time, Pallas kernels for 8%

profile of v10, /device:TPU:0, one launch (start us, length us, event | category | flops | bytes accessed | tf_op | source)
XLA Modules:
  0.0 35.9 jit_solution(15640470920055348663)
XLA Ops:
  0.6 0.5 %collective-permute-start = (f32[3,3,128,128]{3,2,1,0:T(8,128)}, f32[3,3,128,128]{3,2,1,0:T(8,128)S(1)}, u32[]{:S(2)}, u32[]{:S(2)}) collective-permute-start(f32[3,3,128,128]{3,2,1,0:T(8,128)} %blocks.1), channel_id=1, source_target_pairs={{0,1},{1,0},{2,3},{3,2},{4,5},{5,4},{6,7},{7,6},{8,9},{9,8},{10,11... | collective-permute-start | bytes 1769480 | tf_op jit(solution)/shard_map/ppermute | solution.py:77
  1.1 0.1 collective-permute-start.1
  1.2 1.1 %load.1 = (f32[3,3,128,128]{3,2,1,0:T(8,128)S(1)}, s32[3,3]{1,0:T(4,128)S(4)}, s32[3]{0:T(128)S(4)}, f32[96,128]{1,0:T(8,128)S(1)}) custom-call(f32[3,3,128,128]{3,2,1,0:T(8,128)} %blocks.1, s32[3,3]{1,0:T(4,128)} %ids.1, s32[3]{0:T(128)} %counts.1, f32[32,384]{1,0:T(8,128)} %bitcast.2), custom_call_target="tpu_custom_call" | custom-call | tf_op jit(solution)/shard_map/load/pallas_call | solution.py:374
  2.4 0.3 own_transposed.1.started
  2.7 0.3 collective-permute-done.1.other_ids
  3.0 0.0 collective-permute-done.other
  3.0 0.4 %first_transposed.1 = (f32[96,128]{1,0:T(8,128)S(1)}, f32[96,128]{1,0:T(8,128)S(1)}, f32[96,128]{1,0:T(8,128)S(1)}) custom-call(f32[3,3,128,128]{3,2,1,0:T(8,128)S(1)} %collective-permute-done.other, s32[3,3]{1,0:T(4,128)S(1)} %collective-permute-done.1.other_ids, s32[3]{0:T(128)S(4)} %get-tuple-element.28.counts, f32[96,128]{1,0:T(8,128)S(1)} %get-tuple-element.29.tiles, ...), custom_call_target="tpu_custom_call" | custom-call | tf_op jit(solution)/shard_map/first_transposed/pallas_call | solution.py:387
  3.4 4.0 %collective-permute-start.3 = (f32[96,128]{1,0:T(8,128)S(1)}, f32[96,128]{1,0:T(8,128)S(1)}, u32[]{:S(2)}, u32[]{:S(2)}) collective-permute-start(f32[96,128]{1,0:T(8,128)S(1)} %get-tuple-element.38), channel_id=1, source_target_pairs={{0,8},{1,13},{2,10},{3,15},{4,12},{5,9},{6,14},{7,11},{8,0},{9,5},... | collective-permute-start | bytes 147464 | tf_op jit(solution)/shard_map/ppermute | solution.py:85
  7.4 1.6 %collective-permute-start.2 = (f32[96,128]{1,0:T(8,128)S(1)}, f32[96,128]{1,0:T(8,128)S(1)}, u32[]{:S(2)}, u32[]{:S(2)}) collective-permute-start(f32[96,128]{1,0:T(8,128)S(1)} %get-tuple-element.37), channel_id=1, source_target_pairs={{0,4},{4,0},{8,12},{12,8},{1,5},{5,1},{9,13},{13,9},{2,6},{6,2},{1... | collective-permute-start | bytes 147464 | tf_op jit(solution)/shard_map/ppermute | solution.py:77
  9.0 1.2 %collective-permute-done.3.refs_1_ = f32[96,128]{1,0:T(8,128)S(1)} collective-permute-done((f32[96,128]{1,0:T(8,128)S(1)}, f32[96,128]{1,0:T(8,128)S(1)}, u32[]{:S(2)}, u32[]{:S(2)}) %collective-permute-start.3) | collective-permute-done | bytes 49184 | tf_op jit(solution)/shard_map/ppermute | solution.py:85
  10.1 0.0 collective-permute-start.4
  10.2 0.6 %split.1 = (bf16[2304,256]{1,0:T(8,128)(2,1)S(1)}, bf16[2304,128]{1,0:T(8,128)(2,1)S(1)}, bf16[768,768]{1,0:T(8,128)(2,1)S(1)}, bf16[384,768]{1,0:T(8,128)(2,1)S(1)}, s32[3,3]{1,0:T(4,128)S(4)}) custom-call(f32[3,3,128,128]{3,2,1,0:T(8,128)S(1)} %get-tuple-element.27.held, f32[3,3,128,128]{3,2,1,0:T(8,128)S(1)} %collective-permute-done.other, ...), custom_call_target="tpu_custom_call" | custom-call | tf_op jit(solution)/shard_map/split/pallas_call | solution.py:398
  10.8 1.1 %collective-permute-done.2.refs_0_ = f32[96,128]{1,0:T(8,128)S(1)} collective-permute-done((f32[96,128]{1,0:T(8,128)S(1)}, f32[96,128]{1,0:T(8,128)S(1)}, u32[]{:S(2)}, u32[]{:S(2)}) %collective-permute-start.2) | collective-permute-done | bytes 49184 | tf_op jit(solution)/shard_map/ppermute | solution.py:77
  11.9 0.0 collective-permute-done.4.refs_2_
  11.9 0.4 %first_direct.1.refs_0_ = f32[96,128]{1,0:T(8,128)S(1)} custom-call(bf16[2304,256]{1,0:T(8,128)(2,1)S(1)} %get-tuple-element.32.pair, bf16[2304,128]{1,0:T(8,128)(2,1)S(1)} %get-tuple-element.33.low, s32[3,3]{1,0:T(4,128)S(4)} %get-tuple-element.30.ids, s32[3,3]{1,0:T(4,128)S(4)} %get-tuple-element.34.other_ids, s32[3]{0:T(128)S(4)} %get-tuple-element.28.counts, ...), custom_call_target="tpu_custom_call" | custom-call | tf_op jit(solution)/shard_map/first_direct/pallas_call | solution.py:413
  12.4 1.6 %collective-permute-start.5 = (f32[96,128]{1,0:T(8,128)S(1)}, f32[96,128]{1,0:T(8,128)S(1)}, u32[]{:S(2)}, u32[]{:S(2)}) collective-permute-start(f32[96,128]{1,0:T(8,128)S(1)} %first_direct.1.refs_0_), channel_id=1, source_target_pairs={{0,2},{1,3},{2,0},{3,1},{4,6},{5,7},{6,4},{7,5},{8,10},{9,11},{10,... | collective-permute-start | bytes 147464 | tf_op jit(solution)/shard_map/ppermute | solution.py:77
  13.9 2.6 %collective-permute-done.5.refs_1_ = f32[96,128]{1,0:T(8,128)S(1)} collective-permute-done((f32[96,128]{1,0:T(8,128)S(1)}, f32[96,128]{1,0:T(8,128)S(1)}, u32[]{:S(2)}, u32[]{:S(2)}) %collective-permute-start.5) | collective-permute-done | bytes 49184 | tf_op jit(solution)/shard_map/ppermute | solution.py:77
  16.5 0.5 %second_transposed.1 = (f32[104,128]{1,0:T(8,128)S(1)}, f32[104,128]{1,0:T(8,128)S(1)}, f32[96,128]{1,0:T(8,128)S(1)}, f32[96,128]{1,0:T(8,128)S(1)}, f32[8,128]{1,0:T(8,128)S(1)}) custom-call(bf16[768,768]{1,0:T(8,128)(2,1)S(1)} %get-tuple-element.35.pair, bf16[384,768]{1,0:T(8,128)(2,1)S(1)} %get-tuple-element.36.low, s32[3,3]{1,0:T(4,128)S(4)} %get-tuple-element.30.ids, ...), custom_call_target="tpu_custom_call" | custom-call | tf_op jit(solution)/shard_map/second_transposed/pallas_call | solution.py:417
  17.0 2.1 %collective-permute-start.7 = (f32[104,128]{1,0:T(8,128)S(1)}, f32[104,128]{1,0:T(8,128)S(1)}, u32[]{:S(2)}, u32[]{:S(2)}) collective-permute-start(f32[104,128]{1,0:T(8,128)S(1)} %get-tuple-element.42), channel_id=1, source_target_pairs={{0,8},{1,13},{2,10},{3,15},{4,12},{5,9},{6,14},{7,11},{8,0},{9,5},... | collective-permute-start | bytes 159752 | tf_op jit(solution)/shard_map/ppermute | solution.py:85
  19.2 2.1 %collective-permute-start.6 = (f32[104,128]{1,0:T(8,128)S(1)}, f32[104,128]{1,0:T(8,128)S(1)}, u32[]{:S(2)}, u32[]{:S(2)}) collective-permute-start(f32[104,128]{1,0:T(8,128)S(1)} %get-tuple-element.41), channel_id=1, source_target_pairs={{0,4},{4,0},{8,12},{12,8},{1,5},{5,1},{9,13},{13,9},{2,6},{6,2},{1... | collective-permute-start | bytes 159752 | tf_op jit(solution)/shard_map/ppermute | solution.py:77
  21.3 0.8 %collective-permute-done.7.refs_1_ = f32[104,128]{1,0:T(8,128)S(1)} collective-permute-done((f32[104,128]{1,0:T(8,128)S(1)}, f32[104,128]{1,0:T(8,128)S(1)}, u32[]{:S(2)}, u32[]{:S(2)}) %collective-permute-start.7) | collective-permute-done | bytes 53280 | tf_op jit(solution)/shard_map/ppermute | solution.py:85
  22.1 0.0 collective-permute-start.8
  22.1 1.3 %collective-permute-done.6.refs_0_ = f32[104,128]{1,0:T(8,128)S(1)} collective-permute-done((f32[104,128]{1,0:T(8,128)S(1)}, f32[104,128]{1,0:T(8,128)S(1)}, u32[]{:S(2)}, u32[]{:S(2)}) %collective-permute-start.6) | collective-permute-done | bytes 53280 | tf_op jit(solution)/shard_map/ppermute | solution.py:77
  23.4 0.0 collective-permute-done.8.refs_2_
  23.4 0.4 %second_direct.1 = (f32[96,128]{1,0:T(8,128)S(1)}, f32[8,128]{1,0:T(8,128)S(1)}) custom-call(bf16[2304,256]{1,0:T(8,128)(2,1)S(1)} %get-tuple-element.32.pair, bf16[2304,128]{1,0:T(8,128)(2,1)S(1)} %get-tuple-element.33.low, s32[3,3]{1,0:T(4,128)S(4)} %get-tuple-element.30.ids, s32[3,3]{1,0:T(4,128)S(4)} %get-tuple-element.34.other_ids, ...), custom_call_target="tpu_custom_call" | custom-call | tf_op jit(solution)/shard_map/second_direct/pallas_call | solution.py:425
  23.8 1.5 %collective-permute-start.9 = (f32[96,128]{1,0:T(8,128)S(1)}, f32[96,128]{1,0:T(8,128)S(1)}, u32[]{:S(2)}, u32[]{:S(2)}) collective-permute-start(f32[96,128]{1,0:T(8,128)S(1)} %get-tuple-element.47.refs_0_), channel_id=1, source_target_pairs={{0,2},{1,3},{2,0},{3,1},{4,6},{5,7},{6,4},{7,5},{8,10},{9,11},{10,... | collective-permute-start | bytes 147464 | tf_op jit(solution)/shard_map/ppermute | solution.py:77
  25.4 0.8 %factor.1 = (f32[32,32]{1,0:T(8,128)S(1)}, f32[32,384]{1,0:T(8,128)S(1)}) custom-call(f32[8,128]{1,0:T(8,128)S(1)} %get-tuple-element.44.gram, f32[96,128]{1,0:T(8,128)S(1)} %get-tuple-element.40.tiles), custom_call_target="tpu_custom_call" | custom-call | tf_op jit(solution)/shard_map/factor/pallas_call | solution.py:429
  26.2 1.8 %collective-permute-done.9.refs_1_ = f32[96,128]{1,0:T(8,128)S(1)} collective-permute-done((f32[96,128]{1,0:T(8,128)S(1)}, f32[96,128]{1,0:T(8,128)S(1)}, u32[]{:S(2)}, u32[]{:S(2)}) %collective-permute-start.9) | collective-permute-done | bytes 49184 | tf_op jit(solution)/shard_map/ppermute | solution.py:77
  28.0 0.5 %gram.1 = (f32[32,384]{1,0:T(8,128)S(1)}, f32[16,128]{1,0:T(8,128)S(1)}) custom-call(f32[32,32]{1,0:T(8,128)S(1)} %get-tuple-element.45.inverse, f32[32,384]{1,0:T(8,128)S(1)} %get-tuple-element.46.prior, f32[96,128]{1,0:T(8,128)S(1)} %get-tuple-element.47.refs_0_, f32[96,128]{1,0:T(8,128)S(1)} %collective-permute-done.9.refs_1_), custom_call_target="tpu_custom_call" | custom-call | tf_op jit(solution)/shard_map/gram/pallas_call | solution.py:430
  28.4 2.5 %collective-permute-start.11 = (f32[16,128]{1,0:T(8,128)S(1)}, f32[16,128]{1,0:T(8,128)S(1)}, u32[]{:S(2)}, u32[]{:S(2)}) collective-permute-start(f32[16,128]{1,0:T(8,128)S(1)} %get-tuple-element.49.mine), channel_id=1, source_target_pairs={{0,8},{1,13},{2,10},{3,15},{4,12},{5,9},{6,14},{7,11},{8,0},{9,5},... | collective-permute-start | bytes 24584 | tf_op jit(solution)/shard_map/ppermute | solution.py:85
  31.0 1.8 %collective-permute-start.10 = (f32[16,128]{1,0:T(8,128)S(1)}, f32[16,128]{1,0:T(8,128)S(1)}, u32[]{:S(2)}, u32[]{:S(2)}) collective-permute-start(f32[16,128]{1,0:T(8,128)S(1)} %get-tuple-element.49.mine), channel_id=1, source_target_pairs={{0,4},{4,0},{8,12},{12,8},{1,5},{5,1},{9,13},{13,9},{2,6},{6,2},{1... | collective-permute-start | bytes 24584 | tf_op jit(solution)/shard_map/ppermute | solution.py:77
  32.8 0.2 collective-permute-done.11.refs_1_
  33.0 0.0 collective-permute-start.12
  33.0 1.6 %collective-permute-done.10.refs_0_ = f32[16,128]{1,0:T(8,128)S(1)} collective-permute-done((f32[16,128]{1,0:T(8,128)S(1)}, f32[16,128]{1,0:T(8,128)S(1)}, u32[]{:S(2)}, u32[]{:S(2)}) %collective-permute-start.10) | collective-permute-done | bytes 8224 | tf_op jit(solution)/shard_map/ppermute | solution.py:77
  34.6 0.0 collective-permute-done.12.refs_2_
  34.6 1.3 %last.1 = (f32[32,384]{1,0:T(8,128)}, f32[32,32]{1,0:T(8,128)}) custom-call(f32[32,384]{1,0:T(8,128)S(1)} %get-tuple-element.48.image, f32[16,128]{1,0:T(8,128)S(1)} %get-tuple-element.49.mine, f32[16,128]{1,0:T(8,128)S(1)} %collective-permute-done.10.refs_0_, f32[16,128]{1,0:T(8,128)S(1)} %collective-permute-done.11.refs_1_, ...), custom_call_target="tpu_custom_call" | custom-call | tf_op jit(solution)/shard_map/last/pallas_call | solution.py:434
Async XLA Ops:
  0.6 2.4 %collective-permute-start = (f32[3,3,128,128]{3,2,1,0:T(8,128)}, f32[3,3,128,128]{3,2,1,0:T(8,128)S(1)}, u32[]{:S(2)}, u32[]{:S(2)}) collective-permute-start(f32[3,3,128,128]{3,2,1,0:T(8,128)} %blocks.1), channel_id=1, source_target_pairs={{0,1},{1,0},{2,3},{3,2},{4,5},{5,4},{6,7},{7,6},{8,9},{9,8},{10,11... | collective-permute-start | bytes 1769480 | tf_op jit(solution)/shard_map/ppermute | solution.py:77
  1.1 1.8 %collective-permute-start.1 = (s32[3,3]{1,0:T(4,128)}, s32[3,3]{1,0:T(4,128)S(1)}, u32[]{:S(2)}, u32[]{:S(2)}) collective-permute-start(s32[3,3]{1,0:T(4,128)} %ids.1), channel_id=1, source_target_pairs={{0,1},{1,0},{2,3},{3,2},{4,5},{5,4},{6,7},{7,6},{8,9},{9,8},{10,11... | collective-permute-start | bytes 116 | tf_op jit(solution)/shard_map/ppermute | solution.py:77
  3.4 6.8 %collective-permute-start.3 = (f32[96,128]{1,0:T(8,128)S(1)}, f32[96,128]{1,0:T(8,128)S(1)}, u32[]{:S(2)}, u32[]{:S(2)}) collective-permute-start(f32[96,128]{1,0:T(8,128)S(1)} %get-tuple-element.38), channel_id=1, source_target_pairs={{0,8},{1,13},{2,10},{3,15},{4,12},{5,9},{6,14},{7,11},{8,0},{9,5},... | collective-permute-start | bytes 147464 | tf_op jit(solution)/shard_map/ppermute | solution.py:85
  7.4 4.5 %collective-permute-start.2 = (f32[96,128]{1,0:T(8,128)S(1)}, f32[96,128]{1,0:T(8,128)S(1)}, u32[]{:S(2)}, u32[]{:S(2)}) collective-permute-start(f32[96,128]{1,0:T(8,128)S(1)} %get-tuple-element.37), channel_id=1, source_target_pairs={{0,4},{4,0},{8,12},{12,8},{1,5},{5,1},{9,13},{13,9},{2,6},{6,2},{1... | collective-permute-start | bytes 147464 | tf_op jit(solution)/shard_map/ppermute | solution.py:77
  10.1 1.8 %collective-permute-start.4 = (f32[96,128]{1,0:T(8,128)S(1)}, f32[96,128]{1,0:T(8,128)S(1)}, u32[]{:S(2)}, u32[]{:S(2)}) collective-permute-start(f32[96,128]{1,0:T(8,128)S(1)} %collective-permute-done.3.refs_1_), channel_id=1, source_target_pairs={{0,1},{1,0},{2,3},{3,2},{4,5},{5,4},{6,7},{7,6},{8,9},{9,8},{10,11... | collective-permute-start | bytes 147464 | tf_op jit(solution)/shard_map/ppermute | solution.py:77
  12.4 4.2 %collective-permute-start.5 = (f32[96,128]{1,0:T(8,128)S(1)}, f32[96,128]{1,0:T(8,128)S(1)}, u32[]{:S(2)}, u32[]{:S(2)}) collective-permute-start(f32[96,128]{1,0:T(8,128)S(1)} %first_direct.1.refs_0_), channel_id=1, source_target_pairs={{0,2},{1,3},{2,0},{3,1},{4,6},{5,7},{6,4},{7,5},{8,10},{9,11},{10,... | collective-permute-start | bytes 147464 | tf_op jit(solution)/shard_map/ppermute | solution.py:77
  17.0 5.0 %collective-permute-start.7 = (f32[104,128]{1,0:T(8,128)S(1)}, f32[104,128]{1,0:T(8,128)S(1)}, u32[]{:S(2)}, u32[]{:S(2)}) collective-permute-start(f32[104,128]{1,0:T(8,128)S(1)} %get-tuple-element.42), channel_id=1, source_target_pairs={{0,8},{1,13},{2,10},{3,15},{4,12},{5,9},{6,14},{7,11},{8,0},{9,5},... | collective-permute-start | bytes 159752 | tf_op jit(solution)/shard_map/ppermute | solution.py:85
  19.2 4.2 %collective-permute-start.6 = (f32[104,128]{1,0:T(8,128)S(1)}, f32[104,128]{1,0:T(8,128)S(1)}, u32[]{:S(2)}, u32[]{:S(2)}) collective-permute-start(f32[104,128]{1,0:T(8,128)S(1)} %get-tuple-element.41), channel_id=1, source_target_pairs={{0,4},{4,0},{8,12},{12,8},{1,5},{5,1},{9,13},{13,9},{2,6},{6,2},{1... | collective-permute-start | bytes 159752 | tf_op jit(solution)/shard_map/ppermute | solution.py:77
  22.1 1.3 %collective-permute-start.8 = (f32[104,128]{1,0:T(8,128)S(1)}, f32[104,128]{1,0:T(8,128)S(1)}, u32[]{:S(2)}, u32[]{:S(2)}) collective-permute-start(f32[104,128]{1,0:T(8,128)S(1)} %collective-permute-done.7.refs_1_), channel_id=1, source_target_pairs={{0,1},{1,0},{2,3},{3,2},{4,5},{5,4},{6,7},{7,6},{8,9},{9,8},{10,11... | collective-permute-start | bytes 159752 | tf_op jit(solution)/shard_map/ppermute | solution.py:77
  23.8 4.2 %collective-permute-start.9 = (f32[96,128]{1,0:T(8,128)S(1)}, f32[96,128]{1,0:T(8,128)S(1)}, u32[]{:S(2)}, u32[]{:S(2)}) collective-permute-start(f32[96,128]{1,0:T(8,128)S(1)} %get-tuple-element.47.refs_0_), channel_id=1, source_target_pairs={{0,2},{1,3},{2,0},{3,1},{4,6},{5,7},{6,4},{7,5},{8,10},{9,11},{10,... | collective-permute-start | bytes 147464 | tf_op jit(solution)/shard_map/ppermute | solution.py:77
  28.4 4.6 %collective-permute-start.11 = (f32[16,128]{1,0:T(8,128)S(1)}, f32[16,128]{1,0:T(8,128)S(1)}, u32[]{:S(2)}, u32[]{:S(2)}) collective-permute-start(f32[16,128]{1,0:T(8,128)S(1)} %get-tuple-element.49.mine), channel_id=1, source_target_pairs={{0,8},{1,13},{2,10},{3,15},{4,12},{5,9},{6,14},{7,11},{8,0},{9,5},... | collective-permute-start | bytes 24584 | tf_op jit(solution)/shard_map/ppermute | solution.py:85
  31.0 3.7 %collective-permute-start.10 = (f32[16,128]{1,0:T(8,128)S(1)}, f32[16,128]{1,0:T(8,128)S(1)}, u32[]{:S(2)}, u32[]{:S(2)}) collective-permute-start(f32[16,128]{1,0:T(8,128)S(1)} %get-tuple-element.49.mine), channel_id=1, source_target_pairs={{0,4},{4,0},{8,12},{12,8},{1,5},{5,1},{9,13},{13,9},{2,6},{6,2},{1... | collective-permute-start | bytes 24584 | tf_op jit(solution)/shard_map/ppermute | solution.py:77
  33.0 1.6 %collective-permute-start.12 = (f32[16,128]{1,0:T(8,128)S(1)}, f32[16,128]{1,0:T(8,128)S(1)}, u32[]{:S(2)}, u32[]{:S(2)}) collective-permute-start(f32[16,128]{1,0:T(8,128)S(1)} %collective-permute-done.11.refs_1_), channel_id=1, source_target_pairs={{0,1},{1,0},{2,3},{3,2},{4,5},{5,4},{6,7},{7,6},{8,9},{9,8},{10,11... | collective-permute-start | bytes 24584 | tf_op jit(solution)/shard_map/ppermute | solution.py:77

commit v11 on v10

--- a/solution.py
+++ b/solution.py
@@ -77,10 +77,10 @@
     return lax.ppermute(x, axis, [(i, i ^ distance) for i in range(lax.axis_size(axis))])
 
 
-def swap_rows(x, even, odd):
+def swap_rows(x, even, odd, across=0):
     rows, parts = lax.axis_size("row"), lax.axis_size("nbr")
     pairs = [
-        (r * parts + n, (r ^ (odd if n % 2 else even)) * parts + n) for r in range(rows) for n in range(parts)
+        (r * parts + n, (r ^ (odd if n % 2 else even)) * parts + (n ^ across)) for r in range(rows) for n in range(parts)
     ]
     return lax.ppermute(x, ("row", "nbr"), pairs)
 
@@ -92,8 +92,8 @@
         self.odd = self.part & 1
         self.block_rows, self.slots = block_rows, slots
         self.first_row = self.row * self.block_rows
-        self.peers = [self.row ^ 1] + [self.row ^ (k + self.odd) for k in range(2, rows, 2)]
-        self.others_peers = [self.row ^ (k + 1 - self.odd) for k in range(2, rows, 2)]
+        self.peers = [self.row ^ (k + self.odd) for k in range(1, rows - 1, 2)] + [self.row ^ (rows - 1)]
+        self.others_peers = [self.row ^ (k + 1 - self.odd) for k in range(1, rows - 1, 2)]
         self.columns = columns
 
     def column(self, ids, m, i, p):
@@ -108,8 +108,8 @@
         return slice(i * self.columns, (i + 1) * self.columns)
 
     def by_distance(self, mine, received, handed):
-        both = [(jnp.where(self.odd == 0, a, b), jnp.where(self.odd == 0, b, a)) for a, b in zip(received[1:], handed)]
-        return [mine, received[0]] + [x for pair in both for x in pair]
+        both = [(jnp.where(self.odd == 0, a, b), jnp.where(self.odd == 0, b, a)) for a, b in zip(received, handed)]
+        return [mine] + [x for pair in both for x in pair] + [received[-1]]
 
 
 def stacked_blocks(blocks):
@@ -362,12 +362,12 @@
         )
 
     def round_over_rows(messages):
-        received = [swap_rows(m, 2 * k, 2 * k + 1) for k, m in enumerate(messages[1:], 1)]
-        near = swap(messages[0], "row", 1)
-        return [near] + received + [swap(m, "nbr", 1) for m in received]
+        received = [swap_rows(m, 2 * k - 1, 2 * k) for k, m in enumerate(messages[:-1], 1)]
+        last = swap_rows(messages[-1], rows - 1, rows - 1, 1)
+        return received + [last] + [swap(m, "nbr", 1) for m in received]
 
     def sum_over_pairs(image):
-        return [image] + [swap(image, "nbr", s) for s in range(2, parts, 2)]
+        return [image] + [swap(image, "nbr", s + 0) for s in range(2, parts, 2)]
 
     other = swap(blocks, "nbr", 1)
     other_ids = swap(partner_ids, "nbr", 1)

time: 36 us -> 35.3 us (0.981)
  starting transfers between devices: 17.9 us -> 12.9 us
  waiting for transfers between devices: 10.9 us -> 15.3 us
    ppermute x3 -> x6, waiting for transfers between devices: 2.16 us -> 10.2 us  [swap_rows(): return lax.ppermute(x, ('row', 'nbr'), pairs)]
    ppermute x10 -> x7, starting transfers between devices: 9.22 us -> 4.23 us  [swap(): lax.ppermute(x, axis, [(i, i ^ distance) for i in range(lax.axis_size(axi...]
    ppermute x10 -> x7, waiting for transfers between devices: 8.79 us -> 5.11 us  [swap(): lax.ppermute(x, axis, [(i, i ^ distance) for i in range(lax.axis_size(axi...]
    ppermute x3 -> x6, starting transfers between devices: 8.69 us -> 8.64 us  [swap_rows(): return lax.ppermute(x, ('row', 'nbr'), pairs)]
where the time goes in v11:
time: 35.3 us; the launch traced here: 35.2 us
  waiting for transfers between devices  15.3 us (43%)
  starting transfers between devices  12.9 us (37%)
  Pallas kernels  6.32 us (18%)
  between operations  0.69 us (2%)
    ppermute x6, waiting for transfers between devices, swap_rows(): return lax.ppermute(x, ('row', 'nbr'), pairs)  10.2 us
    ppermute x6, starting transfers between devices, swap_rows(): return lax.ppermute(x, ('row', 'nbr'), pairs)  8.64 us
    ppermute x7, waiting for transfers between devices, swap(): lax.ppermute(x, axis, [(i, i ^ distance) for i in range(lax.axis_size(axi...  5.11 us
    ppermute x7, starting transfers between devices, swap(): lax.ppermute(x, axis, [(i, i ^ distance) for i in range(lax.axis_size(axi...  4.23 us
    pallas_call x1, Pallas kernels, body(): call(functools.partial(last_kernel, rows, total), 'last', [VMEM] * (rows...  1.25 us
    pallas_call x1, Pallas kernels, body(): call(load_kernel, 'load', [HBM] * 4, [jax.ShapeDtypeStruct(blocks.shape,...  1.14 us
    pallas_call x1, Pallas kernels, body(): call(functools.partial(factor_kernel, total), 'factor', [VMEM] * 2, [squa...  0.8 us
  transfers between devices with their start and end apart: 13, of which 9 were waited for; matrix products, arithmetic and copies ran while one was open for 0% of the time, Pallas kernels for 8%

profile of v11, /device:TPU:0, one launch (start us, length us, event | category | flops | bytes accessed | tf_op | source)
XLA Modules:
  0.0 35.2 jit_solution(7755744731732952088)
XLA Ops:
  0.6 0.5 %collective-permute-start = (f32[3,3,128,128]{3,2,1,0:T(8,128)}, f32[3,3,128,128]{3,2,1,0:T(8,128)S(1)}, u32[]{:S(2)}, u32[]{:S(2)}) collective-permute-start(f32[3,3,128,128]{3,2,1,0:T(8,128)} %blocks.1), channel_id=1, source_target_pairs={{0,1},{1,0},{2,3},{3,2},{4,5},{5,4},{6,7},{7,6},{8,9},{9,8},{10,11... | collective-permute-start | bytes 1769480 | tf_op jit(solution)/shard_map/ppermute | solution.py:77
  1.1 0.1 collective-permute-start.1
  1.2 1.1 %load.1 = (f32[3,3,128,128]{3,2,1,0:T(8,128)S(1)}, s32[3,3]{1,0:T(4,128)S(4)}, s32[3]{0:T(128)S(4)}, f32[96,128]{1,0:T(8,128)S(1)}) custom-call(f32[3,3,128,128]{3,2,1,0:T(8,128)} %blocks.1, s32[3,3]{1,0:T(4,128)} %ids.1, s32[3]{0:T(128)} %counts.1, f32[32,384]{1,0:T(8,128)} %bitcast.2), custom_call_target="tpu_custom_call" | custom-call | tf_op jit(solution)/shard_map/load/pallas_call | solution.py:374
  2.4 0.3 own_transposed.1.started
  2.7 0.3 collective-permute-done.1.other_ids
  3.0 0.0 collective-permute-done.other
  3.0 0.4 %first_transposed.1 = (f32[96,128]{1,0:T(8,128)S(1)}, f32[96,128]{1,0:T(8,128)S(1)}, f32[96,128]{1,0:T(8,128)S(1)}) custom-call(f32[3,3,128,128]{3,2,1,0:T(8,128)S(1)} %collective-permute-done.other, s32[3,3]{1,0:T(4,128)S(1)} %collective-permute-done.1.other_ids, s32[3]{0:T(128)S(4)} %get-tuple-element.28.counts, f32[96,128]{1,0:T(8,128)S(1)} %get-tuple-element.29.tiles, ...), custom_call_target="tpu_custom_call" | custom-call | tf_op jit(solution)/shard_map/first_transposed/pallas_call | solution.py:387
  3.4 3.0 %collective-permute-start.2 = (f32[96,128]{1,0:T(8,128)S(1)}, f32[96,128]{1,0:T(8,128)S(1)}, u32[]{:S(2)}, u32[]{:S(2)}) collective-permute-start(f32[96,128]{1,0:T(8,128)S(1)} %get-tuple-element.37), channel_id=1, source_target_pairs={{0,4},{1,9},{2,6},{3,11},{4,0},{5,13},{6,2},{7,15},{8,12},{9,1},{1... | collective-permute-start | bytes 147464 | tf_op jit(solution)/shard_map/ppermute | solution.py:85
  6.4 1.8 %collective-permute-start.3 = (f32[96,128]{1,0:T(8,128)S(1)}, f32[96,128]{1,0:T(8,128)S(1)}, u32[]{:S(2)}, u32[]{:S(2)}) collective-permute-start(f32[96,128]{1,0:T(8,128)S(1)} %get-tuple-element.38), channel_id=1, source_target_pairs={{0,13},{1,12},{2,15},{3,14},{4,9},{5,8},{6,11},{7,10},{8,5},{9,4},... | collective-permute-start | bytes 147464 | tf_op jit(solution)/shard_map/ppermute | solution.py:85
  8.2 0.2 collective-permute-done.2.refs_0_
  8.5 0.5 %collective-permute-start.4 = (f32[96,128]{1,0:T(8,128)S(1)}, f32[96,128]{1,0:T(8,128)S(1)}, u32[]{:S(2)}, u32[]{:S(2)}) collective-permute-start(f32[96,128]{1,0:T(8,128)S(1)} %collective-permute-done.2.refs_0_), channel_id=1, source_target_pairs={{0,1},{1,0},{2,3},{3,2},{4,5},{5,4},{6,7},{7,6},{8,9},{9,8},{10,11... | collective-permute-start | bytes 147464 | tf_op jit(solution)/shard_map/ppermute | solution.py:77
  9.0 0.6 %split.1 = (bf16[2304,256]{1,0:T(8,128)(2,1)S(1)}, bf16[2304,128]{1,0:T(8,128)(2,1)S(1)}, bf16[768,768]{1,0:T(8,128)(2,1)S(1)}, bf16[384,768]{1,0:T(8,128)(2,1)S(1)}, s32[3,3]{1,0:T(4,128)S(4)}) custom-call(f32[3,3,128,128]{3,2,1,0:T(8,128)S(1)} %get-tuple-element.27.held, f32[3,3,128,128]{3,2,1,0:T(8,128)S(1)} %collective-permute-done.other, ...), custom_call_target="tpu_custom_call" | custom-call | tf_op jit(solution)/shard_map/split/pallas_call | solution.py:398
  9.6 2.1 %collective-permute-done.3.refs_1_ = f32[96,128]{1,0:T(8,128)S(1)} collective-permute-done((f32[96,128]{1,0:T(8,128)S(1)}, f32[96,128]{1,0:T(8,128)S(1)}, u32[]{:S(2)}, u32[]{:S(2)}) %collective-permute-start.3) | collective-permute-done | bytes 49184 | tf_op jit(solution)/shard_map/ppermute | solution.py:85
  11.7 0.0 collective-permute-done.4.refs_2_
  11.7 0.4 %first_direct.1.refs_0_ = f32[96,128]{1,0:T(8,128)S(1)} custom-call(bf16[2304,256]{1,0:T(8,128)(2,1)S(1)} %get-tuple-element.32.pair, bf16[2304,128]{1,0:T(8,128)(2,1)S(1)} %get-tuple-element.33.low, s32[3,3]{1,0:T(4,128)S(4)} %get-tuple-element.30.ids, s32[3,3]{1,0:T(4,128)S(4)} %get-tuple-element.34.other_ids, s32[3]{0:T(128)S(4)} %get-tuple-element.28.counts, ...), custom_call_target="tpu_custom_call" | custom-call | tf_op jit(solution)/shard_map/first_direct/pallas_call | solution.py:413
  12.2 1.6 %collective-permute-start.5 = (f32[96,128]{1,0:T(8,128)S(1)}, f32[96,128]{1,0:T(8,128)S(1)}, u32[]{:S(2)}, u32[]{:S(2)}) collective-permute-start(f32[96,128]{1,0:T(8,128)S(1)} %first_direct.1.refs_0_), channel_id=1, source_target_pairs={{0,2},{1,3},{2,0},{3,1},{4,6},{5,7},{6,4},{7,5},{8,10},{9,11},{10,... | collective-permute-start | bytes 147464 | tf_op jit(solution)/shard_map/ppermute | solution.py:77
  13.7 3.0 %collective-permute-done.5.refs_1_ = f32[96,128]{1,0:T(8,128)S(1)} collective-permute-done((f32[96,128]{1,0:T(8,128)S(1)}, f32[96,128]{1,0:T(8,128)S(1)}, u32[]{:S(2)}, u32[]{:S(2)}) %collective-permute-start.5) | collective-permute-done | bytes 49184 | tf_op jit(solution)/shard_map/ppermute | solution.py:77
  16.7 0.5 %second_transposed.1 = (f32[104,128]{1,0:T(8,128)S(1)}, f32[104,128]{1,0:T(8,128)S(1)}, f32[96,128]{1,0:T(8,128)S(1)}, f32[96,128]{1,0:T(8,128)S(1)}, f32[8,128]{1,0:T(8,128)S(1)}) custom-call(bf16[768,768]{1,0:T(8,128)(2,1)S(1)} %get-tuple-element.35.pair, bf16[384,768]{1,0:T(8,128)(2,1)S(1)} %get-tuple-element.36.low, s32[3,3]{1,0:T(4,128)S(4)} %get-tuple-element.30.ids, ...), custom_call_target="tpu_custom_call" | custom-call | tf_op jit(solution)/shard_map/second_transposed/pallas_call | solution.py:417
  17.3 0.1 collective-permute-start.6
  17.3 1.5 %collective-permute-start.7 = (f32[104,128]{1,0:T(8,128)S(1)}, f32[104,128]{1,0:T(8,128)S(1)}, u32[]{:S(2)}, u32[]{:S(2)}) collective-permute-start(f32[104,128]{1,0:T(8,128)S(1)} %get-tuple-element.42), channel_id=1, source_target_pairs={{0,13},{1,12},{2,15},{3,14},{4,9},{5,8},{6,11},{7,10},{8,5},{9,4},... | collective-permute-start | bytes 159752 | tf_op jit(solution)/shard_map/ppermute | solution.py:85
  18.8 3.1 %collective-permute-done.6.refs_0_ = f32[104,128]{1,0:T(8,128)S(1)} collective-permute-done((f32[104,128]{1,0:T(8,128)S(1)}, f32[104,128]{1,0:T(8,128)S(1)}, u32[]{:S(2)}, u32[]{:S(2)}) %collective-permute-start.6) | collective-permute-done | bytes 53280 | tf_op jit(solution)/shard_map/ppermute | solution.py:85
  21.9 0.0 collective-permute-start.8
  21.9 1.5 %collective-permute-done.7.refs_1_ = f32[104,128]{1,0:T(8,128)S(1)} collective-permute-done((f32[104,128]{1,0:T(8,128)S(1)}, f32[104,128]{1,0:T(8,128)S(1)}, u32[]{:S(2)}, u32[]{:S(2)}) %collective-permute-start.7) | collective-permute-done | bytes 53280 | tf_op jit(solution)/shard_map/ppermute | solution.py:85
  23.4 0.0 collective-permute-done.8.refs_2_
  23.4 0.4 %second_direct.1 = (f32[96,128]{1,0:T(8,128)S(1)}, f32[8,128]{1,0:T(8,128)S(1)}) custom-call(bf16[2304,256]{1,0:T(8,128)(2,1)S(1)} %get-tuple-element.32.pair, bf16[2304,128]{1,0:T(8,128)(2,1)S(1)} %get-tuple-element.33.low, s32[3,3]{1,0:T(4,128)S(4)} %get-tuple-element.30.ids, s32[3,3]{1,0:T(4,128)S(4)} %get-tuple-element.34.other_ids, ...), custom_call_target="tpu_custom_call" | custom-call | tf_op jit(solution)/shard_map/second_direct/pallas_call | solution.py:425
  23.8 1.6 %collective-permute-start.9 = (f32[96,128]{1,0:T(8,128)S(1)}, f32[96,128]{1,0:T(8,128)S(1)}, u32[]{:S(2)}, u32[]{:S(2)}) collective-permute-start(f32[96,128]{1,0:T(8,128)S(1)} %get-tuple-element.47.refs_0_), channel_id=1, source_target_pairs={{0,2},{1,3},{2,0},{3,1},{4,6},{5,7},{6,4},{7,5},{8,10},{9,11},{10,... | collective-permute-start | bytes 147464 | tf_op jit(solution)/shard_map/ppermute | solution.py:77
  25.4 0.8 %factor.1 = (f32[32,32]{1,0:T(8,128)S(1)}, f32[32,384]{1,0:T(8,128)S(1)}) custom-call(f32[8,128]{1,0:T(8,128)S(1)} %get-tuple-element.44.gram, f32[96,128]{1,0:T(8,128)S(1)} %get-tuple-element.40.tiles), custom_call_target="tpu_custom_call" | custom-call | tf_op jit(solution)/shard_map/factor/pallas_call | solution.py:429
  26.2 1.8 %collective-permute-done.9.refs_1_ = f32[96,128]{1,0:T(8,128)S(1)} collective-permute-done((f32[96,128]{1,0:T(8,128)S(1)}, f32[96,128]{1,0:T(8,128)S(1)}, u32[]{:S(2)}, u32[]{:S(2)}) %collective-permute-start.9) | collective-permute-done | bytes 49184 | tf_op jit(solution)/shard_map/ppermute | solution.py:77
  27.9 0.5 %gram.1 = (f32[32,384]{1,0:T(8,128)S(1)}, f32[16,128]{1,0:T(8,128)S(1)}) custom-call(f32[32,32]{1,0:T(8,128)S(1)} %get-tuple-element.45.inverse, f32[32,384]{1,0:T(8,128)S(1)} %get-tuple-element.46.prior, f32[96,128]{1,0:T(8,128)S(1)} %get-tuple-element.47.refs_0_, f32[96,128]{1,0:T(8,128)S(1)} %collective-permute-done.9.refs_1_), custom_call_target="tpu_custom_call" | custom-call | tf_op jit(solution)/shard_map/gram/pallas_call | solution.py:430
  28.4 0.6 %collective-permute-start.10 = (f32[16,128]{1,0:T(8,128)S(1)}, f32[16,128]{1,0:T(8,128)S(1)}, u32[]{:S(2)}, u32[]{:S(2)}) collective-permute-start(f32[16,128]{1,0:T(8,128)S(1)} %get-tuple-element.49.mine), channel_id=1, source_target_pairs={{0,4},{1,9},{2,6},{3,11},{4,0},{5,13},{6,2},{7,15},{8,12},{9,1},{1... | collective-permute-start | bytes 24584 | tf_op jit(solution)/shard_map/ppermute | solution.py:85
  29.0 1.7 %collective-permute-start.11 = (f32[16,128]{1,0:T(8,128)S(1)}, f32[16,128]{1,0:T(8,128)S(1)}, u32[]{:S(2)}, u32[]{:S(2)}) collective-permute-start(f32[16,128]{1,0:T(8,128)S(1)} %get-tuple-element.49.mine), channel_id=1, source_target_pairs={{0,13},{1,12},{2,15},{3,14},{4,9},{5,8},{6,11},{7,10},{8,5},{9,4},... | collective-permute-start | bytes 24584 | tf_op jit(solution)/shard_map/ppermute | solution.py:85
  30.7 1.4 %collective-permute-done.10.refs_0_ = f32[16,128]{1,0:T(8,128)S(1)} collective-permute-done((f32[16,128]{1,0:T(8,128)S(1)}, f32[16,128]{1,0:T(8,128)S(1)}, u32[]{:S(2)}, u32[]{:S(2)}) %collective-permute-start.10) | collective-permute-done | bytes 8224 | tf_op jit(solution)/shard_map/ppermute | solution.py:85
  32.1 0.0 collective-permute-start.12
  32.1 1.8 %collective-permute-done.11.refs_1_ = f32[16,128]{1,0:T(8,128)S(1)} collective-permute-done((f32[16,128]{1,0:T(8,128)S(1)}, f32[16,128]{1,0:T(8,128)S(1)}, u32[]{:S(2)}, u32[]{:S(2)}) %collective-permute-start.11) | collective-permute-done | bytes 8224 | tf_op jit(solution)/shard_map/ppermute | solution.py:85
  33.9 0.0 collective-permute-done.12.refs_2_
  33.9 1.3 %last.1 = (f32[32,384]{1,0:T(8,128)}, f32[32,32]{1,0:T(8,128)}) custom-call(f32[32,384]{1,0:T(8,128)S(1)} %get-tuple-element.48.image, f32[16,128]{1,0:T(8,128)S(1)} %get-tuple-element.49.mine, f32[16,128]{1,0:T(8,128)S(1)} %collective-permute-done.10.refs_0_, f32[16,128]{1,0:T(8,128)S(1)} %collective-permute-done.11.refs_1_, ...), custom_call_target="tpu_custom_call" | custom-call | tf_op jit(solution)/shard_map/last/pallas_call | solution.py:434
Async XLA Ops:
  0.6 2.4 %collective-permute-start = (f32[3,3,128,128]{3,2,1,0:T(8,128)}, f32[3,3,128,128]{3,2,1,0:T(8,128)S(1)}, u32[]{:S(2)}, u32[]{:S(2)}) collective-permute-start(f32[3,3,128,128]{3,2,1,0:T(8,128)} %blocks.1), channel_id=1, source_target_pairs={{0,1},{1,0},{2,3},{3,2},{4,5},{5,4},{6,7},{7,6},{8,9},{9,8},{10,11... | collective-permute-start | bytes 1769480 | tf_op jit(solution)/shard_map/ppermute | solution.py:77
  1.1 1.8 %collective-permute-start.1 = (s32[3,3]{1,0:T(4,128)}, s32[3,3]{1,0:T(4,128)S(1)}, u32[]{:S(2)}, u32[]{:S(2)}) collective-permute-start(s32[3,3]{1,0:T(4,128)} %ids.1), channel_id=1, source_target_pairs={{0,1},{1,0},{2,3},{3,2},{4,5},{5,4},{6,7},{7,6},{8,9},{9,8},{10,11... | collective-permute-start | bytes 116 | tf_op jit(solution)/shard_map/ppermute | solution.py:77
  3.4 5.1 %collective-permute-start.2 = (f32[96,128]{1,0:T(8,128)S(1)}, f32[96,128]{1,0:T(8,128)S(1)}, u32[]{:S(2)}, u32[]{:S(2)}) collective-permute-start(f32[96,128]{1,0:T(8,128)S(1)} %get-tuple-element.37), channel_id=1, source_target_pairs={{0,4},{1,9},{2,6},{3,11},{4,0},{5,13},{6,2},{7,15},{8,12},{9,1},{1... | collective-permute-start | bytes 147464 | tf_op jit(solution)/shard_map/ppermute | solution.py:85
  6.4 5.3 %collective-permute-start.3 = (f32[96,128]{1,0:T(8,128)S(1)}, f32[96,128]{1,0:T(8,128)S(1)}, u32[]{:S(2)}, u32[]{:S(2)}) collective-permute-start(f32[96,128]{1,0:T(8,128)S(1)} %get-tuple-element.38), channel_id=1, source_target_pairs={{0,13},{1,12},{2,15},{3,14},{4,9},{5,8},{6,11},{7,10},{8,5},{9,4},... | collective-permute-start | bytes 147464 | tf_op jit(solution)/shard_map/ppermute | solution.py:85
  8.5 3.3 %collective-permute-start.4 = (f32[96,128]{1,0:T(8,128)S(1)}, f32[96,128]{1,0:T(8,128)S(1)}, u32[]{:S(2)}, u32[]{:S(2)}) collective-permute-start(f32[96,128]{1,0:T(8,128)S(1)} %collective-permute-done.2.refs_0_), channel_id=1, source_target_pairs={{0,1},{1,0},{2,3},{3,2},{4,5},{5,4},{6,7},{7,6},{8,9},{9,8},{10,11... | collective-permute-start | bytes 147464 | tf_op jit(solution)/shard_map/ppermute | solution.py:77
  12.2 4.6 %collective-permute-start.5 = (f32[96,128]{1,0:T(8,128)S(1)}, f32[96,128]{1,0:T(8,128)S(1)}, u32[]{:S(2)}, u32[]{:S(2)}) collective-permute-start(f32[96,128]{1,0:T(8,128)S(1)} %first_direct.1.refs_0_), channel_id=1, source_target_pairs={{0,2},{1,3},{2,0},{3,1},{4,6},{5,7},{6,4},{7,5},{8,10},{9,11},{10,... | collective-permute-start | bytes 147464 | tf_op jit(solution)/shard_map/ppermute | solution.py:77
  17.3 4.6 %collective-permute-start.6 = (f32[104,128]{1,0:T(8,128)S(1)}, f32[104,128]{1,0:T(8,128)S(1)}, u32[]{:S(2)}, u32[]{:S(2)}) collective-permute-start(f32[104,128]{1,0:T(8,128)S(1)} %get-tuple-element.41), channel_id=1, source_target_pairs={{0,4},{1,9},{2,6},{3,11},{4,0},{5,13},{6,2},{7,15},{8,12},{9,1},{1... | collective-permute-start | bytes 159752 | tf_op jit(solution)/shard_map/ppermute | solution.py:85
  17.3 6.1 %collective-permute-start.7 = (f32[104,128]{1,0:T(8,128)S(1)}, f32[104,128]{1,0:T(8,128)S(1)}, u32[]{:S(2)}, u32[]{:S(2)}) collective-permute-start(f32[104,128]{1,0:T(8,128)S(1)} %get-tuple-element.42), channel_id=1, source_target_pairs={{0,13},{1,12},{2,15},{3,14},{4,9},{5,8},{6,11},{7,10},{8,5},{9,4},... | collective-permute-start | bytes 159752 | tf_op jit(solution)/shard_map/ppermute | solution.py:85
  21.9 1.5 %collective-permute-start.8 = (f32[104,128]{1,0:T(8,128)S(1)}, f32[104,128]{1,0:T(8,128)S(1)}, u32[]{:S(2)}, u32[]{:S(2)}) collective-permute-start(f32[104,128]{1,0:T(8,128)S(1)} %collective-permute-done.6.refs_0_), channel_id=1, source_target_pairs={{0,1},{1,0},{2,3},{3,2},{4,5},{5,4},{6,7},{7,6},{8,9},{9,8},{10,11... | collective-permute-start | bytes 159752 | tf_op jit(solution)/shard_map/ppermute | solution.py:77
  23.8 4.2 %collective-permute-start.9 = (f32[96,128]{1,0:T(8,128)S(1)}, f32[96,128]{1,0:T(8,128)S(1)}, u32[]{:S(2)}, u32[]{:S(2)}) collective-permute-start(f32[96,128]{1,0:T(8,128)S(1)} %get-tuple-element.47.refs_0_), channel_id=1, source_target_pairs={{0,2},{1,3},{2,0},{3,1},{4,6},{5,7},{6,4},{7,5},{8,10},{9,11},{10,... | collective-permute-start | bytes 147464 | tf_op jit(solution)/shard_map/ppermute | solution.py:77
  28.4 3.7 %collective-permute-start.10 = (f32[16,128]{1,0:T(8,128)S(1)}, f32[16,128]{1,0:T(8,128)S(1)}, u32[]{:S(2)}, u32[]{:S(2)}) collective-permute-start(f32[16,128]{1,0:T(8,128)S(1)} %get-tuple-element.49.mine), channel_id=1, source_target_pairs={{0,4},{1,9},{2,6},{3,11},{4,0},{5,13},{6,2},{7,15},{8,12},{9,1},{1... | collective-permute-start | bytes 24584 | tf_op jit(solution)/shard_map/ppermute | solution.py:85
  29.0 4.9 %collective-permute-start.11 = (f32[16,128]{1,0:T(8,128)S(1)}, f32[16,128]{1,0:T(8,128)S(1)}, u32[]{:S(2)}, u32[]{:S(2)}) collective-permute-start(f32[16,128]{1,0:T(8,128)S(1)} %get-tuple-element.49.mine), channel_id=1, source_target_pairs={{0,13},{1,12},{2,15},{3,14},{4,9},{5,8},{6,11},{7,10},{8,5},{9,4},... | collective-permute-start | bytes 24584 | tf_op jit(solution)/shard_map/ppermute | solution.py:85
  32.1 1.8 %collective-permute-start.12 = (f32[16,128]{1,0:T(8,128)S(1)}, f32[16,128]{1,0:T(8,128)S(1)}, u32[]{:S(2)}, u32[]{:S(2)}) collective-permute-start(f32[16,128]{1,0:T(8,128)S(1)} %collective-permute-done.10.refs_0_), channel_id=1, source_target_pairs={{0,1},{1,0},{2,3},{3,2},{4,5},{5,4},{6,7},{7,6},{8,9},{9,8},{10,11... | collective-permute-start | bytes 24584 | tf_op jit(solution)/shard_map/ppermute | solution.py:77

commit v12 on v11

--- a/solution.py
+++ b/solution.py
@@ -85,15 +85,22 @@
     return lax.ppermute(x, ("row", "nbr"), pairs)
 
 
+def shares(rows, common):
+    rest = [d for d in range(1, rows) if d != common]
+    return list(zip(rest[::2], rest[1::2]))
+
+
 class Place:
-    def __init__(self, rows, block_rows, slots, columns):
+    def __init__(self, rows, block_rows, slots, columns, common=None):
         self.row = lax.axis_index("row")
         self.part = lax.axis_index("nbr")
         self.odd = self.part & 1
         self.block_rows, self.slots = block_rows, slots
         self.first_row = self.row * self.block_rows
-        self.peers = [self.row ^ (k + self.odd) for k in range(1, rows - 1, 2)] + [self.row ^ (rows - 1)]
-        self.others_peers = [self.row ^ (k + 1 - self.odd) for k in range(1, rows - 1, 2)]
+        self.rows, self.common = rows, rows - 1 if common is None else common
+        pairs = shares(rows, self.common)
+        self.peers = [self.row ^ jnp.where(self.odd == 0, a, b) for a, b in pairs] + [self.row ^ self.common]
+        self.others_peers = [self.row ^ jnp.where(self.odd == 0, b, a) for a, b in pairs]
         self.columns = columns
 
     def column(self, ids, m, i, p):
@@ -108,8 +115,10 @@
         return slice(i * self.columns, (i + 1) * self.columns)
 
     def by_distance(self, mine, received, handed):
-        both = [(jnp.where(self.odd == 0, a, b), jnp.where(self.odd == 0, b, a)) for a, b in zip(received, handed)]
-        return [mine] + [x for pair in both for x in pair] + [received[-1]]
+        ordered = {0: mine, self.common: received[-1]}
+        for (even, odd), a, b in zip(shares(self.rows, self.common), received, handed):
+            ordered[even], ordered[odd] = jnp.where(self.odd == 0, a, b), jnp.where(self.odd == 0, b, a)
+        return [ordered[d] for d in range(self.rows)]
 
 
 def stacked_blocks(blocks):
@@ -325,7 +334,7 @@
     half = rows // 2
     received, handed, (basis, ritz) = refs[:half], refs[half : rows - 1], refs[rows - 1 :]
     columns = ritz.shape[0]
-    place = Place(rows, 0, 0, columns)
+    place = Place(rows, 0, 0, columns, rows - 2)
     parts = place.by_distance(mine[...], [m[...] for m in received], [m[...] for m in handed])
     both = unfolded(tree(parts) / total, columns)
     ritz[...] = both[columns:]
@@ -361,9 +370,9 @@
             compiler_params=PARAMS,
         )
 
-    def round_over_rows(messages):
-        received = [swap_rows(m, 2 * k - 1, 2 * k) for k, m in enumerate(messages[:-1], 1)]
-        last = swap_rows(messages[-1], rows - 1, rows - 1, 1)
+    def round_over_rows(messages, common):
+        received = [swap_rows(m, *pair) for m, pair in zip(messages, shares(rows, common))]
+        last = swap_rows(messages[-1], common, common, 1)
         return received + [last] + [swap(m, "nbr", 1) for m in received]
 
     def sum_over_pairs(image):
@@ -392,7 +401,7 @@
         [work],
     )(other, other_ids, counts, tiles, started)
     index = [VMEM, VMEM, SMEM, SMEM, SMEM]
-    arrived = round_over_rows(messages)
+    arrived = round_over_rows(messages, rows - 1)
     deep = 2 * block_rows * slots * size
     wide_row = 2 * slots * size
     direct_pair, direct_low, pair, low, other_ids = call(
@@ -421,7 +430,7 @@
         [flat(tall + extra)] * half + [tile, tile, flat(extra)],
         [work],
     )(pair, low, ids, other_ids, counts, *images)
-    arrived = round_over_rows(messages)
+    arrived = round_over_rows(messages, rows - 1)
     image, gram = call(direct, "second_direct", index + [VMEM] * (rows + 2), [tile, flat(extra)], [work])(
         *parted, own, tiles, *arrived, gram
     )
@@ -430,7 +439,7 @@
     image, both = call(gram_kernel, "gram", [VMEM] * (parts // 2 + 2), [across, flat(2 * extra)])(
         inverse, prior, *images
     )
-    arrived = round_over_rows([both] * half)
+    arrived = round_over_rows([both] * half, rows - 2)
     basis, ritz = call(
         functools.partial(last_kernel, rows, total), "last", [VMEM] * (rows + 1), [across, square]
     )(image, both, *arrived)

time: 35.3 us -> 34.7 us (0.983)
  starting transfers between devices: 12.9 us -> 12 us
    ppermute x6, starting transfers between devices: 8.64 us -> 7.73 us  [swap_rows(): return lax.ppermute(x, ('row', 'nbr'), pairs)]
  transfers between devices with their start and end apart: 13 -> 13, of which waited for: 9 -> 10; matrix products, arithmetic and copies ran while one was open for 0% -> 0% of each run, Pallas kernels for 8% -> 8%
where the time goes in v12:
time: 34.7 us; the launch traced here: 34.5 us
  waiting for transfers between devices  15.5 us (45%)
  starting transfers between devices  12 us (35%)
  Pallas kernels  6.33 us (18%)
  between operations  0.69 us (2%)
    ppermute x6, waiting for transfers between devices, swap_rows(): return lax.ppermute(x, ('row', 'nbr'), pairs)  10.1 us
    ppermute x6, starting transfers between devices, swap_rows(): return lax.ppermute(x, ('row', 'nbr'), pairs)  7.73 us
    ppermute x7, waiting for transfers between devices, swap(): lax.ppermute(x, axis, [(i, i ^ distance) for i in range(lax.axis_size(axi...  5.4 us
    ppermute x7, starting transfers between devices, swap(): lax.ppermute(x, axis, [(i, i ^ distance) for i in range(lax.axis_size(axi...  4.23 us
    pallas_call x1, Pallas kernels, body(): call(functools.partial(last_kernel, rows, total), 'last', [VMEM] * (rows...  1.25 us
    pallas_call x1, Pallas kernels, body(): call(load_kernel, 'load', [HBM] * 4, [jax.ShapeDtypeStruct(blocks.shape,...  1.14 us
    pallas_call x1, Pallas kernels, body(): call(functools.partial(factor_kernel, total), 'factor', [VMEM] * 2, [squa...  0.8 us
  transfers between devices with their start and end apart: 13, of which 10 were waited for; matrix products, arithmetic and copies ran while one was open for 0% of the time, Pallas kernels for 8%

profile of v12, /device:TPU:0, one launch (start us, length us, event | category | flops | bytes accessed | tf_op | source)
XLA Modules:
  0.0 34.5 jit_solution(14250364280098559088)
XLA Ops:
  0.6 0.5 %collective-permute-start = (f32[3,3,128,128]{3,2,1,0:T(8,128)}, f32[3,3,128,128]{3,2,1,0:T(8,128)S(1)}, u32[]{:S(2)}, u32[]{:S(2)}) collective-permute-start(f32[3,3,128,128]{3,2,1,0:T(8,128)} %blocks.1), channel_id=1, source_target_pairs={{0,1},{1,0},{2,3},{3,2},{4,5},{5,4},{6,7},{7,6},{8,9},{9,8},{10,11... | collective-permute-start | bytes 1769480 | tf_op jit(solution)/shard_map/ppermute | solution.py:77
  1.1 0.1 collective-permute-start.1
  1.2 1.1 %load.1 = (f32[3,3,128,128]{3,2,1,0:T(8,128)S(1)}, s32[3,3]{1,0:T(4,128)S(4)}, s32[3]{0:T(128)S(4)}, f32[96,128]{1,0:T(8,128)S(1)}) custom-call(f32[3,3,128,128]{3,2,1,0:T(8,128)} %blocks.1, s32[3,3]{1,0:T(4,128)} %ids.1, s32[3]{0:T(128)} %counts.1, f32[32,384]{1,0:T(8,128)} %bitcast.2), custom_call_target="tpu_custom_call" | custom-call | tf_op jit(solution)/shard_map/load/pallas_call | solution.py:383
  2.4 0.3 own_transposed.1.started
  2.7 0.3 collective-permute-done.1.other_ids
  3.0 0.0 collective-permute-done.other
  3.0 0.4 %first_transposed.1 = (f32[96,128]{1,0:T(8,128)S(1)}, f32[96,128]{1,0:T(8,128)S(1)}, f32[96,128]{1,0:T(8,128)S(1)}) custom-call(f32[3,3,128,128]{3,2,1,0:T(8,128)S(1)} %collective-permute-done.other, s32[3,3]{1,0:T(4,128)S(1)} %collective-permute-done.1.other_ids, s32[3]{0:T(128)S(4)} %get-tuple-element.28.counts, f32[96,128]{1,0:T(8,128)S(1)} %get-tuple-element.29.tiles, ...), custom_call_target="tpu_custom_call" | custom-call | tf_op jit(solution)/shard_map/first_transposed/pallas_call | solution.py:396
  3.4 3.0 %collective-permute-start.2 = (f32[96,128]{1,0:T(8,128)S(1)}, f32[96,128]{1,0:T(8,128)S(1)}, u32[]{:S(2)}, u32[]{:S(2)}) collective-permute-start(f32[96,128]{1,0:T(8,128)S(1)} %get-tuple-element.37), channel_id=1, source_target_pairs={{0,4},{1,9},{2,6},{3,11},{4,0},{5,13},{6,2},{7,15},{8,12},{9,1},{1... | collective-permute-start | bytes 147464 | tf_op jit(solution)/shard_map/ppermute | solution.py:85
  6.4 1.8 %collective-permute-start.3 = (f32[96,128]{1,0:T(8,128)S(1)}, f32[96,128]{1,0:T(8,128)S(1)}, u32[]{:S(2)}, u32[]{:S(2)}) collective-permute-start(f32[96,128]{1,0:T(8,128)S(1)} %get-tuple-element.38), channel_id=1, source_target_pairs={{0,13},{1,12},{2,15},{3,14},{4,9},{5,8},{6,11},{7,10},{8,5},{9,4},... | collective-permute-start | bytes 147464 | tf_op jit(solution)/shard_map/ppermute | solution.py:85
  8.2 0.2 collective-permute-done.2.refs_0_
  8.5 0.5 %collective-permute-start.4 = (f32[96,128]{1,0:T(8,128)S(1)}, f32[96,128]{1,0:T(8,128)S(1)}, u32[]{:S(2)}, u32[]{:S(2)}) collective-permute-start(f32[96,128]{1,0:T(8,128)S(1)} %collective-permute-done.2.refs_0_), channel_id=1, source_target_pairs={{0,1},{1,0},{2,3},{3,2},{4,5},{5,4},{6,7},{7,6},{8,9},{9,8},{10,11... | collective-permute-start | bytes 147464 | tf_op jit(solution)/shard_map/ppermute | solution.py:77
  9.0 0.6 %split.1 = (bf16[2304,256]{1,0:T(8,128)(2,1)S(1)}, bf16[2304,128]{1,0:T(8,128)(2,1)S(1)}, bf16[768,768]{1,0:T(8,128)(2,1)S(1)}, bf16[384,768]{1,0:T(8,128)(2,1)S(1)}, s32[3,3]{1,0:T(4,128)S(4)}) custom-call(f32[3,3,128,128]{3,2,1,0:T(8,128)S(1)} %get-tuple-element.27.held, f32[3,3,128,128]{3,2,1,0:T(8,128)S(1)} %collective-permute-done.other, ...), custom_call_target="tpu_custom_call" | custom-call | tf_op jit(solution)/shard_map/split/pallas_call | solution.py:407
  9.6 2.1 %collective-permute-done.3.refs_1_ = f32[96,128]{1,0:T(8,128)S(1)} collective-permute-done((f32[96,128]{1,0:T(8,128)S(1)}, f32[96,128]{1,0:T(8,128)S(1)}, u32[]{:S(2)}, u32[]{:S(2)}) %collective-permute-start.3) | collective-permute-done | bytes 49184 | tf_op jit(solution)/shard_map/ppermute | solution.py:85
  11.7 0.0 collective-permute-done.4.refs_2_
  11.7 0.4 %first_direct.1.refs_0_ = f32[96,128]{1,0:T(8,128)S(1)} custom-call(bf16[2304,256]{1,0:T(8,128)(2,1)S(1)} %get-tuple-element.32.pair, bf16[2304,128]{1,0:T(8,128)(2,1)S(1)} %get-tuple-element.33.low, s32[3,3]{1,0:T(4,128)S(4)} %get-tuple-element.30.ids, s32[3,3]{1,0:T(4,128)S(4)} %get-tuple-element.34.other_ids, s32[3]{0:T(128)S(4)} %get-tuple-element.28.counts, ...), custom_call_target="tpu_custom_call" | custom-call | tf_op jit(solution)/shard_map/first_direct/pallas_call | solution.py:422
  12.2 1.6 %collective-permute-start.5 = (f32[96,128]{1,0:T(8,128)S(1)}, f32[96,128]{1,0:T(8,128)S(1)}, u32[]{:S(2)}, u32[]{:S(2)}) collective-permute-start(f32[96,128]{1,0:T(8,128)S(1)} %first_direct.1.refs_0_), channel_id=1, source_target_pairs={{0,2},{1,3},{2,0},{3,1},{4,6},{5,7},{6,4},{7,5},{8,10},{9,11},{10,... | collective-permute-start | bytes 147464 | tf_op jit(solution)/shard_map/ppermute | solution.py:77
  13.7 3.0 %collective-permute-done.5.refs_1_ = f32[96,128]{1,0:T(8,128)S(1)} collective-permute-done((f32[96,128]{1,0:T(8,128)S(1)}, f32[96,128]{1,0:T(8,128)S(1)}, u32[]{:S(2)}, u32[]{:S(2)}) %collective-permute-start.5) | collective-permute-done | bytes 49184 | tf_op jit(solution)/shard_map/ppermute | solution.py:77
  16.7 0.5 %second_transposed.1 = (f32[104,128]{1,0:T(8,128)S(1)}, f32[104,128]{1,0:T(8,128)S(1)}, f32[96,128]{1,0:T(8,128)S(1)}, f32[96,128]{1,0:T(8,128)S(1)}, f32[8,128]{1,0:T(8,128)S(1)}) custom-call(bf16[768,768]{1,0:T(8,128)(2,1)S(1)} %get-tuple-element.35.pair, bf16[384,768]{1,0:T(8,128)(2,1)S(1)} %get-tuple-element.36.low, s32[3,3]{1,0:T(4,128)S(4)} %get-tuple-element.30.ids, ...), custom_call_target="tpu_custom_call" | custom-call | tf_op jit(solution)/shard_map/second_transposed/pallas_call | solution.py:426
  17.3 0.1 collective-permute-start.6
  17.3 1.5 %collective-permute-start.7 = (f32[104,128]{1,0:T(8,128)S(1)}, f32[104,128]{1,0:T(8,128)S(1)}, u32[]{:S(2)}, u32[]{:S(2)}) collective-permute-start(f32[104,128]{1,0:T(8,128)S(1)} %get-tuple-element.42), channel_id=1, source_target_pairs={{0,13},{1,12},{2,15},{3,14},{4,9},{5,8},{6,11},{7,10},{8,5},{9,4},... | collective-permute-start | bytes 159752 | tf_op jit(solution)/shard_map/ppermute | solution.py:85
  18.8 3.1 %collective-permute-done.6.refs_0_ = f32[104,128]{1,0:T(8,128)S(1)} collective-permute-done((f32[104,128]{1,0:T(8,128)S(1)}, f32[104,128]{1,0:T(8,128)S(1)}, u32[]{:S(2)}, u32[]{:S(2)}) %collective-permute-start.6) | collective-permute-done | bytes 53280 | tf_op jit(solution)/shard_map/ppermute | solution.py:85
  21.9 0.0 collective-permute-start.8
  21.9 1.5 %collective-permute-done.7.refs_1_ = f32[104,128]{1,0:T(8,128)S(1)} collective-permute-done((f32[104,128]{1,0:T(8,128)S(1)}, f32[104,128]{1,0:T(8,128)S(1)}, u32[]{:S(2)}, u32[]{:S(2)}) %collective-permute-start.7) | collective-permute-done | bytes 53280 | tf_op jit(solution)/shard_map/ppermute | solution.py:85
  23.4 0.0 collective-permute-done.8.refs_2_
  23.4 0.4 %second_direct.1 = (f32[96,128]{1,0:T(8,128)S(1)}, f32[8,128]{1,0:T(8,128)S(1)}) custom-call(bf16[2304,256]{1,0:T(8,128)(2,1)S(1)} %get-tuple-element.32.pair, bf16[2304,128]{1,0:T(8,128)(2,1)S(1)} %get-tuple-element.33.low, s32[3,3]{1,0:T(4,128)S(4)} %get-tuple-element.30.ids, s32[3,3]{1,0:T(4,128)S(4)} %get-tuple-element.34.other_ids, ...), custom_call_target="tpu_custom_call" | custom-call | tf_op jit(solution)/shard_map/second_direct/pallas_call | solution.py:434
  23.8 1.6 %collective-permute-start.9 = (f32[96,128]{1,0:T(8,128)S(1)}, f32[96,128]{1,0:T(8,128)S(1)}, u32[]{:S(2)}, u32[]{:S(2)}) collective-permute-start(f32[96,128]{1,0:T(8,128)S(1)} %get-tuple-element.47.refs_0_), channel_id=1, source_target_pairs={{0,2},{1,3},{2,0},{3,1},{4,6},{5,7},{6,4},{7,5},{8,10},{9,11},{10,... | collective-permute-start | bytes 147464 | tf_op jit(solution)/shard_map/ppermute | solution.py:77
  25.4 0.8 %factor.1 = (f32[32,32]{1,0:T(8,128)S(1)}, f32[32,384]{1,0:T(8,128)S(1)}) custom-call(f32[8,128]{1,0:T(8,128)S(1)} %get-tuple-element.44.gram, f32[96,128]{1,0:T(8,128)S(1)} %get-tuple-element.40.tiles), custom_call_target="tpu_custom_call" | custom-call | tf_op jit(solution)/shard_map/factor/pallas_call | solution.py:438
  26.2 1.8 %collective-permute-done.9.refs_1_ = f32[96,128]{1,0:T(8,128)S(1)} collective-permute-done((f32[96,128]{1,0:T(8,128)S(1)}, f32[96,128]{1,0:T(8,128)S(1)}, u32[]{:S(2)}, u32[]{:S(2)}) %collective-permute-start.9) | collective-permute-done | bytes 49184 | tf_op jit(solution)/shard_map/ppermute | solution.py:77
  27.9 0.5 %gram.1 = (f32[32,384]{1,0:T(8,128)S(1)}, f32[16,128]{1,0:T(8,128)S(1)}) custom-call(f32[32,32]{1,0:T(8,128)S(1)} %get-tuple-element.45.inverse, f32[32,384]{1,0:T(8,128)S(1)} %get-tuple-element.46.prior, f32[96,128]{1,0:T(8,128)S(1)} %get-tuple-element.47.refs_0_, f32[96,128]{1,0:T(8,128)S(1)} %collective-permute-done.9.refs_1_), custom_call_target="tpu_custom_call" | custom-call | tf_op jit(solution)/shard_map/gram/pallas_call | solution.py:439
  28.4 0.6 %collective-permute-start.10 = (f32[16,128]{1,0:T(8,128)S(1)}, f32[16,128]{1,0:T(8,128)S(1)}, u32[]{:S(2)}, u32[]{:S(2)}) collective-permute-start(f32[16,128]{1,0:T(8,128)S(1)} %get-tuple-element.49.mine), channel_id=1, source_target_pairs={{0,4},{1,13},{2,6},{3,15},{4,0},{5,9},{6,2},{7,11},{8,12},{9,5},{1... | collective-permute-start | bytes 24584 | tf_op jit(solution)/shard_map/ppermute | solution.py:85
  29.0 0.8 %collective-permute-start.11 = (f32[16,128]{1,0:T(8,128)S(1)}, f32[16,128]{1,0:T(8,128)S(1)}, u32[]{:S(2)}, u32[]{:S(2)}) collective-permute-start(f32[16,128]{1,0:T(8,128)S(1)} %get-tuple-element.49.mine), channel_id=1, source_target_pairs={{0,9},{1,8},{2,11},{3,10},{4,13},{5,12},{6,15},{7,14},{8,1},{9,0},... | collective-permute-start | bytes 24584 | tf_op jit(solution)/shard_map/ppermute | solution.py:85
  29.8 2.3 %collective-permute-done.10.refs_0_ = f32[16,128]{1,0:T(8,128)S(1)} collective-permute-done((f32[16,128]{1,0:T(8,128)S(1)}, f32[16,128]{1,0:T(8,128)S(1)}, u32[]{:S(2)}, u32[]{:S(2)}) %collective-permute-start.10) | collective-permute-done | bytes 8224 | tf_op jit(solution)/shard_map/ppermute | solution.py:85
  32.1 0.0 collective-permute-start.12
  32.1 0.9 %collective-permute-done.11.refs_1_ = f32[16,128]{1,0:T(8,128)S(1)} collective-permute-done((f32[16,128]{1,0:T(8,128)S(1)}, f32[16,128]{1,0:T(8,128)S(1)}, u32[]{:S(2)}, u32[]{:S(2)}) %collective-permute-start.11) | collective-permute-done | bytes 8224 | tf_op jit(solution)/shard_map/ppermute | solution.py:85
  33.0 0.3 collective-permute-done.12.refs_2_
  33.3 1.3 %last.1 = (f32[32,384]{1,0:T(8,128)}, f32[32,32]{1,0:T(8,128)}) custom-call(f32[32,384]{1,0:T(8,128)S(1)} %get-tuple-element.48.image, f32[16,128]{1,0:T(8,128)S(1)} %get-tuple-element.49.mine, f32[16,128]{1,0:T(8,128)S(1)} %collective-permute-done.10.refs_0_, f32[16,128]{1,0:T(8,128)S(1)} %collective-permute-done.11.refs_1_, ...), custom_call_target="tpu_custom_call" | custom-call | tf_op jit(solution)/shard_map/last/pallas_call | solution.py:443
Async XLA Ops:
  0.6 2.4 %collective-permute-start = (f32[3,3,128,128]{3,2,1,0:T(8,128)}, f32[3,3,128,128]{3,2,1,0:T(8,128)S(1)}, u32[]{:S(2)}, u32[]{:S(2)}) collective-permute-start(f32[3,3,128,128]{3,2,1,0:T(8,128)} %blocks.1), channel_id=1, source_target_pairs={{0,1},{1,0},{2,3},{3,2},{4,5},{5,4},{6,7},{7,6},{8,9},{9,8},{10,11... | collective-permute-start | bytes 1769480 | tf_op jit(solution)/shard_map/ppermute | solution.py:77
  1.1 1.8 %collective-permute-start.1 = (s32[3,3]{1,0:T(4,128)}, s32[3,3]{1,0:T(4,128)S(1)}, u32[]{:S(2)}, u32[]{:S(2)}) collective-permute-start(s32[3,3]{1,0:T(4,128)} %ids.1), channel_id=1, source_target_pairs={{0,1},{1,0},{2,3},{3,2},{4,5},{5,4},{6,7},{7,6},{8,9},{9,8},{10,11... | collective-permute-start | bytes 116 | tf_op jit(solution)/shard_map/ppermute | solution.py:77
  3.4 5.1 %collective-permute-start.2 = (f32[96,128]{1,0:T(8,128)S(1)}, f32[96,128]{1,0:T(8,128)S(1)}, u32[]{:S(2)}, u32[]{:S(2)}) collective-permute-start(f32[96,128]{1,0:T(8,128)S(1)} %get-tuple-element.37), channel_id=1, source_target_pairs={{0,4},{1,9},{2,6},{3,11},{4,0},{5,13},{6,2},{7,15},{8,12},{9,1},{1... | collective-permute-start | bytes 147464 | tf_op jit(solution)/shard_map/ppermute | solution.py:85
  6.4 5.3 %collective-permute-start.3 = (f32[96,128]{1,0:T(8,128)S(1)}, f32[96,128]{1,0:T(8,128)S(1)}, u32[]{:S(2)}, u32[]{:S(2)}) collective-permute-start(f32[96,128]{1,0:T(8,128)S(1)} %get-tuple-element.38), channel_id=1, source_target_pairs={{0,13},{1,12},{2,15},{3,14},{4,9},{5,8},{6,11},{7,10},{8,5},{9,4},... | collective-permute-start | bytes 147464 | tf_op jit(solution)/shard_map/ppermute | solution.py:85
  8.5 3.3 %collective-permute-start.4 = (f32[96,128]{1,0:T(8,128)S(1)}, f32[96,128]{1,0:T(8,128)S(1)}, u32[]{:S(2)}, u32[]{:S(2)}) collective-permute-start(f32[96,128]{1,0:T(8,128)S(1)} %collective-permute-done.2.refs_0_), channel_id=1, source_target_pairs={{0,1},{1,0},{2,3},{3,2},{4,5},{5,4},{6,7},{7,6},{8,9},{9,8},{10,11... | collective-permute-start | bytes 147464 | tf_op jit(solution)/shard_map/ppermute | solution.py:77
  12.2 4.6 %collective-permute-start.5 = (f32[96,128]{1,0:T(8,128)S(1)}, f32[96,128]{1,0:T(8,128)S(1)}, u32[]{:S(2)}, u32[]{:S(2)}) collective-permute-start(f32[96,128]{1,0:T(8,128)S(1)} %first_direct.1.refs_0_), channel_id=1, source_target_pairs={{0,2},{1,3},{2,0},{3,1},{4,6},{5,7},{6,4},{7,5},{8,10},{9,11},{10,... | collective-permute-start | bytes 147464 | tf_op jit(solution)/shard_map/ppermute | solution.py:77
  17.3 4.6 %collective-permute-start.6 = (f32[104,128]{1,0:T(8,128)S(1)}, f32[104,128]{1,0:T(8,128)S(1)}, u32[]{:S(2)}, u32[]{:S(2)}) collective-permute-start(f32[104,128]{1,0:T(8,128)S(1)} %get-tuple-element.41), channel_id=1, source_target_pairs={{0,4},{1,9},{2,6},{3,11},{4,0},{5,13},{6,2},{7,15},{8,12},{9,1},{1... | collective-permute-start | bytes 159752 | tf_op jit(solution)/shard_map/ppermute | solution.py:85
  17.3 6.1 %collective-permute-start.7 = (f32[104,128]{1,0:T(8,128)S(1)}, f32[104,128]{1,0:T(8,128)S(1)}, u32[]{:S(2)}, u32[]{:S(2)}) collective-permute-start(f32[104,128]{1,0:T(8,128)S(1)} %get-tuple-element.42), channel_id=1, source_target_pairs={{0,13},{1,12},{2,15},{3,14},{4,9},{5,8},{6,11},{7,10},{8,5},{9,4},... | collective-permute-start | bytes 159752 | tf_op jit(solution)/shard_map/ppermute | solution.py:85
  21.9 1.5 %collective-permute-start.8 = (f32[104,128]{1,0:T(8,128)S(1)}, f32[104,128]{1,0:T(8,128)S(1)}, u32[]{:S(2)}, u32[]{:S(2)}) collective-permute-start(f32[104,128]{1,0:T(8,128)S(1)} %collective-permute-done.6.refs_0_), channel_id=1, source_target_pairs={{0,1},{1,0},{2,3},{3,2},{4,5},{5,4},{6,7},{7,6},{8,9},{9,8},{10,11... | collective-permute-start | bytes 159752 | tf_op jit(solution)/shard_map/ppermute | solution.py:77
  23.8 4.2 %collective-permute-start.9 = (f32[96,128]{1,0:T(8,128)S(1)}, f32[96,128]{1,0:T(8,128)S(1)}, u32[]{:S(2)}, u32[]{:S(2)}) collective-permute-start(f32[96,128]{1,0:T(8,128)S(1)} %get-tuple-element.47.refs_0_), channel_id=1, source_target_pairs={{0,2},{1,3},{2,0},{3,1},{4,6},{5,7},{6,4},{7,5},{8,10},{9,11},{10,... | collective-permute-start | bytes 147464 | tf_op jit(solution)/shard_map/ppermute | solution.py:77
  28.4 3.7 %collective-permute-start.10 = (f32[16,128]{1,0:T(8,128)S(1)}, f32[16,128]{1,0:T(8,128)S(1)}, u32[]{:S(2)}, u32[]{:S(2)}) collective-permute-start(f32[16,128]{1,0:T(8,128)S(1)} %get-tuple-element.49.mine), channel_id=1, source_target_pairs={{0,4},{1,13},{2,6},{3,15},{4,0},{5,9},{6,2},{7,11},{8,12},{9,5},{1... | collective-permute-start | bytes 24584 | tf_op jit(solution)/shard_map/ppermute | solution.py:85
  29.0 4.0 %collective-permute-start.11 = (f32[16,128]{1,0:T(8,128)S(1)}, f32[16,128]{1,0:T(8,128)S(1)}, u32[]{:S(2)}, u32[]{:S(2)}) collective-permute-start(f32[16,128]{1,0:T(8,128)S(1)} %get-tuple-element.49.mine), channel_id=1, source_target_pairs={{0,9},{1,8},{2,11},{3,10},{4,13},{5,12},{6,15},{7,14},{8,1},{9,0},... | collective-permute-start | bytes 24584 | tf_op jit(solution)/shard_map/ppermute | solution.py:85
  32.1 1.2 %collective-permute-start.12 = (f32[16,128]{1,0:T(8,128)S(1)}, f32[16,128]{1,0:T(8,128)S(1)}, u32[]{:S(2)}, u32[]{:S(2)}) collective-permute-start(f32[16,128]{1,0:T(8,128)S(1)} %collective-permute-done.10.refs_0_), channel_id=1, source_target_pairs={{0,1},{1,0},{2,3},{3,2},{4,5},{5,4},{6,7},{7,6},{8,9},{9,8},{10,11... | collective-permute-start | bytes 24584 | tf_op jit(solution)/shard_map/ppermute | solution.py:77

commit v13 on v12

--- a/solution.py
+++ b/solution.py
@@ -77,11 +77,14 @@
     return lax.ppermute(x, axis, [(i, i ^ distance) for i in range(lax.axis_size(axis))])
 
 
-def swap_rows(x, even, odd, across=0):
+def swap_rows(x, even, odd, across=None, alternate=False):
     rows, parts = lax.axis_size("row"), lax.axis_size("nbr")
-    pairs = [
-        (r * parts + n, (r ^ (odd if n % 2 else even)) * parts + (n ^ across)) for r in range(rows) for n in range(parts)
-    ]
+    pairs = []
+    for r in range(rows):
+        for n in range(parts):
+            d = odd if (n + alternate * bin(r).count("1")) % 2 else even
+            m = n ^ (alternate * bin(d).count("1") % 2 if across is None else across)
+            pairs.append((r * parts + n, (r ^ d) * parts + m))
     return lax.ppermute(x, ("row", "nbr"), pairs)
 
 
@@ -99,8 +102,11 @@
         self.first_row = self.row * self.block_rows
         self.rows, self.common = rows, rows - 1 if common is None else common
         pairs = shares(rows, self.common)
-        self.peers = [self.row ^ jnp.where(self.odd == 0, a, b) for a, b in pairs] + [self.row ^ self.common]
-        self.others_peers = [self.row ^ jnp.where(self.odd == 0, b, a) for a, b in pairs]
+        self.role = self.odd
+        for k in range(0 if common is None else (rows - 1).bit_length()):
+            self.role = self.role ^ ((self.row >> k) & 1)
+        self.peers = [self.row ^ jnp.where(self.role == 0, a, b) for a, b in pairs] + [self.row ^ self.common]
+        self.others_peers = [self.row ^ jnp.where(self.role == 0, b, a) for a, b in pairs]
         self.columns = columns
 
     def column(self, ids, m, i, p):
@@ -117,7 +123,7 @@
     def by_distance(self, mine, received, handed):
         ordered = {0: mine, self.common: received[-1]}
         for (even, odd), a, b in zip(shares(self.rows, self.common), received, handed):
-            ordered[even], ordered[odd] = jnp.where(self.odd == 0, a, b), jnp.where(self.odd == 0, b, a)
+            ordered[even], ordered[odd] = jnp.where(self.role == 0, a, b), jnp.where(self.role == 0, b, a)
         return [ordered[d] for d in range(self.rows)]
 
 
@@ -371,7 +377,7 @@
         )
 
     def round_over_rows(messages, common):
-        received = [swap_rows(m, *pair) for m, pair in zip(messages, shares(rows, common))]
+        received = [swap_rows(m, *pair, alternate=common == rows - 2) for m, pair in zip(messages, shares(rows, common))]
         last = swap_rows(messages[-1], common, common, 1)
         return received + [last] + [swap(m, "nbr", 1) for m in received]
 

time: 34.7 us -> 34.2 us (0.986)
  waiting for transfers between devices: 15.5 us -> 13 us
  starting transfers between devices: 12 us -> 14 us
    ppermute x6, waiting for transfers between devices: 10.1 us -> 7.81 us  [swap_rows(): return lax.ppermute(x, ('row', 'nbr'), pairs)]
    ppermute x6, starting transfers between devices: 7.73 us -> 9.32 us  [swap_rows(): return lax.ppermute(x, ('row', 'nbr'), pairs)]
    ppermute x7, starting transfers between devices: 4.23 us -> 4.72 us  [swap(): lax.ppermute(x, axis, [(i, i ^ distance) for i in range(lax.axis_size(axi...]
where the time goes in v13:
time: 34.2 us; the launch traced here: 34.1 us
  starting transfers between devices  14 us (41%)
  waiting for transfers between devices  13 us (38%)
  Pallas kernels  6.33 us (19%)
  between operations  0.69 us (2%)
    ppermute x6, starting transfers between devices, swap_rows(): return lax.ppermute(x, ('row', 'nbr'), pairs)  9.32 us
    ppermute x6, waiting for transfers between devices, swap_rows(): return lax.ppermute(x, ('row', 'nbr'), pairs)  7.81 us
    ppermute x7, waiting for transfers between devices, swap(): lax.ppermute(x, axis, [(i, i ^ distance) for i in range(lax.axis_size(axi...  5.21 us
    ppermute x7, starting transfers between devices, swap(): lax.ppermute(x, axis, [(i, i ^ distance) for i in range(lax.axis_size(axi...  4.72 us
    pallas_call x1, Pallas kernels, body(): call(functools.partial(last_kernel, rows, total), 'last', [VMEM] * (rows...  1.25 us
    pallas_call x1, Pallas kernels, body(): call(load_kernel, 'load', [HBM] * 4, [jax.ShapeDtypeStruct(blocks.shape,...  1.14 us
    pallas_call x1, Pallas kernels, body(): call(functools.partial(factor_kernel, total), 'factor', [VMEM] * 2, [squa...  0.8 us
  transfers between devices with their start and end apart: 13, of which 10 were waited for; matrix products, arithmetic and copies ran while one was open for 0% of the time, Pallas kernels for 8%

profile of v13, /device:TPU:0, one launch (start us, length us, event | category | flops | bytes accessed | tf_op | source)
XLA Modules:
  0.0 34.1 jit_solution(10975187300652188032)
XLA Ops:
  0.6 0.5 %collective-permute-start = (f32[3,3,128,128]{3,2,1,0:T(8,128)}, f32[3,3,128,128]{3,2,1,0:T(8,128)S(1)}, u32[]{:S(2)}, u32[]{:S(2)}) collective-permute-start(f32[3,3,128,128]{3,2,1,0:T(8,128)} %blocks.1), channel_id=1, source_target_pairs={{0,1},{1,0},{2,3},{3,2},{4,5},{5,4},{6,7},{7,6},{8,9},{9,8},{10,11... | collective-permute-start | bytes 1769480 | tf_op jit(solution)/shard_map/ppermute | solution.py:77
  1.1 0.1 collective-permute-start.1
  1.2 1.1 %load.1 = (f32[3,3,128,128]{3,2,1,0:T(8,128)S(1)}, s32[3,3]{1,0:T(4,128)S(4)}, s32[3]{0:T(128)S(4)}, f32[96,128]{1,0:T(8,128)S(1)}) custom-call(f32[3,3,128,128]{3,2,1,0:T(8,128)} %blocks.1, s32[3,3]{1,0:T(4,128)} %ids.1, s32[3]{0:T(128)} %counts.1, f32[32,384]{1,0:T(8,128)} %bitcast.2), custom_call_target="tpu_custom_call" | custom-call | tf_op jit(solution)/shard_map/load/pallas_call | solution.py:389
  2.4 0.3 own_transposed.1.started
  2.7 0.3 collective-permute-done.1.other_ids
  3.0 0.0 collective-permute-done.other
  3.0 0.4 %first_transposed.1 = (f32[96,128]{1,0:T(8,128)S(1)}, f32[96,128]{1,0:T(8,128)S(1)}, f32[96,128]{1,0:T(8,128)S(1)}) custom-call(f32[3,3,128,128]{3,2,1,0:T(8,128)S(1)} %collective-permute-done.other, s32[3,3]{1,0:T(4,128)S(1)} %collective-permute-done.1.other_ids, s32[3]{0:T(128)S(4)} %get-tuple-element.28.counts, f32[96,128]{1,0:T(8,128)S(1)} %get-tuple-element.29.tiles, ...), custom_call_target="tpu_custom_call" | custom-call | tf_op jit(solution)/shard_map/first_transposed/pallas_call | solution.py:402
  3.4 3.0 %collective-permute-start.2 = (f32[96,128]{1,0:T(8,128)S(1)}, f32[96,128]{1,0:T(8,128)S(1)}, u32[]{:S(2)}, u32[]{:S(2)}) collective-permute-start(f32[96,128]{1,0:T(8,128)S(1)} %get-tuple-element.37), channel_id=1, source_target_pairs={{0,4},{1,9},{2,6},{3,11},{4,0},{5,13},{6,2},{7,15},{8,12},{9,1},{1... | collective-permute-start | bytes 147464 | tf_op jit(solution)/shard_map/ppermute | solution.py:88
  6.4 1.8 %collective-permute-start.3 = (f32[96,128]{1,0:T(8,128)S(1)}, f32[96,128]{1,0:T(8,128)S(1)}, u32[]{:S(2)}, u32[]{:S(2)}) collective-permute-start(f32[96,128]{1,0:T(8,128)S(1)} %get-tuple-element.38), channel_id=1, source_target_pairs={{0,13},{1,12},{2,15},{3,14},{4,9},{5,8},{6,11},{7,10},{8,5},{9,4},... | collective-permute-start | bytes 147464 | tf_op jit(solution)/shard_map/ppermute | solution.py:88
  8.2 0.2 collective-permute-done.2.refs_0_
  8.5 0.5 %collective-permute-start.4 = (f32[96,128]{1,0:T(8,128)S(1)}, f32[96,128]{1,0:T(8,128)S(1)}, u32[]{:S(2)}, u32[]{:S(2)}) collective-permute-start(f32[96,128]{1,0:T(8,128)S(1)} %collective-permute-done.2.refs_0_), channel_id=1, source_target_pairs={{0,1},{1,0},{2,3},{3,2},{4,5},{5,4},{6,7},{7,6},{8,9},{9,8},{10,11... | collective-permute-start | bytes 147464 | tf_op jit(solution)/shard_map/ppermute | solution.py:77
  9.0 0.6 %split.1 = (bf16[2304,256]{1,0:T(8,128)(2,1)S(1)}, bf16[2304,128]{1,0:T(8,128)(2,1)S(1)}, bf16[768,768]{1,0:T(8,128)(2,1)S(1)}, bf16[384,768]{1,0:T(8,128)(2,1)S(1)}, s32[3,3]{1,0:T(4,128)S(4)}) custom-call(f32[3,3,128,128]{3,2,1,0:T(8,128)S(1)} %get-tuple-element.27.held, f32[3,3,128,128]{3,2,1,0:T(8,128)S(1)} %collective-permute-done.other, ...), custom_call_target="tpu_custom_call" | custom-call | tf_op jit(solution)/shard_map/split/pallas_call | solution.py:413
  9.6 2.1 %collective-permute-done.3.refs_1_ = f32[96,128]{1,0:T(8,128)S(1)} collective-permute-done((f32[96,128]{1,0:T(8,128)S(1)}, f32[96,128]{1,0:T(8,128)S(1)}, u32[]{:S(2)}, u32[]{:S(2)}) %collective-permute-start.3) | collective-permute-done | bytes 49184 | tf_op jit(solution)/shard_map/ppermute | solution.py:88
  11.7 0.0 collective-permute-done.4.refs_2_
  11.7 0.4 %first_direct.1.refs_0_ = f32[96,128]{1,0:T(8,128)S(1)} custom-call(bf16[2304,256]{1,0:T(8,128)(2,1)S(1)} %get-tuple-element.32.pair, bf16[2304,128]{1,0:T(8,128)(2,1)S(1)} %get-tuple-element.33.low, s32[3,3]{1,0:T(4,128)S(4)} %get-tuple-element.30.ids, s32[3,3]{1,0:T(4,128)S(4)} %get-tuple-element.34.other_ids, s32[3]{0:T(128)S(4)} %get-tuple-element.28.counts, ...), custom_call_target="tpu_custom_call" | custom-call | tf_op jit(solution)/shard_map/first_direct/pallas_call | solution.py:428
  12.2 1.6 %collective-permute-start.5 = (f32[96,128]{1,0:T(8,128)S(1)}, f32[96,128]{1,0:T(8,128)S(1)}, u32[]{:S(2)}, u32[]{:S(2)}) collective-permute-start(f32[96,128]{1,0:T(8,128)S(1)} %first_direct.1.refs_0_), channel_id=1, source_target_pairs={{0,2},{1,3},{2,0},{3,1},{4,6},{5,7},{6,4},{7,5},{8,10},{9,11},{10,... | collective-permute-start | bytes 147464 | tf_op jit(solution)/shard_map/ppermute | solution.py:77
  13.7 3.0 %collective-permute-done.5.refs_1_ = f32[96,128]{1,0:T(8,128)S(1)} collective-permute-done((f32[96,128]{1,0:T(8,128)S(1)}, f32[96,128]{1,0:T(8,128)S(1)}, u32[]{:S(2)}, u32[]{:S(2)}) %collective-permute-start.5) | collective-permute-done | bytes 49184 | tf_op jit(solution)/shard_map/ppermute | solution.py:77
  16.7 0.5 %second_transposed.1 = (f32[104,128]{1,0:T(8,128)S(1)}, f32[104,128]{1,0:T(8,128)S(1)}, f32[96,128]{1,0:T(8,128)S(1)}, f32[96,128]{1,0:T(8,128)S(1)}, f32[8,128]{1,0:T(8,128)S(1)}) custom-call(bf16[768,768]{1,0:T(8,128)(2,1)S(1)} %get-tuple-element.35.pair, bf16[384,768]{1,0:T(8,128)(2,1)S(1)} %get-tuple-element.36.low, s32[3,3]{1,0:T(4,128)S(4)} %get-tuple-element.30.ids, ...), custom_call_target="tpu_custom_call" | custom-call | tf_op jit(solution)/shard_map/second_transposed/pallas_call | solution.py:432
  17.3 0.1 collective-permute-start.6
  17.3 1.5 %collective-permute-start.7 = (f32[104,128]{1,0:T(8,128)S(1)}, f32[104,128]{1,0:T(8,128)S(1)}, u32[]{:S(2)}, u32[]{:S(2)}) collective-permute-start(f32[104,128]{1,0:T(8,128)S(1)} %get-tuple-element.42), channel_id=1, source_target_pairs={{0,13},{1,12},{2,15},{3,14},{4,9},{5,8},{6,11},{7,10},{8,5},{9,4},... | collective-permute-start | bytes 159752 | tf_op jit(solution)/shard_map/ppermute | solution.py:88
  18.8 3.1 %collective-permute-done.6.refs_0_ = f32[104,128]{1,0:T(8,128)S(1)} collective-permute-done((f32[104,128]{1,0:T(8,128)S(1)}, f32[104,128]{1,0:T(8,128)S(1)}, u32[]{:S(2)}, u32[]{:S(2)}) %collective-permute-start.6) | collective-permute-done | bytes 53280 | tf_op jit(solution)/shard_map/ppermute | solution.py:88
  21.9 0.0 collective-permute-start.8
  21.9 1.5 %collective-permute-done.7.refs_1_ = f32[104,128]{1,0:T(8,128)S(1)} collective-permute-done((f32[104,128]{1,0:T(8,128)S(1)}, f32[104,128]{1,0:T(8,128)S(1)}, u32[]{:S(2)}, u32[]{:S(2)}) %collective-permute-start.7) | collective-permute-done | bytes 53280 | tf_op jit(solution)/shard_map/ppermute | solution.py:88
  23.4 0.0 collective-permute-done.8.refs_2_
  23.4 0.4 %second_direct.1 = (f32[96,128]{1,0:T(8,128)S(1)}, f32[8,128]{1,0:T(8,128)S(1)}) custom-call(bf16[2304,256]{1,0:T(8,128)(2,1)S(1)} %get-tuple-element.32.pair, bf16[2304,128]{1,0:T(8,128)(2,1)S(1)} %get-tuple-element.33.low, s32[3,3]{1,0:T(4,128)S(4)} %get-tuple-element.30.ids, s32[3,3]{1,0:T(4,128)S(4)} %get-tuple-element.34.other_ids, ...), custom_call_target="tpu_custom_call" | custom-call | tf_op jit(solution)/shard_map/second_direct/pallas_call | solution.py:440
  23.8 1.6 %collective-permute-start.9 = (f32[96,128]{1,0:T(8,128)S(1)}, f32[96,128]{1,0:T(8,128)S(1)}, u32[]{:S(2)}, u32[]{:S(2)}) collective-permute-start(f32[96,128]{1,0:T(8,128)S(1)} %get-tuple-element.47.refs_0_), channel_id=1, source_target_pairs={{0,2},{1,3},{2,0},{3,1},{4,6},{5,7},{6,4},{7,5},{8,10},{9,11},{10,... | collective-permute-start | bytes 147464 | tf_op jit(solution)/shard_map/ppermute | solution.py:77
  25.4 0.8 %factor.1 = (f32[32,32]{1,0:T(8,128)S(1)}, f32[32,384]{1,0:T(8,128)S(1)}) custom-call(f32[8,128]{1,0:T(8,128)S(1)} %get-tuple-element.44.gram, f32[96,128]{1,0:T(8,128)S(1)} %get-tuple-element.40.tiles), custom_call_target="tpu_custom_call" | custom-call | tf_op jit(solution)/shard_map/factor/pallas_call | solution.py:444
  26.2 1.8 %collective-permute-done.9.refs_1_ = f32[96,128]{1,0:T(8,128)S(1)} collective-permute-done((f32[96,128]{1,0:T(8,128)S(1)}, f32[96,128]{1,0:T(8,128)S(1)}, u32[]{:S(2)}, u32[]{:S(2)}) %collective-permute-start.9) | collective-permute-done | bytes 49184 | tf_op jit(solution)/shard_map/ppermute | solution.py:77
  28.0 0.5 %gram.1 = (f32[32,384]{1,0:T(8,128)S(1)}, f32[16,128]{1,0:T(8,128)S(1)}) custom-call(f32[32,32]{1,0:T(8,128)S(1)} %get-tuple-element.45.inverse, f32[32,384]{1,0:T(8,128)S(1)} %get-tuple-element.46.prior, f32[96,128]{1,0:T(8,128)S(1)} %get-tuple-element.47.refs_0_, f32[96,128]{1,0:T(8,128)S(1)} %collective-permute-done.9.refs_1_), custom_call_target="tpu_custom_call" | custom-call | tf_op jit(solution)/shard_map/gram/pallas_call | solution.py:445
  28.4 0.1 collective-permute-start.10
  28.6 2.8 %collective-permute-start.11 = (f32[16,128]{1,0:T(8,128)S(1)}, f32[16,128]{1,0:T(8,128)S(1)}, u32[]{:S(2)}, u32[]{:S(2)}) collective-permute-start(f32[16,128]{1,0:T(8,128)S(1)} %get-tuple-element.49.mine), channel_id=1, source_target_pairs={{0,9},{1,8},{2,11},{3,10},{4,13},{5,12},{6,15},{7,14},{8,1},{9,0},... | collective-permute-start | bytes 24584 | tf_op jit(solution)/shard_map/ppermute | solution.py:88
  31.3 0.2 collective-permute-done.10.refs_0_
  31.5 0.5 %collective-permute-start.12 = (f32[16,128]{1,0:T(8,128)S(1)}, f32[16,128]{1,0:T(8,128)S(1)}, u32[]{:S(2)}, u32[]{:S(2)}) collective-permute-start(f32[16,128]{1,0:T(8,128)S(1)} %collective-permute-done.10.refs_0_), channel_id=1, source_target_pairs={{0,1},{1,0},{2,3},{3,2},{4,5},{5,4},{6,7},{7,6},{8,9},{9,8},{10,11... | collective-permute-start | bytes 24584 | tf_op jit(solution)/shard_map/ppermute | solution.py:77
  32.0 0.7 %collective-permute-done.11.refs_1_ = f32[16,128]{1,0:T(8,128)S(1)} collective-permute-done((f32[16,128]{1,0:T(8,128)S(1)}, f32[16,128]{1,0:T(8,128)S(1)}, u32[]{:S(2)}, u32[]{:S(2)}) %collective-permute-start.11) | collective-permute-done | bytes 8224 | tf_op jit(solution)/shard_map/ppermute | solution.py:88
  32.7 0.1 collective-permute-done.12.refs_2_
  32.8 1.3 %last.1 = (f32[32,384]{1,0:T(8,128)}, f32[32,32]{1,0:T(8,128)}) custom-call(f32[32,384]{1,0:T(8,128)S(1)} %get-tuple-element.48.image, f32[16,128]{1,0:T(8,128)S(1)} %get-tuple-element.49.mine, f32[16,128]{1,0:T(8,128)S(1)} %collective-permute-done.10.refs_0_, f32[16,128]{1,0:T(8,128)S(1)} %collective-permute-done.11.refs_1_, ...), custom_call_target="tpu_custom_call" | custom-call | tf_op jit(solution)/shard_map/last/pallas_call | solution.py:449
Async XLA Ops:
  0.6 2.4 %collective-permute-start = (f32[3,3,128,128]{3,2,1,0:T(8,128)}, f32[3,3,128,128]{3,2,1,0:T(8,128)S(1)}, u32[]{:S(2)}, u32[]{:S(2)}) collective-permute-start(f32[3,3,128,128]{3,2,1,0:T(8,128)} %blocks.1), channel_id=1, source_target_pairs={{0,1},{1,0},{2,3},{3,2},{4,5},{5,4},{6,7},{7,6},{8,9},{9,8},{10,11... | collective-permute-start | bytes 1769480 | tf_op jit(solution)/shard_map/ppermute | solution.py:77
  1.1 1.8 %collective-permute-start.1 = (s32[3,3]{1,0:T(4,128)}, s32[3,3]{1,0:T(4,128)S(1)}, u32[]{:S(2)}, u32[]{:S(2)}) collective-permute-start(s32[3,3]{1,0:T(4,128)} %ids.1), channel_id=1, source_target_pairs={{0,1},{1,0},{2,3},{3,2},{4,5},{5,4},{6,7},{7,6},{8,9},{9,8},{10,11... | collective-permute-start | bytes 116 | tf_op jit(solution)/shard_map/ppermute | solution.py:77
  3.4 5.1 %collective-permute-start.2 = (f32[96,128]{1,0:T(8,128)S(1)}, f32[96,128]{1,0:T(8,128)S(1)}, u32[]{:S(2)}, u32[]{:S(2)}) collective-permute-start(f32[96,128]{1,0:T(8,128)S(1)} %get-tuple-element.37), channel_id=1, source_target_pairs={{0,4},{1,9},{2,6},{3,11},{4,0},{5,13},{6,2},{7,15},{8,12},{9,1},{1... | collective-permute-start | bytes 147464 | tf_op jit(solution)/shard_map/ppermute | solution.py:88
  6.4 5.3 %collective-permute-start.3 = (f32[96,128]{1,0:T(8,128)S(1)}, f32[96,128]{1,0:T(8,128)S(1)}, u32[]{:S(2)}, u32[]{:S(2)}) collective-permute-start(f32[96,128]{1,0:T(8,128)S(1)} %get-tuple-element.38), channel_id=1, source_target_pairs={{0,13},{1,12},{2,15},{3,14},{4,9},{5,8},{6,11},{7,10},{8,5},{9,4},... | collective-permute-start | bytes 147464 | tf_op jit(solution)/shard_map/ppermute | solution.py:88
  8.5 3.3 %collective-permute-start.4 = (f32[96,128]{1,0:T(8,128)S(1)}, f32[96,128]{1,0:T(8,128)S(1)}, u32[]{:S(2)}, u32[]{:S(2)}) collective-permute-start(f32[96,128]{1,0:T(8,128)S(1)} %collective-permute-done.2.refs_0_), channel_id=1, source_target_pairs={{0,1},{1,0},{2,3},{3,2},{4,5},{5,4},{6,7},{7,6},{8,9},{9,8},{10,11... | collective-permute-start | bytes 147464 | tf_op jit(solution)/shard_map/ppermute | solution.py:77
  12.2 4.6 %collective-permute-start.5 = (f32[96,128]{1,0:T(8,128)S(1)}, f32[96,128]{1,0:T(8,128)S(1)}, u32[]{:S(2)}, u32[]{:S(2)}) collective-permute-start(f32[96,128]{1,0:T(8,128)S(1)} %first_direct.1.refs_0_), channel_id=1, source_target_pairs={{0,2},{1,3},{2,0},{3,1},{4,6},{5,7},{6,4},{7,5},{8,10},{9,11},{10,... | collective-permute-start | bytes 147464 | tf_op jit(solution)/shard_map/ppermute | solution.py:77
  17.3 4.6 %collective-permute-start.6 = (f32[104,128]{1,0:T(8,128)S(1)}, f32[104,128]{1,0:T(8,128)S(1)}, u32[]{:S(2)}, u32[]{:S(2)}) collective-permute-start(f32[104,128]{1,0:T(8,128)S(1)} %get-tuple-element.41), channel_id=1, source_target_pairs={{0,4},{1,9},{2,6},{3,11},{4,0},{5,13},{6,2},{7,15},{8,12},{9,1},{1... | collective-permute-start | bytes 159752 | tf_op jit(solution)/shard_map/ppermute | solution.py:88
  17.3 6.1 %collective-permute-start.7 = (f32[104,128]{1,0:T(8,128)S(1)}, f32[104,128]{1,0:T(8,128)S(1)}, u32[]{:S(2)}, u32[]{:S(2)}) collective-permute-start(f32[104,128]{1,0:T(8,128)S(1)} %get-tuple-element.42), channel_id=1, source_target_pairs={{0,13},{1,12},{2,15},{3,14},{4,9},{5,8},{6,11},{7,10},{8,5},{9,4},... | collective-permute-start | bytes 159752 | tf_op jit(solution)/shard_map/ppermute | solution.py:88
  21.9 1.5 %collective-permute-start.8 = (f32[104,128]{1,0:T(8,128)S(1)}, f32[104,128]{1,0:T(8,128)S(1)}, u32[]{:S(2)}, u32[]{:S(2)}) collective-permute-start(f32[104,128]{1,0:T(8,128)S(1)} %collective-permute-done.6.refs_0_), channel_id=1, source_target_pairs={{0,1},{1,0},{2,3},{3,2},{4,5},{5,4},{6,7},{7,6},{8,9},{9,8},{10,11... | collective-permute-start | bytes 159752 | tf_op jit(solution)/shard_map/ppermute | solution.py:77
  23.8 4.2 %collective-permute-start.9 = (f32[96,128]{1,0:T(8,128)S(1)}, f32[96,128]{1,0:T(8,128)S(1)}, u32[]{:S(2)}, u32[]{:S(2)}) collective-permute-start(f32[96,128]{1,0:T(8,128)S(1)} %get-tuple-element.47.refs_0_), channel_id=1, source_target_pairs={{0,2},{1,3},{2,0},{3,1},{4,6},{5,7},{6,4},{7,5},{8,10},{9,11},{10,... | collective-permute-start | bytes 147464 | tf_op jit(solution)/shard_map/ppermute | solution.py:77
  28.4 3.1 %collective-permute-start.10 = (f32[16,128]{1,0:T(8,128)S(1)}, f32[16,128]{1,0:T(8,128)S(1)}, u32[]{:S(2)}, u32[]{:S(2)}) collective-permute-start(f32[16,128]{1,0:T(8,128)S(1)} %get-tuple-element.49.mine), channel_id=1, source_target_pairs={{0,5},{1,13},{2,7},{3,15},{4,8},{5,0},{6,10},{7,2},{8,4},{9,12},{1... | collective-permute-start | bytes 24584 | tf_op jit(solution)/shard_map/ppermute | solution.py:88
  28.6 4.1 %collective-permute-start.11 = (f32[16,128]{1,0:T(8,128)S(1)}, f32[16,128]{1,0:T(8,128)S(1)}, u32[]{:S(2)}, u32[]{:S(2)}) collective-permute-start(f32[16,128]{1,0:T(8,128)S(1)} %get-tuple-element.49.mine), channel_id=1, source_target_pairs={{0,9},{1,8},{2,11},{3,10},{4,13},{5,12},{6,15},{7,14},{8,1},{9,0},... | collective-permute-start | bytes 24584 | tf_op jit(solution)/shard_map/ppermute | solution.py:88
  31.5 1.3 %collective-permute-start.12 = (f32[16,128]{1,0:T(8,128)S(1)}, f32[16,128]{1,0:T(8,128)S(1)}, u32[]{:S(2)}, u32[]{:S(2)}) collective-permute-start(f32[16,128]{1,0:T(8,128)S(1)} %collective-permute-done.10.refs_0_), channel_id=1, source_target_pairs={{0,1},{1,0},{2,3},{3,2},{4,5},{5,4},{6,7},{7,6},{8,9},{9,8},{10,11... | collective-permute-start | bytes 24584 | tf_op jit(solution)/shard_map/ppermute | solution.py:77

commit v14 on v13

--- a/solution.py
+++ b/solution.py
@@ -340,7 +340,7 @@
     half = rows // 2
     received, handed, (basis, ritz) = refs[:half], refs[half : rows - 1], refs[rows - 1 :]
     columns = ritz.shape[0]
-    place = Place(rows, 0, 0, columns, rows - 2)
+    place = Place(rows, 0, 0, columns, 1)
     parts = place.by_distance(mine[...], [m[...] for m in received], [m[...] for m in handed])
     both = unfolded(tree(parts) / total, columns)
     ritz[...] = both[columns:]
@@ -377,7 +377,7 @@
         )
 
     def round_over_rows(messages, common):
-        received = [swap_rows(m, *pair, alternate=common == rows - 2) for m, pair in zip(messages, shares(rows, common))]
+        received = [swap_rows(m, *pair, alternate=common == 1) for m, pair in zip(messages, shares(rows, common))]
         last = swap_rows(messages[-1], common, common, 1)
         return received + [last] + [swap(m, "nbr", 1) for m in received]
 
@@ -445,7 +445,7 @@
     image, both = call(gram_kernel, "gram", [VMEM] * (parts // 2 + 2), [across, flat(2 * extra)])(
         inverse, prior, *images
     )
-    arrived = round_over_rows([both] * half, rows - 2)
+    arrived = round_over_rows([both] * half, 1)
     basis, ritz = call(
         functools.partial(last_kernel, rows, total), "last", [VMEM] * (rows + 1), [across, square]
     )(image, both, *arrived)

time: 34.2 us -> 35 us (1.023)
  waiting for transfers between devices: 13 us -> 14.2 us
  starting transfers between devices: 14 us -> 13.6 us
    ppermute x7, waiting for transfers between devices: 5.21 us -> 5.96 us  [swap(): lax.ppermute(x, axis, [(i, i ^ distance) for i in range(lax.axis_size(axi...]
    ppermute x7, starting transfers between devices: 4.72 us -> 4.24 us  [swap(): lax.ppermute(x, axis, [(i, i ^ distance) for i in range(lax.axis_size(axi...]
    ppermute x6, waiting for transfers between devices: 7.81 us -> 8.28 us  [swap_rows(): return lax.ppermute(x, ('row', 'nbr'), pairs)]
where the time goes in v14:
time: 35 us; the launch traced here: 34.8 us
  waiting for transfers between devices  14.2 us (41%)
  starting transfers between devices  13.6 us (39%)
  Pallas kernels  6.33 us (18%)
  between operations  0.69 us (2%)
    ppermute x6, starting transfers between devices, swap_rows(): return lax.ppermute(x, ('row', 'nbr'), pairs)  9.32 us
    ppermute x6, waiting for transfers between devices, swap_rows(): return lax.ppermute(x, ('row', 'nbr'), pairs)  8.28 us
    ppermute x7, waiting for transfers between devices, swap(): lax.ppermute(x, axis, [(i, i ^ distance) for i in range(lax.axis_size(axi...  5.96 us
    ppermute x7, starting transfers between devices, swap(): lax.ppermute(x, axis, [(i, i ^ distance) for i in range(lax.axis_size(axi...  4.24 us
    pallas_call x1, Pallas kernels, body(): call(functools.partial(last_kernel, rows, total), 'last', [VMEM] * (rows...  1.25 us
    pallas_call x1, Pallas kernels, body(): call(load_kernel, 'load', [HBM] * 4, [jax.ShapeDtypeStruct(blocks.shape,...  1.14 us
    pallas_call x1, Pallas kernels, body(): call(functools.partial(factor_kernel, total), 'factor', [VMEM] * 2, [squa...  0.8 us
  transfers between devices with their start and end apart: 13, of which 10 were waited for; matrix products, arithmetic and copies ran while one was open for 0% of the time, Pallas kernels for 8%

profile of v14, /device:TPU:0, one launch (start us, length us, event | category | flops | bytes accessed | tf_op | source)
XLA Modules:
  0.0 34.8 jit_solution(14894369101992423018)
XLA Ops:
  0.6 0.5 %collective-permute-start = (f32[3,3,128,128]{3,2,1,0:T(8,128)}, f32[3,3,128,128]{3,2,1,0:T(8,128)S(1)}, u32[]{:S(2)}, u32[]{:S(2)}) collective-permute-start(f32[3,3,128,128]{3,2,1,0:T(8,128)} %blocks.1), channel_id=1, source_target_pairs={{0,1},{1,0},{2,3},{3,2},{4,5},{5,4},{6,7},{7,6},{8,9},{9,8},{10,11... | collective-permute-start | bytes 1769480 | tf_op jit(solution)/shard_map/ppermute | solution.py:77
  1.1 0.1 collective-permute-start.1
  1.2 1.1 %load.1 = (f32[3,3,128,128]{3,2,1,0:T(8,128)S(1)}, s32[3,3]{1,0:T(4,128)S(4)}, s32[3]{0:T(128)S(4)}, f32[96,128]{1,0:T(8,128)S(1)}) custom-call(f32[3,3,128,128]{3,2,1,0:T(8,128)} %blocks.1, s32[3,3]{1,0:T(4,128)} %ids.1, s32[3]{0:T(128)} %counts.1, f32[32,384]{1,0:T(8,128)} %bitcast.2), custom_call_target="tpu_custom_call" | custom-call | tf_op jit(solution)/shard_map/load/pallas_call | solution.py:389
  2.4 0.3 own_transposed.1.started
  2.7 0.3 collective-permute-done.1.other_ids
  3.0 0.0 collective-permute-done.other
  3.0 0.4 %first_transposed.1 = (f32[96,128]{1,0:T(8,128)S(1)}, f32[96,128]{1,0:T(8,128)S(1)}, f32[96,128]{1,0:T(8,128)S(1)}) custom-call(f32[3,3,128,128]{3,2,1,0:T(8,128)S(1)} %collective-permute-done.other, s32[3,3]{1,0:T(4,128)S(1)} %collective-permute-done.1.other_ids, s32[3]{0:T(128)S(4)} %get-tuple-element.28.counts, f32[96,128]{1,0:T(8,128)S(1)} %get-tuple-element.29.tiles, ...), custom_call_target="tpu_custom_call" | custom-call | tf_op jit(solution)/shard_map/first_transposed/pallas_call | solution.py:402
  3.4 3.0 %collective-permute-start.2 = (f32[96,128]{1,0:T(8,128)S(1)}, f32[96,128]{1,0:T(8,128)S(1)}, u32[]{:S(2)}, u32[]{:S(2)}) collective-permute-start(f32[96,128]{1,0:T(8,128)S(1)} %get-tuple-element.37), channel_id=1, source_target_pairs={{0,4},{1,9},{2,6},{3,11},{4,0},{5,13},{6,2},{7,15},{8,12},{9,1},{1... | collective-permute-start | bytes 147464 | tf_op jit(solution)/shard_map/ppermute | solution.py:88
  6.4 1.8 %collective-permute-start.3 = (f32[96,128]{1,0:T(8,128)S(1)}, f32[96,128]{1,0:T(8,128)S(1)}, u32[]{:S(2)}, u32[]{:S(2)}) collective-permute-start(f32[96,128]{1,0:T(8,128)S(1)} %get-tuple-element.38), channel_id=1, source_target_pairs={{0,13},{1,12},{2,15},{3,14},{4,9},{5,8},{6,11},{7,10},{8,5},{9,4},... | collective-permute-start | bytes 147464 | tf_op jit(solution)/shard_map/ppermute | solution.py:88
  8.2 0.2 collective-permute-done.2.refs_0_
  8.5 0.5 %collective-permute-start.4 = (f32[96,128]{1,0:T(8,128)S(1)}, f32[96,128]{1,0:T(8,128)S(1)}, u32[]{:S(2)}, u32[]{:S(2)}) collective-permute-start(f32[96,128]{1,0:T(8,128)S(1)} %collective-permute-done.2.refs_0_), channel_id=1, source_target_pairs={{0,1},{1,0},{2,3},{3,2},{4,5},{5,4},{6,7},{7,6},{8,9},{9,8},{10,11... | collective-permute-start | bytes 147464 | tf_op jit(solution)/shard_map/ppermute | solution.py:77
  9.0 0.6 %split.1 = (bf16[2304,256]{1,0:T(8,128)(2,1)S(1)}, bf16[2304,128]{1,0:T(8,128)(2,1)S(1)}, bf16[768,768]{1,0:T(8,128)(2,1)S(1)}, bf16[384,768]{1,0:T(8,128)(2,1)S(1)}, s32[3,3]{1,0:T(4,128)S(4)}) custom-call(f32[3,3,128,128]{3,2,1,0:T(8,128)S(1)} %get-tuple-element.27.held, f32[3,3,128,128]{3,2,1,0:T(8,128)S(1)} %collective-permute-done.other, ...), custom_call_target="tpu_custom_call" | custom-call | tf_op jit(solution)/shard_map/split/pallas_call | solution.py:413
  9.6 2.1 %collective-permute-done.3.refs_1_ = f32[96,128]{1,0:T(8,128)S(1)} collective-permute-done((f32[96,128]{1,0:T(8,128)S(1)}, f32[96,128]{1,0:T(8,128)S(1)}, u32[]{:S(2)}, u32[]{:S(2)}) %collective-permute-start.3) | collective-permute-done | bytes 49184 | tf_op jit(solution)/shard_map/ppermute | solution.py:88
  11.7 0.0 collective-permute-done.4.refs_2_
  11.7 0.4 %first_direct.1.refs_0_ = f32[96,128]{1,0:T(8,128)S(1)} custom-call(bf16[2304,256]{1,0:T(8,128)(2,1)S(1)} %get-tuple-element.32.pair, bf16[2304,128]{1,0:T(8,128)(2,1)S(1)} %get-tuple-element.33.low, s32[3,3]{1,0:T(4,128)S(4)} %get-tuple-element.30.ids, s32[3,3]{1,0:T(4,128)S(4)} %get-tuple-element.34.other_ids, s32[3]{0:T(128)S(4)} %get-tuple-element.28.counts, ...), custom_call_target="tpu_custom_call" | custom-call | tf_op jit(solution)/shard_map/first_direct/pallas_call | solution.py:428
  12.2 1.6 %collective-permute-start.5 = (f32[96,128]{1,0:T(8,128)S(1)}, f32[96,128]{1,0:T(8,128)S(1)}, u32[]{:S(2)}, u32[]{:S(2)}) collective-permute-start(f32[96,128]{1,0:T(8,128)S(1)} %first_direct.1.refs_0_), channel_id=1, source_target_pairs={{0,2},{1,3},{2,0},{3,1},{4,6},{5,7},{6,4},{7,5},{8,10},{9,11},{10,... | collective-permute-start | bytes 147464 | tf_op jit(solution)/shard_map/ppermute | solution.py:77
  13.7 3.0 %collective-permute-done.5.refs_1_ = f32[96,128]{1,0:T(8,128)S(1)} collective-permute-done((f32[96,128]{1,0:T(8,128)S(1)}, f32[96,128]{1,0:T(8,128)S(1)}, u32[]{:S(2)}, u32[]{:S(2)}) %collective-permute-start.5) | collective-permute-done | bytes 49184 | tf_op jit(solution)/shard_map/ppermute | solution.py:77
  16.7 0.5 %second_transposed.1 = (f32[104,128]{1,0:T(8,128)S(1)}, f32[104,128]{1,0:T(8,128)S(1)}, f32[96,128]{1,0:T(8,128)S(1)}, f32[96,128]{1,0:T(8,128)S(1)}, f32[8,128]{1,0:T(8,128)S(1)}) custom-call(bf16[768,768]{1,0:T(8,128)(2,1)S(1)} %get-tuple-element.35.pair, bf16[384,768]{1,0:T(8,128)(2,1)S(1)} %get-tuple-element.36.low, s32[3,3]{1,0:T(4,128)S(4)} %get-tuple-element.30.ids, ...), custom_call_target="tpu_custom_call" | custom-call | tf_op jit(solution)/shard_map/second_transposed/pallas_call | solution.py:432
  17.3 0.1 collective-permute-start.6
  17.3 1.5 %collective-permute-start.7 = (f32[104,128]{1,0:T(8,128)S(1)}, f32[104,128]{1,0:T(8,128)S(1)}, u32[]{:S(2)}, u32[]{:S(2)}) collective-permute-start(f32[104,128]{1,0:T(8,128)S(1)} %get-tuple-element.42), channel_id=1, source_target_pairs={{0,13},{1,12},{2,15},{3,14},{4,9},{5,8},{6,11},{7,10},{8,5},{9,4},... | collective-permute-start | bytes 159752 | tf_op jit(solution)/shard_map/ppermute | solution.py:88
  18.8 3.1 %collective-permute-done.6.refs_0_ = f32[104,128]{1,0:T(8,128)S(1)} collective-permute-done((f32[104,128]{1,0:T(8,128)S(1)}, f32[104,128]{1,0:T(8,128)S(1)}, u32[]{:S(2)}, u32[]{:S(2)}) %collective-permute-start.6) | collective-permute-done | bytes 53280 | tf_op jit(solution)/shard_map/ppermute | solution.py:88
  21.9 0.0 collective-permute-start.8
  21.9 1.5 %collective-permute-done.7.refs_1_ = f32[104,128]{1,0:T(8,128)S(1)} collective-permute-done((f32[104,128]{1,0:T(8,128)S(1)}, f32[104,128]{1,0:T(8,128)S(1)}, u32[]{:S(2)}, u32[]{:S(2)}) %collective-permute-start.7) | collective-permute-done | bytes 53280 | tf_op jit(solution)/shard_map/ppermute | solution.py:88
  23.4 0.0 collective-permute-done.8.refs_2_
  23.4 0.4 %second_direct.1 = (f32[96,128]{1,0:T(8,128)S(1)}, f32[8,128]{1,0:T(8,128)S(1)}) custom-call(bf16[2304,256]{1,0:T(8,128)(2,1)S(1)} %get-tuple-element.32.pair, bf16[2304,128]{1,0:T(8,128)(2,1)S(1)} %get-tuple-element.33.low, s32[3,3]{1,0:T(4,128)S(4)} %get-tuple-element.30.ids, s32[3,3]{1,0:T(4,128)S(4)} %get-tuple-element.34.other_ids, ...), custom_call_target="tpu_custom_call" | custom-call | tf_op jit(solution)/shard_map/second_direct/pallas_call | solution.py:440
  23.8 1.6 %collective-permute-start.9 = (f32[96,128]{1,0:T(8,128)S(1)}, f32[96,128]{1,0:T(8,128)S(1)}, u32[]{:S(2)}, u32[]{:S(2)}) collective-permute-start(f32[96,128]{1,0:T(8,128)S(1)} %get-tuple-element.47.refs_0_), channel_id=1, source_target_pairs={{0,2},{1,3},{2,0},{3,1},{4,6},{5,7},{6,4},{7,5},{8,10},{9,11},{10,... | collective-permute-start | bytes 147464 | tf_op jit(solution)/shard_map/ppermute | solution.py:77
  25.4 0.8 %factor.1 = (f32[32,32]{1,0:T(8,128)S(1)}, f32[32,384]{1,0:T(8,128)S(1)}) custom-call(f32[8,128]{1,0:T(8,128)S(1)} %get-tuple-element.44.gram, f32[96,128]{1,0:T(8,128)S(1)} %get-tuple-element.40.tiles), custom_call_target="tpu_custom_call" | custom-call | tf_op jit(solution)/shard_map/factor/pallas_call | solution.py:444
  26.2 1.8 %collective-permute-done.9.refs_1_ = f32[96,128]{1,0:T(8,128)S(1)} collective-permute-done((f32[96,128]{1,0:T(8,128)S(1)}, f32[96,128]{1,0:T(8,128)S(1)}, u32[]{:S(2)}, u32[]{:S(2)}) %collective-permute-start.9) | collective-permute-done | bytes 49184 | tf_op jit(solution)/shard_map/ppermute | solution.py:77
  27.9 0.5 %gram.1 = (f32[32,384]{1,0:T(8,128)S(1)}, f32[16,128]{1,0:T(8,128)S(1)}) custom-call(f32[32,32]{1,0:T(8,128)S(1)} %get-tuple-element.45.inverse, f32[32,384]{1,0:T(8,128)S(1)} %get-tuple-element.46.prior, f32[96,128]{1,0:T(8,128)S(1)} %get-tuple-element.47.refs_0_, f32[96,128]{1,0:T(8,128)S(1)} %collective-permute-done.9.refs_1_), custom_call_target="tpu_custom_call" | custom-call | tf_op jit(solution)/shard_map/gram/pallas_call | solution.py:445
  28.4 0.2 collective-permute-start.10
  28.6 2.7 %collective-permute-start.11 = (f32[16,128]{1,0:T(8,128)S(1)}, f32[16,128]{1,0:T(8,128)S(1)}, u32[]{:S(2)}, u32[]{:S(2)}) collective-permute-start(f32[16,128]{1,0:T(8,128)S(1)} %get-tuple-element.49.mine), channel_id=1, source_target_pairs={{0,5},{1,4},{2,7},{3,6},{4,1},{5,0},{6,3},{7,2},{8,13},{9,12},{10,... | collective-permute-start | bytes 24584 | tf_op jit(solution)/shard_map/ppermute | solution.py:88
  31.3 1.1 %collective-permute-done.10.refs_0_ = f32[16,128]{1,0:T(8,128)S(1)} collective-permute-done((f32[16,128]{1,0:T(8,128)S(1)}, f32[16,128]{1,0:T(8,128)S(1)}, u32[]{:S(2)}, u32[]{:S(2)}) %collective-permute-start.10) | collective-permute-done | bytes 8224 | tf_op jit(solution)/shard_map/ppermute | solution.py:88
  32.4 0.0 collective-permute-start.12
  32.4 0.3 collective-permute-done.11.refs_1_
  32.7 0.9 %collective-permute-done.12.refs_2_ = f32[16,128]{1,0:T(8,128)S(1)} collective-permute-done((f32[16,128]{1,0:T(8,128)S(1)}, f32[16,128]{1,0:T(8,128)S(1)}, u32[]{:S(2)}, u32[]{:S(2)}) %collective-permute-start.12) | collective-permute-done | bytes 8224 | tf_op jit(solution)/shard_map/ppermute | solution.py:77
  33.6 1.3 %last.1 = (f32[32,384]{1,0:T(8,128)}, f32[32,32]{1,0:T(8,128)}) custom-call(f32[32,384]{1,0:T(8,128)S(1)} %get-tuple-element.48.image, f32[16,128]{1,0:T(8,128)S(1)} %get-tuple-element.49.mine, f32[16,128]{1,0:T(8,128)S(1)} %collective-permute-done.10.refs_0_, f32[16,128]{1,0:T(8,128)S(1)} %collective-permute-done.11.refs_1_, ...), custom_call_target="tpu_custom_call" | custom-call | tf_op jit(solution)/shard_map/last/pallas_call | solution.py:449
Async XLA Ops:
  0.6 2.4 %collective-permute-start = (f32[3,3,128,128]{3,2,1,0:T(8,128)}, f32[3,3,128,128]{3,2,1,0:T(8,128)S(1)}, u32[]{:S(2)}, u32[]{:S(2)}) collective-permute-start(f32[3,3,128,128]{3,2,1,0:T(8,128)} %blocks.1), channel_id=1, source_target_pairs={{0,1},{1,0},{2,3},{3,2},{4,5},{5,4},{6,7},{7,6},{8,9},{9,8},{10,11... | collective-permute-start | bytes 1769480 | tf_op jit(solution)/shard_map/ppermute | solution.py:77
  1.1 1.8 %collective-permute-start.1 = (s32[3,3]{1,0:T(4,128)}, s32[3,3]{1,0:T(4,128)S(1)}, u32[]{:S(2)}, u32[]{:S(2)}) collective-permute-start(s32[3,3]{1,0:T(4,128)} %ids.1), channel_id=1, source_target_pairs={{0,1},{1,0},{2,3},{3,2},{4,5},{5,4},{6,7},{7,6},{8,9},{9,8},{10,11... | collective-permute-start | bytes 116 | tf_op jit(solution)/shard_map/ppermute | solution.py:77
  3.4 5.1 %collective-permute-start.2 = (f32[96,128]{1,0:T(8,128)S(1)}, f32[96,128]{1,0:T(8,128)S(1)}, u32[]{:S(2)}, u32[]{:S(2)}) collective-permute-start(f32[96,128]{1,0:T(8,128)S(1)} %get-tuple-element.37), channel_id=1, source_target_pairs={{0,4},{1,9},{2,6},{3,11},{4,0},{5,13},{6,2},{7,15},{8,12},{9,1},{1... | collective-permute-start | bytes 147464 | tf_op jit(solution)/shard_map/ppermute | solution.py:88
  6.4 5.3 %collective-permute-start.3 = (f32[96,128]{1,0:T(8,128)S(1)}, f32[96,128]{1,0:T(8,128)S(1)}, u32[]{:S(2)}, u32[]{:S(2)}) collective-permute-start(f32[96,128]{1,0:T(8,128)S(1)} %get-tuple-element.38), channel_id=1, source_target_pairs={{0,13},{1,12},{2,15},{3,14},{4,9},{5,8},{6,11},{7,10},{8,5},{9,4},... | collective-permute-start | bytes 147464 | tf_op jit(solution)/shard_map/ppermute | solution.py:88
  8.5 3.3 %collective-permute-start.4 = (f32[96,128]{1,0:T(8,128)S(1)}, f32[96,128]{1,0:T(8,128)S(1)}, u32[]{:S(2)}, u32[]{:S(2)}) collective-permute-start(f32[96,128]{1,0:T(8,128)S(1)} %collective-permute-done.2.refs_0_), channel_id=1, source_target_pairs={{0,1},{1,0},{2,3},{3,2},{4,5},{5,4},{6,7},{7,6},{8,9},{9,8},{10,11... | collective-permute-start | bytes 147464 | tf_op jit(solution)/shard_map/ppermute | solution.py:77
  12.2 4.6 %collective-permute-start.5 = (f32[96,128]{1,0:T(8,128)S(1)}, f32[96,128]{1,0:T(8,128)S(1)}, u32[]{:S(2)}, u32[]{:S(2)}) collective-permute-start(f32[96,128]{1,0:T(8,128)S(1)} %first_direct.1.refs_0_), channel_id=1, source_target_pairs={{0,2},{1,3},{2,0},{3,1},{4,6},{5,7},{6,4},{7,5},{8,10},{9,11},{10,... | collective-permute-start | bytes 147464 | tf_op jit(solution)/shard_map/ppermute | solution.py:77
  17.3 4.6 %collective-permute-start.6 = (f32[104,128]{1,0:T(8,128)S(1)}, f32[104,128]{1,0:T(8,128)S(1)}, u32[]{:S(2)}, u32[]{:S(2)}) collective-permute-start(f32[104,128]{1,0:T(8,128)S(1)} %get-tuple-element.41), channel_id=1, source_target_pairs={{0,4},{1,9},{2,6},{3,11},{4,0},{5,13},{6,2},{7,15},{8,12},{9,1},{1... | collective-permute-start | bytes 159752 | tf_op jit(solution)/shard_map/ppermute | solution.py:88
  17.3 6.1 %collective-permute-start.7 = (f32[104,128]{1,0:T(8,128)S(1)}, f32[104,128]{1,0:T(8,128)S(1)}, u32[]{:S(2)}, u32[]{:S(2)}) collective-permute-start(f32[104,128]{1,0:T(8,128)S(1)} %get-tuple-element.42), channel_id=1, source_target_pairs={{0,13},{1,12},{2,15},{3,14},{4,9},{5,8},{6,11},{7,10},{8,5},{9,4},... | collective-permute-start | bytes 159752 | tf_op jit(solution)/shard_map/ppermute | solution.py:88
  21.9 1.5 %collective-permute-start.8 = (f32[104,128]{1,0:T(8,128)S(1)}, f32[104,128]{1,0:T(8,128)S(1)}, u32[]{:S(2)}, u32[]{:S(2)}) collective-permute-start(f32[104,128]{1,0:T(8,128)S(1)} %collective-permute-done.6.refs_0_), channel_id=1, source_target_pairs={{0,1},{1,0},{2,3},{3,2},{4,5},{5,4},{6,7},{7,6},{8,9},{9,8},{10,11... | collective-permute-start | bytes 159752 | tf_op jit(solution)/shard_map/ppermute | solution.py:77
  23.8 4.2 %collective-permute-start.9 = (f32[96,128]{1,0:T(8,128)S(1)}, f32[96,128]{1,0:T(8,128)S(1)}, u32[]{:S(2)}, u32[]{:S(2)}) collective-permute-start(f32[96,128]{1,0:T(8,128)S(1)} %get-tuple-element.47.refs_0_), channel_id=1, source_target_pairs={{0,2},{1,3},{2,0},{3,1},{4,6},{5,7},{6,4},{7,5},{8,10},{9,11},{10,... | collective-permute-start | bytes 147464 | tf_op jit(solution)/shard_map/ppermute | solution.py:77
  28.4 4.0 %collective-permute-start.10 = (f32[16,128]{1,0:T(8,128)S(1)}, f32[16,128]{1,0:T(8,128)S(1)}, u32[]{:S(2)}, u32[]{:S(2)}) collective-permute-start(f32[16,128]{1,0:T(8,128)S(1)} %get-tuple-element.49.mine), channel_id=1, source_target_pairs={{0,9},{1,13},{2,11},{3,15},{4,8},{5,12},{6,10},{7,14},{8,4},{9,0},... | collective-permute-start | bytes 24584 | tf_op jit(solution)/shard_map/ppermute | solution.py:88
  28.6 4.1 %collective-permute-start.11 = (f32[16,128]{1,0:T(8,128)S(1)}, f32[16,128]{1,0:T(8,128)S(1)}, u32[]{:S(2)}, u32[]{:S(2)}) collective-permute-start(f32[16,128]{1,0:T(8,128)S(1)} %get-tuple-element.49.mine), channel_id=1, source_target_pairs={{0,5},{1,4},{2,7},{3,6},{4,1},{5,0},{6,3},{7,2},{8,13},{9,12},{10,... | collective-permute-start | bytes 24584 | tf_op jit(solution)/shard_map/ppermute | solution.py:88
  32.4 1.2 %collective-permute-start.12 = (f32[16,128]{1,0:T(8,128)S(1)}, f32[16,128]{1,0:T(8,128)S(1)}, u32[]{:S(2)}, u32[]{:S(2)}) collective-permute-start(f32[16,128]{1,0:T(8,128)S(1)} %collective-permute-done.10.refs_0_), channel_id=1, source_target_pairs={{0,1},{1,0},{2,3},{3,2},{4,5},{5,4},{6,7},{7,6},{8,9},{9,8},{10,11... | collective-permute-start | bytes 24584 | tf_op jit(solution)/shard_map/ppermute | solution.py:77
